TPU v7x, 32 devices: a whole 2x2x4 slice. The times are simulated.
32 devices in a mesh: fsdp: 8 (over z, y), seq: 4 (over x, core).
Axes of the slice: x: 2, y: 2, z: 4, core: 2. Of those that a mesh axis runs over, the one named last changes fastest.
Arguments:
- inputs: bfloat16 [2, 16, 320, 1024], P(None, 'fsdp', 'seq'), may hold values from -6 to 6
- keep_mask: int32 [2, 16, 320], P(None, 'fsdp'), may hold values from 0 to 1, as said below
- cotangent: bfloat16 [2, 16, 320, 1024], P(None, 'fsdp', 'seq'), may hold values from -6 to 6
- first_gain: bfloat16 [1024], P(('fsdp', 'seq')), may hold values from 0.099609375 to 1.8984375
- first_shift: bfloat16 [1024], P(('fsdp', 'seq')), may hold values from -3 to 3
- qkv_weight: bfloat16 [1024, 3072], P(('fsdp', 'seq')), may hold values from -0.1875 to 0.1875
- query_bias: bfloat16 [1024], P(('fsdp', 'seq')), may hold values from -3 to 3
- value_bias: bfloat16 [1024], P(('fsdp', 'seq')), may hold values from -3 to 3
- out_weight: bfloat16 [1024, 1024], P(('fsdp', 'seq')), may hold values from -0.75 to 0.75
- out_bias: bfloat16 [1024], P(('fsdp', 'seq')), may hold values from -3 to 3
- second_gain: bfloat16 [1024], P(('fsdp', 'seq')), may hold values from 0.099609375 to 1.8984375
- second_shift: bfloat16 [1024], P(('fsdp', 'seq')), may hold values from -3 to 3
- up_weight: bfloat16 [1024, 4096], P(('fsdp', 'seq')), may hold values from -0.1875 to 0.1875
- up_bias: bfloat16 [4096], P(('fsdp', 'seq')), may hold values from -3 to 3
- down_weight: bfloat16 [4096, 1024], P(('fsdp', 'seq')), may hold values from -0.09375 to 0.09375
- down_bias: bfloat16 [1024], P(('fsdp', 'seq')), may hold values from -3 to 3
Outputs:
- layer_out: bfloat16 [2, 16, 320, 1024], P(None, 'fsdp', 'seq')
- input_grad: bfloat16 [2, 16, 320, 1024], P(None, 'fsdp', 'seq')
- first_gain_grad: float32 [1024], P(('fsdp', 'seq'))
- first_shift_grad: float32 [1024], P(('fsdp', 'seq'))
- qkv_weight_grad: float32 [1024, 3072], P(('fsdp', 'seq'))
- query_bias_grad: float32 [1024], P(('fsdp', 'seq'))
- value_bias_grad: float32 [1024], P(('fsdp', 'seq'))
- out_weight_grad: float32 [1024, 1024], P(('fsdp', 'seq'))
- out_bias_grad: float32 [1024], P(('fsdp', 'seq'))
- second_gain_grad: float32 [1024], P(('fsdp', 'seq'))
- second_shift_grad: float32 [1024], P(('fsdp', 'seq'))
- up_weight_grad: float32 [1024, 4096], P(('fsdp', 'seq'))
- up_bias_grad: float32 [4096], P(('fsdp', 'seq'))
- down_weight_grad: float32 [4096, 1024], P(('fsdp', 'seq'))
- down_bias_grad: float32 [1024], P(('fsdp', 'seq'))
Inputs may be any that keep to these rules, and one draw needn't show every extreme that they name: `keep_mask`: in each image, k of its 320 keys are 0, k between 32 and 128, at random places.
All inputs are finite; a program needn't handle non-finite values.
Results may differ from a plain program's by a relative error of at most 0.015.
Values may be sent and summed in bfloat16 or wider, within the bound.
No kernel may reach another device: no remote copies, remote signals or barrier semaphores. Data moves between devices by JAX's collectives and lax.ppermute only.
A program may use at most 256 MiB of HBM per device.

v0:
```python
import jax
import jax.numpy as jnp
from jax import lax
from jax.sharding import PartitionSpec as P

HEADS = 16
HEAD_DIM = 64


negative_fill = -1e30


def layer_norm(values, gain_row, shift_row):
    average = jnp.mean(values, axis=-1, keepdims=True)
    centred = values - average
    spread = jnp.mean(centred * centred, axis=-1, keepdims=True)
    return centred * lax.rsqrt(spread + 1e-06) * gain_row + shift_row


def exact_gelu(values):
    return jax.nn.gelu(values, approximate=False)


def contract_rows(left, right):
    return lax.dot_general(
        left, right, (((0,), (0,)), ((), ())), preferred_element_type=jnp.float32
    )


def contract_cols(left, right):
    return lax.dot_general(
        left, right, (((1,), (1,)), ((), ())), preferred_element_type=jnp.float32
    )


def masked_scores(queries, key_full, keep_row):
    scores = jnp.einsum(
        "nqhe,nkhe->nhqk", queries, key_full, preferred_element_type=jnp.float32
    ) * HEAD_DIM ** (-0.5)
    return jnp.where(keep_row[:, None, None, :] > 0, scores, negative_fill)


def forward_pass(block_rows, keep_row, weights):
    (
        first_gain,
        first_shift,
        qkv_weight,
        query_bias,
        value_bias,
        out_weight,
        out_bias,
        second_gain,
        second_shift,
        up_weight,
        up_bias,
        down_weight,
        down_bias,
    ) = weights
    image_count, token_count, model_width = block_rows.shape
    row_count = image_count * token_count
    source = block_rows.astype(jnp.float32).reshape(row_count, model_width)
    normed_one = layer_norm(
        source, first_gain.astype(jnp.float32), first_shift.astype(jnp.float32)
    ).astype(jnp.bfloat16)
    joined = jnp.dot(normed_one, qkv_weight, preferred_element_type=jnp.float32)
    queries = (joined[:, :model_width] + query_bias.astype(jnp.float32)).astype(jnp.bfloat16)
    key_local = (
        joined[:, model_width : 2 * model_width]
        .astype(jnp.bfloat16)
        .reshape(image_count, token_count, model_width)
    )
    value_local = (joined[:, 2 * model_width :] + value_bias.astype(jnp.float32)).astype(
        jnp.bfloat16
    )
    value_local = value_local.reshape(image_count, token_count, model_width)
    key_full, value_full = (
        lax.all_gather(key_local, "seq", axis=1, tiled=True),
        lax.all_gather(value_local, "seq", axis=1, tiled=True),
    )
    queries4 = queries.reshape(image_count, token_count, HEADS, HEAD_DIM)
    key_full4 = key_full.reshape(image_count, -1, HEADS, HEAD_DIM)
    value_full4 = value_full.reshape(image_count, -1, HEADS, HEAD_DIM)
    scores = masked_scores(queries4, key_full4, keep_row)
    ceiling = jnp.max(scores, axis=-1, keepdims=True)
    exponent = jnp.exp(scores - ceiling)
    total_mass = jnp.sum(exponent, axis=-1, keepdims=True)
    attention_weights = (exponent / total_mass).astype(jnp.bfloat16)
    log_total = ceiling + jnp.log(total_mass)
    attended = jnp.einsum(
        "nhqk,nkhe->nqhe", attention_weights, value_full4, preferred_element_type=jnp.float32
    )
    attended = attended.astype(jnp.bfloat16).reshape(row_count, model_width)
    middle = (
        source
        + jnp.dot(attended, out_weight, preferred_element_type=jnp.float32)
        + out_bias.astype(jnp.float32)
    )
    normed_two = layer_norm(
        middle, second_gain.astype(jnp.float32), second_shift.astype(jnp.float32)
    ).astype(jnp.bfloat16)
    hidden = jnp.dot(normed_two, up_weight, preferred_element_type=jnp.float32) + up_bias.astype(
        jnp.float32
    )
    active = exact_gelu(hidden).astype(jnp.bfloat16)
    result = (
        middle
        + jnp.dot(active, down_weight, preferred_element_type=jnp.float32)
        + down_bias.astype(jnp.float32)
    )
    saved = (
        source,
        normed_one,
        queries4,
        key_local,
        value_local,
        key_full4,
        value_full4,
        log_total,
        attended,
        middle,
        normed_two,
        hidden,
        active,
    )
    return (result.astype(jnp.bfloat16).reshape(image_count, token_count, model_width), saved)


def backward_pass(grad_rows, keep_row, weights, saved, grads):
    (
        first_gain,
        first_shift,
        qkv_weight,
        query_bias,
        value_bias,
        out_weight,
        out_bias,
        second_gain,
        second_shift,
        up_weight,
        up_bias,
        down_weight,
        down_bias,
    ) = weights
    (
        source,
        normed_one,
        queries4,
        key_local,
        value_local,
        key_full4,
        value_full4,
        log_total,
        attended,
        middle,
        normed_two,
        hidden,
        active,
    ) = saved
    image_count, token_count, model_width = grad_rows.shape
    row_count = image_count * token_count
    cot_rows = grad_rows.reshape(row_count, model_width)
    cot_float = cot_rows.astype(jnp.float32)
    grad_active = contract_cols(cot_rows, down_weight)
    _, gelu_pull = jax.vjp(exact_gelu, hidden)
    grad_hidden = gelu_pull(grad_active)[0].astype(jnp.bfloat16)
    grad_two = contract_cols(grad_hidden, up_weight)
    _, second_pull = jax.vjp(
        layer_norm, middle, second_gain.astype(jnp.float32), second_shift.astype(jnp.float32)
    )
    middle_part, second_gain_step, second_shift_step = second_pull(grad_two)
    feed_totals = (
        grads[7] + second_gain_step,
        grads[8] + second_shift_step,
        grads[9] + contract_rows(normed_two, grad_hidden),
        grads[10] + jnp.sum(grad_hidden.astype(jnp.float32), axis=0),
        grads[11] + contract_rows(active, cot_rows),
        grads[12] + jnp.sum(cot_float, axis=0),
    )
    grad_middle = cot_float + middle_part
    grad_branch = grad_middle.astype(jnp.bfloat16)
    projection_totals = (
        grads[5] + contract_rows(attended, grad_branch),
        grads[6] + jnp.sum(grad_branch.astype(jnp.float32), axis=0),
    )
    grad_attended = contract_cols(grad_branch, out_weight).astype(jnp.bfloat16)
    grad_attended4 = grad_attended.reshape(image_count, token_count, HEADS, HEAD_DIM)
    scores = masked_scores(queries4, key_full4, keep_row)
    attention_weights = jnp.exp(scores - log_total)
    grad_values_part = jnp.einsum(
        "nhqk,nqhe->nkhe",
        attention_weights.astype(jnp.bfloat16),
        grad_attended4,
        preferred_element_type=jnp.float32,
    )
    grad_weights = jnp.einsum(
        "nqhe,nkhe->nhqk", grad_attended4, value_full4, preferred_element_type=jnp.float32
    )
    centre_term = jnp.sum(attention_weights * grad_weights, axis=-1, keepdims=True)
    grad_scores = (attention_weights * (grad_weights - centre_term)).astype(jnp.bfloat16)
    grad_queries = jnp.einsum(
        "nhqk,nkhe->nqhe", grad_scores, key_full4, preferred_element_type=jnp.float32
    ) * HEAD_DIM ** (-0.5)
    grad_queries = grad_queries.astype(jnp.bfloat16).reshape(row_count, model_width)
    grad_keys_part = jnp.einsum(
        "nhqk,nqhe->nkhe", grad_scores, queries4, preferred_element_type=jnp.float32
    ) * HEAD_DIM ** (-0.5)
    full_rows = grad_keys_part.shape[1]
    grad_keys_local, grad_values_local = (
        lax.psum_scatter(
            grad_keys_part.reshape(image_count, full_rows, model_width).astype(jnp.bfloat16),
            "seq",
            scatter_dimension=1,
            tiled=True,
        ).astype(jnp.float32),
        lax.psum_scatter(
            grad_values_part.reshape(image_count, full_rows, model_width).astype(jnp.bfloat16),
            "seq",
            scatter_dimension=1,
            tiled=True,
        ).astype(jnp.float32),
    )
    grad_keys = grad_keys_local.astype(jnp.bfloat16).reshape(row_count, model_width)
    grad_values = grad_values_local.astype(jnp.bfloat16).reshape(row_count, model_width)
    grad_joined = jnp.concatenate([grad_queries, grad_keys, grad_values], axis=1)
    grad_one = contract_cols(grad_joined, qkv_weight)
    _, first_pull = jax.vjp(
        layer_norm, source, first_gain.astype(jnp.float32), first_shift.astype(jnp.float32)
    )
    source_part, first_gain_step, first_shift_step = first_pull(grad_one)
    input_rows = (
        (grad_middle + source_part)
        .astype(jnp.bfloat16)
        .reshape(image_count, token_count, model_width)
    )
    input_totals = (
        grads[0] + first_gain_step,
        grads[1] + first_shift_step,
        grads[2] + contract_rows(normed_one, grad_joined),
        grads[3] + jnp.sum(grad_queries.astype(jnp.float32), axis=0),
        grads[4] + jnp.sum(grad_values.astype(jnp.float32), axis=0),
    )
    return (tuple(input_totals) + tuple(projection_totals) + tuple(feed_totals), input_rows)


def on_device(
    inputs,
    keep_mask,
    cotangent,
    first_gain,
    first_shift,
    qkv_weight,
    query_bias,
    value_bias,
    out_weight,
    out_bias,
    second_gain,
    second_shift,
    up_weight,
    up_bias,
    down_weight,
    down_bias,
):
    gathered = (
        lax.all_gather(first_gain, ("fsdp", "seq"), axis=0, tiled=True),
        lax.all_gather(first_shift, ("fsdp", "seq"), axis=0, tiled=True),
        lax.all_gather(qkv_weight, ("fsdp", "seq"), axis=0, tiled=True),
        lax.all_gather(query_bias, ("fsdp", "seq"), axis=0, tiled=True),
        lax.all_gather(value_bias, ("fsdp", "seq"), axis=0, tiled=True),
        lax.all_gather(out_weight, ("fsdp", "seq"), axis=0, tiled=True),
        lax.all_gather(out_bias, ("fsdp", "seq"), axis=0, tiled=True),
        lax.all_gather(second_gain, ("fsdp", "seq"), axis=0, tiled=True),
        lax.all_gather(second_shift, ("fsdp", "seq"), axis=0, tiled=True),
        lax.all_gather(up_weight, ("fsdp", "seq"), axis=0, tiled=True),
        lax.all_gather(up_bias, ("fsdp", "seq"), axis=0, tiled=True),
        lax.all_gather(down_weight, ("fsdp", "seq"), axis=0, tiled=True),
        lax.all_gather(down_bias, ("fsdp", "seq"), axis=0, tiled=True),
    )
    micro_count = inputs.shape[0]
    outputs = []
    kept_states = []
    for micro_index in range(micro_count):
        result, saved = forward_pass(inputs[micro_index], keep_mask[micro_index], gathered)
        outputs.append(result)
        kept_states.append(saved)
    back_weights = (
        lax.all_gather(first_gain, ("fsdp", "seq"), axis=0, tiled=True),
        lax.all_gather(first_shift, ("fsdp", "seq"), axis=0, tiled=True),
        lax.all_gather(qkv_weight, ("fsdp", "seq"), axis=0, tiled=True),
        lax.all_gather(query_bias, ("fsdp", "seq"), axis=0, tiled=True),
        lax.all_gather(value_bias, ("fsdp", "seq"), axis=0, tiled=True),
        lax.all_gather(out_weight, ("fsdp", "seq"), axis=0, tiled=True),
        lax.all_gather(out_bias, ("fsdp", "seq"), axis=0, tiled=True),
        lax.all_gather(second_gain, ("fsdp", "seq"), axis=0, tiled=True),
        lax.all_gather(second_shift, ("fsdp", "seq"), axis=0, tiled=True),
        lax.all_gather(up_weight, ("fsdp", "seq"), axis=0, tiled=True),
        lax.all_gather(up_bias, ("fsdp", "seq"), axis=0, tiled=True),
        lax.all_gather(down_weight, ("fsdp", "seq"), axis=0, tiled=True),
        lax.all_gather(down_bias, ("fsdp", "seq"), axis=0, tiled=True),
    )
    grads = tuple((jnp.zeros(weight.shape, jnp.float32) for weight in back_weights))
    input_parts = []
    for micro_index in range(micro_count):
        grads, input_rows = backward_pass(
            cotangent[micro_index],
            keep_mask[micro_index],
            back_weights,
            kept_states[micro_index],
            grads,
        )
        input_parts.append(input_rows)
    summed = (
        lax.psum_scatter(grads[0], ("fsdp", "seq"), scatter_dimension=0, tiled=True),
        lax.psum_scatter(grads[1], ("fsdp", "seq"), scatter_dimension=0, tiled=True),
        lax.psum_scatter(grads[2], ("fsdp", "seq"), scatter_dimension=0, tiled=True),
        lax.psum_scatter(grads[3], ("fsdp", "seq"), scatter_dimension=0, tiled=True),
        lax.psum_scatter(grads[4], ("fsdp", "seq"), scatter_dimension=0, tiled=True),
        lax.psum_scatter(grads[5], ("fsdp", "seq"), scatter_dimension=0, tiled=True),
        lax.psum_scatter(grads[6], ("fsdp", "seq"), scatter_dimension=0, tiled=True),
        lax.psum_scatter(grads[7], ("fsdp", "seq"), scatter_dimension=0, tiled=True),
        lax.psum_scatter(grads[8], ("fsdp", "seq"), scatter_dimension=0, tiled=True),
        lax.psum_scatter(grads[9], ("fsdp", "seq"), scatter_dimension=0, tiled=True),
        lax.psum_scatter(grads[10], ("fsdp", "seq"), scatter_dimension=0, tiled=True),
        lax.psum_scatter(grads[11], ("fsdp", "seq"), scatter_dimension=0, tiled=True),
        lax.psum_scatter(grads[12], ("fsdp", "seq"), scatter_dimension=0, tiled=True),
    )
    return (jnp.stack(outputs), jnp.stack(input_parts)) + tuple(summed)


def solution(mesh):
    in_specs = (
        P(None, "fsdp", "seq", None),
        P(None, "fsdp", None),
        P(None, "fsdp", "seq", None),
        P(("fsdp", "seq")),
        P(("fsdp", "seq")),
        P(("fsdp", "seq"), None),
        P(("fsdp", "seq")),
        P(("fsdp", "seq")),
        P(("fsdp", "seq"), None),
        P(("fsdp", "seq")),
        P(("fsdp", "seq")),
        P(("fsdp", "seq")),
        P(("fsdp", "seq"), None),
        P(("fsdp", "seq")),
        P(("fsdp", "seq"), None),
        P(("fsdp", "seq")),
    )
    out_specs = (
        P(None, "fsdp", "seq", None),
        P(None, "fsdp", "seq", None),
        P(("fsdp", "seq")),
        P(("fsdp", "seq")),
        P(("fsdp", "seq"), None),
        P(("fsdp", "seq")),
        P(("fsdp", "seq")),
        P(("fsdp", "seq"), None),
        P(("fsdp", "seq")),
        P(("fsdp", "seq")),
        P(("fsdp", "seq")),
        P(("fsdp", "seq"), None),
        P(("fsdp", "seq")),
        P(("fsdp", "seq"), None),
        P(("fsdp", "seq")),
    )
    return jax.shard_map(
        on_device, mesh=mesh, in_specs=in_specs, out_specs=out_specs, check_vma=False
    )
```

profile of v0, /device:TPU:0, one launch (start us, length us, event | category | flops | bytes accessed | tf_op | source)
XLA Modules:
  0.0 1225.8 jit_solution(18119783327986389347)
XLA Ops:
  14.7 42.6 %all-reduce.18 = (bf16[1024]{0:T(1024)(128)(2,1)S(1)}, bf16[1024]{0:T(1024)(128)(2,1)S(1)}, bf16[1024]{0:T(1024)(128)(2,1)S(1)}, bf16[1024]{0:T(1024)(128)(2,1)S...) all-reduce(bf16[1024]{0:T(1024)(128)(2,1)S(1)} %dynamic-update-slic, ...), channel_id=1, replica_groups=mesh['fsdp'=8,'seq'=4] {'fsdp','seq'}, use_global_device_ids=true, to_apply=%add.1 | all-reduce | flops 8192 | bytes 32768
  61.6 21.6 %all-gather.10.cloned.1.call-done = bf16[1024,3072]{1,0:T(8,128)(2,1)} async-done(((bf16[32,3072]{1,0:T(8,128)(2,1)}), bf16[1024,3072]{1,0:T(8,128)(2,1)}) %all-gather.10.cloned.1.call-update) | async-done | bytes 6291472 | tf_op jit(solution)/shard_map/all_gather | solution.py:266
  83.2 4.0 fusion.59
  88.8 4.0 fusion.60
  99.4 39.0 %all-gather = bf16[32,1,128]{2,1,0:T(2,128)(2,1)S(1)} all-gather(bf16[1,1,128]{2,1,0:T(2,128)(2,1)S(1)} %bitcast.166), channel_id=1, replica_groups=mesh['fsdp'=8,'seq'=4] {'fsdp','seq'}, dimensions={0}, use_global_device_ids=true | all-gather | bytes 8448 | tf_op jit(solution)/shard_map/all_gather | solution.py:274
  146.0 2.3 copy.63
  148.4 2.3 fusion.72
  157.3 6.8 all-gather.22.cloned.1.call-done
  173.3 50.0 %all-gather.16.cloned.1.call-done = bf16[1024,1024]{1,0:T(8,128)(2,1)} async-done(((bf16[32,1024]{1,0:T(8,128)(2,1)}), bf16[1024,1024]{1,0:T(8,128)(2,1)}) %all-gather.16.cloned.1.call-update) | async-done | bytes 2097168 | tf_op jit(solution)/shard_map/all_gather | solution.py:269
  223.2 2.5 fusion.73
  228.0 74.4 %all-gather.18.cloned.1.call-done = bf16[1024,4096]{1,0:T(8,128)(2,1)} async-done(((bf16[32,4096]{1,0:T(8,128)(2,1)}), bf16[1024,4096]{1,0:T(8,128)(2,1)}) %all-gather.18.cloned.1.call-update) | async-done | bytes 8388624 | tf_op jit(solution)/shard_map/all_gather | solution.py:273
  302.4 6.6 convolution_add_fusion.4
  309.1 3.2 convolution_add_fusion.3
  312.3 69.1 %all-gather.20.cloned.1.call-done = bf16[4096,1024]{1,0:T(8,128)(2,1)} async-done(((bf16[128,1024]{1,0:T(8,128)(2,1)}), bf16[4096,1024]{1,0:T(8,128)(2,1)}) %all-gather.20.cloned.1.call-update) | async-done | bytes 8388624 | tf_op jit(solution)/shard_map/all_gather | solution.py:275
  381.4 13.1 %convert_reduce_fusion = (f32[4096]{0:T(1024)}, bf16[160,4096]{1,0:T(8,128)(2,1)S(1)}, f32[160,4096]{1,0:T(8,128)}) fusion(f32[160,4096]{1,0:T(8,128)} %convolution_add_fusion.3, bf16[160,1024]{1,0:T(8,128)(2,1)} %bitcast.144, bf16[4096,1024]{1,0:T(8,128)(2,1)} %all-gather.20.cloned.1.call-done), kind=kOutput, calls=%fused_computation.27 | convolution fusion | flops 1390669824 | bytes 15286272 | tf_op jit(solution)/shard_map/dot_general | solution.py:31
  394.4 6.8 fusion.74
  401.3 10.5 convert_reduce_fusion.1
  411.8 3.7 multiply_reduce_fusion.3
  423.0 2.4 copy.71
  425.4 4.2 fusion.24
  429.6 2.5 copy.76
  432.2 4.3 multiply_reduce_fusion.1
  440.5 2.5 copy.74
  449.6 4.0 fusion.27
  453.6 2.6 copy.82
  456.4 3.7 multiply_reduce_fusion
  465.7 2.8 convolution_add_fusion.5
  468.8 3.8 convert_reduce_fusion.2
  472.6 2.4 copy.78
  477.3 3.0 convert_reduce_fusion.3
  483.1 3.3 reduce-scatter.9.cloned.1.call-done
  486.5 7.6 fusion.51
  494.1 21.5 %reduce-scatter.15.cloned.1.call-done = bf16[2,80,1024]{2,1,0:T(8,128)(2,1)} async-done(((bf16[2,320,1024]{2,1,0:T(8,128)(2,1)}), bf16[2,80,1024]{2,1,0:T(8,128)(2,1)}) %reduce-scatter.15.cloned.1.call-update) | async-done | bytes 327696 | tf_op jit(solution)/shard_map/reduce_scatter | solution.py:215
  515.6 29.1 %reduce-scatter.13.cloned.1.call-done = bf16[2,80,1024]{2,1,0:T(8,128)(2,1)} async-done(((bf16[2,320,1024]{2,1,0:T(8,128)(2,1)}), bf16[2,80,1024]{2,1,0:T(8,128)(2,1)}) %reduce-scatter.13.cloned.1.call-update) | async-done | bytes 327696 | tf_op jit(solution)/shard_map/reduce_scatter | solution.py:209
  544.7 11.2 convolution_add_fusion.2
  557.2 2.5 fusion.61
  559.7 9.6 convolution_add_fusion.1
  569.7 3.0 multiply_convert_fusion.5
  572.7 2.4 fusion.76
  576.7 8.2 convolution_add_fusion
  586.9 5.1 fusion.42
  592.1 5.2 fusion.43
  600.6 2.5 fusion.62
  606.3 40.6 %all-reduce.17 = (f32[1024]{0:T(1024)S(1)}, f32[1024]{0:T(1024)S(1)}, f32[1024]{0:T(1024)S(1)}, f32[1024]{0:T(1024)S(1)}, f32[1024]{0:T(1024)S(1)}, /*index=5*/f...) all-reduce(f32[1024]{0:T(1024)S(1)} %add.301, ...), channel_id=6, replica_groups=mesh['fsdp'=8,'seq'=4] {'fsdp','seq'}, use_global_device_ids=true, to_apply=%region_28.29.clone | all-reduce | flops 12288 | bytes 98304
  653.7 35.3 %reduce-scatter.19.cloned.1.call-done = f32[32,1024]{1,0:T(8,128)} async-done(((f32[1024,1024]{1,0:T(8,128)}), f32[32,1024]{1,0:T(8,128)}) %reduce-scatter.19.cloned.1.call-update) | async-done | bytes 131088 | tf_op jit(solution)/shard_map/reduce_scatter | solution.py:317
  689.0 157.8 %reduce-scatter.17.cloned.1.call-done = f32[32,3072]{1,0:T(8,128)} async-done(((f32[1024,3072]{1,0:T(8,128)}), f32[32,3072]{1,0:T(8,128)}) %reduce-scatter.17.cloned.1.call-update) | async-done | bytes 393232 | tf_op jit(solution)/shard_map/reduce_scatter | solution.py:314
  846.8 184.7 %reduce-scatter.21.cloned.1.call-done = f32[32,4096]{1,0:T(8,128)} async-done(((f32[1024,4096]{1,0:T(8,128)}), f32[32,4096]{1,0:T(8,128)}) %reduce-scatter.21.cloned.1.call-update) | async-done | bytes 524304 | tf_op jit(solution)/shard_map/reduce_scatter | solution.py:321
  1031.5 187.3 %reduce-scatter.23.cloned.1.call-done = f32[128,1024]{1,0:T(8,128)} async-done(((f32[4096,1024]{1,0:T(8,128)}), f32[128,1024]{1,0:T(8,128)}) %reduce-scatter.23.cloned.1.call-update) | async-done | bytes 524304 | tf_op jit(solution)/shard_map/reduce_scatter | solution.py:323
  (358 shorter events, 92.1 us)
Async XLA Ops:
  7.2 76.1 %all-gather.10.cloned.1.call-start = ((), (), s32[]{:S(2)}) async-start(), calls=%async_computation.8 | async-start | bytes 6488064 | tf_op jit(solution)/shard_map/all_gather | solution.py:266
  7.9 136.3 %all-gather.14.cloned.1.call-start = ((), (), s32[]{:S(2)}) async-start(), calls=%async_computation.10 | async-start | bytes 1638400 | tf_op jit(solution)/shard_map/all_gather | solution.py:77
  58.6 28.7 %copy-start.79 = (f32[160]{0:T(256)}, f32[160]{0:T(256)S(1)}, u32[]{:S(2)}) copy-start(f32[160]{0:T(256)S(1)} %div.108) | copy-start | bytes 1924
  58.7 28.6 %copy-start.81 = (f32[160]{0:T(256)}, f32[160]{0:T(256)S(1)}, u32[]{:S(2)}) copy-start(f32[160]{0:T(256)S(1)} %div.101) | copy-start | bytes 1924
  60.3 26.9 %copy-start.83 = (f32[160]{0:T(256)}, f32[160]{0:T(256)S(1)}, u32[]{:S(2)}) copy-start(f32[160]{0:T(256)S(1)} %add.265) | copy-start | bytes 1924
  60.3 27.0 %copy-start.63 = (f32[160]{0:T(256)}, f32[160]{0:T(256)S(1)}, u32[]{:S(2)}) copy-start(f32[160]{0:T(256)S(1)} %rsqrt.44) | copy-start | bytes 1924
  61.6 25.7 %copy-start.20 = (f32[160,1024]{1,0:T(8,128)}, f32[160,1024]{1,0:T(8,128)S(1)}, u32[]{:S(2)}) copy-start(f32[160,1024]{1,0:T(8,128)S(1)} %get-tuple-element.72) | copy-start | bytes 1966084
  61.6 27.2 %copy-start.16 = (f32[160,1024]{1,0:T(8,128)}, f32[160,1024]{1,0:T(8,128)S(1)}, u32[]{:S(2)}) copy-start(f32[160,1024]{1,0:T(8,128)S(1)} %get-tuple-element.73) | copy-start | bytes 1966084
  88.1 57.9 %all-gather.12.cloned.1.call-start = ((), (), s32[]{:S(2)}) async-start(), calls=%async_computation.9 | async-start | bytes 1638400 | tf_op jit(solution)/shard_map/all_gather | solution.py:78
  92.9 45.6 %copy-start.91 = (s32[2,2,320]{2,1,0:T(2,128)S(1)}, s32[2,2,320]{2,1,0:T(2,128)}, u32[]{:S(2)}) copy-start(s32[2,2,320]{2,1,0:T(2,128)} %param.17) | copy-start | bytes 15364
  92.9 45.6 %copy-start.49 = (bf16[2,2,80,1024]{3,2,1,0:T(8,128)(2,1)S(1)}, bf16[2,2,80,1024]{3,2,1,0:T(8,128)(2,1)}, u32[]{:S(2)}) copy-start(bf16[2,2,80,1024]{3,2,1,0:T(8,128)(2,1)} %param.18) | copy-start | bytes 1966084
  94.6 44.8 %copy-start.12 = (bf16[2,2,80,1024]{3,2,1,0:T(8,128)(2,1)S(1)}, bf16[2,2,80,1024]{3,2,1,0:T(8,128)(2,1)}, u32[]{:S(2)}) copy-start(bf16[2,2,80,1024]{3,2,1,0:T(8,128)(2,1)} %param.16) | copy-start | bytes 1966084
  94.7 46.0 %copy-start.54 = (bf16[160,1024]{1,0:T(8,128)(2,1)S(1)}, bf16[160,1024]{1,0:T(8,128)(2,1)}, u32[]{:S(2)}) copy-start(bf16[160,1024]{1,0:T(8,128)(2,1)} %get-tuple-element.66) | copy-start | bytes 983044
  94.7 60.8 %all-gather.24.cloned.1.call-start = ((), (), s32[]{:S(2)}) async-start(), calls=%async_computation.15 | async-start | bytes 1638400 | tf_op jit(solution)/shard_map/all_gather | solution.py:77
  96.7 67.4 %all-gather.22.cloned.1.call-start = ((), (), s32[]{:S(2)}) async-start(), calls=%async_computation.14 | async-start | bytes 1638400 | tf_op jit(solution)/shard_map/all_gather | solution.py:78
  97.3 126.0 %all-gather.16.cloned.1.call-start = ((), (), s32[]{:S(2)}) async-start(), calls=%async_computation.11 | async-start | bytes 2162688 | tf_op jit(solution)/shard_map/all_gather | solution.py:269
  97.8 204.6 %all-gather.18.cloned.1.call-start = ((), (), s32[]{:S(2)}) async-start(), calls=%async_computation.12 | async-start | bytes 8650752 | tf_op jit(solution)/shard_map/all_gather | solution.py:273
  98.6 282.8 %all-gather.20.cloned.1.call-start = ((), (), s32[]{:S(2)}) async-start(), calls=%async_computation.13 | async-start | bytes 8650752 | tf_op jit(solution)/shard_map/all_gather | solution.py:275
  99.3 383.8 %reduce-scatter.11.cloned.1.call-start = ((), (), s32[]{:S(2)}) async-start(), calls=%async_computation.17 | async-start | bytes 1638400 | tf_op jit(solution)/shard_map/reduce_scatter | solution.py:215
  157.3 10.9 copy-start.15
  170.2 53.1 %copy-start.40 = (bf16[160,1024]{1,0:T(8,128)(2,1)S(1)}, bf16[160,1024]{1,0:T(8,128)(2,1)}, u32[]{:S(2)}) copy-start(bf16[160,1024]{1,0:T(8,128)(2,1)} %reshape.325) | copy-start | bytes 983044
  225.7 189.8 %copy-start.59 = (f32[160]{0:T(256)}, f32[160]{0:T(256)S(1)}, u32[]{:S(2)}) copy-start(f32[160]{0:T(256)S(1)} %broadcast_multiply_fusion.1) | copy-start | bytes 1924
  227.7 187.9 %copy-start.61 = (f32[160]{0:T(256)}, f32[160]{0:T(256)S(1)}, u32[]{:S(2)}) copy-start(f32[160]{0:T(256)S(1)} %broadcast_multiply_fusion) | copy-start | bytes 1924
  228.0 187.6 %copy-start.67 = (f32[160]{0:T(256)}, f32[160]{0:T(256)S(1)}, u32[]{:S(2)}) copy-start(f32[160]{0:T(256)S(1)} %fusion.53) | copy-start | bytes 1924
  228.0 187.6 %copy-start.65 = (f32[160]{0:T(256)}, f32[160]{0:T(256)S(1)}, u32[]{:S(2)}) copy-start(f32[160]{0:T(256)S(1)} %fusion.54) | copy-start | bytes 1924
  381.4 19.9 %copy-start.5 = (bf16[4096,1024]{1,0:T(8,128)(2,1)S(1)}, bf16[4096,1024]{1,0:T(8,128)(2,1)}, u32[]{:S(2)}) copy-start(bf16[4096,1024]{1,0:T(8,128)(2,1)} %all-gather.20.cloned.1.call-done) | copy-start | bytes 25165828
  394.4 17.4 %slice-start = ((s8[8388608]{0:T(1024)(128)(4,1)}), s8[4194304]{0:T(1024)(128)(4,1)S(1)}, s32[]{:S(2)}) async-start(s8[8388608]{0:T(1024)(128)(4,1)} %bitcast.126), calls=%async_computation.24 | async-start | bytes 8388608
  401.3 10.5 slice-start.1
  416.8 8.5 copy-start.87
  432.1 54.4 %reduce-scatter.9.cloned.1.call-start = ((), (), s32[]{:S(2)}) async-start(), calls=%async_computation.16 | async-start | bytes 1638400 | tf_op jit(solution)/shard_map/reduce_scatter | solution.py:209
  443.1 72.5 %reduce-scatter.15.cloned.1.call-start = ((), (), s32[]{:S(2)}) async-start(), calls=%async_computation.19 | async-start | bytes 1638400 | tf_op jit(solution)/shard_map/reduce_scatter | solution.py:215
  456.3 88.4 %reduce-scatter.13.cloned.1.call-start = ((), (), s32[]{:S(2)}) async-start(), calls=%async_computation.18 | async-start | bytes 1638400 | tf_op jit(solution)/shard_map/reduce_scatter | solution.py:209
  464.6 224.4 %reduce-scatter.19.cloned.1.call-start = ((), (), s32[]{:S(2)}) async-start(), calls=%async_computation.21 | async-start | bytes 4325376 | tf_op jit(solution)/shard_map/reduce_scatter | solution.py:317
  468.6 8.8 copy-start.10
  468.6 378.2 %reduce-scatter.17.cloned.1.call-start = ((), (), s32[]{:S(2)}) async-start(), calls=%async_computation.20 | async-start | bytes 12976128 | tf_op jit(solution)/shard_map/reduce_scatter | solution.py:314
  477.3 9.2 copy-start.64
  486.5 58.2 %copy-start.17 = (f32[160,1024]{1,0:T(8,128)S(1)}, f32[160,1024]{1,0:T(8,128)}, u32[]{:S(2)}) copy-start(f32[160,1024]{1,0:T(8,128)} %copy-done.16) | copy-start | bytes 1966084
  486.5 58.2 %copy-start.51 = (bf16[160,1024]{1,0:T(8,128)(2,1)S(1)}, bf16[160,1024]{1,0:T(8,128)(2,1)}, u32[]{:S(2)}) copy-start(bf16[160,1024]{1,0:T(8,128)(2,1)} %reshape.337) | copy-start | bytes 983044
  486.5 58.2 %copy-start.70 = (f32[160]{0:T(256)S(1)}, f32[160]{0:T(256)}, u32[]{:S(2)}) copy-start(f32[160]{0:T(256)} %copy-done.69) | copy-start | bytes 1924
  556.0 475.6 %reduce-scatter.21.cloned.1.call-start = ((), (), s32[]{:S(2)}) async-start(), calls=%async_computation.22 | async-start | bytes 17301504 | tf_op jit(solution)/shard_map/reduce_scatter | solution.py:321
  569.4 649.4 %reduce-scatter.23.cloned.1.call-start = ((), (), s32[]{:S(2)}) async-start(), calls=%async_computation.23 | async-start | bytes 17301504 | tf_op jit(solution)/shard_map/reduce_scatter | solution.py:323
  586.9 11.3 slice-start.2
  603.2 49.0 %copy-start.28 = (f32[160,1024]{1,0:T(8,128)S(1)}, f32[160,1024]{1,0:T(8,128)}, u32[]{:S(2)}) copy-start(f32[160,1024]{1,0:T(8,128)} %copy-done.27) | copy-start | bytes 1966084
  603.2 49.0 %copy-start.34 = (bf16[1,2,80,1024]{3,2,1,0:T(8,128)(2,1)S(1)}, bf16[1,2,80,1024]{3,2,1,0:T(8,128)(2,1)}, u32[]{:S(2)}) copy-start(bf16[1,2,80,1024]{3,2,1,0:T(8,128)(2,1)} %get-tuple-element.70) | copy-start | bytes 983044
  603.2 49.0 %copy-start.88 = (f32[160]{0:T(256)S(1)}, f32[160]{0:T(256)}, u32[]{:S(2)}) copy-start(f32[160]{0:T(256)} %copy-done.87) | copy-start | bytes 1924
  603.9 48.6 %copy-start.29 = (f32[160,1024]{1,0:T(8,128)S(1)}, f32[160,1024]{1,0:T(8,128)}, u32[]{:S(2)}) copy-start(f32[160,1024]{1,0:T(8,128)} %get-tuple-element.81) | copy-start | bytes 1966084
  603.9 48.6 %copy-start.37 = (bf16[1,2,80,1024]{3,2,1,0:T(8,128)(2,1)S(1)}, bf16[1,2,80,1024]{3,2,1,0:T(8,128)(2,1)}, u32[]{:S(2)}) copy-start(bf16[1,2,80,1024]{3,2,1,0:T(8,128)(2,1)} %get-tuple-element.71) | copy-start | bytes 983044
  603.9 48.6 %copy-start.90 = (f32[160]{0:T(256)S(1)}, f32[160]{0:T(256)}, u32[]{:S(2)}) copy-start(f32[160]{0:T(256)} %copy-done.89) | copy-start | bytes 1924
  (66 other events, 197.6 us)
Sparse Core Ops, SparseCore 0:
  10.9 72.3 all-gather.9
  88.2 16.6 all-gather.13
  106.5 18.2 all-gather.11
  126.2 18.1 all-gather.23
  145.9 18.1 all-gather.21
  166.8 56.3 all-gather.15
  226.1 76.2 all-gather.17
  305.3 76.0 all-gather.19
  432.2 25.1 reduce-scatter.10
  459.9 26.5 reduce-scatter.8
  489.0 26.5 reduce-scatter.14
  518.2 26.5 reduce-scatter.12
  547.6 141.4 reduce-scatter.18
  695.5 151.2 reduce-scatter.16
  849.6 181.8 reduce-scatter.20
  1034.4 184.3 reduce-scatter.22
where the time goes:
time: 1230 us
  waiting for transfers between devices  844 us (69%)
  matrix products  152 us (12%)
  blocking collectives  122 us (10%)
  local copies, waits for them, and re-layouts  64.6 us (5%)
  other arithmetic  25.5 us (2%)
  between operations  15.9 us (1%)
    reduce_scatter x1, waiting for transfers between devices, on_device(): lax.psum_scatter(grads[11], ('fsdp', 'seq'), scatter_dimension=0, tiled=T...  187 us
    reduce_scatter x1, waiting for transfers between devices, on_device(): lax.psum_scatter(grads[9], ('fsdp', 'seq'), scatter_dimension=0, tiled=True)  185 us
    reduce_scatter x1, waiting for transfers between devices, on_device(): lax.psum_scatter(grads[2], ('fsdp', 'seq'), scatter_dimension=0, tiled=True)  158 us
    unnamed x2, blocking collectives  83.2 us
    all_gather x1, waiting for transfers between devices, on_device(): lax.all_gather(up_weight, ('fsdp', 'seq'), axis=0, tiled=True)  74.4 us
    all_gather x1, waiting for transfers between devices, on_device(): lax.all_gather(down_weight, ('fsdp', 'seq'), axis=0, tiled=True)  69.1 us
    all_gather x1, waiting for transfers between devices, on_device(): lax.all_gather(out_weight, ('fsdp', 'seq'), axis=0, tiled=True)  50 us
    dot_general x8, matrix products, contract_rows(): lax.dot_general(left, right, (((0,), (0,)), ((), ())), preferred_element_...  45.1 us
  transfers between devices with their start and end apart: 16, of which 12 were waited for; matrix products, arithmetic and copies ran while one was open for 14% of the time, Pallas kernels for 0%

commit v1 on v0

v1 whole, which is shorter than its diff:
```python
import functools

import jax
import jax.numpy as jnp
from jax import lax
from jax.experimental import pallas as pl
from jax.experimental.pallas import tpu as pltpu
from jax.sharding import PartitionSpec as P

HEADS = 16
HEAD_DIM = 64
SEQ = 4
BF = jnp.bfloat16
F32 = jnp.float32
FILL = -1e30
BOTH = ("fsdp", "seq")


def hop(array, mask):
    return lax.ppermute(array, "seq", [(i, i ^ mask) for i in range(SEQ)])


def by_xor(pieces, place):
    low, high = (place & 1) == 1, (place & 2) == 2
    a, b, c, d = pieces
    a, b, c, d = (
        jnp.where(low, b, a),
        jnp.where(low, a, b),
        jnp.where(low, d, c),
        jnp.where(low, c, d),
    )
    return [
        jnp.where(high, c, a),
        jnp.where(high, d, b),
        jnp.where(high, a, c),
        jnp.where(high, b, d),
    ]


def seq_gather(array):
    far = hop(array, 2)
    return [array, hop(array, 1), far, hop(far, 1)]


def seq_exchange(pieces):
    return [pieces[0]] + [hop(pieces[d], d) for d in (1, 2, 3)]


def seq_scatter(pieces):
    far = pieces[2].astype(F32) + hop(pieces[3], 1).astype(F32)
    arrived = hop(far.astype(pieces[0].dtype), 2)
    near = pieces[0].astype(F32) + hop(pieces[1], 1).astype(F32)
    return near + arrived.astype(F32)


def digits_of(size):
    digits, stride = [], 1
    while stride < size:
        radix = 2 if stride == 1 or size // stride < 4 else 4
        digits.append((stride, radix))
        stride *= radix
    return digits


def shift(array, size, stride, radix, step):
    pairs = []
    for i in range(size):
        digit = i // stride % radix
        pairs.append((i, i + ((digit + step) % radix - digit) * stride))
    return lax.ppermute(array, "fsdp", pairs)


def fsdp_gather(array, size, place):
    pieces = [(array, place)]
    for stride, radix in reversed(digits_of(size)):
        digit = place // stride % radix
        more = []
        for step in range(1, radix):
            change = ((digit + radix - step) % radix - digit) * stride
            for piece, owner in pieces:
                more.append((shift(piece, size, stride, radix, step), owner + change))
        pieces = pieces + more
    out = jnp.zeros((size,) + array.shape, array.dtype)
    for piece, owner in pieces:
        out = lax.dynamic_update_index_in_dim(out, piece, owner, 0)
    return out


def fsdp_scatter(array, size, place):
    kind = array.dtype
    rest = array.shape[1:]
    acc = array
    for stride, radix in digits_of(size):
        digit = place // stride % radix
        outer = acc.shape[0] // radix
        blocks = acc.reshape((outer, radix) + rest)
        mine = lax.dynamic_index_in_dim(blocks, digit, 1, keepdims=False).astype(F32)
        for step in range(1, radix):
            away = lax.dynamic_index_in_dim(
                blocks, (digit + step) % radix, 1, keepdims=False
            ).astype(kind)
            mine = mine + shift(away, size, stride, radix, step).astype(F32)
        acc = mine.astype(kind) if outer > 1 else mine
    return acc.reshape(rest)


def rows_dot(left, right):
    return lax.dot_general(left, right, (((0,), (0,)), ((), ())), preferred_element_type=F32)


def cols_dot(left, right):
    return lax.dot_general(left, right, (((1,), (1,)), ((), ())), preferred_element_type=F32)


def plain_dot(left, right):
    return jnp.dot(left, right, preferred_element_type=F32)


def norm_parts(values):
    average = jnp.mean(values, axis=-1, keepdims=True)
    centred = values - average
    scale = lax.rsqrt(jnp.mean(centred * centred, axis=-1, keepdims=True) + 1e-06)
    return centred * scale, scale


def norm_back(grad, hat, scale, gain):
    spread = grad * gain
    return scale * (
        spread
        - jnp.mean(spread, axis=-1, keepdims=True)
        - hat * jnp.mean(spread * hat, axis=-1, keepdims=True)
    )


def attention_kernel(joined_ref, keep_ref, out0, out1, out2, out3, probs_ref):
    tokens = joined_ref.shape[2]
    rows = SEQ * tokens
    width = joined_ref.shape[3] // 3
    joined = joined_ref[...].reshape(rows, 3 * width)
    keep = keep_ref[0] > 0
    outs = []
    for head in range(width // HEAD_DIM):
        low = head * HEAD_DIM
        q = joined[:, low : low + HEAD_DIM]
        k = joined[:, width + low : width + low + HEAD_DIM]
        v = joined[:, 2 * width + low : 2 * width + low + HEAD_DIM]
        scores = cols_dot(k, q) * HEAD_DIM ** (-0.5)
        scores = jnp.where(keep, scores, FILL)
        top = jnp.max(scores, axis=0, keepdims=True)
        mass = jnp.exp(scores - top)
        probs = (mass / jnp.sum(mass, axis=0, keepdims=True)).astype(BF)
        probs_ref[0, head] = probs
        outs.append(rows_dot(v, probs))
    attended = jnp.concatenate(outs, axis=0).T.astype(BF).reshape(SEQ, tokens, width)
    for at, ref in enumerate((out0, out1, out2, out3)):
        ref[0] = attended[at]


def attention(joined, keep):
    _, images, tokens, triple = joined.shape
    width = triple // 3
    rows = SEQ * tokens
    heads = width // HEAD_DIM
    return pl.pallas_call(
        attention_kernel,
        grid=(images,),
        in_specs=[
            pl.BlockSpec((SEQ, 1, tokens, triple), lambda i: (0, i, 0, 0)),
            pl.BlockSpec((1, rows, 1), lambda i: (i, 0, 0)),
        ],
        out_specs=[pl.BlockSpec((1, tokens, width), lambda i: (i, 0, 0))] * SEQ
        + [pl.BlockSpec((1, heads, rows, rows), lambda i: (i, 0, 0, 0))],
        out_shape=[jax.ShapeDtypeStruct((images, tokens, width), BF)] * SEQ
        + [jax.ShapeDtypeStruct((images, heads, rows, rows), BF)],
        compiler_params=pltpu.CompilerParams(vmem_limit_bytes=40 * 2**20),
    )(joined, keep)


def attention_back_kernel(joined_ref, probs_ref, ga0, ga1, ga2, ga3, out_ref):
    tokens = joined_ref.shape[2]
    rows = SEQ * tokens
    width = joined_ref.shape[3] // 3
    joined = joined_ref[...].reshape(rows, 3 * width)
    grad = jnp.concatenate([ga0[0], ga1[0], ga2[0], ga3[0]], axis=0)
    scale = HEAD_DIM ** (-0.5)
    queries, keys, values = [], [], []
    for head in range(width // HEAD_DIM):
        low = head * HEAD_DIM
        q = joined[:, low : low + HEAD_DIM]
        k = joined[:, width + low : width + low + HEAD_DIM]
        v = joined[:, 2 * width + low : 2 * width + low + HEAD_DIM]
        ga = grad[:, low : low + HEAD_DIM]
        probs = probs_ref[0, head]
        values.append(plain_dot(probs, ga))
        wide = probs.astype(F32)
        grad_probs = cols_dot(v, ga)
        centre = jnp.sum(wide * grad_probs, axis=0, keepdims=True)
        grad_scores = (wide * (grad_probs - centre)).astype(BF)
        keys.append(plain_dot(grad_scores, q) * scale)
        queries.append(rows_dot(k, grad_scores) * scale)
    out_ref[...] = jnp.concatenate(
        [jnp.concatenate(queries, axis=0).T.astype(BF)]
        + [x.astype(BF) for x in keys]
        + [x.astype(BF) for x in values],
        axis=1,
    ).reshape(SEQ, 1, tokens, 3 * width)


def attention_back(joined, probs, grads):
    _, images, tokens, triple = joined.shape
    width = triple // 3
    rows = SEQ * tokens
    heads = width // HEAD_DIM
    return pl.pallas_call(
        attention_back_kernel,
        grid=(images,),
        in_specs=[
            pl.BlockSpec((SEQ, 1, tokens, triple), lambda i: (0, i, 0, 0)),
            pl.BlockSpec((1, heads, rows, rows), lambda i: (i, 0, 0, 0)),
        ]
        + [pl.BlockSpec((1, tokens, width), lambda i: (i, 0, 0))] * SEQ,
        out_specs=pl.BlockSpec((SEQ, 1, tokens, triple), lambda i: (0, i, 0, 0)),
        out_shape=jax.ShapeDtypeStruct(joined.shape, BF),
        compiler_params=pltpu.CompilerParams(vmem_limit_bytes=40 * 2**20),
    )(joined, probs, *grads)


def on_device(
    fsdp,
    inputs,
    keep_mask,
    cotangent,
    first_gain,
    first_shift,
    qkv_weight,
    query_bias,
    value_bias,
    out_weight,
    out_bias,
    second_gain,
    second_shift,
    up_weight,
    up_bias,
    down_weight,
    down_bias,
):
    micros, images, tokens, model = inputs.shape
    rows = images * tokens
    at_f, at_s = lax.axis_index("fsdp"), lax.axis_index("seq")
    depth = qkv_weight.shape[0]
    block = SEQ * depth
    width = model // SEQ
    hidden_block = up_bias.shape[0]
    hidden_part = fsdp * hidden_block
    micro_range = range(micros)

    x_pieces = [seq_gather(inputs[m].reshape(rows, model)) for m in micro_range]

    vectors = jnp.stack(
        [
            first_gain,
            first_shift,
            query_bias,
            value_bias,
            out_bias,
            second_gain,
            second_shift,
            down_bias,
        ]
    )
    count = vectors.shape[0]
    seq_vectors = jnp.stack(by_xor(seq_exchange([vectors] * SEQ), at_s))
    flat = jnp.concatenate([seq_vectors.reshape(-1), up_bias])
    padded = -(-flat.shape[0] // 128) * 128
    small = jnp.pad(flat, (0, padded - flat.shape[0])).reshape(-1, 128)
    small = fsdp_gather(small, fsdp, at_f).reshape(fsdp, padded)
    up_bias_part = small[:, block * count : block * count + hidden_block].reshape(hidden_part)
    full = small[:, : block * count].reshape(fsdp, SEQ, count, depth)
    full = full.transpose(2, 0, 1, 3).reshape(count, model).astype(F32)
    g1, b1, q_bias, v_bias, o_bias, g2, b2, d_bias = [full[i] for i in range(count)]
    q_part = lax.dynamic_slice_in_dim(q_bias, at_s * width, width)
    v_part = lax.dynamic_slice_in_dim(v_bias, at_s * width, width)
    joined_bias = jnp.concatenate([q_part, jnp.zeros_like(q_part), v_part])

    def columns_gather(weight, order):
        parts = [order(weight, s) for s in range(SEQ)]
        arrived = by_xor(seq_exchange(by_xor(parts, at_s)), at_s)
        return fsdp_gather(jnp.concatenate(arrived, axis=0), fsdp, at_f)

    def qkv_order(weight, s):
        return weight.reshape(depth, 3, SEQ, width)[:, :, s].reshape(depth, 3 * width)

    def up_order(weight, s):
        return weight.reshape(depth, fsdp, SEQ, hidden_block)[:, :, s].reshape(depth, hidden_part)

    w_qkv = columns_gather(qkv_weight, qkv_order).reshape(model, 3 * width)
    half = model // 2
    halves = [out_weight[:, :half], out_weight[:, half:]]
    core = at_s & 1
    own_half = jnp.where(core == 1, halves[1], halves[0])
    other_half = jnp.where(core == 1, halves[0], halves[1])
    came = hop(other_half, 1)
    two = jnp.stack([jnp.where(core == 1, came, own_half), jnp.where(core == 1, own_half, came)])
    two_far = hop(two, 2)
    high = at_s >= 2
    four = jnp.concatenate(
        [jnp.where(high, two_far, two), jnp.where(high, two, two_far)], axis=0
    ).reshape(block, half)
    w_out_half = fsdp_gather(four, fsdp, at_f).reshape(model, half)
    w_out_other = hop(w_out_half, 1)
    w_out = jnp.concatenate(
        [
            jnp.where(core == 1, w_out_other, w_out_half),
            jnp.where(core == 1, w_out_half, w_out_other),
        ],
        axis=1,
    )
    w_up = columns_gather(up_weight, up_order).reshape(model, hidden_part)
    w_down = fsdp_gather(down_weight, fsdp, at_f).reshape(hidden_part, model)

    c_pieces = [seq_gather(cotangent[m].reshape(rows, model)) for m in micro_range]

    kept = []
    outputs = []
    for m in micro_range:
        hats = [norm_parts(p.astype(F32)) for p in x_pieces[m]]
        normed_one = jnp.concatenate([(hat * g1 + b1).astype(BF) for hat, _ in hats], axis=0)
        joined = (plain_dot(normed_one, w_qkv) + joined_bias).astype(BF)
        joined = joined.reshape(SEQ, images, tokens, 3 * width)
        keep = keep_mask[m].reshape(images, SEQ, tokens)
        keep = jnp.stack(by_xor([keep[:, s] for s in range(SEQ)], at_s), axis=1)
        *heads_out, probs = attention(joined, keep.reshape(images, SEQ * tokens, 1))
        arrived = seq_exchange([h.reshape(rows, width) for h in heads_out])
        attended = jnp.concatenate(by_xor(arrived, at_s), axis=1)
        middle = x_pieces[m][0].astype(F32) + plain_dot(attended, w_out) + o_bias
        hat_two, scale_two = norm_parts(middle)
        two_pieces = seq_gather((hat_two * g2 + b2).astype(BF))
        normed_two = jnp.concatenate(two_pieces, axis=0)
        hidden = plain_dot(normed_two, w_up) + up_bias_part.astype(F32)
        active = jax.nn.gelu(hidden, approximate=False).astype(BF)
        partial = plain_dot(active, w_down).astype(BF).reshape(SEQ, rows, model)
        result = middle + seq_scatter([partial[d] for d in range(SEQ)]) + d_bias
        outputs.append(result.astype(BF).reshape(images, tokens, model))
        kept.append(
            (hats[0], normed_one, joined, probs, attended, hat_two, scale_two, normed_two, hidden, active)
        )

    stages = []
    inputs_back = []
    small_sums = []
    for m in micro_range:
        hat_one, normed_one, joined, probs, attended, hat_two, scale_two, normed_two, hidden, active = kept[m]
        cot = jnp.concatenate(c_pieces[m], axis=0)
        cot_own = c_pieces[m][0].astype(F32)
        _, pull = jax.vjp(lambda v: jax.nn.gelu(v, approximate=False), hidden)
        grad_hidden = pull(cols_dot(cot, w_down))[0].astype(BF)
        partial = cols_dot(grad_hidden, w_up).astype(BF).reshape(SEQ, rows, model)
        grad_two = seq_scatter([partial[d] for d in range(SEQ)])
        grad_middle = cot_own + norm_back(grad_two, hat_two, scale_two, g2)
        grad_branch = grad_middle.astype(BF)
        grad_attended = cols_dot(grad_branch, w_out).astype(BF)
        parts = [grad_attended[:, s * width : (s + 1) * width] for s in range(SEQ)]
        arrived = seq_exchange(by_xor(parts, at_s))
        grad_joined = attention_back(
            joined, probs, [a.reshape(images, tokens, width) for a in arrived]
        ).reshape(SEQ * rows, 3 * width)
        partial = cols_dot(grad_joined, w_qkv).astype(BF).reshape(SEQ, rows, model)
        grad_one = seq_scatter([partial[d] for d in range(SEQ)])
        grad_input = grad_middle + norm_back(grad_one, hat_one[0], hat_one[1], g1)
        inputs_back.append(grad_input.astype(BF).reshape(images, tokens, model))
        stages.append((normed_one, grad_joined, attended, grad_branch, normed_two, grad_hidden, active, cot))
        sums = lambda v: jnp.sum(v.astype(F32), axis=0)
        small_sums.append(
            (
                sums(grad_one * hat_one[0]),
                sums(grad_one),
                sums(grad_joined[:, :width]),
                sums(grad_joined[:, 2 * width :]),
                sums(grad_branch),
                sums(grad_two * hat_two),
                sums(grad_two),
                sums(cot_own),
                sums(grad_hidden),
            )
        )

    def joint(at):
        return jnp.concatenate([stages[m][at] for m in micro_range], axis=0)

    down_grad = rows_dot(joint(6), joint(7)).astype(BF)
    down_grad = fsdp_scatter(down_grad.reshape(fsdp, hidden_block, model), fsdp, at_f)

    def columns_scatter(grad, order):
        mine = fsdp_scatter(grad.astype(BF).reshape(fsdp, block, grad.shape[1]), fsdp, at_f)
        parts = [mine[s * depth : (s + 1) * depth].astype(BF) for s in range(SEQ)]
        arrived = by_xor(seq_exchange(by_xor(parts, at_s)), at_s)
        return order(jnp.stack(arrived).astype(F32))

    def up_back(parts):
        return parts.reshape(SEQ, depth, fsdp, hidden_block).transpose(1, 2, 0, 3).reshape(depth, -1)

    def qkv_back(parts):
        return parts.reshape(SEQ, depth, 3, width).transpose(1, 2, 0, 3).reshape(depth, -1)

    up_grad = columns_scatter(rows_dot(joint(4), joint(5)), up_back)

    out_grad = rows_dot(joint(2), joint(3)).astype(BF)
    halves = [out_grad[:, :half], out_grad[:, half:]]
    own_half = jnp.where(core == 1, halves[1], halves[0])
    other_half = jnp.where(core == 1, halves[0], halves[1])
    chip_half = (own_half.astype(F32) + hop(other_half, 1).astype(F32)).astype(BF)
    mine = fsdp_scatter(chip_half.reshape(fsdp, block, half), fsdp, at_f).astype(BF)
    mine = mine.reshape(2, 2 * depth, half)
    own_rows = jnp.where(high, mine[1], mine[0])
    other_rows = jnp.where(high, mine[0], mine[1])
    pair = own_rows.astype(F32) + hop(other_rows, 2).astype(F32)
    pair = pair.astype(BF).reshape(2, depth, half)
    own_rows = jnp.where(core == 1, pair[1], pair[0])
    other_rows = hop(jnp.where(core == 1, pair[0], pair[1]), 1)
    out_weight_grad = jnp.concatenate(
        [
            jnp.where(core == 1, other_rows, own_rows),
            jnp.where(core == 1, own_rows, other_rows),
        ],
        axis=1,
    ).astype(F32)

    qkv_grad = columns_scatter(rows_dot(joint(0), joint(1)), qkv_back)

    totals = [sum(parts) for parts in zip(*small_sums)]

    def spread(part):
        return lax.dynamic_update_slice_in_dim(jnp.zeros((model,), F32), part, at_s * width, 0)

    eight = jnp.stack(
        totals[:2] + [spread(totals[2]), spread(totals[3])] + totals[4:8]
    )
    eight = eight.reshape(count, fsdp, SEQ, depth).transpose(2, 1, 0, 3)
    eight = seq_scatter(by_xor([eight[s] for s in range(SEQ)], at_s))
    both = jnp.concatenate(
        [eight.reshape(fsdp, count * depth), totals[8].reshape(fsdp, hidden_block)], axis=1
    )
    both = fsdp_scatter(both, fsdp, at_f)
    vector_grads = both[: count * depth].reshape(count, depth)
    up_bias_grad = both[count * depth :]

    return (
        jnp.stack(outputs),
        jnp.stack(inputs_back),
        vector_grads[0],
        vector_grads[1],
        qkv_grad,
        vector_grads[2],
        vector_grads[3],
        out_weight_grad,
        vector_grads[4],
        vector_grads[5],
        vector_grads[6],
        up_grad,
        up_bias_grad,
        down_grad,
        vector_grads[7],
    )


def solution(mesh):
    shard = P(BOTH)
    tokens = P(None, "fsdp", "seq", None)
    in_specs = (tokens, P(None, "fsdp", None), tokens) + (shard,) * 13
    out_specs = (tokens, tokens) + (shard,) * 13
    return jax.shard_map(
        functools.partial(on_device, mesh.shape["fsdp"]),
        mesh=mesh,
        in_specs=in_specs,
        out_specs=out_specs,
        check_vma=False,
    )
```

time: 1230 us -> 526 us (0.43)
  waiting for transfers between devices: 844 us -> 223 us
  starting transfers between devices: 1.28 us -> 131 us
  blocking collectives: 122 us -> 0 us
  matrix products: 152 us -> 59.2 us
  local copies, waits for them, and re-layouts: 64.6 us -> 40.8 us
  other arithmetic: 25.5 us -> 46.1 us
  Pallas kernels: 0 us -> 14.9 us
  between operations: 15.9 us -> 3.26 us
    reduce_scatter x8 -> x0, waiting for transfers between devices: 619 us -> none  [the longest x1 187 us: on_device(): lax.psum_scatter(grads[11], ('fsdp', 'seq'), scatter_dimension=0, tiled=T...]
    ppermute x0 -> x127, waiting for transfers between devices: none -> 223 us  [the longest x55 161 us: shift(): return lax.ppermute(array, 'fsdp', pairs)]
    all_gather x8 -> x0, waiting for transfers between devices: 222 us -> none  [the longest x1 74.4 us: on_device(): lax.all_gather(up_weight, ('fsdp', 'seq'), axis=0, tiled=True)]
    ppermute x0 -> x127, starting transfers between devices: none -> 131 us  [the longest x55 88.5 us: shift(): return lax.ppermute(array, 'fsdp', pairs)]
    dot_general x36 -> x20, matrix products: 152 us -> 59.2 us  [the longest x8 27.4 us: plain_dot(): return jnp.dot(left, right, preferred_element_type=F32)]
    unnamed x2 -> x0, blocking collectives: 83.2 us -> none
    all_gather x1 -> x0, blocking collectives: 39 us -> none  [on_device(): lax.all_gather(up_bias, ('fsdp', 'seq'), axis=0, tiled=True)]
    pallas_call x0 -> x4, Pallas kernels: none -> 14.9 us  [the longest x2 8.15 us: attention_back(): pl.pallas_call(attention_back_kernel, grid=(images,), in_specs=[pl.BlockS...]
  transfers between devices with their start and end apart: 16 -> 127, of which waited for: 12 -> 53; matrix products, arithmetic and copies ran while one was open for 14% -> 23% of each run, Pallas kernels for 0% -> 3%
where the time goes in v1:
time: 526 us; the launch traced here: 518 us
  waiting for transfers between devices  223 us (42%)
  starting transfers between devices  131 us (25%)
  matrix products  59.2 us (11%)
  other arithmetic  46.1 us (9%)
  local copies, waits for them, and re-layouts  40.8 us (8%)
  Pallas kernels  14.9 us (3%)
    ppermute x55, waiting for transfers between devices, shift(): return lax.ppermute(array, 'fsdp', pairs)  161 us
    ppermute x55, starting transfers between devices, shift(): return lax.ppermute(array, 'fsdp', pairs)  88.5 us
    ppermute x72, waiting for transfers between devices, hop(): return lax.ppermute(array, 'seq', [(i, i ^ mask) for i in range(SEQ)])  62.4 us
    ppermute x72, starting transfers between devices, hop(): return lax.ppermute(array, 'seq', [(i, i ^ mask) for i in range(SEQ)])  42.1 us
    dot_general x8, matrix products, plain_dot(): return jnp.dot(left, right, preferred_element_type=F32)  27.4 us
    dot_general x8, matrix products, cols_dot(): lax.dot_general(left, right, (((1,), (1,)), ((), ())), preferred_element_...  18.4 us
    dot_general x4, matrix products, rows_dot(): lax.dot_general(left, right, (((0,), (0,)), ((), ())), preferred_element_...  13.3 us
  transfers between devices with their start and end apart: 127, of which 53 were waited for; matrix products, arithmetic and copies ran while one was open for 23% of the time, Pallas kernels for 3%

profile of v1, /device:TPU:0, one launch (start us, length us, event | category | flops | bytes accessed | tf_op | source)
XLA Modules:
  0.0 517.9 jit_solution(4345328362126492150)
XLA Ops:
  44.6 3.5 collective-permute-done.27
  50.8 10.1 %collective-permute-done.28 = bf16[128,512]{1,0:T(8,128)(2,1)S(1)} collective-permute-done((bf16[128,512]{1,0:T(8,128)(2,1)S(1)}, bf16[128,512]{1,0:T(8,128)(2,1)S(1)}, u32[]{:S(2)}, u32[]{:S(2)}) %collective-permute-start.28) | collective-permute-done | bytes 131104 | tf_op jit(solution)/shard_map/ppermute | solution.py:70
  60.9 4.1 collective-permute-start.29
  65.0 6.8 %collective-permute-done.29 = bf16[128,512]{1,0:T(8,128)(2,1)S(1)} collective-permute-done((bf16[128,512]{1,0:T(8,128)(2,1)S(1)}, bf16[128,512]{1,0:T(8,128)(2,1)S(1)}, u32[]{:S(2)}, u32[]{:S(2)}) %collective-permute-start.29) | collective-permute-done | bytes 131104 | tf_op jit(solution)/shard_map/ppermute | solution.py:70
  71.8 5.3 %collective-permute-done.30 = bf16[128,512]{1,0:T(8,128)(2,1)S(1)} collective-permute-done((bf16[128,512]{1,0:T(8,128)(2,1)S(1)}, bf16[128,512]{1,0:T(8,128)(2,1)S(1)}, u32[]{:S(2)}, u32[]{:S(2)}) %collective-permute-start.30) | collective-permute-done | bytes 131104 | tf_op jit(solution)/shard_map/ppermute | solution.py:70
  78.6 3.4 collective-permute-done.31
  82.1 9.4 %collective-permute-done.16 = bf16[128,768]{1,0:T(8,128)(2,1)S(1)} collective-permute-done((bf16[128,768]{1,0:T(8,128)(2,1)S(1)}, bf16[128,768]{1,0:T(8,128)(2,1)S(1)}, u32[]{:S(2)}, u32[]{:S(2)}) %collective-permute-start.16) | collective-permute-done | bytes 196640 | tf_op jit(solution)/shard_map/ppermute | solution.py:70
  91.5 8.3 %collective-permute-done.17 = bf16[128,768]{1,0:T(8,128)(2,1)S(1)} collective-permute-done((bf16[128,768]{1,0:T(8,128)(2,1)S(1)}, bf16[128,768]{1,0:T(8,128)(2,1)S(1)}, u32[]{:S(2)}, u32[]{:S(2)}) %collective-permute-start.17) | collective-permute-done | bytes 196640 | tf_op jit(solution)/shard_map/ppermute | solution.py:70
  99.8 5.6 %collective-permute-done.18 = bf16[128,768]{1,0:T(8,128)(2,1)S(1)} collective-permute-done((bf16[128,768]{1,0:T(8,128)(2,1)S(1)}, bf16[128,768]{1,0:T(8,128)(2,1)S(1)}, u32[]{:S(2)}, u32[]{:S(2)}) %collective-permute-start.18) | collective-permute-done | bytes 196640 | tf_op jit(solution)/shard_map/ppermute | solution.py:70
  107.0 5.6 %collective-permute-done.19 = bf16[128,768]{1,0:T(8,128)(2,1)S(1)} collective-permute-done((bf16[128,768]{1,0:T(8,128)(2,1)S(1)}, bf16[128,768]{1,0:T(8,128)(2,1)S(1)}, u32[]{:S(2)}, u32[]{:S(2)}) %collective-permute-start.19) | collective-permute-done | bytes 196640 | tf_op jit(solution)/shard_map/ppermute | solution.py:70
  125.4 10.1 %collective-permute-done.42 = bf16[128,1024]{1,0:T(8,128)(2,1)S(1)} collective-permute-done((bf16[128,1024]{1,0:T(8,128)(2,1)S(1)}, bf16[128,1024]{1,0:T(8,128)(2,1)S(1)}, u32[]{:S(2)}, u32[]{:S(2)}) %collective-permute-start.42) | collective-permute-done | bytes 262176 | tf_op jit(solution)/shard_map/ppermute | solution.py:70
  135.8 12.6 %collective-permute-done.43 = bf16[128,1024]{1,0:T(8,128)(2,1)S(1)} collective-permute-done((bf16[128,1024]{1,0:T(8,128)(2,1)S(1)}, bf16[128,1024]{1,0:T(8,128)(2,1)S(1)}, u32[]{:S(2)}, u32[]{:S(2)}) %collective-permute-start.43) | collective-permute-done | bytes 262176 | tf_op jit(solution)/shard_map/ppermute | solution.py:70
  153.0 3.7 collective-permute-done.44
  181.5 5.6 %collective-permute-done.53 = bf16[128,1024]{1,0:T(8,128)(2,1)S(1)} collective-permute-done((bf16[128,1024]{1,0:T(8,128)(2,1)S(1)}, bf16[128,1024]{1,0:T(8,128)(2,1)S(1)}, u32[]{:S(2)}, u32[]{:S(2)}) %collective-permute-start.53) | collective-permute-done | bytes 262176 | tf_op jit(solution)/shard_map/ppermute | solution.py:70
  189.4 3.4 collective-permute-done.54
  195.0 3.4 collective-permute-done.55
  200.6 3.4 collective-permute-done.46
  204.0 5.6 %collective-permute-done.47 = bf16[128,1024]{1,0:T(8,128)(2,1)S(1)} collective-permute-done((bf16[128,1024]{1,0:T(8,128)(2,1)S(1)}, bf16[128,1024]{1,0:T(8,128)(2,1)S(1)}, u32[]{:S(2)}, u32[]{:S(2)}) %collective-permute-start.47) | collective-permute-done | bytes 262176 | tf_op jit(solution)/shard_map/ppermute | solution.py:70
  209.6 4.2 collective-permute-done.48
  215.8 3.4 shard_map.271
  224.1 3.4 shard_map.272
  237.7 8.1 %collective-permute-done.37 = bf16[160,1024]{1,0:T(8,128)(2,1)S(1)} collective-permute-done((bf16[160,1024]{1,0:T(8,128)(2,1)S(1)}, bf16[160,1024]{1,0:T(8,128)(2,1)S(1)}, u32[]{:S(2)}, u32[]{:S(2)}) %collective-permute-start.37) | collective-permute-done | bytes 327712 | tf_op jit(solution)/shard_map/ppermute | solution.py:20
  249.9 7.5 %collective-permute-done.66 = bf16[160,1024]{1,0:T(8,128)(2,1)S(1)} collective-permute-done((bf16[160,1024]{1,0:T(8,128)(2,1)S(1)}, bf16[160,1024]{1,0:T(8,128)(2,1)S(1)}, u32[]{:S(2)}, u32[]{:S(2)}) %collective-permute-start.66) | collective-permute-done | bytes 327712 | tf_op jit(solution)/shard_map/ppermute | solution.py:20
  260.6 16.1 %multiply_convert_fusion.1 = (bf16[640,1024]{1,0:T(8,128)(2,1)S(1)}, f32[640,1024]{1,0:T(8,128)S(1)}, bf16[640,1024]{1,0:T(8,128)(2,1)S(1)}, f32[640,1024]{1,0:T(8,128)S(1)}, f32[640,1024]{1,0:T(8,128)}) fusion(f32[1024]{0:T(1024)S(1)} %copy-done.46, f32[640,1024]{1,0:T(8,128)S(1)} %fusion.58, bf16[1024,1024]{1,0:T(8,128)(2,1)S(1)} %bitcast.423, ...), kind=kOutput, calls=%fused_computation.29 | convolution fusion | flops 1433927680 | bytes 16519168 | tf_op jit(solution)/shard_map/dot_general | solution.py:116
  276.7 6.0 %convert_reduce_fusion.1 = (f32[1024]{0:T(1024)S(1)}, bf16[640,1024]{1,0:T(8,128)(2,1)S(1)}) fusion(f32[640,1024]{1,0:T(8,128)S(1)} %get-tuple-element.98, bf16[1024,1024]{1,0:T(8,128)(2,1)} %bitcast.70, bf16[160,1024]{1,0:T(8,128)(2,1)S(1)} %collective-permute-done.73, bf16[160,1024]{1,0:T(8,128)(2,1)S(1)} %collective-permute-done.72, ...), kind=kOutput, calls=%fused_computation.13 | convolution fusion | flops 1358560256 | bytes 9969664 | tf_op jit(solution)/shard_map/dot_general | solution.py:112
  284.9 4.2 convert_reduce_fusion
  291.3 3.1 convolution_convert_fusion.5
  294.6 3.1 convolution_convert_fusion.6
  297.8 3.2 fusion.29
  301.0 3.4 fusion.26
  312.3 5.9 %collective-permute-done.76 = bf16[160,1024]{1,0:T(8,128)(2,1)S(1)} collective-permute-done((bf16[160,1024]{1,0:T(8,128)(2,1)S(1)}, bf16[160,1024]{1,0:T(8,128)(2,1)S(1)}, u32[]{:S(2)}, u32[]{:S(2)}) %collective-permute-start.76) | collective-permute-done | bytes 327712 | tf_op jit(solution)/shard_map/ppermute | solution.py:20
  319.8 4.7 collective-permute-done.88
  328.0 7.2 %collective-permute-done.70 = bf16[160,1024]{1,0:T(8,128)(2,1)S(1)} collective-permute-done((bf16[160,1024]{1,0:T(8,128)(2,1)S(1)}, bf16[160,1024]{1,0:T(8,128)(2,1)S(1)}, u32[]{:S(2)}, u32[]{:S(2)}) %collective-permute-start.70) | collective-permute-done | bytes 327712 | tf_op jit(solution)/shard_map/ppermute | solution.py:20
  355.7 3.9 shard_map.273
  361.7 4.2 shard_map.274
  374.7 4.2 fusion.32
  381.8 4.0 collective-permute-start.119
  392.9 4.0 collective-permute-start.126
  396.9 10.3 %collective-permute-done.118 = bf16[1,128,1024]{2,1,0:T(8,128)(2,1)S(1)} collective-permute-done((bf16[1,128,1024]{2,1,0:T(8,128)(2,1)S(1)}, bf16[1,128,1024]{2,1,0:T(8,128)(2,1)S(1)}, u32[]{:S(2)}, u32[]{:S(2)}) %collective-permute-start.118) | collective-permute-done | bytes 262176 | tf_op jit(solution)/shard_map/ppermute | solution.py:70
  407.3 14.0 %collective-permute-start.124 = (bf16[1,128,1024]{2,1,0:T(8,128)(2,1)S(1)}, bf16[1,128,1024]{2,1,0:T(8,128)(2,1)S(1)}, u32[]{:S(2)}, u32[]{:S(2)}) collective-permute-start(bf16[1,128,1024]{2,1,0:T(8,128)(2,1)S(1)} %get-tuple-element.127), channel_id=1, source_target_pairs={{0,8},{4,12},{8,16},{12,20},{16,24},{20,28},{24,0},{28,4},{1,9},{5... | collective-permute-start | bytes 786440 | tf_op jit(solution)/shard_map/ppermute | solution.py:70
  421.6 7.4 %collective-permute-done.125 = bf16[1,128,1024]{2,1,0:T(8,128)(2,1)S(1)} collective-permute-done((bf16[1,128,1024]{2,1,0:T(8,128)(2,1)S(1)}, bf16[1,128,1024]{2,1,0:T(8,128)(2,1)S(1)}, u32[]{:S(2)}, u32[]{:S(2)}) %collective-permute-start.125) | collective-permute-done | bytes 262176 | tf_op jit(solution)/shard_map/ppermute | solution.py:70
  438.3 7.3 %collective-permute-done.82 = bf16[160,1024]{1,0:T(8,128)(2,1)S(1)} collective-permute-done((bf16[160,1024]{1,0:T(8,128)(2,1)}, bf16[160,1024]{1,0:T(8,128)(2,1)S(1)}, u32[]{:S(2)}, u32[]{:S(2)}) %collective-permute-start.82) | collective-permute-done | bytes 327712 | tf_op jit(solution)/shard_map/ppermute | solution.py:20
  467.9 4.2 collective-permute-start.101
  485.7 5.0 collective-permute-done.105
  490.7 6.4 %collective-permute-done.104 = bf16[1,128,768]{2,1,0:T(8,128)(2,1)S(1)} collective-permute-done((bf16[1,128,768]{2,1,0:T(8,128)(2,1)S(1)}, bf16[1,128,768]{2,1,0:T(8,128)(2,1)S(1)}, u32[]{:S(2)}, u32[]{:S(2)}) %collective-permute-start.104) | collective-permute-done | bytes 196640 | tf_op jit(solution)/shard_map/ppermute | solution.py:70
  497.5 3.7 collective-permute-start.112
  505.1 5.7 %collective-permute-done.112 = bf16[1,128,512]{2,1,0:T(8,128)(2,1)S(1)} collective-permute-done((bf16[1,128,512]{2,1,0:T(8,128)(2,1)S(1)}, bf16[1,128,512]{2,1,0:T(8,128)(2,1)S(1)}, u32[]{:S(2)}, u32[]{:S(2)}) %collective-permute-start.112) | collective-permute-done | bytes 131104 | tf_op jit(solution)/shard_map/ppermute | solution.py:70
  512.2 3.0 collective-permute-done.114
  (622 shorter events, 234.1 us)
Async XLA Ops:
  1.6 14.2 %collective-permute-start = (bf16[8,32]{1,0:T(8,128)(2,1)S(1)}, bf16[8,32]{1,0:T(8,128)(2,1)S(1)}, u32[]{:S(2)}, u32[]{:S(2)}) collective-permute-start(bf16[8,32]{1,0:T(8,128)(2,1)S(1)} %stack.126), channel_id=1, source_target_pairs={{0,3},{1,2},{2,1},{3,0},{4,7},{5,6},{6,5},{7,4},{8,11},{9,10},{10,... | collective-permute-start | bytes 1544 | tf_op jit(solution)/shard_map/ppermute | solution.py:20
  5.9 117.2 %collective-permute-start.10 = (bf16[160,1024]{1,0:T(8,128)(2,1)S(1)}, bf16[160,1024]{1,0:T(8,128)(2,1)S(1)}, u32[]{:S(2)}, u32[]{:S(2)}) collective-permute-start(bf16[160,1024]{1,0:T(8,128)(2,1)S(1)} %bitcast.407), channel_id=1, source_target_pairs={{0,1},{1,0},{2,3},{3,2},{4,5},{5,4},{6,7},{7,6},{8,9},{9,8},{10,11... | collective-permute-start | bytes 983048 | tf_op jit(solution)/shard_map/ppermute | solution.py:20
  27.9 95.6 %collective-permute-start.11 = (bf16[160,1024]{1,0:T(8,128)(2,1)S(1)}, bf16[160,1024]{1,0:T(8,128)(2,1)S(1)}, u32[]{:S(2)}, u32[]{:S(2)}) collective-permute-start(bf16[160,1024]{1,0:T(8,128)(2,1)S(1)} %bitcast.408), channel_id=1, source_target_pairs={{0,2},{1,3},{2,0},{3,1},{4,6},{5,7},{6,4},{7,5},{8,10},{9,11},{10,... | collective-permute-start | bytes 983048 | tf_op jit(solution)/shard_map/ppermute | solution.py:20
  41.3 73.6 %collective-permute-start.49 = (bf16[128,1024]{1,0:T(8,128)(2,1)}, bf16[128,1024]{1,0:T(8,128)(2,1)S(1)}, u32[]{:S(2)}, u32[]{:S(2)}) collective-permute-start(bf16[128,1024]{1,0:T(8,128)(2,1)} %param.30), channel_id=1, source_target_pairs={{0,8},{4,12},{8,16},{12,20},{16,24},{20,28},{24,0},{28,4},{1,9},{5... | collective-permute-start | bytes 786440 | tf_op jit(solution)/shard_map/ppermute | solution.py:70
  43.4 73.9 %collective-permute-start.50 = (bf16[128,1024]{1,0:T(8,128)(2,1)}, bf16[128,1024]{1,0:T(8,128)(2,1)S(1)}, u32[]{:S(2)}, u32[]{:S(2)}) collective-permute-start(bf16[128,1024]{1,0:T(8,128)(2,1)} %param.30), channel_id=1, source_target_pairs={{0,16},{4,20},{8,24},{12,28},{16,0},{20,4},{24,8},{28,12},{1,17},{... | collective-permute-start | bytes 786440 | tf_op jit(solution)/shard_map/ppermute | solution.py:70
  119.2 31.9 %collective-permute-start.60 = (bf16[160,1024]{1,0:T(8,128)(2,1)S(1)}, bf16[160,1024]{1,0:T(8,128)(2,1)S(1)}, u32[]{:S(2)}, u32[]{:S(2)}) collective-permute-start(bf16[160,1024]{1,0:T(8,128)(2,1)S(1)} %bitcast.404), channel_id=1, source_target_pairs={{0,2},{1,3},{2,0},{3,1},{4,6},{5,7},{6,4},{7,5},{8,10},{9,11},{10,... | collective-permute-start | bytes 983048 | tf_op jit(solution)/shard_map/ppermute | solution.py:20
  121.6 40.3 %collective-permute-start.72 = (bf16[160,1024]{1,0:T(8,128)(2,1)S(1)}, bf16[160,1024]{1,0:T(8,128)(2,1)S(1)}, u32[]{:S(2)}, u32[]{:S(2)}) collective-permute-start(bf16[160,1024]{1,0:T(8,128)(2,1)S(1)} %bitcast.415), channel_id=1, source_target_pairs={{0,2},{1,3},{2,0},{3,1},{4,6},{5,7},{6,4},{7,5},{8,10},{9,11},{10,... | collective-permute-start | bytes 983048 | tf_op jit(solution)/shard_map/ppermute | solution.py:20
  123.1 38.2 %collective-permute-start.71 = (bf16[160,1024]{1,0:T(8,128)(2,1)S(1)}, bf16[160,1024]{1,0:T(8,128)(2,1)S(1)}, u32[]{:S(2)}, u32[]{:S(2)}) collective-permute-start(bf16[160,1024]{1,0:T(8,128)(2,1)S(1)} %bitcast.416), channel_id=1, source_target_pairs={{0,1},{1,0},{2,3},{3,2},{4,5},{5,4},{6,7},{7,6},{8,9},{9,8},{10,11... | collective-permute-start | bytes 983048 | tf_op jit(solution)/shard_map/ppermute | solution.py:20
  123.5 106.4 %collective-permute-start.84 = (bf16[160,1024]{1,0:T(8,128)(2,1)}, bf16[160,1024]{1,0:T(8,128)(2,1)S(1)}, u32[]{:S(2)}, u32[]{:S(2)}) collective-permute-start(bf16[160,1024]{1,0:T(8,128)(2,1)} %bitcast.86), channel_id=1, source_target_pairs={{0,2},{1,3},{2,0},{3,1},{4,6},{5,7},{6,4},{7,5},{8,10},{9,11},{10,... | collective-permute-start | bytes 983048 | tf_op jit(solution)/shard_map/ppermute | solution.py:20
  163.5 13.8 %collective-permute-start.21 = (bf16[128,768]{1,0:T(8,128)(2,1)S(1)}, bf16[128,768]{1,0:T(8,128)(2,1)S(1)}, u32[]{:S(2)}, u32[]{:S(2)}) collective-permute-start(bf16[128,768]{1,0:T(8,128)(2,1)S(1)} %collective-permute-done.17), channel_id=1, source_target_pairs={{0,4},{4,0},{8,12},{12,8},{16,20},{20,16},{24,28},{28,24},{1,5},{5... | collective-permute-start | bytes 589832 | tf_op jit(solution)/shard_map/ppermute | solution.py:70
  166.0 15.4 %collective-permute-start.22 = (bf16[128,768]{1,0:T(8,128)(2,1)S(1)}, bf16[128,768]{1,0:T(8,128)(2,1)S(1)}, u32[]{:S(2)}, u32[]{:S(2)}) collective-permute-start(bf16[128,768]{1,0:T(8,128)(2,1)S(1)} %collective-permute-done.18), channel_id=1, source_target_pairs={{0,4},{4,0},{8,12},{12,8},{16,20},{20,16},{24,28},{28,24},{1,5},{5... | collective-permute-start | bytes 589832 | tf_op jit(solution)/shard_map/ppermute | solution.py:70
  168.8 18.3 %collective-permute-start.53 = (bf16[128,1024]{1,0:T(8,128)(2,1)S(1)}, bf16[128,1024]{1,0:T(8,128)(2,1)S(1)}, u32[]{:S(2)}, u32[]{:S(2)}) collective-permute-start(bf16[128,1024]{1,0:T(8,128)(2,1)S(1)} %collective-permute-done.49), channel_id=1, source_target_pairs={{0,4},{4,0},{8,12},{12,8},{16,20},{20,16},{24,28},{28,24},{1,5},{5... | collective-permute-start | bytes 786440 | tf_op jit(solution)/shard_map/ppermute | solution.py:70
  173.1 19.7 %collective-permute-start.54 = (bf16[128,1024]{1,0:T(8,128)(2,1)S(1)}, bf16[128,1024]{1,0:T(8,128)(2,1)S(1)}, u32[]{:S(2)}, u32[]{:S(2)}) collective-permute-start(bf16[128,1024]{1,0:T(8,128)(2,1)S(1)} %collective-permute-done.50), channel_id=1, source_target_pairs={{0,4},{4,0},{8,12},{12,8},{16,20},{20,16},{24,28},{28,24},{1,5},{5... | collective-permute-start | bytes 786440 | tf_op jit(solution)/shard_map/ppermute | solution.py:70
  177.3 21.1 %collective-permute-start.55 = (bf16[128,1024]{1,0:T(8,128)(2,1)S(1)}, bf16[128,1024]{1,0:T(8,128)(2,1)S(1)}, u32[]{:S(2)}, u32[]{:S(2)}) collective-permute-start(bf16[128,1024]{1,0:T(8,128)(2,1)S(1)} %collective-permute-done.51), channel_id=1, source_target_pairs={{0,4},{4,0},{8,12},{12,8},{16,20},{20,16},{24,28},{28,24},{1,5},{5... | collective-permute-start | bytes 786440 | tf_op jit(solution)/shard_map/ppermute | solution.py:70
  181.5 32.4 %collective-permute-start.12 = (bf16[160,1024]{1,0:T(8,128)(2,1)S(1)}, bf16[160,1024]{1,0:T(8,128)(2,1)S(1)}, u32[]{:S(2)}, u32[]{:S(2)}) collective-permute-start(bf16[160,1024]{1,0:T(8,128)(2,1)S(1)} %collective-permute-done.11), channel_id=1, source_target_pairs={{0,1},{1,0},{2,3},{3,2},{4,5},{5,4},{6,7},{7,6},{8,9},{9,8},{10,11... | collective-permute-start | bytes 983048 | tf_op jit(solution)/shard_map/ppermute | solution.py:20
  187.1 16.9 %collective-permute-start.46 = (bf16[128,1024]{1,0:T(8,128)(2,1)S(1)}, bf16[128,1024]{1,0:T(8,128)(2,1)S(1)}, u32[]{:S(2)}, u32[]{:S(2)}) collective-permute-start(bf16[128,1024]{1,0:T(8,128)(2,1)S(1)} %collective-permute-done.42), channel_id=1, source_target_pairs={{0,4},{4,0},{8,12},{12,8},{16,20},{20,16},{24,28},{28,24},{1,5},{5... | collective-permute-start | bytes 786440 | tf_op jit(solution)/shard_map/ppermute | solution.py:70
  192.7 16.9 %collective-permute-start.47 = (bf16[128,1024]{1,0:T(8,128)(2,1)S(1)}, bf16[128,1024]{1,0:T(8,128)(2,1)S(1)}, u32[]{:S(2)}, u32[]{:S(2)}) collective-permute-start(bf16[128,1024]{1,0:T(8,128)(2,1)S(1)} %collective-permute-done.43), channel_id=1, source_target_pairs={{0,4},{4,0},{8,12},{12,8},{16,20},{20,16},{24,28},{28,24},{1,5},{5... | collective-permute-start | bytes 786440 | tf_op jit(solution)/shard_map/ppermute | solution.py:70
  198.3 15.5 %collective-permute-start.48 = (bf16[128,1024]{1,0:T(8,128)(2,1)S(1)}, bf16[128,1024]{1,0:T(8,128)(2,1)S(1)}, u32[]{:S(2)}, u32[]{:S(2)}) collective-permute-start(bf16[128,1024]{1,0:T(8,128)(2,1)S(1)} %collective-permute-done.44), channel_id=1, source_target_pairs={{0,4},{4,0},{8,12},{12,8},{16,20},{20,16},{24,28},{28,24},{1,5},{5... | collective-permute-start | bytes 786440 | tf_op jit(solution)/shard_map/ppermute | solution.py:70
  204.0 16.5 %collective-permute-start.61 = (bf16[160,1024]{1,0:T(8,128)(2,1)S(1)}, bf16[160,1024]{1,0:T(8,128)(2,1)S(1)}, u32[]{:S(2)}, u32[]{:S(2)}) collective-permute-start(bf16[160,1024]{1,0:T(8,128)(2,1)S(1)} %collective-permute-done.60), channel_id=1, source_target_pairs={{0,1},{1,0},{2,3},{3,2},{4,5},{5,4},{6,7},{7,6},{8,9},{9,8},{10,11... | collective-permute-start | bytes 983048 | tf_op jit(solution)/shard_map/ppermute | solution.py:20
  209.6 17.9 %collective-permute-start.73 = (bf16[160,1024]{1,0:T(8,128)(2,1)S(1)}, bf16[160,1024]{1,0:T(8,128)(2,1)S(1)}, u32[]{:S(2)}, u32[]{:S(2)}) collective-permute-start(bf16[160,1024]{1,0:T(8,128)(2,1)S(1)} %collective-permute-done.72), channel_id=1, source_target_pairs={{0,1},{1,0},{2,3},{3,2},{4,5},{5,4},{6,7},{7,6},{8,9},{9,8},{10,11... | collective-permute-start | bytes 983048 | tf_op jit(solution)/shard_map/ppermute | solution.py:20
  213.8 20.4 %collective-permute-start.35 = (bf16[1024,512]{1,0:T(8,128)(2,1)S(1)}, bf16[1024,512]{1,0:T(8,128)(2,1)S(1)}, u32[]{:S(2)}, u32[]{:S(2)}) collective-permute-start(bf16[1024,512]{1,0:T(8,128)(2,1)S(1)} %bitcast.413), channel_id=1, source_target_pairs={{0,1},{1,0},{2,3},{3,2},{4,5},{5,4},{6,7},{7,6},{8,9},{9,8},{10,11... | collective-permute-start | bytes 3145736 | tf_op jit(solution)/shard_map/ppermute | solution.py:20
  229.9 20.0 %collective-permute-start.83 = (bf16[160,1024]{1,0:T(8,128)(2,1)}, bf16[160,1024]{1,0:T(8,128)(2,1)S(1)}, u32[]{:S(2)}, u32[]{:S(2)}) collective-permute-start(bf16[160,1024]{1,0:T(8,128)(2,1)} %bitcast.86), channel_id=1, source_target_pairs={{0,1},{1,0},{2,3},{3,2},{4,5},{5,4},{6,7},{7,6},{8,9},{9,8},{10,11... | collective-permute-start | bytes 983048 | tf_op jit(solution)/shard_map/ppermute | solution.py:20
  231.8 25.7 %collective-permute-start.85 = (bf16[160,1024]{1,0:T(8,128)(2,1)S(1)}, bf16[160,1024]{1,0:T(8,128)(2,1)S(1)}, u32[]{:S(2)}, u32[]{:S(2)}) collective-permute-start(bf16[160,1024]{1,0:T(8,128)(2,1)S(1)} %collective-permute-done.84), channel_id=1, source_target_pairs={{0,1},{1,0},{2,3},{3,2},{4,5},{5,4},{6,7},{7,6},{8,9},{9,8},{10,11... | collective-permute-start | bytes 983048 | tf_op jit(solution)/shard_map/ppermute | solution.py:20
  284.3 22.9 %collective-permute-start.75 = (bf16[160,1024]{1,0:T(8,128)(2,1)S(1)}, bf16[160,1024]{1,0:T(8,128)(2,1)S(1)}, u32[]{:S(2)}, u32[]{:S(2)}) collective-permute-start(bf16[160,1024]{1,0:T(8,128)(2,1)S(1)} %get-tuple-element.118), channel_id=1, source_target_pairs={{0,1},{1,0},{2,3},{3,2},{4,5},{5,4},{6,7},{7,6},{8,9},{9,8},{10,11... | collective-permute-start | bytes 983048 | tf_op jit(solution)/shard_map/ppermute | solution.py:20
  284.5 25.7 %collective-permute-start.74 = (bf16[160,1024]{1,0:T(8,128)(2,1)S(1)}, bf16[160,1024]{1,0:T(8,128)(2,1)S(1)}, u32[]{:S(2)}, u32[]{:S(2)}) collective-permute-start(bf16[160,1024]{1,0:T(8,128)(2,1)S(1)} %get-tuple-element.117), channel_id=1, source_target_pairs={{0,1},{1,0},{2,3},{3,2},{4,5},{5,4},{6,7},{7,6},{8,9},{9,8},{10,11... | collective-permute-start | bytes 983048 | tf_op jit(solution)/shard_map/ppermute | solution.py:20
  290.7 17.0 %collective-permute-start.87 = (bf16[160,1024]{1,0:T(8,128)(2,1)S(1)}, bf16[160,1024]{1,0:T(8,128)(2,1)S(1)}, u32[]{:S(2)}, u32[]{:S(2)}) collective-permute-start(bf16[160,1024]{1,0:T(8,128)(2,1)S(1)} %get-tuple-element.122), channel_id=1, source_target_pairs={{0,1},{1,0},{2,3},{3,2},{4,5},{5,4},{6,7},{7,6},{8,9},{9,8},{10,11... | collective-permute-start | bytes 983048 | tf_op jit(solution)/shard_map/ppermute | solution.py:20
  290.9 19.9 %collective-permute-start.86 = (bf16[160,1024]{1,0:T(8,128)(2,1)S(1)}, bf16[160,1024]{1,0:T(8,128)(2,1)S(1)}, u32[]{:S(2)}, u32[]{:S(2)}) collective-permute-start(bf16[160,1024]{1,0:T(8,128)(2,1)S(1)} %get-tuple-element.121), channel_id=1, source_target_pairs={{0,1},{1,0},{2,3},{3,2},{4,5},{5,4},{6,7},{7,6},{8,9},{9,8},{10,11... | collective-permute-start | bytes 983048 | tf_op jit(solution)/shard_map/ppermute | solution.py:20
  294.4 14.5 %collective-permute-start.69 = (bf16[160,1024]{1,0:T(8,128)(2,1)S(1)}, bf16[160,1024]{1,0:T(8,128)(2,1)S(1)}, u32[]{:S(2)}, u32[]{:S(2)}) collective-permute-start(bf16[160,1024]{1,0:T(8,128)(2,1)S(1)} %get-tuple-element.126), channel_id=1, source_target_pairs={{0,1},{1,0},{2,3},{3,2},{4,5},{5,4},{6,7},{7,6},{8,9},{9,8},{10,11... | collective-permute-start | bytes 983048 | tf_op jit(solution)/shard_map/ppermute | solution.py:20
  309.0 15.5 %collective-permute-start.88 = (bf16[160,1024]{1,0:T(8,128)(2,1)S(1)}, bf16[160,1024]{1,0:T(8,128)(2,1)S(1)}, u32[]{:S(2)}, u32[]{:S(2)}) collective-permute-start(bf16[160,1024]{1,0:T(8,128)(2,1)S(1)} %add_convert_fusion.6), channel_id=1, source_target_pairs={{0,2},{1,3},{2,0},{3,1},{4,6},{5,7},{6,4},{7,5},{8,10},{9,11},{10,... | collective-permute-start | bytes 983048 | tf_op jit(solution)/shard_map/ppermute | solution.py:20
  310.1 16.9 %collective-permute-start.68 = (bf16[160,1024]{1,0:T(8,128)(2,1)S(1)}, bf16[160,1024]{1,0:T(8,128)(2,1)S(1)}, u32[]{:S(2)}, u32[]{:S(2)}) collective-permute-start(bf16[160,1024]{1,0:T(8,128)(2,1)S(1)} %get-tuple-element.125), channel_id=1, source_target_pairs={{0,1},{1,0},{2,3},{3,2},{4,5},{5,4},{6,7},{7,6},{8,9},{9,8},{10,11... | collective-permute-start | bytes 983048 | tf_op jit(solution)/shard_map/ppermute | solution.py:20
  310.3 28.2 %collective-permute-start.56 = (bf16[160,1024]{1,0:T(8,128)(2,1)S(1)}, bf16[160,1024]{1,0:T(8,128)(2,1)S(1)}, u32[]{:S(2)}, u32[]{:S(2)}) collective-permute-start(bf16[160,1024]{1,0:T(8,128)(2,1)S(1)} %get-tuple-element.123), channel_id=1, source_target_pairs={{0,1},{1,0},{2,3},{3,2},{4,5},{5,4},{6,7},{7,6},{8,9},{9,8},{10,11... | collective-permute-start | bytes 983048 | tf_op jit(solution)/shard_map/ppermute | solution.py:20
  310.8 69.1 %collective-permute-start.116 = (bf16[4,128,1024]{2,1,0:T(8,128)(2,1)}, bf16[4,128,1024]{2,1,0:T(8,128)(2,1)}, u32[]{:S(2)}, u32[]{:S(2)}) collective-permute-start(bf16[4,128,1024]{2,1,0:T(8,128)(2,1)} %dynamic-slice_bitcast_fusion.1), channel_id=1, source_target_pairs={{0,4},{4,0},{8,12},{12,8},{16,20},{20,16},{24,28},{28,24},{1,5},{5... | collective-permute-start | bytes 3145736 | tf_op jit(solution)/shard_map/ppermute | solution.py:70
  318.3 67.5 %collective-permute-start.123 = (bf16[4,128,1024]{2,1,0:T(8,128)(2,1)}, bf16[4,128,1024]{2,1,0:T(8,128)(2,1)}, u32[]{:S(2)}, u32[]{:S(2)}) collective-permute-start(bf16[4,128,1024]{2,1,0:T(8,128)(2,1)} %dynamic-slice_bitcast_fusion), channel_id=1, source_target_pairs={{0,4},{4,0},{8,12},{12,8},{16,20},{20,16},{24,28},{28,24},{1,5},{5... | collective-permute-start | bytes 3145736 | tf_op jit(solution)/shard_map/ppermute | solution.py:70
  327.0 13.6 %collective-permute-start.58 = (bf16[160,1024]{1,0:T(8,128)(2,1)S(1)}, bf16[160,1024]{1,0:T(8,128)(2,1)S(1)}, u32[]{:S(2)}, u32[]{:S(2)}) collective-permute-start(bf16[160,1024]{1,0:T(8,128)(2,1)S(1)} %add_convert_fusion.13), channel_id=1, source_target_pairs={{0,2},{1,3},{2,0},{3,1},{4,6},{5,7},{6,4},{7,5},{8,10},{9,11},{10,... | collective-permute-start | bytes 983048 | tf_op jit(solution)/shard_map/ppermute | solution.py:20
  361.0 118.4 %collective-permute-start.109 = (bf16[1024,512]{1,0:T(8,128)(2,1)}, bf16[1024,512]{1,0:T(8,128)(2,1)}, u32[]{:S(2)}, u32[]{:S(2)}) collective-permute-start(bf16[1024,512]{1,0:T(8,128)(2,1)} %broadcast_select_fusion), channel_id=1, source_target_pairs={{0,1},{1,0},{2,3},{3,2},{4,5},{5,4},{6,7},{7,6},{8,9},{9,8},{10,11... | collective-permute-start | bytes 3145736 | tf_op jit(solution)/shard_map/ppermute | solution.py:20
  370.1 17.5 %collective-permute-start.93 = (bf16[160,1024]{1,0:T(8,128)(2,1)S(1)}, bf16[160,1024]{1,0:T(8,128)(2,1)S(1)}, u32[]{:S(2)}, u32[]{:S(2)}) collective-permute-start(bf16[160,1024]{1,0:T(8,128)(2,1)S(1)} %get-tuple-element.120), channel_id=1, source_target_pairs={{0,1},{1,0},{2,3},{3,2},{4,5},{5,4},{6,7},{7,6},{8,9},{9,8},{10,11... | collective-permute-start | bytes 983048 | tf_op jit(solution)/shard_map/ppermute | solution.py:20
  370.9 19.1 %collective-permute-start.81 = (bf16[160,1024]{1,0:T(8,128)(2,1)S(1)}, bf16[160,1024]{1,0:T(8,128)(2,1)S(1)}, u32[]{:S(2)}, u32[]{:S(2)}) collective-permute-start(bf16[160,1024]{1,0:T(8,128)(2,1)S(1)} %get-tuple-element.116), channel_id=1, source_target_pairs={{0,1},{1,0},{2,3},{3,2},{4,5},{5,4},{6,7},{7,6},{8,9},{9,8},{10,11... | collective-permute-start | bytes 983048 | tf_op jit(solution)/shard_map/ppermute | solution.py:20
  385.8 21.4 %collective-permute-start.118 = (bf16[1,128,1024]{2,1,0:T(8,128)(2,1)S(1)}, bf16[1,128,1024]{2,1,0:T(8,128)(2,1)S(1)}, u32[]{:S(2)}, u32[]{:S(2)}) collective-permute-start(bf16[1,128,1024]{2,1,0:T(8,128)(2,1)S(1)} %get-tuple-element.132), channel_id=1, source_target_pairs={{0,16},{4,20},{8,24},{12,28},{16,0},{20,4},{24,8},{28,12},{1,17},{... | collective-permute-start | bytes 786440 | tf_op jit(solution)/shard_map/ppermute | solution.py:70
  387.5 19.7 %collective-permute-start.117 = (bf16[1,128,1024]{2,1,0:T(8,128)(2,1)S(1)}, bf16[1,128,1024]{2,1,0:T(8,128)(2,1)S(1)}, u32[]{:S(2)}, u32[]{:S(2)}) collective-permute-start(bf16[1,128,1024]{2,1,0:T(8,128)(2,1)S(1)} %get-tuple-element.130), channel_id=1, source_target_pairs={{0,8},{4,12},{8,16},{12,20},{16,24},{20,28},{24,0},{28,4},{1,9},{5... | collective-permute-start | bytes 786440 | tf_op jit(solution)/shard_map/ppermute | solution.py:70
  390.0 57.7 %collective-permute-start.92 = (bf16[160,1024]{1,0:T(8,128)(2,1)}, bf16[160,1024]{1,0:T(8,128)(2,1)S(1)}, u32[]{:S(2)}, u32[]{:S(2)}) collective-permute-start(bf16[160,1024]{1,0:T(8,128)(2,1)} %get-tuple-element.119), channel_id=1, source_target_pairs={{0,1},{1,0},{2,3},{3,2},{4,5},{5,4},{6,7},{7,6},{8,9},{9,8},{10,11... | collective-permute-start | bytes 983048 | tf_op jit(solution)/shard_map/ppermute | solution.py:20
  392.9 28.6 %collective-permute-start.126 = (bf16[1,128,1024]{2,1,0:T(8,128)(2,1)S(1)}, bf16[1,128,1024]{2,1,0:T(8,128)(2,1)S(1)}, u32[]{:S(2)}, u32[]{:S(2)}) collective-permute-start(bf16[1,128,1024]{2,1,0:T(8,128)(2,1)S(1)} %get-tuple-element.128), channel_id=1, source_target_pairs={{0,24},{4,28},{8,0},{12,4},{16,8},{20,12},{24,16},{28,20},{1,25},{... | collective-permute-start | bytes 786440 | tf_op jit(solution)/shard_map/ppermute | solution.py:70
  407.2 21.7 %collective-permute-start.125 = (bf16[1,128,1024]{2,1,0:T(8,128)(2,1)S(1)}, bf16[1,128,1024]{2,1,0:T(8,128)(2,1)S(1)}, u32[]{:S(2)}, u32[]{:S(2)}) collective-permute-start(bf16[1,128,1024]{2,1,0:T(8,128)(2,1)S(1)} %get-tuple-element.129), channel_id=1, source_target_pairs={{0,16},{4,20},{8,24},{12,28},{16,0},{20,4},{24,8},{28,12},{1,17},{... | collective-permute-start | bytes 786440 | tf_op jit(solution)/shard_map/ppermute | solution.py:70
  407.3 22.8 %collective-permute-start.124 = (bf16[1,128,1024]{2,1,0:T(8,128)(2,1)S(1)}, bf16[1,128,1024]{2,1,0:T(8,128)(2,1)S(1)}, u32[]{:S(2)}, u32[]{:S(2)}) collective-permute-start(bf16[1,128,1024]{2,1,0:T(8,128)(2,1)S(1)} %get-tuple-element.127), channel_id=1, source_target_pairs={{0,8},{4,12},{8,16},{12,20},{16,24},{20,28},{24,0},{28,4},{1,9},{5... | collective-permute-start | bytes 786440 | tf_op jit(solution)/shard_map/ppermute | solution.py:70
  433.3 44.9 %collective-permute-start.102 = (bf16[4,128,768]{2,1,0:T(8,128)(2,1)}, bf16[4,128,768]{2,1,0:T(8,128)(2,1)}, u32[]{:S(2)}, u32[]{:S(2)}) collective-permute-start(bf16[4,128,768]{2,1,0:T(8,128)(2,1)} %dynamic-slice_bitcast_fusion.2), channel_id=1, source_target_pairs={{0,4},{4,0},{8,12},{12,8},{16,20},{20,16},{24,28},{28,24},{1,5},{5... | collective-permute-start | bytes 2359304 | tf_op jit(solution)/shard_map/ppermute | solution.py:70
  481.2 16.1 %collective-permute-start.110 = (bf16[4,128,512]{2,1,0:T(8,128)(2,1)S(1)}, bf16[4,128,512]{2,1,0:T(8,128)(2,1)S(1)}, u32[]{:S(2)}, u32[]{:S(2)}) collective-permute-start(bf16[4,128,512]{2,1,0:T(8,128)(2,1)S(1)} %dynamic-slice_bitcast_fusion.3), channel_id=1, source_target_pairs={{0,4},{4,0},{8,12},{12,8},{16,20},{20,16},{24,28},{28,24},{1,5},{5... | collective-permute-start | bytes 1572872 | tf_op jit(solution)/shard_map/ppermute | solution.py:70
  482.6 14.5 %collective-permute-start.104 = (bf16[1,128,768]{2,1,0:T(8,128)(2,1)S(1)}, bf16[1,128,768]{2,1,0:T(8,128)(2,1)S(1)}, u32[]{:S(2)}, u32[]{:S(2)}) collective-permute-start(bf16[1,128,768]{2,1,0:T(8,128)(2,1)S(1)} %get-tuple-element.135), channel_id=1, source_target_pairs={{0,16},{4,20},{8,24},{12,28},{16,0},{20,4},{24,8},{28,12},{1,17},{... | collective-permute-start | bytes 589832 | tf_op jit(solution)/shard_map/ppermute | solution.py:70
  483.3 13.8 %collective-permute-start.103 = (bf16[1,128,768]{2,1,0:T(8,128)(2,1)S(1)}, bf16[1,128,768]{2,1,0:T(8,128)(2,1)S(1)}, u32[]{:S(2)}, u32[]{:S(2)}) collective-permute-start(bf16[1,128,768]{2,1,0:T(8,128)(2,1)S(1)} %get-tuple-element.133), channel_id=1, source_target_pairs={{0,8},{4,12},{8,16},{12,20},{16,24},{20,28},{24,0},{28,4},{1,9},{5... | collective-permute-start | bytes 589832 | tf_op jit(solution)/shard_map/ppermute | solution.py:70
  497.5 13.3 %collective-permute-start.112 = (bf16[1,128,512]{2,1,0:T(8,128)(2,1)S(1)}, bf16[1,128,512]{2,1,0:T(8,128)(2,1)S(1)}, u32[]{:S(2)}, u32[]{:S(2)}) collective-permute-start(bf16[1,128,512]{2,1,0:T(8,128)(2,1)S(1)} %get-tuple-element.144), channel_id=1, source_target_pairs={{0,16},{4,20},{8,24},{12,28},{16,0},{20,4},{24,8},{28,12},{1,17},{... | collective-permute-start | bytes 393224 | tf_op jit(solution)/shard_map/ppermute | solution.py:70
  (127 other events, 1590.2 us)

commit v2 on v1

v2 whole, which is shorter than its diff:
```python
import functools

import jax
import jax.numpy as jnp
from jax import lax
from jax.experimental import pallas as pl
from jax.experimental.pallas import tpu as pltpu
from jax.sharding import PartitionSpec as P

HEAD_DIM = 64
SEQ = 4
BF = jnp.bfloat16
F32 = jnp.float32
FILL = -1e30
LANES = 128
VECTORS = 8
SCALE = HEAD_DIM ** (-0.5)
BOTH = ("fsdp", "seq")
ORDER = (0, 2, 1, 3)
ANY = pl.BlockSpec(memory_space=pl.ANY)
SMEM = pl.BlockSpec(memory_space=pltpu.SMEM)
VMEM = pl.BlockSpec(memory_space=pltpu.VMEM)


def hop(array, mask):
    return lax.ppermute(array, "seq", [(i, i ^ mask) for i in range(SEQ)])


def seq_gather(array):
    far = hop(array, 2)
    return [array, far, hop(array, 1), hop(far, 1)]


def seq_exchange(pieces):
    return [pieces[0]] + [hop(pieces[k], ORDER[k]) for k in (1, 2, 3)]


def seq_scatter(chip, sibling):
    came = hop(sibling, 1)
    return came, (chip[1].astype(F32) + came[1].astype(F32)).astype(BF)


def digits_of(size):
    digits, stride = [], 1
    while stride < size:
        radix = 2 if stride == 1 or size // stride < 4 else 4
        digits.append((stride, radix))
        stride *= radix
    return digits


def shift(array, size, stride, radix, step):
    pairs = []
    for i in range(size):
        digit = i // stride % radix
        pairs.append((i, i + ((digit + step) % radix - digit) * stride))
    return lax.ppermute(array, "fsdp", pairs)


def steps_of(radix):
    return [step for _, step in sorted((min(s, radix - s), s) for s in range(1, radix))]


def fsdp_owners(size, place):
    owners = [place]
    for stride, radix in reversed(digits_of(size)):
        digit = place // stride % radix
        changes = [((digit + radix - step) % radix - digit) * stride for step in steps_of(radix)]
        owners = owners + [o + change for change in changes for o in owners]
    return owners


def after(array, *done):
    return lax.optimization_barrier((array,) + done)[0] if done else array


def fsdp_gather(array, size):
    pieces = [array]
    for stride, radix in reversed(digits_of(size)):
        pieces = pieces + [
            shift(piece, size, stride, radix, step) for step in steps_of(radix) for piece in pieces
        ]
    return pieces


class Gather:
    def __init__(self, array, size):
        self.array, self.size = array, size
        self.near, self.far = digits_of(size)
        self.steps = steps_of(self.far[1])
        self.came, self.passed = {}, {}

    def send(self, at, *done):
        self.came[at] = shift(after(self.array, *done), self.size, *self.far, self.steps[at])
        return self.came[at]

    def forward(self, at, *done):
        source = self.array if at is None else self.came[at]
        self.passed[at] = shift(after(source, *done), self.size, *self.near, 1)
        return self.passed[at]

    def pieces(self):
        order = range(len(self.steps))
        return (
            [self.array]
            + [self.came[at] for at in order]
            + [self.passed[None]]
            + [self.passed[at] for at in order]
        )


def split_kernel(count, radix, digit_ref, *refs):
    parts, outs = refs[:count], refs[count:]
    digit = digit_ref[0]
    for step, out in zip([0] + steps_of(radix), outs):
        at = lax.rem(digit + step, radix)
        out[0] = functools.reduce(jnp.add, [part[0, at].astype(F32) for part in parts]).astype(out.dtype)


def split_sum(parts, outer, radix, digit):
    rows, cols = parts[0].shape[1:]
    return pl.pallas_call(
        functools.partial(split_kernel, len(parts), radix),
        grid=(outer,),
        in_specs=[SMEM]
        + [pl.BlockSpec((1, radix, rows, cols), lambda i: (i, 0, 0, 0))] * len(parts),
        out_specs=[pl.BlockSpec((1, rows, cols), lambda i: (i, 0, 0))] * radix,
        out_shape=[jax.ShapeDtypeStruct((outer, rows, cols), BF)] * radix,
        compiler_params=params(),
        name="split",
    )(digit, *[part.reshape(outer, radix, rows, cols) for part in parts])


def scatter_near(keep, send, size, place):
    digits = digits_of(size)
    parts = [keep, shift(send, size, *digits[0], 1)]
    stride, radix = digits[1]
    digit = place // stride % radix
    outer = keep.shape[0] // radix
    return split_sum(parts, outer, radix, jnp.asarray(digit, jnp.int32).reshape(1))


def scatter_far(blocks, size, place):
    digits = digits_of(size)
    for at, (stride, radix) in enumerate(digits[1:]):
        parts = list(blocks[:1]) + [
            shift(block, size, stride, radix, step) for block, step in zip(blocks[1:], steps_of(radix))
        ]
        if at + 2 < len(digits):
            stride, radix = digits[at + 2]
            digit = place // stride % radix
            outer = parts[0].shape[0] // radix
            blocks = split_sum(parts, outer, radix, jnp.asarray(digit, jnp.int32).reshape(1))
    return functools.reduce(jnp.add, [part[0].astype(F32) for part in parts])


def rows_dot(left, right):
    return lax.dot_general(left, right, (((0,), (0,)), ((), ())), preferred_element_type=F32)


def cols_dot(left, right):
    return lax.dot_general(left, right, (((1,), (1,)), ((), ())), preferred_element_type=F32)


def plain_dot(left, right):
    return jnp.dot(left, right, preferred_element_type=F32)


def norm_parts(values):
    average = jnp.mean(values, axis=-1, keepdims=True)
    centred = values - average
    scale = lax.rsqrt(jnp.mean(centred * centred, axis=-1, keepdims=True) + 1e-06)
    return centred * scale, scale


def norm_back(grad, hat, scale, gain):
    spread = grad * gain
    return scale * (
        spread
        - jnp.mean(spread, axis=-1, keepdims=True)
        - hat * jnp.mean(spread * hat, axis=-1, keepdims=True)
    )


def column_sums(values):
    return jnp.sum(values, axis=0, keepdims=True)


def params():
    return pltpu.CompilerParams(vmem_limit_bytes=60 * 2**20)


def estimate(flops, moved):
    return pl.CostEstimate(flops=int(flops), bytes_accessed=int(moved), transcendentals=0)


def pack_kernel(fsdp, qkv, out, vectors, up, ref):
    width = qkv.shape[1] // 3 // SEQ
    half = out.shape[1] // 2
    block = up.shape[1] // SEQ // fsdp
    for s in range(SEQ):
        spans = [(qkv, (part * SEQ + s) * width, width) for part in range(3)]
        spans += [(vectors, 0, LANES), (out, (s % 2) * half, half)]
        spans += [(up, (f * SEQ + s) * block, block) for f in range(fsdp)]
        low = 0
        for source, start, cols in spans:
            ref[s, :, low : low + cols] = source[:, start : start + cols]
            low += cols


def pack(fsdp, qkv, out, vectors, up):
    depth = qkv.shape[0]
    cols = (qkv.shape[1] + up.shape[1]) // SEQ + LANES + out.shape[1] // 2
    return pl.pallas_call(
        functools.partial(pack_kernel, fsdp),
        in_specs=[VMEM] * 4,
        out_specs=VMEM,
        out_shape=jax.ShapeDtypeStruct((SEQ, depth, cols), BF),
        compiler_params=params(),
        name="pack",
    )(qkv, out, vectors, up)


def unpack_kernel(ref, qkv, out, up, vectors):
    width = qkv.shape[1] // 3 // SEQ
    half = out.shape[1] // 2
    units = up.shape[1] // SEQ
    low = 3 * width + LANES
    block = ref.shape[1] * SEQ
    for s in range(SEQ):
        for part in range(3):
            at = (part * SEQ + s) * width
            qkv[:, at : at + width] = ref[s, :, part * width : (part + 1) * width].astype(F32)
        for part in range(units // block):
            at = (part * SEQ + s) * block
            start = low + half + part * block
            up[:, at : at + block] = ref[s, :, start : start + block].astype(F32)
    wide = lambda s, start, cols: ref[s, :, start : start + cols].astype(F32)
    vectors[...] = functools.reduce(jnp.add, [wide(s, 3 * width, LANES) for s in range(SEQ)])
    for core in range(2):
        out[:, core * half : (core + 1) * half] = wide(core, low, half) + wide(core + 2, low, half)


def unpack(came, model, units):
    depth = came.shape[1]
    cols = (3 * model, model, SEQ * units, LANES)
    return pl.pallas_call(
        unpack_kernel,
        in_specs=[VMEM],
        out_specs=[VMEM] * 4,
        out_shape=[jax.ShapeDtypeStruct((depth, n), F32) for n in cols],
        compiler_params=params(),
        name="unpack",
    )(came)


def place_kernel(count, spans, vectors, info, *refs):
    pieces, outs = refs[:count], refs[count : count + len(spans)]
    block = pieces[0].shape[0]
    for at, piece in enumerate(pieces):
        place = pl.ds(pl.multiple_of(info[at] * block, block), block)
        for (low, cols), out in zip(spans, outs):
            out[place, :] = piece[:, low : low + cols]
    if vectors:
        rows = refs[-1]
        rows[...] = outs[-1][...].astype(F32).T[: rows.shape[0]]


def placed(info, pieces, *spans, vectors=False):
    count = len(pieces)
    rows = count * pieces[0].shape[0]
    shapes = [jax.ShapeDtypeStruct((rows, cols), BF) for _, cols in spans]
    if vectors:
        shapes.append(jax.ShapeDtypeStruct((16, rows), F32))
    return pl.pallas_call(
        functools.partial(place_kernel, count, spans, vectors),
        in_specs=[SMEM] + [VMEM] * count,
        out_specs=[VMEM] * len(shapes),
        out_shape=shapes,
        compiler_params=params(),
        name="placed",
    )(info, *pieces)


def row_copies(sources, target, sem):
    copies, low = [], 0
    for at, source in enumerate(sources):
        rows = source.shape[0]
        copies.append(pltpu.make_async_copy(source, target.at[pl.ds(low, rows), :], sem.at[at]))
        low += rows
    return copies


def weight_grad_kernel(lefts, rights, left_at, right_at, info, *refs):
    more = len(refs) - lefts - rights - 8
    left_refs, right_refs = refs[:lefts], refs[lefts : lefts + rights]
    extra = refs[lefts + rights : lefts + rights + more]
    keep, send, left, right, out, left_sem, right_sem, out_sem = refs[lefts + rights + more :]
    copies = row_copies(left_at(info, left_refs), left, left_sem) + row_copies(
        right_at(info, right_refs), right, right_sem
    )
    for copy in copies:
        copy.start()
    total, cols = left.shape[1], right.shape[1]
    if more:
        sums = functools.reduce(jnp.add, [ref[...] for ref in extra])
        sums = jnp.concatenate([sums, jnp.zeros((LANES - sums.shape[0], total), F32)], axis=0)
        out[:, cols:] = sums.T.astype(BF)
    for copy in copies:
        copy.wait()
    tile = min(256, total)
    for low in range(0, total, tile):
        out[low : low + tile, :cols] = rows_dot(left[:, low : low + tile], right[...]).astype(BF)
    groups, block = keep.shape[:2]
    low_digit = info[0] % 2
    moves = []
    for at in range(groups):
        for which, (ref, side) in enumerate(((keep, low_digit), (send, 1 - low_digit))):
            start = pl.multiple_of((2 * at + side) * block, block)
            moves.append(
                pltpu.make_async_copy(out.at[pl.ds(start, block), :], ref.at[at], out_sem.at[2 * at + which])
            )
    for move in moves:
        move.start()
    for move in moves:
        move.wait()


def feed_grads_kernel(micros, tokens_at, info, *refs):
    n2 = refs[: micros * SEQ]
    actives, hiddens = refs[micros * SEQ : micros * (SEQ + 1)], refs[micros * (SEQ + 1) : micros * (SEQ + 2)]
    cot, out = refs[micros * (SEQ + 2) : micros * (SEQ + 2) + 2]
    c_in, act_in, n2_in, gh_in, c_sem, act_sem, n2_sem, gh_sem = refs[micros * (SEQ + 2) + 2 :]
    cots = [cot.at[info[tokens_at + k], m] for m in range(micros) for k in range(SEQ)]
    first = row_copies(cots, c_in, c_sem) + row_copies(actives, act_in, act_sem)
    second = row_copies(n2, n2_in, n2_sem) + row_copies(hiddens, gh_in, gh_sem)
    for copy in first + second:
        copy.start()
    block = out.shape[2]
    step = max(256 // block, 1)
    for which, (left, right, copies) in enumerate(((act_in, c_in, first), (n2_in, gh_in, second))):
        for copy in copies:
            copy.wait()
        for low in range(0, out.shape[0], step):
            part = rows_dot(left[:, low * block : (low + step) * block], right[...]).astype(BF)
            out[low : low + step, which] = part.reshape(step, block, part.shape[1])


def feed_grads(info, fsdp, n2, actives, hiddens, c_all):
    micros = len(actives)
    rows, units = actives[0].shape
    model = c_all.shape[3]
    block = model // fsdp
    wide = pltpu.VMEM((micros * rows, model), BF)
    return pl.pallas_call(
        functools.partial(feed_grads_kernel, micros, fsdp + 2),
        in_specs=[SMEM] + [ANY] * (micros * (SEQ + 2) + 1),
        out_specs=VMEM,
        out_shape=jax.ShapeDtypeStruct((fsdp, 2, block, model), BF),
        scratch_shapes=[wide] * 4
        + [pltpu.SemaphoreType.DMA((16,))] * 4,
        compiler_params=params(),
        cost_estimate=estimate(4 * micros * rows * units * model, 16 * 2**20),
        name="feed_grads",
    )(info, *n2, *actives, *hiddens, c_all)


def plain_rows(info, refs):
    return refs


def weight_grad(info, fsdp, lefts, rights, left_at=plain_rows, right_at=plain_rows, sums=(), shape=None):
    rows, total, cols = shape
    wide = cols + (LANES if sums else 0)
    out = jax.ShapeDtypeStruct((fsdp // 2, total // fsdp, wide), BF)
    return pl.pallas_call(
        functools.partial(weight_grad_kernel, len(lefts), len(rights), left_at, right_at),
        in_specs=[SMEM] + [ANY] * (len(lefts) + len(rights)) + [VMEM] * len(sums),
        out_specs=[ANY] * 2,
        out_shape=[out] * 2,
        scratch_shapes=[
            pltpu.VMEM((rows, total), BF),
            pltpu.VMEM((rows, cols), BF),
            pltpu.VMEM((total, wide), BF),
            pltpu.SemaphoreType.DMA((16,)),
            pltpu.SemaphoreType.DMA((16,)),
            pltpu.SemaphoreType.DMA((fsdp,)),
        ],
        compiler_params=params(),
        cost_estimate=estimate(2 * rows * total * cols, 2 * rows * (total + cols) + 2 * total * cols),
        name="weight_grad",
    )(info, *lefts, *rights, *sums)


def core_grad_kernel(count, core_at, info, *refs):
    lefts, rights = refs[:count], refs[count : 2 * count]
    here, there = refs[2 * count :]
    total, half = here.shape
    core = info[core_at]
    for ref, side in ((here, core), (there, 1 - core)):
        cols = pl.ds(pl.multiple_of(side * half, half), half)
        ref[...] = functools.reduce(
            jnp.add, [rows_dot(left[...], right[:, cols]) for left, right in zip(lefts, rights)]
        ).astype(BF)


def core_grad(info, fsdp, lefts, rights):
    model = lefts[0].shape[1]
    half = jax.ShapeDtypeStruct((model, model // 2), BF)
    rows = lefts[0].shape[0] * len(lefts)
    return pl.pallas_call(
        functools.partial(core_grad_kernel, len(lefts), fsdp + 1),
        in_specs=[SMEM] + [VMEM] * (2 * len(lefts)),
        out_specs=[VMEM] * 2,
        out_shape=[half] * 2,
        compiler_params=params(),
        cost_estimate=estimate(2 * rows * model * model, 4 * 2**20),
        name="core_grad",
    )(info, *lefts, *rights)


def core_split_kernel(info, here, came, keep, send):
    groups, block = keep.shape[:2]
    low_digit = info[0] % 2
    for at in range(groups):
        for ref, side in ((keep, low_digit), (send, 1 - low_digit)):
            place = pl.ds(pl.multiple_of((2 * at + side) * block, block), block)
            ref[at] = (here[place].astype(F32) + came[place].astype(F32)).astype(BF)


def core_split(info, fsdp, here, came):
    total, half = here.shape
    out = jax.ShapeDtypeStruct((fsdp // 2, total // fsdp, half), BF)
    return pl.pallas_call(
        core_split_kernel,
        in_specs=[SMEM] + [VMEM] * 2,
        out_specs=[VMEM] * 2,
        out_shape=[out] * 2,
        compiler_params=params(),
        name="core_split",
    )(info, here, came)


def attention_kernel(count, info, x_ref, keep_ref, vec, source, *refs):
    n1_ref, hat_ref, joined_ref, e0, e1, e2, e3, probs_ref, weight, sem = refs
    tokens, model = x_ref.shape[3:]
    rows = SEQ * tokens
    triple = weight.shape[1]
    width = triple // 3
    fetch = pltpu.make_async_copy(source, weight, sem)

    @pl.when(pl.program_id(0) == 0)
    def _():
        fetch.start()

    values = jnp.concatenate(
        [x_ref[info[count + 2 + k], 0, 0].astype(F32) for k in range(SEQ)], axis=0
    )
    hat, _ = norm_parts(values)
    hat_ref[...] = hat.astype(BF).reshape(hat_ref.shape)
    normed = (hat * vec[0:1, :] + vec[1:2, :]).astype(BF)
    n1_ref[...] = normed.reshape(n1_ref.shape)

    @pl.when(pl.program_id(0) == 0)
    def _():
        fetch.wait()

    place = pl.multiple_of(info[count] * width, width)
    bias = jnp.concatenate(
        [
            vec[2:3, pl.ds(place, width)],
            jnp.zeros((1, width), F32),
            vec[3:4, pl.ds(place, width)],
        ],
        axis=1,
    )
    joined = (plain_dot(normed, weight[...]) + bias).astype(BF)
    joined_ref[...] = joined.reshape(joined_ref.shape)
    keep = keep_ref[0] > 0
    outs = []
    for head in range(width // HEAD_DIM):
        low = head * HEAD_DIM
        q = joined[:, low : low + HEAD_DIM] * jnp.asarray(SCALE, BF)
        k = joined[:, width + low : width + low + HEAD_DIM]
        v = joined[:, 2 * width + low : 2 * width + low + HEAD_DIM]
        scores = jnp.where(keep, cols_dot(k, q), FILL)
        mass = jnp.exp(scores - jnp.max(scores, axis=0, keepdims=True))
        probs = (mass * (1.0 / jnp.sum(mass, axis=0, keepdims=True))).astype(BF)
        probs_ref[0, head] = probs
        outs.append(rows_dot(v, probs))
    attended = jnp.concatenate(outs, axis=0).T.astype(BF)
    for at, ref in enumerate((e0, e1, e2, e3)):
        ref[0] = attended[at * tokens : (at + 1) * tokens]


def attention(info, count, micro, x_all, keep, vec, weight):
    images, tokens, model = x_all.shape[2:]
    triple = weight.shape[1]
    width = triple // 3
    rows = SEQ * tokens
    heads = width // HEAD_DIM
    token_block = lambda cols: pl.BlockSpec((1, tokens, cols), lambda i: (i, 0, 0))
    group_block = lambda cols: pl.BlockSpec((SEQ, 1, tokens, cols), lambda i: (0, i, 0, 0))
    group_shape = lambda cols: jax.ShapeDtypeStruct((SEQ, images, tokens, cols), BF)
    return pl.pallas_call(
        functools.partial(attention_kernel, count),
        grid=(images,),
        in_specs=[SMEM]
        + [
            pl.BlockSpec((SEQ, 1, 1, tokens, model), lambda i: (0, micro, i, 0, 0)),
            pl.BlockSpec((1, rows, 1), lambda i: (i, 0, 0)),
            pl.BlockSpec(vec.shape, lambda i: (0, 0)),
            ANY,
        ],
        out_specs=[group_block(model), group_block(model), group_block(triple)]
        + [token_block(width)] * SEQ
        + [pl.BlockSpec((1, heads, rows, rows), lambda i: (i, 0, 0, 0))],
        out_shape=[group_shape(model), group_shape(model), group_shape(triple)]
        + [jax.ShapeDtypeStruct((images, tokens, width), BF)] * SEQ
        + [jax.ShapeDtypeStruct((images, heads, rows, rows), BF)],
        scratch_shapes=[pltpu.VMEM((model, triple), BF), pltpu.SemaphoreType.DMA],
        compiler_params=params(),
        cost_estimate=estimate(
            2 * images * rows * (model * triple + 4 * width * rows), 8 * 2**20
        ),
        name="attention",
    )(info, x_all, keep, vec, weight)


def out_weight_copies(info, count, mine, other, target, sem):
    half = mine.shape[1]
    core = info[count + 1]
    return [
        pltpu.make_async_copy(
            source, target.at[:, pl.ds(pl.multiple_of(side * half, half), half)], sem.at[which]
        )
        for which, (source, side) in enumerate(((mine, core), (other, 1 - core)))
    ]


def middle_kernel(count, info, e0, e1, e2, e3, x_ref, vec, mine, other, att_ref, mid_ref, n2_ref, weight, sem):
    copies = out_weight_copies(info, count, mine, other, weight, sem)
    for copy in copies:
        copy.start()
    width = e0.shape[1]
    for at, ref in enumerate((e0, e1, e2, e3)):
        place = info[count + 2 + at]
        att_ref[:, pl.ds(pl.multiple_of(place * width, width), width)] = ref[...]
    for copy in copies:
        copy.wait()
    middle = x_ref[...].astype(F32) + plain_dot(att_ref[...], weight[...]) + vec[4:5, :]
    mid_ref[...] = middle
    hat, _ = norm_parts(middle)
    n2_ref[...] = (hat * vec[5:6, :] + vec[6:7, :]).astype(BF)


def middle_part(info, count, heads, x_own, vec, mine, other):
    rows, model = x_own.shape
    return pl.pallas_call(
        functools.partial(middle_kernel, count),
        in_specs=[SMEM] + [VMEM] * 6 + [ANY] * 2,
        out_specs=[VMEM] * 3,
        out_shape=[
            jax.ShapeDtypeStruct((rows, model), BF),
            jax.ShapeDtypeStruct((rows, model), F32),
            jax.ShapeDtypeStruct((rows, model), BF),
        ],
        scratch_shapes=[
            pltpu.VMEM((model, model), BF),
            pltpu.SemaphoreType.DMA((2,)),
        ],
        compiler_params=params(),
        cost_estimate=estimate(2 * rows * model * model, 4 * 2**20),
        name="middle",
    )(info, *heads, x_own, vec, mine, other)


def feed_kernel(count, micro, info, *refs):
    n2 = refs[:SEQ]
    cot, vec = refs[SEQ : SEQ + 2]
    up_ref, down_ref = refs[SEQ + 2 : SEQ + 4]
    act_out, gh_out, down_chip, down_sib, up_chip, up_sib, sums = refs[SEQ + 4 : SEQ + 11]
    w_up, w_down, n2_in, c_in, up_sem, down_sem, n2_sem, c_sem = refs[SEQ + 11 :]
    rows = n2[0].shape[0]
    hidden = w_up.shape[1]
    ups = [pltpu.make_async_copy(up_ref, w_up, up_sem)]
    downs = [pltpu.make_async_copy(down_ref, w_down, down_sem)]
    n2_copies = row_copies(n2, n2_in, n2_sem)
    c_copies = row_copies([cot.at[info[count + 2 + k], micro] for k in range(SEQ)], c_in, c_sem)
    for copy in n2_copies + ups + c_copies + downs:
        copy.start()
    for copy in n2_copies + ups:
        copy.wait()
    total = jnp.zeros((1, hidden), F32)
    for half in range(2):
        span = slice(half * 2 * rows, (half + 1) * 2 * rows)
        values = plain_dot(n2_in[span], w_up[...]) + vec[8:9, :]
        normal = 0.5 * (1.0 + lax.erf(values * (2.0**-0.5)))
        slope = normal + values * (jnp.exp(values * values * -0.5) * 0.3989422804014327)
        active = (values * normal).astype(BF)
        act_out[span] = active
        if half == 0:
            for copy in c_copies + downs:
                copy.wait()
        grad_hidden = (slope * cols_dot(c_in[span], w_down[...])).astype(BF)
        gh_out[span] = grad_hidden
        total = total + column_sums(grad_hidden.astype(F32))
        shape = up_chip.shape
        (down_chip, down_sib)[half][...] = plain_dot(active, w_down[...]).astype(BF).reshape(shape)
        (up_chip, up_sib)[half][...] = cols_dot(grad_hidden, w_up[...]).astype(BF).reshape(shape)
    sums[...] = jnp.zeros(sums.shape, F32)
    sums[8:9, :] = total


def feed(info, count, micro, n2_pieces, c_all, vec, w_up, w_down):
    rows, model = n2_pieces[0].shape
    hidden = w_down.shape[0]
    hiddens = jax.ShapeDtypeStruct((SEQ * rows, hidden), BF)
    pair = jax.ShapeDtypeStruct((2, rows, model), BF)
    return pl.pallas_call(
        functools.partial(feed_kernel, count, micro),
        in_specs=[SMEM] + [ANY] * (SEQ + 1) + [VMEM] + [ANY] * 2,
        out_specs=[VMEM] * 7,
        out_shape=[hiddens, hiddens] + [pair] * 4 + [jax.ShapeDtypeStruct((16, model), F32)],
        scratch_shapes=[
            pltpu.VMEM((model, hidden), BF),
            pltpu.VMEM((hidden, model), BF),
            pltpu.VMEM((SEQ * rows, model), BF),
            pltpu.VMEM((SEQ * rows, model), BF),
            pltpu.SemaphoreType.DMA,
            pltpu.SemaphoreType.DMA,
            pltpu.SemaphoreType.DMA((SEQ,)),
            pltpu.SemaphoreType.DMA((SEQ,)),
        ],
        compiler_params=params(),
        cost_estimate=estimate(8 * SEQ * rows * model * hidden, 16 * 2**20),
        name="feed",
    )(info, *n2_pieces, c_all, vec, w_up, w_down)


def middle_back_kernel(count, info, p0, p1, p2, mid_ref, c_ref, vec, mine, other, gm_ref, gb_ref, g0, g1, g2, g3, sums, weight, scratch, sem):
    copies = out_weight_copies(info, count, mine, other, weight, sem)
    for copy in copies:
        copy.start()
    grad_two = p0[0].astype(F32) + p1[0].astype(F32) + p2[...].astype(F32)
    hat, scale = norm_parts(mid_ref[...])
    cot = c_ref[...].astype(F32)
    grad_middle = cot + norm_back(grad_two, hat, scale, vec[5:6, :])
    gm_ref[...] = grad_middle
    branch = grad_middle.astype(BF)
    gb_ref[...] = branch
    sums[...] = jnp.zeros(sums.shape, F32)
    sums[4:5, :] = column_sums(branch.astype(F32))
    sums[5:6, :] = column_sums(grad_two * hat)
    sums[6:7, :] = column_sums(grad_two)
    sums[7:8, :] = column_sums(cot)
    for copy in copies:
        copy.wait()
    scratch[...] = cols_dot(branch, weight[...]).astype(BF)
    width = g0.shape[1]
    for at, ref in enumerate((g0, g1, g2, g3)):
        place = info[count + 2 + at]
        ref[...] = scratch[:, pl.ds(pl.multiple_of(place * width, width), width)]


def middle_back(info, count, parts, middle, c_own, vec, mine, other):
    rows, model = middle.shape
    piece = jax.ShapeDtypeStruct((rows, model // SEQ), BF)
    return pl.pallas_call(
        functools.partial(middle_back_kernel, count),
        in_specs=[SMEM] + [VMEM] * 6 + [ANY] * 2,
        out_specs=[VMEM] * 7,
        out_shape=[
            jax.ShapeDtypeStruct((rows, model), F32),
            jax.ShapeDtypeStruct((rows, model), BF),
        ]
        + [piece] * 4
        + [jax.ShapeDtypeStruct((16, model), F32)],
        scratch_shapes=[
            pltpu.VMEM((model, model), BF),
            pltpu.VMEM((rows, model), BF),
            pltpu.SemaphoreType.DMA((2,)),
        ],
        compiler_params=params(),
        cost_estimate=estimate(2 * rows * model * model, 4 * 2**20),
        name="middle_back",
    )(info, *parts, middle, c_own, vec, mine, other)


def attention_back_kernel(count, info, joined_ref, probs_ref, g0, g1, g2, g3, hat_ref, source, *refs):
    out_ref, chip_ref, sib_ref, sums, weight, sem = refs
    tokens = joined_ref.shape[2]
    rows = SEQ * tokens
    triple = joined_ref.shape[3]
    width = triple // 3
    model = weight.shape[0]
    fetch = pltpu.make_async_copy(source, weight, sem)

    @pl.when(pl.program_id(0) == 0)
    def _():
        fetch.start()
        sums[...] = jnp.zeros(sums.shape, F32)

    joined = joined_ref[...].reshape(rows, triple)
    grad = jnp.concatenate([g0[0], g1[0], g2[0], g3[0]], axis=0)
    queries, keys, values = [], [], []
    for head in range(width // HEAD_DIM):
        low = head * HEAD_DIM
        q = joined[:, low : low + HEAD_DIM] * jnp.asarray(SCALE, BF)
        k = joined[:, width + low : width + low + HEAD_DIM] * jnp.asarray(SCALE, BF)
        v = joined[:, 2 * width + low : 2 * width + low + HEAD_DIM]
        ga = grad[:, low : low + HEAD_DIM]
        probs = probs_ref[0, head]
        values.append(plain_dot(probs, ga).astype(BF))
        wide = probs.astype(F32)
        weighted = wide * cols_dot(v, ga)
        centre = jnp.sum(weighted, axis=0, keepdims=True)
        grad_scores = (weighted - wide * centre).astype(BF)
        keys.append(plain_dot(grad_scores, q).astype(BF))
        queries.append(rows_dot(k, grad_scores))
    grad_joined = jnp.concatenate(
        [jnp.concatenate(queries, axis=0).T.astype(BF)] + keys + values, axis=1
    )
    out_ref[...] = grad_joined.reshape(out_ref.shape)
    wide = grad_joined.astype(F32)
    place = pl.multiple_of(info[count] * width, width)
    sums[2:3, pl.ds(place, width)] += column_sums(wide[:, :width])
    sums[3:4, pl.ds(place, width)] += column_sums(wide[:, 2 * width :])

    @pl.when(pl.program_id(0) == 0)
    def _():
        fetch.wait()

    partial = cols_dot(grad_joined, weight[...])
    hat = hat_ref[...].reshape(rows, model).astype(F32)
    sums[0:1, :] += column_sums(partial * hat)
    sums[1:2, :] += column_sums(partial)
    low = partial.astype(BF)
    half = rows // 2
    chip_ref[...] = low[:half].reshape(chip_ref.shape)
    sib_ref[...] = low[half:].reshape(sib_ref.shape)


def attention_back(info, count, joined, probs, grads, hat, weight):
    _, images, tokens, triple = joined.shape
    model = hat.shape[3]
    width = triple // 3
    rows = SEQ * tokens
    heads = width // HEAD_DIM
    pair = jax.ShapeDtypeStruct((2, images, tokens, model), BF)
    group_block = lambda n, cols: pl.BlockSpec((n, 1, tokens, cols), lambda i: (0, i, 0, 0))
    return pl.pallas_call(
        functools.partial(attention_back_kernel, count),
        grid=(images,),
        in_specs=[
            SMEM,
            group_block(SEQ, triple),
            pl.BlockSpec((1, heads, rows, rows), lambda i: (i, 0, 0, 0)),
        ]
        + [pl.BlockSpec((1, tokens, width), lambda i: (i, 0, 0))] * SEQ
        + [group_block(SEQ, model), ANY],
        out_specs=[
            group_block(SEQ, triple),
            group_block(2, model),
            group_block(2, model),
            pl.BlockSpec((16, model), lambda i: (0, 0)),
        ],
        out_shape=[
            jax.ShapeDtypeStruct(joined.shape, BF),
            pair,
            pair,
            jax.ShapeDtypeStruct((16, model), F32),
        ],
        scratch_shapes=[pltpu.VMEM((model, triple), BF), pltpu.SemaphoreType.DMA],
        compiler_params=params(),
        cost_estimate=estimate(
            2 * images * rows * (model * triple + 8 * width * rows), 8 * 2**20
        ),
        name="attention_back",
    )(info, joined, probs, *grads, hat, weight)


def on_device(
    fsdp,
    inputs,
    keep_mask,
    cotangent,
    first_gain,
    first_shift,
    qkv_weight,
    query_bias,
    value_bias,
    out_weight,
    out_bias,
    second_gain,
    second_shift,
    up_weight,
    up_bias,
    down_weight,
    down_bias,
):
    micros, images, tokens, model = inputs.shape
    rows = images * tokens
    at_f, at_s = lax.axis_index("fsdp"), lax.axis_index("seq")
    depth = qkv_weight.shape[0]
    block = SEQ * depth
    width = model // SEQ
    triple = 3 * width
    half = model // 2
    unit_block = up_bias.shape[0]
    units = fsdp * unit_block
    core = at_s & 1
    micro_range = range(micros)
    info = jnp.stack(
        [jnp.asarray(v, jnp.int32) for v in fsdp_owners(fsdp, at_f)]
        + [at_s, core]
        + [at_s ^ mask for mask in ORDER]
    )

    vectors = jnp.stack(
        [
            first_gain,
            first_shift,
            query_bias,
            value_bias,
            out_bias,
            second_gain,
            second_shift,
            down_bias,
        ],
        axis=1,
    )
    vectors = jnp.pad(vectors, ((0, 0), (0, LANES - VECTORS)))
    to_send = pack(fsdp, qkv_weight, out_weight, vectors, up_weight)
    arrived = lax.all_to_all(to_send, "seq", 0, 0, tiled=True).reshape(block, -1)
    early = triple + LANES
    bias_column = jnp.pad(up_bias[:, None], ((0, 0), (VECTORS, LANES - VECTORS - 1)))
    first_group = jnp.concatenate(
        [arrived[:, :triple], arrived[:, triple:early] + bias_column], axis=1
    )
    second_group = arrived[:, early:]
    x_all = lax.all_gather(inputs, "seq")
    c_all = lax.all_gather(cotangent.reshape(micros, rows, model), "seq")
    ordered = len(digits_of(fsdp)) == 2 and digits_of(fsdp)[1][1] == 4
    if ordered:
        down = Gather(down_weight, fsdp)
        down.send(0), down.send(1), down.forward(None)
        first = Gather(first_group, fsdp)
        first.send(0, down.came[0])
        first.send(1, down.came[1])
        first.send(2, down.passed[None])
        first.forward(None, down.passed[None])
        for at in range(3):
            first.forward(at)
        second = Gather(second_group, fsdp)
        second.send(0, first.came[0], first.came[1])
        second.send(1, first.came[2])
        second.forward(None, first.passed[0])
        down.forward(0, first.passed[1])
        down.forward(1, first.passed[1])
        first_pieces = first.pieces()
    else:
        first_pieces = fsdp_gather(first_group, fsdp)
        second_pieces = fsdp_gather(second_group, fsdp)
        down_pieces = fsdp_gather(down_weight, fsdp)
    x_own = [inputs[m].reshape(rows, model) for m in micro_range]
    c_own = [cotangent[m].reshape(rows, model) for m in micro_range]

    w_qkv, _, vec = placed(info, first_pieces, (0, triple), (triple, LANES), vectors=True)
    n1s, hats, joineds, probs, heads_in = [], [], [], [], []
    for m in micro_range:
        keep = keep_mask[m].reshape(images, SEQ, tokens)
        keep = jnp.stack(
            [lax.dynamic_index_in_dim(keep, at_s ^ mask, 1, keepdims=False) for mask in ORDER], axis=1
        )
        keep = after(keep, *joineds[-1:])
        n1, hat, joined, *heads_out, prob = attention(
            info,
            fsdp,
            m,
            x_all,
            keep.reshape(images, SEQ * tokens, 1),
            vec,
            w_qkv,
        )
        n1s.append(n1)
        hats.append(hat)
        joineds.append(joined)
        probs.append(prob)
        heads_in.append(seq_exchange([h.reshape(rows, width) for h in heads_out]))
        if ordered and m == 0:
            second.send(2, joined)
            second.forward(0, joined)
            second.forward(1, joined)
            down.send(2, joined, second.came[0])
        if ordered and m == micros - 1:
            second.forward(2, joined)
            down.forward(2, joined)
            second_pieces, down_pieces = second.pieces(), down.pieces()

    out_mine, w_up = placed(info, second_pieces, (0, half), (half, units))
    (w_down,) = placed(info, down_pieces, (0, model))
    out_other = hop(out_mine, 1)

    attendeds, middles, n2_pieces = [], [], []
    heads_in[0][0] = after(heads_in[0][0], joineds[-1])
    for m in micro_range:
        attended, middle, normed = middle_part(
            info, fsdp, heads_in[m], x_own[m], vec, out_mine, out_other
        )
        attendeds.append(attended)
        middles.append(middle)
        if m + 1 < micros:
            heads_in[m + 1][0] = after(heads_in[m + 1][0], middle)
        n2_pieces.append(seq_gather(normed))

    actives, grad_hiddens, two_parts, down_parts, sums = [], [], [], [], []
    n2_pieces[0][0] = after(n2_pieces[0][0], middles[-1])
    for m in micro_range:
        active, grad_hidden, down_chip, down_sib, up_chip, up_sib, part = feed(
            info, fsdp, m, n2_pieces[m], c_all, vec, w_up, w_down
        )
        actives.append(active)
        grad_hiddens.append(grad_hidden)
        sums.append(part)
        down_parts.append((down_chip, down_sib))
        came, far = seq_scatter(up_chip, up_sib)
        two_parts.append((up_chip, came, hop(far, 2)))
        if m + 1 < micros:
            n2_pieces[m + 1][0] = after(n2_pieces[m + 1][0], far)
        else:
            actives[0] = after(actives[0], far)

    group_rows = micros * SEQ * rows

    feed_grad = feed_grads(info, fsdp, n2_pieces[0] + n2_pieces[1], actives, grad_hiddens, c_all)
    down_grad, up_grad = lax.psum_scatter(feed_grad, "fsdp", scatter_dimension=0, tiled=False)
    down_grad = down_grad.astype(F32)

    grad_middles, branches, grads_in = [], [], []
    for m in micro_range:
        grad_middle, branch, *grads_out, part = middle_back(
            info, fsdp, two_parts[m], after(middles[m], feed_grad), c_own[m], vec, out_mine, out_other
        )
        grad_middles.append(grad_middle)
        branches.append(branch)
        sums.append(part)
        if m + 1 < micros:
            middles[m + 1] = after(middles[m + 1], branch)
        grads_in.append(seq_exchange(grads_out))

    out_here, out_there = core_grad(info, fsdp, attendeds, branches)
    out_blocks = core_split(info, fsdp, out_here, hop(out_there, 1))
    out_grad = scatter_far(scatter_near(*out_blocks, fsdp, at_f), fsdp, at_f)

    grads_in[0][0] = after(grads_in[0][0], branches[-1])
    joined_grads, inputs_back = [], []
    one_parts = []
    for m in micro_range:
        grad_joined, chip, sib, part = attention_back(
            info,
            fsdp,
            joineds[m],
            probs[m],
            [g.reshape(images, tokens, width) for g in grads_in[m]],
            hats[m],
            w_qkv,
        )
        joined_grads.append(grad_joined.reshape(SEQ * rows, triple))
        sums.append(part)
        if m + 1 < micros:
            joineds[m + 1] = after(joineds[m + 1], grad_joined)
        chip = chip.reshape(2, rows, model)
        came, far = seq_scatter(chip, sib.reshape(2, rows, model))
        one_parts.append((chip[0], came[0], hop(far, 2)))
    outputs = []
    for m in micro_range:
        chip, sib = down_parts[m]
        came, far = seq_scatter(chip, after(sib, branches[-1]))
        total = chip[0].astype(F32) + came[0].astype(F32) + hop(far, 2).astype(F32)
        result = middles[m] + total + vec[7:8]
        outputs.append(result.astype(BF).reshape(images, tokens, model))
    for m in micro_range:
        a, b, c = one_parts[m]
        grad_one = a.astype(F32) + b.astype(F32) + c.astype(F32)
        hat, scale = norm_parts(x_own[m].astype(F32))
        back = grad_middles[m] + norm_back(grad_one, hat, scale, vec[0:1])
        inputs_back.append(back.astype(BF).reshape(images, tokens, model))

    qkv_grad = weight_grad(
        info,
        fsdp,
        [n.reshape(SEQ * rows, model) for n in n1s],
        joined_grads,
        sums=sums,
        shape=(group_rows, model, triple),
    )
    qkv_grad = scatter_far(scatter_near(*qkv_grad, fsdp, at_f), fsdp, at_f)
    up_bias_grad = qkv_grad[:, triple + VECTORS]

    last = jnp.concatenate([qkv_grad.astype(BF), out_grad.astype(BF), up_grad], axis=1)
    last = lax.all_to_all(last.reshape(SEQ, depth, -1), "seq", 0, 0, tiled=True)
    qkv_weight_grad, out_weight_grad, up_weight_grad, vector_grads = unpack(last, model, units)
    vector_grads = vector_grads[:, :VECTORS].T

    return (
        jnp.stack(outputs),
        jnp.stack(inputs_back),
        vector_grads[0],
        vector_grads[1],
        qkv_weight_grad,
        vector_grads[2],
        vector_grads[3],
        out_weight_grad,
        vector_grads[4],
        vector_grads[5],
        vector_grads[6],
        up_weight_grad,
        up_bias_grad,
        down_grad,
        vector_grads[7],
    )


def solution(mesh):
    shard = P(BOTH)
    tokens = P(None, "fsdp", "seq", None)
    in_specs = (tokens, P(None, "fsdp", None), tokens) + (shard,) * 13
    out_specs = (tokens, tokens) + (shard,) * 13
    return jax.shard_map(
        functools.partial(on_device, mesh.shape["fsdp"]),
        mesh=mesh,
        in_specs=in_specs,
        out_specs=out_specs,
        check_vma=False,
    )
```

time: 526 us -> 372 us (0.71)
  Pallas kernels: 14.9 us -> 120 us
  waiting for transfers between devices: 223 us -> 122 us
  starting transfers between devices: 131 us -> 68.9 us
  matrix products: 59.2 us -> 0 us
  other arithmetic: 46.1 us -> 17.5 us
  local copies, waits for them, and re-layouts: 40.8 us -> 21.9 us
  between operations: 3.26 us -> 15 us
    pallas_call x4 -> x21, Pallas kernels: 14.9 us -> 120 us  [the longest x2 21.4 us: feed(): pl.pallas_call(functools.partial(feed_kernel, count, micro), in_specs=[SM...]
    ppermute x55 -> x29, waiting for transfers between devices: 161 us -> 72.3 us  [shift(): return lax.ppermute(array, 'fsdp', pairs)]
    dot_general x20 -> x0, matrix products: 59.2 us -> none  [the longest x8 27.4 us: plain_dot(): return jnp.dot(left, right, preferred_element_type=F32)]
    ppermute x55 -> x29, starting transfers between devices: 88.5 us -> 41.7 us  [shift(): return lax.ppermute(array, 'fsdp', pairs)]
    ppermute x72 -> x32, waiting for transfers between devices: 62.4 us -> 32 us  [hop(): return lax.ppermute(array, 'seq', [(i, i ^ mask) for i in range(SEQ)])]
    ppermute x72 -> x32, starting transfers between devices: 42.1 us -> 19.3 us  [hop(): return lax.ppermute(array, 'seq', [(i, i ^ mask) for i in range(SEQ)])]
    all_to_all x0 -> x2, waiting for transfers between devices: none -> 15.8 us  [the longest x1 8 us: on_device(): last = lax.all_to_all(last.reshape(SEQ, depth, -1), 'seq', 0, 0, tiled=True)]
    dynamic_update_slice x41 -> x0, local copies, waits for them, and re-layouts: 7.89 us -> none  [the longest x38 7.35 us: fsdp_gather(): out = lax.dynamic_update_index_in_dim(out, piece, owner, 0)]
  transfers between devices with their start and end apart: 127 -> 66, of which waited for: 53 -> 24; matrix products, arithmetic and copies ran while one was open for 23% -> 6% of each run, Pallas kernels for 3% -> 23%
where the time goes in v2:
time: 372 us; the launch traced here: 365 us
  waiting for transfers between devices  122 us (33%)
  Pallas kernels  120 us (32%)
  starting transfers between devices  68.9 us (19%)
  local copies, waits for them, and re-layouts  21.9 us (6%)
  other arithmetic  17.5 us (5%)
  between operations  15 us (4%)
    ppermute x29, waiting for transfers between devices, shift(): return lax.ppermute(array, 'fsdp', pairs)  72.3 us
    ppermute x29, starting transfers between devices, shift(): return lax.ppermute(array, 'fsdp', pairs)  41.7 us
    ppermute x32, waiting for transfers between devices, hop(): return lax.ppermute(array, 'seq', [(i, i ^ mask) for i in range(SEQ)])  32 us
    pallas_call x2, Pallas kernels, feed(): pl.pallas_call(functools.partial(feed_kernel, count, micro), in_specs=[SM...  21.4 us
    ppermute x32, starting transfers between devices, hop(): return lax.ppermute(array, 'seq', [(i, i ^ mask) for i in range(SEQ)])  19.3 us
    pallas_call x2, Pallas kernels, attention(): pl.pallas_call(functools.partial(attention_kernel, count), grid=(images,)...  19 us
    pallas_call x2, Pallas kernels, attention_back(): pl.pallas_call(functools.partial(attention_back_kernel, count), grid=(ima...  16.3 us
    pallas_call x1, Pallas kernels, feed_grads(): pl.pallas_call(functools.partial(feed_grads_kernel, micros, fsdp + 2), in...  12.7 us
  transfers between devices with their start and end apart: 66, of which 24 were waited for; matrix products, arithmetic and copies ran while one was open for 6% of the time, Pallas kernels for 23%

profile of v2, /device:TPU:0, one launch (start us, length us, event | category | flops | bytes accessed | tf_op | source)
XLA Modules:
  0.0 364.6 jit_solution(9152077058952227965)
XLA Ops:
  9.6 2.0 pack.1
  11.6 4.3 %all-to-all-start = ((bf16[4,32,2432]{2,1,0:T(8,128)(2,1)}), bf16[4,32,2432]{2,1,0:T(8,128)(2,1)S(1)}, u32[]{:S(2)}, u32[]{:S(2)}) async-start(bf16[4,32,2432]{2,1,0:T(8,128)(2,1)} %pack.1), calls=%async_computation | async-start | bytes 1245184 | tf_op jit(solution)/shard_map/all_to_all | solution.py:835
  15.9 4.4 %collective-permute-start.2 = (bf16[128,1024]{1,0:T(8,128)(2,1)S(1)}, bf16[128,1024]{1,0:T(8,128)(2,1)S(1)}, u32[]{:S(2)}, u32[]{:S(2)}) collective-permute-start(bf16[128,1024]{1,0:T(8,128)(2,1)S(1)} %copy-done.30), channel_id=1, source_target_pairs={{0,24},{4,28},{8,0},{12,4},{16,8},{20,12},{24,16},{28,20},{1,25},{... | collective-permute-start | bytes 786440 | tf_op jit(solution)/shard_map/ppermute | solution.py:57
  22.0 7.8 %all-to-all-done = bf16[4,32,2432]{2,1,0:T(8,128)(2,1)S(1)} async-done(((bf16[4,32,2432]{2,1,0:T(8,128)(2,1)}), bf16[4,32,2432]{2,1,0:T(8,128)(2,1)S(1)}, u32[]{:S(2)}, u32[]{:S(2)}) %all-to-all-start) | async-done | bytes 622624 | tf_op jit(solution)/shard_map/all_to_all | solution.py:835
  30.0 5.1 %collective-permute-start.3 = (bf16[128,896]{1,0:T(8,128)(2,1)S(1)}, bf16[128,896]{1,0:T(8,128)(2,1)S(1)}, u32[]{:S(2)}, u32[]{:S(2)}) collective-permute-start(bf16[128,896]{1,0:T(8,128)(2,1)S(1)} %pad_maximum_fusion.3.refs_0_), channel_id=1, source_target_pairs={{0,24},{4,28},{8,0},{12,4},{16,8},{20,12},{24,16},{28,20},{1,25},{... | collective-permute-start | bytes 688136 | tf_op jit(solution)/shard_map/ppermute | solution.py:57
  37.6 3.6 collective-permute-done.3.refs_2_
  42.7 3.8 %collective-permute-done.1.refs_1_ = bf16[128,896]{1,0:T(8,128)(2,1)S(1)} collective-permute-done((bf16[128,896]{1,0:T(8,128)(2,1)S(1)}, bf16[128,896]{1,0:T(8,128)(2,1)S(1)}, u32[]{:S(2)}, u32[]{:S(2)}) %collective-permute-start.1) | collective-permute-done | bytes 229408 | tf_op jit(solution)/shard_map/ppermute | solution.py:57
  48.0 5.3 %collective-permute-done.5.refs_3_ = bf16[128,896]{1,0:T(8,128)(2,1)S(1)} collective-permute-done((bf16[128,896]{1,0:T(8,128)(2,1)S(1)}, bf16[128,896]{1,0:T(8,128)(2,1)S(1)}, u32[]{:S(2)}, u32[]{:S(2)}) %collective-permute-start.5) | collective-permute-done | bytes 229408 | tf_op jit(solution)/shard_map/ppermute | solution.py:57
  57.6 2.9 collective-permute-start.14
  61.2 2.9 placed.3
  64.2 9.4 %attention.2 = (bf16[4,2,80,1024]{3,2,1,0:T(8,128)(2,1)}, bf16[4,2,80,1024]{3,2,1,0:T(8,128)(2,1)}, bf16[4,2,80,768]{3,2,1,0:T(8,128)(2,1)}, bf16[2,80,256]{2,1,...) custom-call(s32[14]{0:T(128)} %stack.103.info, ...), custom_call_target="tpu_custom_call" | custom-call | flops 1426063360 | bytes 8388608 | tf_op jit(solution)/shard_map/attention/pallas_call | solution.py:505
  79.0 9.6 %attention.3 = (bf16[4,2,80,1024]{3,2,1,0:T(8,128)(2,1)}, bf16[4,2,80,1024]{3,2,1,0:T(8,128)(2,1)}, bf16[4,2,80,768]{3,2,1,0:T(8,128)(2,1)}, bf16[2,80,256]{2,1,...) custom-call(s32[14]{0:T(128)} %stack.103.info, ...), custom_call_target="tpu_custom_call" | custom-call | flops 1426063360 | bytes 8388608 | tf_op jit(solution)/shard_map/attention/pallas_call | solution.py:505
  88.7 5.1 %collective-permute-done.15.refs_3_ = bf16[128,1536]{1,0:T(8,128)(2,1)S(1)} collective-permute-done((bf16[128,1536]{1,0:T(8,128)(2,1)S(1)}, bf16[128,1536]{1,0:T(8,128)(2,1)S(1)}, u32[]{:S(2)}, u32[]{:S(2)}) %collective-permute-start.15) | collective-permute-done | bytes 393248 | tf_op jit(solution)/shard_map/ppermute | solution.py:57
  95.1 8.4 %collective-permute-done.18.refs_6_ = bf16[128,1536]{1,0:T(8,128)(2,1)S(1)} collective-permute-done((bf16[128,1536]{1,0:T(8,128)(2,1)S(1)}, bf16[128,1536]{1,0:T(8,128)(2,1)S(1)}, u32[]{:S(2)}, u32[]{:S(2)}) %collective-permute-start.18) | collective-permute-done | bytes 393248 | tf_op jit(solution)/shard_map/ppermute | solution.py:57
  103.5 5.4 %collective-permute-done.19.refs_7_ = bf16[128,1536]{1,0:T(8,128)(2,1)} collective-permute-done((bf16[128,1536]{1,0:T(8,128)(2,1)S(1)}, bf16[128,1536]{1,0:T(8,128)(2,1)}, u32[]{:S(2)}, u32[]{:S(2)}) %collective-permute-start.19) | collective-permute-done | bytes 393248 | tf_op jit(solution)/shard_map/ppermute | solution.py:57
  108.9 3.8 %placed.4 = (bf16[1024,512]{1,0:T(8,128)(2,1)}, bf16[1024,1024]{1,0:T(8,128)(2,1)}) custom-call(s32[14]{0:T(128)} %stack.103.info, bf16[128,1536]{1,0:T(8,128)(2,1)} %copy-done.8, bf16[128,1536]{1,0:T(8,128)(2,1)} %copy-done.22, bf16[128,1536]{1,0:T(8,128)(2,1)} %copy-done.23, bf16[128,1536]{1,0:T(8,128)(2,1)} %copy-done.24, bf16[128,1536]{1,0:T(8,128)(2,1)} %copy-done.25, ...), custom_call_target="tpu_custom_call" | custom-call | tf_op jit(solution)/shard_map/placed/pallas_call | solution.py:275
  112.7 2.3 collective-permute-start.10
  120.5 4.3 %middle.2 = (bf16[160,1024]{1,0:T(8,128)(2,1)}, f32[160,1024]{1,0:T(8,128)}, bf16[160,1024]{1,0:T(8,128)(2,1)}) custom-call(s32[14]{0:T(128)} %stack.103.info, bf16[160,256]{1,0:T(8,128)(2,1)} %bitcast.154, bf16[160,256]{1,0:T(8,128)(2,1)} %copy-done.49, bf16[160,256]{1,0:T(8,128)(2,1)} %copy-done.50, bf16[160,256]{1,0:T(8,128)(2,1)} %copy-done.52, ...), custom_call_target="tpu_custom_call" | custom-call | flops 335544320 | bytes 4194304 | tf_op jit(solution)/shard_map/middle/pallas_call | solution.py:559
  126.5 2.4 collective-permute-start.27
  130.9 10.3 %collective-permute-done.27.refs_3_ = bf16[128,1024]{1,0:T(8,128)(2,1)S(1)} collective-permute-done((bf16[128,1024]{1,0:T(8,128)(2,1)S(1)}, bf16[128,1024]{1,0:T(8,128)(2,1)S(1)}, u32[]{:S(2)}, u32[]{:S(2)}) %collective-permute-start.27) | collective-permute-done | bytes 262176 | tf_op jit(solution)/shard_map/ppermute | solution.py:57
  142.8 5.7 %collective-permute-done.30.refs_7_ = bf16[128,1024]{1,0:T(8,128)(2,1)S(1)} collective-permute-done((bf16[128,1024]{1,0:T(8,128)(2,1)S(1)}, bf16[128,1024]{1,0:T(8,128)(2,1)S(1)}, u32[]{:S(2)}, u32[]{:S(2)}) %collective-permute-start.30) | collective-permute-done | bytes 262176 | tf_op jit(solution)/shard_map/ppermute | solution.py:57
  149.3 3.0 placed.5.refs_7_
  153.1 4.2 %middle.3 = (bf16[160,1024]{1,0:T(8,128)(2,1)}, f32[160,1024]{1,0:T(8,128)}, bf16[160,1024]{1,0:T(8,128)(2,1)}) custom-call(s32[14]{0:T(128)} %stack.103.info, bf16[160,256]{1,0:T(8,128)(2,1)} %bitcast.153, bf16[160,256]{1,0:T(8,128)(2,1)} %copy-done.47, bf16[160,256]{1,0:T(8,128)(2,1)} %copy-done.48, bf16[160,256]{1,0:T(8,128)(2,1)} %copy-done.51, ...), custom_call_target="tpu_custom_call" | custom-call | flops 335544320 | bytes 4194304 | tf_op jit(solution)/shard_map/middle/pallas_call | solution.py:559
  158.2 10.5 %feed.2 = (bf16[640,1024]{1,0:T(8,128)(2,1)}, bf16[640,1024]{1,0:T(8,128)(2,1)}, bf16[2,160,1024]{2,1,0:T(8,128)(2,1)}, bf16[2,160,1024]{2,1,0:T(8,128)(2,1)}, b...) custom-call(s32[14]{0:T(128)} %stack.103.info, ...), custom_call_target="tpu_custom_call" | custom-call | flops 5368709120 | bytes 16777216 | tf_op jit(solution)/shard_map/feed/pallas_call | solution.py:620
  170.1 8.8 %collective-permute-done.32.refs_1_.refs_5_ = bf16[160,1024]{1,0:T(8,128)(2,1)S(1)} collective-permute-done((bf16[160,1024]{1,0:T(8,128)(2,1)S(1)}, bf16[160,1024]{1,0:T(8,128)(2,1)S(1)}, u32[]{:S(2)}, u32[]{:S(2)}) %collective-permute-start.32) | collective-permute-done | bytes 327712 | tf_op jit(solution)/shard_map/ppermute | solution.py:26
  181.8 10.9 %feed.3 = (bf16[640,1024]{1,0:T(8,128)(2,1)}, bf16[640,1024]{1,0:T(8,128)(2,1)}, bf16[2,160,1024]{2,1,0:T(8,128)(2,1)}, bf16[2,160,1024]{2,1,0:T(8,128)(2,1)}, b...) custom-call(s32[14]{0:T(128)} %stack.103.info, ...), custom_call_target="tpu_custom_call" | custom-call | flops 5368709120 | bytes 16777216 | tf_op jit(solution)/shard_map/feed/pallas_call | solution.py:620
  196.4 12.7 %feed_grads.1 = bf16[8,2,128,1024]{3,2,1,0:T(8,128)(2,1)} custom-call(s32[14]{0:T(128)} %stack.103.info, bf16[160,1024]{1,0:T(8,128)(2,1)} %get-tuple-element.151.refs_0_, bf16[160,1024]{1,0:T(8,128)(2,1)} %copy-done.63, bf16[160,1024]{1,0:T(8,128)(2,1)} %copy-done.64, bf16[160,1024]{1,0:T(8,128)(2,1)} %copy-done.65, ...), custom_call_target="tpu_custom_call" | custom-call | flops 5368709120 | bytes 16777216 | tf_op jit(solution)/shard_map/feed_grads/pallas_call | solution.py:355
  214.4 7.3 %collective-permute-done.37.p2 = bf16[160,1024]{1,0:T(8,128)(2,1)S(1)} collective-permute-done((bf16[160,1024]{1,0:T(8,128)(2,1)S(1)}, bf16[160,1024]{1,0:T(8,128)(2,1)S(1)}, u32[]{:S(2)}, u32[]{:S(2)}) %collective-permute-start.37) | collective-permute-done | bytes 327712 | tf_op jit(solution)/shard_map/ppermute | solution.py:26
  222.4 4.9 %middle_back.2 = (f32[160,1024]{1,0:T(8,128)}, bf16[160,1024]{1,0:T(8,128)(2,1)}, bf16[160,256]{1,0:T(8,128)(2,1)}, bf16[160,256]{1,0:T(8,128)(2,1)}, bf16[160,2...) custom-call(s32[14]{0:T(128)} %stack.103.info, bf16[2,160,1024]{2,1,0:T(8,128)(2,1)} %get-tuple-element.160.p0, ...), custom_call_target="tpu_custom_call" | custom-call | flops 335544320 | bytes 4194304 | tf_op jit(solution)/shard_map/middle_back/pallas_call | solution.py:669
  230.2 4.9 %middle_back.3 = (f32[160,1024]{1,0:T(8,128)}, bf16[160,1024]{1,0:T(8,128)(2,1)}, bf16[160,256]{1,0:T(8,128)(2,1)}, bf16[160,256]{1,0:T(8,128)(2,1)}, bf16[160,2...) custom-call(s32[14]{0:T(128)} %stack.103.info, bf16[2,160,1024]{2,1,0:T(8,128)(2,1)} %get-tuple-element.163.p0, ...), custom_call_target="tpu_custom_call" | custom-call | flops 335544320 | bytes 4194304 | tf_op jit(solution)/shard_map/middle_back/pallas_call | solution.py:669
  236.3 3.8 %core_grad.1 = (bf16[1024,512]{1,0:T(8,128)(2,1)}, bf16[1024,512]{1,0:T(8,128)(2,1)}) custom-call(s32[14]{0:T(128)} %stack.103.info, bf16[160,1024]{1,0:T(8,128)(2,1)} %get-tuple-element.215.refs_0_, bf16[160,1024]{1,0:T(8,128)(2,1)} %get-tuple-element.216.refs_1_, bf16[160,1024]{1,0:T(8,128)(2,1)} %get-tuple-element.171.refs_2_, ...), custom_call_target="tpu_custom_call" | custom-call | flops 671088640 | bytes 4194304 | tf_op jit(solution)/shard_map/core_grad/pallas_call | solution.py:411
  241.9 8.1 %attention_back.2 = (bf16[4,2,80,768]{3,2,1,0:T(8,128)(2,1)}, bf16[2,2,80,1024]{3,2,1,0:T(8,128)(2,1)}, bf16[2,2,80,1024]{3,2,1,0:T(8,128)(2,1)}, f32[16,1024]{1,0:T(8,128)}) custom-call(s32[14]{0:T(128)} %stack.103.info, bf16[4,2,80,768]{3,2,1,0:T(8,128)(2,1)} %get-tuple-element.128.joined_ref, bf16[2,4,320,320]{3,2,1,0:T(8,128)(2,1)} %get-tuple-element.180.probs_ref, ...), custom_call_target="tpu_custom_call" | custom-call | flops 1845493760 | bytes 8388608 | tf_op jit(solution)/shard_map/attention_back/pallas_call | solution.py:752
  252.5 8.2 %attention_back.3 = (bf16[4,2,80,768]{3,2,1,0:T(8,128)(2,1)}, bf16[2,2,80,1024]{3,2,1,0:T(8,128)(2,1)}, bf16[2,2,80,1024]{3,2,1,0:T(8,128)(2,1)}, f32[16,1024]{1,0:T(8,128)}) custom-call(s32[14]{0:T(128)} %stack.103.info, bf16[4,2,80,768]{3,2,1,0:T(8,128)(2,1)} %get-tuple-element.191.joined_ref, bf16[2,4,320,320]{3,2,1,0:T(8,128)(2,1)} %get-tuple-element.192.probs_ref, ...), custom_call_target="tpu_custom_call" | custom-call | flops 1845493760 | bytes 8388608 | tf_op jit(solution)/shard_map/attention_back/pallas_call | solution.py:752
  260.7 7.3 %weight_grad.1 = (bf16[4,128,896]{2,1,0:T(8,128)(2,1)}, bf16[4,128,896]{2,1,0:T(8,128)(2,1)}) custom-call(s32[14]{0:T(128)} %stack.103.info, bf16[640,1024]{1,0:T(8,128)(2,1)} %bitcast.183, bf16[640,1024]{1,0:T(8,128)(2,1)} %bitcast.184, bf16[640,768]{1,0:T(8,128)(2,1)} %bitcast.185, bf16[640,768]{1,0:T(8,128)(2,1)} %bitcast.186, ...), custom_call_target="tpu_custom_call" | custom-call | flops 2013265920 | bytes 6160384 | tf_op jit(solution)/shard_map/weight_grad/pallas_call | solution.py:376
  276.6 4.2 %collective-permute-done.41 = bf16[160,1024]{1,0:T(8,128)(2,1)S(1)} collective-permute-done((bf16[160,1024]{1,0:T(8,128)(2,1)S(1)}, bf16[160,1024]{1,0:T(8,128)(2,1)S(1)}, u32[]{:S(2)}, u32[]{:S(2)}) %collective-permute-start.41) | collective-permute-done | bytes 327712 | tf_op jit(solution)/shard_map/ppermute | solution.py:26
  281.8 6.0 %collective-permute-done.39 = bf16[160,1024]{1,0:T(8,128)(2,1)S(1)} collective-permute-done((bf16[160,1024]{1,0:T(8,128)(2,1)S(1)}, bf16[160,1024]{1,0:T(8,128)(2,1)S(1)}, u32[]{:S(2)}, u32[]{:S(2)}) %collective-permute-start.39) | collective-permute-done | bytes 327712 | tf_op jit(solution)/shard_map/ppermute | solution.py:26
  290.2 6.3 %collective-permute-done.52 = bf16[4,128,896]{2,1,0:T(8,128)(2,1)S(1)} collective-permute-done((bf16[4,128,896]{2,1,0:T(8,128)(2,1)}, bf16[4,128,896]{2,1,0:T(8,128)(2,1)S(1)}, u32[]{:S(2)}, u32[]{:S(2)}) %collective-permute-start.52) | collective-permute-done | bytes 917536 | tf_op jit(solution)/shard_map/ppermute | solution.py:57
  297.5 2.4 split.2
  300.7 3.1 collective-permute-start.54
  304.8 2.7 core_split.1
  311.5 9.1 %collective-permute-done.57 = bf16[4,128,512]{2,1,0:T(8,128)(2,1)S(1)} collective-permute-done((bf16[4,128,512]{2,1,0:T(8,128)(2,1)}, bf16[4,128,512]{2,1,0:T(8,128)(2,1)S(1)}, u32[]{:S(2)}, u32[]{:S(2)}) %collective-permute-start.57) | collective-permute-done | bytes 524320 | tf_op jit(solution)/shard_map/ppermute | solution.py:57
  321.5 2.0 split.3
  324.5 2.8 collective-permute-start.59
  328.6 3.4 collective-permute-done.58
  332.0 5.1 %collective-permute-done.60 = bf16[1,128,512]{2,1,0:T(8,128)(2,1)S(1)} collective-permute-done((bf16[1,128,512]{2,1,0:T(8,128)(2,1)}, bf16[1,128,512]{2,1,0:T(8,128)(2,1)S(1)}, u32[]{:S(2)}, u32[]{:S(2)}) %collective-permute-start.60) | collective-permute-done | bytes 131104 | tf_op jit(solution)/shard_map/ppermute | solution.py:57
  340.0 3.5 all-to-all-start.1
  345.4 8.0 %all-to-all-done.1.ref = bf16[4,32,2432]{2,1,0:T(8,128)(2,1)S(1)} async-done(((bf16[4,32,2432]{2,1,0:T(8,128)(2,1)}), bf16[4,32,2432]{2,1,0:T(8,128)(2,1)S(1)}, u32[]{:S(2)}, u32[]{:S(2)}) %all-to-all-start.1) | async-done | bytes 622624 | tf_op jit(solution)/shard_map/all_to_all | solution.py:1002
  354.2 2.1 unpack.1
  (332 shorter events, 85.2 us)
Async XLA Ops:
  7.3 56.9 %all-gather.6.cloned.1.call-start = ((), (), s32[]{:S(2)}) async-start(), calls=%async_computation.5 | async-start | bytes 3276800 | tf_op jit(solution)/shard_map/all_gather | solution.py:842
  8.0 149.3 %all-gather.4.cloned.1.call-start = ((), (), s32[]{:S(2)}) async-start(), calls=%async_computation.3 | async-start | bytes 3276800 | tf_op jit(solution)/shard_map/all_gather | solution.py:843
  11.6 18.2 %all-to-all-start = ((bf16[4,32,2432]{2,1,0:T(8,128)(2,1)}), bf16[4,32,2432]{2,1,0:T(8,128)(2,1)S(1)}, u32[]{:S(2)}, u32[]{:S(2)}) async-start(bf16[4,32,2432]{2,1,0:T(8,128)(2,1)} %pack.1), calls=%async_computation | async-start | bytes 1245184 | tf_op jit(solution)/shard_map/all_to_all | solution.py:835
  15.9 321.3 %reduce-scatter.2.cloned.1.call-start = ((), (), s32[]{:S(2)}) async-start(), calls=%async_computation.4 | async-start | bytes 4718592 | tf_op jit(solution)/shard_map/reduce_scatter | solution.py:937
  15.9 14.0 %collective-permute-start.2 = (bf16[128,1024]{1,0:T(8,128)(2,1)S(1)}, bf16[128,1024]{1,0:T(8,128)(2,1)S(1)}, u32[]{:S(2)}, u32[]{:S(2)}) collective-permute-start(bf16[128,1024]{1,0:T(8,128)(2,1)S(1)} %copy-done.30), channel_id=1, source_target_pairs={{0,24},{4,28},{8,0},{12,4},{16,8},{20,12},{24,16},{28,20},{1,25},{... | collective-permute-start | bytes 786440 | tf_op jit(solution)/shard_map/ppermute | solution.py:57
  20.4 14.7 %collective-permute-start = (bf16[128,1024]{1,0:T(8,128)(2,1)S(1)}, bf16[128,1024]{1,0:T(8,128)(2,1)S(1)}, u32[]{:S(2)}, u32[]{:S(2)}) collective-permute-start(bf16[128,1024]{1,0:T(8,128)(2,1)S(1)} %copy-done.30), channel_id=1, source_target_pairs={{0,8},{4,12},{8,16},{12,20},{16,24},{20,28},{24,0},{28,4},{1,9},{5... | collective-permute-start | bytes 786440 | tf_op jit(solution)/shard_map/ppermute | solution.py:57
  20.4 14.7 %collective-permute-start.4 = (bf16[128,1024]{1,0:T(8,128)(2,1)S(1)}, bf16[128,1024]{1,0:T(8,128)(2,1)S(1)}, u32[]{:S(2)}, u32[]{:S(2)}) collective-permute-start(bf16[128,1024]{1,0:T(8,128)(2,1)S(1)} %copy-done.30), channel_id=1, source_target_pairs={{0,4},{4,0},{8,12},{12,8},{16,20},{20,16},{24,28},{28,24},{1,5},{5... | collective-permute-start | bytes 786440 | tf_op jit(solution)/shard_map/ppermute | solution.py:57
  30.0 11.2 %collective-permute-start.3 = (bf16[128,896]{1,0:T(8,128)(2,1)S(1)}, bf16[128,896]{1,0:T(8,128)(2,1)S(1)}, u32[]{:S(2)}, u32[]{:S(2)}) collective-permute-start(bf16[128,896]{1,0:T(8,128)(2,1)S(1)} %pad_maximum_fusion.3.refs_0_), channel_id=1, source_target_pairs={{0,24},{4,28},{8,0},{12,4},{16,8},{20,12},{24,16},{28,20},{1,25},{... | collective-permute-start | bytes 688136 | tf_op jit(solution)/shard_map/ppermute | solution.py:57
  35.1 11.4 %collective-permute-start.1 = (bf16[128,896]{1,0:T(8,128)(2,1)S(1)}, bf16[128,896]{1,0:T(8,128)(2,1)S(1)}, u32[]{:S(2)}, u32[]{:S(2)}) collective-permute-start(bf16[128,896]{1,0:T(8,128)(2,1)S(1)} %pad_maximum_fusion.3.refs_0_), channel_id=1, source_target_pairs={{0,8},{4,12},{8,16},{12,20},{16,24},{20,28},{24,0},{28,4},{1,9},{5... | collective-permute-start | bytes 688136 | tf_op jit(solution)/shard_map/ppermute | solution.py:57
  35.1 18.2 %collective-permute-start.5 = (bf16[128,896]{1,0:T(8,128)(2,1)S(1)}, bf16[128,896]{1,0:T(8,128)(2,1)S(1)}, u32[]{:S(2)}, u32[]{:S(2)}) collective-permute-start(bf16[128,896]{1,0:T(8,128)(2,1)S(1)} %pad_maximum_fusion.3.refs_0_), channel_id=1, source_target_pairs={{0,16},{4,20},{8,24},{12,28},{16,0},{20,4},{24,8},{28,12},{1,17},{... | collective-permute-start | bytes 688136 | tf_op jit(solution)/shard_map/ppermute | solution.py:57
  36.0 21.6 %collective-permute-start.6 = (bf16[128,896]{1,0:T(8,128)(2,1)S(1)}, bf16[128,896]{1,0:T(8,128)(2,1)S(1)}, u32[]{:S(2)}, u32[]{:S(2)}) collective-permute-start(bf16[128,896]{1,0:T(8,128)(2,1)S(1)} %pad_maximum_fusion.3.refs_0_), channel_id=1, source_target_pairs={{0,4},{4,0},{8,12},{12,8},{16,20},{20,16},{24,28},{28,24},{1,5},{5... | collective-permute-start | bytes 688136 | tf_op jit(solution)/shard_map/ppermute | solution.py:57
  41.2 19.4 %collective-permute-start.8 = (bf16[128,896]{1,0:T(8,128)(2,1)S(1)}, bf16[128,896]{1,0:T(8,128)(2,1)S(1)}, u32[]{:S(2)}, u32[]{:S(2)}) collective-permute-start(bf16[128,896]{1,0:T(8,128)(2,1)S(1)} %collective-permute-done.3.refs_2_), channel_id=1, source_target_pairs={{0,4},{4,0},{8,12},{12,8},{16,20},{20,16},{24,28},{28,24},{1,5},{5... | collective-permute-start | bytes 688136 | tf_op jit(solution)/shard_map/ppermute | solution.py:57
  46.5 14.1 %collective-permute-start.7 = (bf16[128,896]{1,0:T(8,128)(2,1)S(1)}, bf16[128,896]{1,0:T(8,128)(2,1)}, u32[]{:S(2)}, u32[]{:S(2)}) collective-permute-start(bf16[128,896]{1,0:T(8,128)(2,1)S(1)} %collective-permute-done.1.refs_1_), channel_id=1, source_target_pairs={{0,4},{4,0},{8,12},{12,8},{16,20},{20,16},{24,28},{28,24},{1,5},{5... | collective-permute-start | bytes 688136 | tf_op jit(solution)/shard_map/ppermute | solution.py:57
  56.7 20.3 %collective-permute-start.13 = (bf16[128,1536]{1,0:T(8,128)(2,1)S(1)}, bf16[128,1536]{1,0:T(8,128)(2,1)S(1)}, u32[]{:S(2)}, u32[]{:S(2)}) collective-permute-start(bf16[128,1536]{1,0:T(8,128)(2,1)S(1)} %slice.174.refs_0_), channel_id=1, source_target_pairs={{0,8},{4,12},{8,16},{12,20},{16,24},{20,28},{24,0},{28,4},{1,9},{5... | collective-permute-start | bytes 1179656 | tf_op jit(solution)/shard_map/ppermute | solution.py:57
  57.6 19.9 %collective-permute-start.14 = (bf16[128,1536]{1,0:T(8,128)(2,1)S(1)}, bf16[128,1536]{1,0:T(8,128)(2,1)S(1)}, u32[]{:S(2)}, u32[]{:S(2)}) collective-permute-start(bf16[128,1536]{1,0:T(8,128)(2,1)S(1)} %slice.174.refs_0_), channel_id=1, source_target_pairs={{0,24},{4,28},{8,0},{12,4},{16,8},{20,12},{24,16},{28,20},{1,25},{... | collective-permute-start | bytes 1179656 | tf_op jit(solution)/shard_map/ppermute | solution.py:57
  73.6 20.2 %collective-permute-start.15 = (bf16[128,1536]{1,0:T(8,128)(2,1)S(1)}, bf16[128,1536]{1,0:T(8,128)(2,1)S(1)}, u32[]{:S(2)}, u32[]{:S(2)}) collective-permute-start(bf16[128,1536]{1,0:T(8,128)(2,1)S(1)} %slice.174.refs_0_), channel_id=1, source_target_pairs={{0,16},{4,20},{8,24},{12,28},{16,0},{20,4},{24,8},{28,12},{1,17},{... | collective-permute-start | bytes 1179656 | tf_op jit(solution)/shard_map/ppermute | solution.py:57
  74.5 19.9 %collective-permute-start.16 = (bf16[128,1536]{1,0:T(8,128)(2,1)S(1)}, bf16[128,1536]{1,0:T(8,128)(2,1)S(1)}, u32[]{:S(2)}, u32[]{:S(2)}) collective-permute-start(bf16[128,1536]{1,0:T(8,128)(2,1)S(1)} %slice.174.refs_0_), channel_id=1, source_target_pairs={{0,4},{4,0},{8,12},{12,8},{16,20},{20,16},{24,28},{28,24},{1,5},{5... | collective-permute-start | bytes 1179656 | tf_op jit(solution)/shard_map/ppermute | solution.py:57
  77.0 18.1 %collective-permute-start.17 = (bf16[128,1536]{1,0:T(8,128)(2,1)S(1)}, bf16[128,1536]{1,0:T(8,128)(2,1)S(1)}, u32[]{:S(2)}, u32[]{:S(2)}) collective-permute-start(bf16[128,1536]{1,0:T(8,128)(2,1)S(1)} %collective-permute-done.13.refs_1_), channel_id=1, source_target_pairs={{0,4},{4,0},{8,12},{12,8},{16,20},{20,16},{24,28},{28,24},{1,5},{5... | collective-permute-start | bytes 1179656 | tf_op jit(solution)/shard_map/ppermute | solution.py:57
  77.5 26.0 %collective-permute-start.18 = (bf16[128,1536]{1,0:T(8,128)(2,1)S(1)}, bf16[128,1536]{1,0:T(8,128)(2,1)S(1)}, u32[]{:S(2)}, u32[]{:S(2)}) collective-permute-start(bf16[128,1536]{1,0:T(8,128)(2,1)S(1)} %collective-permute-done.14.refs_2_), channel_id=1, source_target_pairs={{0,4},{4,0},{8,12},{12,8},{16,20},{20,16},{24,28},{28,24},{1,5},{5... | collective-permute-start | bytes 1179656 | tf_op jit(solution)/shard_map/ppermute | solution.py:57
  93.8 15.1 %collective-permute-start.19 = (bf16[128,1536]{1,0:T(8,128)(2,1)S(1)}, bf16[128,1536]{1,0:T(8,128)(2,1)}, u32[]{:S(2)}, u32[]{:S(2)}) collective-permute-start(bf16[128,1536]{1,0:T(8,128)(2,1)S(1)} %collective-permute-done.15.refs_3_), channel_id=1, source_target_pairs={{0,4},{4,0},{8,12},{12,8},{16,20},{20,16},{24,28},{28,24},{1,5},{5... | collective-permute-start | bytes 1179656 | tf_op jit(solution)/shard_map/ppermute | solution.py:57
  124.8 17.0 %collective-permute-start.24 = (bf16[160,1024]{1,0:T(8,128)(2,1)}, bf16[160,1024]{1,0:T(8,128)(2,1)S(1)}, u32[]{:S(2)}, u32[]{:S(2)}) collective-permute-start(bf16[160,1024]{1,0:T(8,128)(2,1)} %get-tuple-element.151.refs_0_), channel_id=1, source_target_pairs={{0,2},{1,3},{2,0},{3,1},{4,6},{5,7},{6,4},{7,5},{8,10},{9,11},{10,... | collective-permute-start | bytes 983048 | tf_op jit(solution)/shard_map/ppermute | solution.py:26
  126.5 14.7 %collective-permute-start.27 = (bf16[128,1024]{1,0:T(8,128)(2,1)S(1)}, bf16[128,1024]{1,0:T(8,128)(2,1)S(1)}, u32[]{:S(2)}, u32[]{:S(2)}) collective-permute-start(bf16[128,1024]{1,0:T(8,128)(2,1)S(1)} %copy-done.30), channel_id=1, source_target_pairs={{0,16},{4,20},{8,24},{12,28},{16,0},{20,4},{24,8},{28,12},{1,17},{... | collective-permute-start | bytes 786440 | tf_op jit(solution)/shard_map/ppermute | solution.py:57
  128.8 13.5 %collective-permute-start.28 = (bf16[128,1024]{1,0:T(8,128)(2,1)S(1)}, bf16[128,1024]{1,0:T(8,128)(2,1)S(1)}, u32[]{:S(2)}, u32[]{:S(2)}) collective-permute-start(bf16[128,1024]{1,0:T(8,128)(2,1)S(1)} %copy-done.34), channel_id=1, source_target_pairs={{0,4},{4,0},{8,12},{12,8},{16,20},{20,16},{24,28},{28,24},{1,5},{5... | collective-permute-start | bytes 786440 | tf_op jit(solution)/shard_map/ppermute | solution.py:57
  129.4 13.4 %collective-permute-start.29 = (bf16[128,1024]{1,0:T(8,128)(2,1)S(1)}, bf16[128,1024]{1,0:T(8,128)(2,1)S(1)}, u32[]{:S(2)}, u32[]{:S(2)}) collective-permute-start(bf16[128,1024]{1,0:T(8,128)(2,1)S(1)} %copy-done.32), channel_id=1, source_target_pairs={{0,4},{4,0},{8,12},{12,8},{16,20},{20,16},{24,28},{28,24},{1,5},{5... | collective-permute-start | bytes 786440 | tf_op jit(solution)/shard_map/ppermute | solution.py:57
  141.8 15.6 %collective-permute-start.25 = (bf16[160,1024]{1,0:T(8,128)(2,1)}, bf16[160,1024]{1,0:T(8,128)(2,1)S(1)}, u32[]{:S(2)}, u32[]{:S(2)}) collective-permute-start(bf16[160,1024]{1,0:T(8,128)(2,1)} %get-tuple-element.151.refs_0_), channel_id=1, source_target_pairs={{0,1},{1,0},{2,3},{3,2},{4,5},{5,4},{6,7},{7,6},{8,9},{9,8},{10,11... | collective-permute-start | bytes 983048 | tf_op jit(solution)/shard_map/ppermute | solution.py:26
  141.8 15.6 %collective-permute-start.26 = (bf16[160,1024]{1,0:T(8,128)(2,1)S(1)}, bf16[160,1024]{1,0:T(8,128)(2,1)S(1)}, u32[]{:S(2)}, u32[]{:S(2)}) collective-permute-start(bf16[160,1024]{1,0:T(8,128)(2,1)S(1)} %collective-permute-done.24.refs_1_), channel_id=1, source_target_pairs={{0,1},{1,0},{2,3},{3,2},{4,5},{5,4},{6,7},{7,6},{8,9},{9,8},{10,11... | collective-permute-start | bytes 983048 | tf_op jit(solution)/shard_map/ppermute | solution.py:26
  211.1 10.5 %collective-permute-start.37 = (bf16[160,1024]{1,0:T(8,128)(2,1)S(1)}, bf16[160,1024]{1,0:T(8,128)(2,1)S(1)}, u32[]{:S(2)}, u32[]{:S(2)}) collective-permute-start(bf16[160,1024]{1,0:T(8,128)(2,1)S(1)} %fusion.16), channel_id=1, source_target_pairs={{0,2},{1,3},{2,0},{3,1},{4,6},{5,7},{6,4},{7,5},{8,10},{9,11},{10,... | collective-permute-start | bytes 983048 | tf_op jit(solution)/shard_map/ppermute | solution.py:26
  212.2 17.3 %collective-permute-start.36 = (bf16[160,1024]{1,0:T(8,128)(2,1)S(1)}, bf16[160,1024]{1,0:T(8,128)(2,1)S(1)}, u32[]{:S(2)}, u32[]{:S(2)}) collective-permute-start(bf16[160,1024]{1,0:T(8,128)(2,1)S(1)} %fusion.17), channel_id=1, source_target_pairs={{0,2},{1,3},{2,0},{3,1},{4,6},{5,7},{6,4},{7,5},{8,10},{9,11},{10,... | collective-permute-start | bytes 983048 | tf_op jit(solution)/shard_map/ppermute | solution.py:26
  227.3 12.8 %collective-permute-start.42 = (bf16[160,256]{1,0:T(8,128)(2,1)}, bf16[160,256]{1,0:T(8,128)(2,1)S(1)}, u32[]{:S(2)}, u32[]{:S(2)}) collective-permute-start(bf16[160,256]{1,0:T(8,128)(2,1)} %get-tuple-element.183), channel_id=1, source_target_pairs={{0,2},{1,3},{2,0},{3,1},{4,6},{5,7},{6,4},{7,5},{8,10},{9,11},{10,... | collective-permute-start | bytes 245768 | tf_op jit(solution)/shard_map/ppermute | solution.py:26
  228.4 12.8 %collective-permute-start.43 = (bf16[160,256]{1,0:T(8,128)(2,1)}, bf16[160,256]{1,0:T(8,128)(2,1)S(1)}, u32[]{:S(2)}, u32[]{:S(2)}) collective-permute-start(bf16[160,256]{1,0:T(8,128)(2,1)} %get-tuple-element.184), channel_id=1, source_target_pairs={{0,1},{1,0},{2,3},{3,2},{4,5},{5,4},{6,7},{7,6},{8,9},{9,8},{10,11... | collective-permute-start | bytes 245768 | tf_op jit(solution)/shard_map/ppermute | solution.py:26
  228.4 12.8 %collective-permute-start.44 = (bf16[160,256]{1,0:T(8,128)(2,1)}, bf16[160,256]{1,0:T(8,128)(2,1)S(1)}, u32[]{:S(2)}, u32[]{:S(2)}) collective-permute-start(bf16[160,256]{1,0:T(8,128)(2,1)} %get-tuple-element.185), channel_id=1, source_target_pairs={{0,3},{1,2},{2,1},{3,0},{4,7},{5,6},{6,5},{7,4},{8,11},{9,10},{10,... | collective-permute-start | bytes 245768 | tf_op jit(solution)/shard_map/ppermute | solution.py:26
  235.1 16.1 %collective-permute-start.47 = (bf16[160,256]{1,0:T(8,128)(2,1)}, bf16[160,256]{1,0:T(8,128)(2,1)S(1)}, u32[]{:S(2)}, u32[]{:S(2)}) collective-permute-start(bf16[160,256]{1,0:T(8,128)(2,1)} %get-tuple-element.194), channel_id=1, source_target_pairs={{0,2},{1,3},{2,0},{3,1},{4,6},{5,7},{6,4},{7,5},{8,10},{9,11},{10,... | collective-permute-start | bytes 245768 | tf_op jit(solution)/shard_map/ppermute | solution.py:26
  236.3 15.5 %collective-permute-start.48 = (bf16[160,256]{1,0:T(8,128)(2,1)}, bf16[160,256]{1,0:T(8,128)(2,1)S(1)}, u32[]{:S(2)}, u32[]{:S(2)}) collective-permute-start(bf16[160,256]{1,0:T(8,128)(2,1)} %get-tuple-element.195), channel_id=1, source_target_pairs={{0,1},{1,0},{2,3},{3,2},{4,5},{5,4},{6,7},{7,6},{8,9},{9,8},{10,11... | collective-permute-start | bytes 245768 | tf_op jit(solution)/shard_map/ppermute | solution.py:26
  240.1 11.7 %collective-permute-start.49 = (bf16[160,256]{1,0:T(8,128)(2,1)S(1)}, bf16[160,256]{1,0:T(8,128)(2,1)S(1)}, u32[]{:S(2)}, u32[]{:S(2)}) collective-permute-start(bf16[160,256]{1,0:T(8,128)(2,1)S(1)} %copy-done.76), channel_id=1, source_target_pairs={{0,3},{1,2},{2,1},{3,0},{4,7},{5,6},{6,5},{7,4},{8,11},{9,10},{10,... | collective-permute-start | bytes 245768 | tf_op jit(solution)/shard_map/ppermute | solution.py:26
  241.2 62.5 %collective-permute-start.56 = (bf16[1024,512]{1,0:T(8,128)(2,1)}, bf16[1024,512]{1,0:T(8,128)(2,1)S(1)}, u32[]{:S(2)}, u32[]{:S(2)}) collective-permute-start(bf16[1024,512]{1,0:T(8,128)(2,1)} %get-tuple-element.218), channel_id=1, source_target_pairs={{0,1},{1,0},{2,3},{3,2},{4,5},{5,4},{6,7},{7,6},{8,9},{9,8},{10,11... | collective-permute-start | bytes 3145736 | tf_op jit(solution)/shard_map/ppermute | solution.py:26
  241.3 27.4 %collective-permute-start.40 = (bf16[2,160,1024]{2,1,0:T(8,128)(2,1)}, bf16[2,160,1024]{2,1,0:T(8,128)(2,1)}, u32[]{:S(2)}, u32[]{:S(2)}) collective-permute-start(bf16[2,160,1024]{2,1,0:T(8,128)(2,1)} %get-tuple-element.178), channel_id=1, source_target_pairs={{0,1},{1,0},{2,3},{3,2},{4,5},{5,4},{6,7},{7,6},{8,9},{9,8},{10,11... | collective-permute-start | bytes 1966088 | tf_op jit(solution)/shard_map/ppermute | solution.py:26
  251.2 21.3 %collective-permute-start.45 = (bf16[2,160,1024]{2,1,0:T(8,128)(2,1)}, bf16[2,160,1024]{2,1,0:T(8,128)(2,1)}, u32[]{:S(2)}, u32[]{:S(2)}) collective-permute-start(bf16[2,160,1024]{2,1,0:T(8,128)(2,1)} %bitcast.51), channel_id=1, source_target_pairs={{0,1},{1,0},{2,3},{3,2},{4,5},{5,4},{6,7},{7,6},{8,9},{9,8},{10,11... | collective-permute-start | bytes 1966088 | tf_op jit(solution)/shard_map/ppermute | solution.py:26
  251.7 18.4 %collective-permute-start.38 = (bf16[2,160,1024]{2,1,0:T(8,128)(2,1)}, bf16[2,160,1024]{2,1,0:T(8,128)(2,1)}, u32[]{:S(2)}, u32[]{:S(2)}) collective-permute-start(bf16[2,160,1024]{2,1,0:T(8,128)(2,1)} %get-tuple-element.175), channel_id=1, source_target_pairs={{0,1},{1,0},{2,3},{3,2},{4,5},{5,4},{6,7},{7,6},{8,9},{9,8},{10,11... | collective-permute-start | bytes 1966088 | tf_op jit(solution)/shard_map/ppermute | solution.py:26
  268.0 28.5 %collective-permute-start.52 = (bf16[4,128,896]{2,1,0:T(8,128)(2,1)}, bf16[4,128,896]{2,1,0:T(8,128)(2,1)S(1)}, u32[]{:S(2)}, u32[]{:S(2)}) collective-permute-start(bf16[4,128,896]{2,1,0:T(8,128)(2,1)} %get-tuple-element.210), channel_id=1, source_target_pairs={{0,4},{4,0},{8,12},{12,8},{16,20},{20,16},{24,28},{28,24},{1,5},{5... | collective-permute-start | bytes 2752520 | tf_op jit(solution)/shard_map/ppermute | solution.py:57
  270.2 10.6 %collective-permute-start.41 = (bf16[160,1024]{1,0:T(8,128)(2,1)S(1)}, bf16[160,1024]{1,0:T(8,128)(2,1)S(1)}, u32[]{:S(2)}, u32[]{:S(2)}) collective-permute-start(bf16[160,1024]{1,0:T(8,128)(2,1)S(1)} %fusion.19), channel_id=1, source_target_pairs={{0,2},{1,3},{2,0},{3,1},{4,6},{5,7},{6,4},{7,5},{8,10},{9,11},{10,... | collective-permute-start | bytes 983048 | tf_op jit(solution)/shard_map/ppermute | solution.py:26
  272.5 15.3 %collective-permute-start.39 = (bf16[160,1024]{1,0:T(8,128)(2,1)S(1)}, bf16[160,1024]{1,0:T(8,128)(2,1)S(1)}, u32[]{:S(2)}, u32[]{:S(2)}) collective-permute-start(bf16[160,1024]{1,0:T(8,128)(2,1)S(1)} %fusion.18), channel_id=1, source_target_pairs={{0,2},{1,3},{2,0},{3,1},{4,6},{5,7},{6,4},{7,5},{8,10},{9,11},{10,... | collective-permute-start | bytes 983048 | tf_op jit(solution)/shard_map/ppermute | solution.py:26
  274.6 32.9 %collective-permute-start.46 = (bf16[160,1024]{1,0:T(8,128)(2,1)S(1)}, bf16[160,1024]{1,0:T(8,128)(2,1)S(1)}, u32[]{:S(2)}, u32[]{:S(2)}) collective-permute-start(bf16[160,1024]{1,0:T(8,128)(2,1)S(1)} %fusion.7), channel_id=1, source_target_pairs={{0,2},{1,3},{2,0},{3,1},{4,6},{5,7},{6,4},{7,5},{8,10},{9,11},{10,... | collective-permute-start | bytes 983048 | tf_op jit(solution)/shard_map/ppermute | solution.py:26
  280.8 27.7 %collective-permute-start.51 = (bf16[160,1024]{1,0:T(8,128)(2,1)}, bf16[160,1024]{1,0:T(8,128)(2,1)S(1)}, u32[]{:S(2)}, u32[]{:S(2)}) collective-permute-start(bf16[160,1024]{1,0:T(8,128)(2,1)} %fusion.4), channel_id=1, source_target_pairs={{0,2},{1,3},{2,0},{3,1},{4,6},{5,7},{6,4},{7,5},{8,10},{9,11},{10,... | collective-permute-start | bytes 983048 | tf_op jit(solution)/shard_map/ppermute | solution.py:26
  299.9 27.4 %collective-permute-start.53 = (bf16[1,128,896]{2,1,0:T(8,128)(2,1)}, bf16[1,128,896]{2,1,0:T(8,128)(2,1)}, u32[]{:S(2)}, u32[]{:S(2)}) collective-permute-start(bf16[1,128,896]{2,1,0:T(8,128)(2,1)} %get-tuple-element.212), channel_id=1, source_target_pairs={{0,8},{4,12},{8,16},{12,20},{16,24},{20,28},{24,0},{28,4},{1,9},{5... | collective-permute-start | bytes 688136 | tf_op jit(solution)/shard_map/ppermute | solution.py:57
  300.7 26.6 %collective-permute-start.54 = (bf16[1,128,896]{2,1,0:T(8,128)(2,1)}, bf16[1,128,896]{2,1,0:T(8,128)(2,1)}, u32[]{:S(2)}, u32[]{:S(2)}) collective-permute-start(bf16[1,128,896]{2,1,0:T(8,128)(2,1)} %get-tuple-element.213), channel_id=1, source_target_pairs={{0,24},{4,28},{8,0},{12,4},{16,8},{20,12},{24,16},{28,20},{1,25},{... | collective-permute-start | bytes 688136 | tf_op jit(solution)/shard_map/ppermute | solution.py:57
  303.8 23.5 %collective-permute-start.55 = (bf16[1,128,896]{2,1,0:T(8,128)(2,1)}, bf16[1,128,896]{2,1,0:T(8,128)(2,1)}, u32[]{:S(2)}, u32[]{:S(2)}) collective-permute-start(bf16[1,128,896]{2,1,0:T(8,128)(2,1)} %get-tuple-element.214), channel_id=1, source_target_pairs={{0,16},{4,20},{8,24},{12,28},{16,0},{20,4},{24,8},{28,12},{1,17},{... | collective-permute-start | bytes 688136 | tf_op jit(solution)/shard_map/ppermute | solution.py:57
  307.5 13.1 %collective-permute-start.57 = (bf16[4,128,512]{2,1,0:T(8,128)(2,1)}, bf16[4,128,512]{2,1,0:T(8,128)(2,1)S(1)}, u32[]{:S(2)}, u32[]{:S(2)}) collective-permute-start(bf16[4,128,512]{2,1,0:T(8,128)(2,1)} %get-tuple-element.220), channel_id=1, source_target_pairs={{0,4},{4,0},{8,12},{12,8},{16,20},{20,16},{24,28},{28,24},{1,5},{5... | collective-permute-start | bytes 1572872 | tf_op jit(solution)/shard_map/ppermute | solution.py:57
  340.0 13.4 %all-to-all-start.1 = ((bf16[4,32,2432]{2,1,0:T(8,128)(2,1)}), bf16[4,32,2432]{2,1,0:T(8,128)(2,1)S(1)}, u32[]{:S(2)}, u32[]{:S(2)}) async-start(bf16[4,32,2432]{2,1,0:T(8,128)(2,1)} %pad_maximum_fusion.2), calls=%async_computation.2 | async-start | bytes 1245184 | tf_op jit(solution)/shard_map/all_to_all | solution.py:1002
  (101 other events, 793.2 us)
Sparse Core Ops, SparseCore 0:
  9.7 31.7 all-gather.5
  43.0 26.5 all-gather.3
  209.3 93.3 reduce-scatter.1

commit v3 on v2

--- a/solution.py
+++ b/solution.py
@@ -22,6 +22,10 @@
 VMEM = pl.BlockSpec(memory_space=pltpu.VMEM)
 
 
+def after(array, *done):
+    return lax.optimization_barrier((array,) + done)[0] if done else array
+
+
 def hop(array, mask):
     return lax.ppermute(array, "seq", [(i, i ^ mask) for i in range(SEQ)])
 
@@ -29,6 +33,11 @@
 def seq_gather(array):
     far = hop(array, 2)
     return [array, far, hop(array, 1), hop(far, 1)]
+
+
+def seq_gather(array, *done):
+    far = hop(array, 2)
+    return [array, far, hop(array, 1), hop(after(far, *done), 1)]
 
 
 def seq_exchange(pieces):
@@ -70,10 +79,6 @@
     return owners
 
 
-def after(array, *done):
-    return lax.optimization_barrier((array,) + done)[0] if done else array
-
-
 def fsdp_gather(array, size):
     pieces = [array]
     for stride, radix in reversed(digits_of(size)):
@@ -81,32 +86,6 @@
             shift(piece, size, stride, radix, step) for step in steps_of(radix) for piece in pieces
         ]
     return pieces
-
-
-class Gather:
-    def __init__(self, array, size):
-        self.array, self.size = array, size
-        self.near, self.far = digits_of(size)
-        self.steps = steps_of(self.far[1])
-        self.came, self.passed = {}, {}
-
-    def send(self, at, *done):
-        self.came[at] = shift(after(self.array, *done), self.size, *self.far, self.steps[at])
-        return self.came[at]
-
-    def forward(self, at, *done):
-        source = self.array if at is None else self.came[at]
-        self.passed[at] = shift(after(source, *done), self.size, *self.near, 1)
-        return self.passed[at]
-
-    def pieces(self):
-        order = range(len(self.steps))
-        return (
-            [self.array]
-            + [self.came[at] for at in order]
-            + [self.passed[None]]
-            + [self.passed[at] for at in order]
-        )
 
 
 def split_kernel(count, radix, digit_ref, *refs):
@@ -151,7 +130,7 @@
             digit = place // stride % radix
             outer = parts[0].shape[0] // radix
             blocks = split_sum(parts, outer, radix, jnp.asarray(digit, jnp.int32).reshape(1))
-    return functools.reduce(jnp.add, [part[0].astype(F32) for part in parts])
+    return parts
 
 
 def rows_dot(left, right):
@@ -184,6 +163,19 @@
 
 def column_sums(values):
     return jnp.sum(values, axis=0, keepdims=True)
+
+
+def piece_copies(info, pieces, low, target, sem):
+    block = pieces[0].shape[0]
+    cols = target.shape[1]
+    return [
+        pltpu.make_async_copy(
+            piece.at[:, pl.ds(low, cols)],
+            target.at[pl.ds(pl.multiple_of(info[at] * block, block), block), :],
+            sem.at[at],
+        )
+        for at, piece in enumerate(pieces)
+    ]
 
 
 def params():
@@ -219,6 +211,33 @@
         compiler_params=params(),
         name="pack",
     )(qkv, out, vectors, up)
+
+
+def collect_kernel(counts, *refs):
+    *parts, out, wide = refs
+    low = at = 0
+    for group, count in enumerate(counts):
+        blocks = [part[...].reshape(part.shape[-2:]).astype(F32) for part in parts[at : at + count]]
+        total = functools.reduce(jnp.add, blocks)
+        out[:, low : low + total.shape[1]] = total.astype(BF)
+        if group == 0:
+            wide[...] = total[:, total.shape[1] - LANES :]
+        low += total.shape[1]
+        at += count
+
+
+def collect(*groups):
+    rows = groups[0][0].shape[-2]
+    cols = sum(group[0].shape[-1] for group in groups)
+    parts = [part for group in groups for part in group]
+    return pl.pallas_call(
+        functools.partial(collect_kernel, [len(group) for group in groups]),
+        in_specs=[VMEM] * len(parts),
+        out_specs=[VMEM] * 2,
+        out_shape=[jax.ShapeDtypeStruct((rows, cols), BF), jax.ShapeDtypeStruct((rows, LANES), F32)],
+        compiler_params=params(),
+        name="collect",
+    )(*parts)
 
 
 def unpack_kernel(ref, qkv, out, up, vectors):
@@ -254,29 +273,25 @@
     )(came)
 
 
-def place_kernel(count, spans, vectors, info, *refs):
-    pieces, outs = refs[:count], refs[count : count + len(spans)]
-    block = pieces[0].shape[0]
-    for at, piece in enumerate(pieces):
-        place = pl.ds(pl.multiple_of(info[at] * block, block), block)
-        for (low, cols), out in zip(spans, outs):
-            out[place, :] = piece[:, low : low + cols]
-    if vectors:
-        rows = refs[-1]
-        rows[...] = outs[-1][...].astype(F32).T[: rows.shape[0]]
-
-
-def placed(info, pieces, *spans, vectors=False):
+def place_kernel(count, low, info, *refs):
+    pieces, out, scratch, sem = refs[:count], refs[count], refs[count + 1], refs[count + 2]
+    copies = piece_copies(info, pieces, low, scratch, sem)
+    for copy in copies:
+        copy.start()
+    for copy in copies:
+        copy.wait()
+    out[...] = scratch[...]
+
+
+def placed(info, pieces, low, cols):
     count = len(pieces)
     rows = count * pieces[0].shape[0]
-    shapes = [jax.ShapeDtypeStruct((rows, cols), BF) for _, cols in spans]
-    if vectors:
-        shapes.append(jax.ShapeDtypeStruct((16, rows), F32))
-    return pl.pallas_call(
-        functools.partial(place_kernel, count, spans, vectors),
-        in_specs=[SMEM] + [VMEM] * count,
-        out_specs=[VMEM] * len(shapes),
-        out_shape=shapes,
+    return pl.pallas_call(
+        functools.partial(place_kernel, count, low),
+        in_specs=[SMEM] + [ANY] * count,
+        out_specs=VMEM,
+        out_shape=jax.ShapeDtypeStruct((rows, cols), BF),
+        scratch_shapes=[pltpu.VMEM((rows, cols), BF), pltpu.SemaphoreType.DMA((count,))],
         compiler_params=params(),
         name="placed",
     )(info, *pieces)
@@ -326,45 +341,6 @@
         move.wait()
 
 
-def feed_grads_kernel(micros, tokens_at, info, *refs):
-    n2 = refs[: micros * SEQ]
-    actives, hiddens = refs[micros * SEQ : micros * (SEQ + 1)], refs[micros * (SEQ + 1) : micros * (SEQ + 2)]
-    cot, out = refs[micros * (SEQ + 2) : micros * (SEQ + 2) + 2]
-    c_in, act_in, n2_in, gh_in, c_sem, act_sem, n2_sem, gh_sem = refs[micros * (SEQ + 2) + 2 :]
-    cots = [cot.at[info[tokens_at + k], m] for m in range(micros) for k in range(SEQ)]
-    first = row_copies(cots, c_in, c_sem) + row_copies(actives, act_in, act_sem)
-    second = row_copies(n2, n2_in, n2_sem) + row_copies(hiddens, gh_in, gh_sem)
-    for copy in first + second:
-        copy.start()
-    block = out.shape[2]
-    step = max(256 // block, 1)
-    for which, (left, right, copies) in enumerate(((act_in, c_in, first), (n2_in, gh_in, second))):
-        for copy in copies:
-            copy.wait()
-        for low in range(0, out.shape[0], step):
-            part = rows_dot(left[:, low * block : (low + step) * block], right[...]).astype(BF)
-            out[low : low + step, which] = part.reshape(step, block, part.shape[1])
-
-
-def feed_grads(info, fsdp, n2, actives, hiddens, c_all):
-    micros = len(actives)
-    rows, units = actives[0].shape
-    model = c_all.shape[3]
-    block = model // fsdp
-    wide = pltpu.VMEM((micros * rows, model), BF)
-    return pl.pallas_call(
-        functools.partial(feed_grads_kernel, micros, fsdp + 2),
-        in_specs=[SMEM] + [ANY] * (micros * (SEQ + 2) + 1),
-        out_specs=VMEM,
-        out_shape=jax.ShapeDtypeStruct((fsdp, 2, block, model), BF),
-        scratch_shapes=[wide] * 4
-        + [pltpu.SemaphoreType.DMA((16,))] * 4,
-        compiler_params=params(),
-        cost_estimate=estimate(4 * micros * rows * units * model, 16 * 2**20),
-        name="feed_grads",
-    )(info, *n2, *actives, *hiddens, c_all)
-
-
 def plain_rows(info, refs):
     return refs
 
@@ -441,30 +417,28 @@
     )(info, here, came)
 
 
-def attention_kernel(count, info, x_ref, keep_ref, vec, source, *refs):
-    n1_ref, hat_ref, joined_ref, e0, e1, e2, e3, probs_ref, weight, sem = refs
-    tokens, model = x_ref.shape[3:]
+def attention_kernel(count, info, x0, x1, x2, x3, keep_ref, *refs):
+    pieces = refs[:count]
+    n1_ref, hat_ref, joined_ref, e0, e1, e2, e3, probs_ref, vec, weight, sem = refs[count:]
+    tokens, model = x0.shape[1:]
     rows = SEQ * tokens
-    triple = weight.shape[1]
+    triple = weight.shape[1] - LANES
     width = triple // 3
-    fetch = pltpu.make_async_copy(source, weight, sem)
+    copies = piece_copies(info, pieces, 0, weight, sem)
 
     @pl.when(pl.program_id(0) == 0)
     def _():
-        fetch.start()
-
-    values = jnp.concatenate(
-        [x_ref[info[count + 2 + k], 0, 0].astype(F32) for k in range(SEQ)], axis=0
-    )
+        for copy in copies:
+            copy.start()
+        for copy in copies:
+            copy.wait()
+        vec[...] = weight[:, triple:].astype(F32).T[: vec.shape[0]]
+
+    values = jnp.concatenate([x[0].astype(F32) for x in (x0, x1, x2, x3)], axis=0)
     hat, _ = norm_parts(values)
     hat_ref[...] = hat.astype(BF).reshape(hat_ref.shape)
     normed = (hat * vec[0:1, :] + vec[1:2, :]).astype(BF)
     n1_ref[...] = normed.reshape(n1_ref.shape)
-
-    @pl.when(pl.program_id(0) == 0)
-    def _():
-        fetch.wait()
-
     place = pl.multiple_of(info[count] * width, width)
     bias = jnp.concatenate(
         [
@@ -474,7 +448,7 @@
         ],
         axis=1,
     )
-    joined = (plain_dot(normed, weight[...]) + bias).astype(BF)
+    joined = (plain_dot(normed, weight[:, :triple]) + bias).astype(BF)
     joined_ref[...] = joined.reshape(joined_ref.shape)
     keep = keep_ref[0] > 0
     outs = []
@@ -490,41 +464,46 @@
         outs.append(rows_dot(v, probs))
     attended = jnp.concatenate(outs, axis=0).T.astype(BF)
     for at, ref in enumerate((e0, e1, e2, e3)):
-        ref[0] = attended[at * tokens : (at + 1) * tokens]
-
-
-def attention(info, count, micro, x_all, keep, vec, weight):
-    images, tokens, model = x_all.shape[2:]
-    triple = weight.shape[1]
+        ref[...] = attended[at * tokens : (at + 1) * tokens]
+
+
+def attention(info, x_pieces, keep, pieces, triple):
+    images, tokens, model = x_pieces[0].shape
+    count = len(pieces)
     width = triple // 3
     rows = SEQ * tokens
     heads = width // HEAD_DIM
-    token_block = lambda cols: pl.BlockSpec((1, tokens, cols), lambda i: (i, 0, 0))
     group_block = lambda cols: pl.BlockSpec((SEQ, 1, tokens, cols), lambda i: (0, i, 0, 0))
     group_shape = lambda cols: jax.ShapeDtypeStruct((SEQ, images, tokens, cols), BF)
     return pl.pallas_call(
         functools.partial(attention_kernel, count),
         grid=(images,),
         in_specs=[SMEM]
+        + [pl.BlockSpec((1, tokens, model), lambda i: (i, 0, 0))] * SEQ
+        + [pl.BlockSpec((1, rows, 1), lambda i: (i, 0, 0))]
+        + [ANY] * count,
+        out_specs=[group_block(model), group_block(model), group_block(triple)]
+        + [pl.BlockSpec((tokens, width), lambda i: (i, 0))] * SEQ
         + [
-            pl.BlockSpec((SEQ, 1, 1, tokens, model), lambda i: (0, micro, i, 0, 0)),
-            pl.BlockSpec((1, rows, 1), lambda i: (i, 0, 0)),
-            pl.BlockSpec(vec.shape, lambda i: (0, 0)),
-            ANY,
-        ],
-        out_specs=[group_block(model), group_block(model), group_block(triple)]
-        + [token_block(width)] * SEQ
-        + [pl.BlockSpec((1, heads, rows, rows), lambda i: (i, 0, 0, 0))],
+            pl.BlockSpec((1, heads, rows, rows), lambda i: (i, 0, 0, 0)),
+            pl.BlockSpec((16, model), lambda i: (0, 0)),
+        ],
         out_shape=[group_shape(model), group_shape(model), group_shape(triple)]
-        + [jax.ShapeDtypeStruct((images, tokens, width), BF)] * SEQ
-        + [jax.ShapeDtypeStruct((images, heads, rows, rows), BF)],
-        scratch_shapes=[pltpu.VMEM((model, triple), BF), pltpu.SemaphoreType.DMA],
+        + [jax.ShapeDtypeStruct((images * tokens, width), BF)] * SEQ
+        + [
+            jax.ShapeDtypeStruct((images, heads, rows, rows), BF),
+            jax.ShapeDtypeStruct((16, model), F32),
+        ],
+        scratch_shapes=[
+            pltpu.VMEM((model, triple + LANES), BF),
+            pltpu.SemaphoreType.DMA((count,)),
+        ],
         compiler_params=params(),
         cost_estimate=estimate(
-            2 * images * rows * (model * triple + 4 * width * rows), 8 * 2**20
+            2 * images * rows * (model * triple + 4 * width * rows), 16 * 2**20
         ),
         name="attention",
-    )(info, x_all, keep, vec, weight)
+    )(info, *x_pieces, keep, *pieces)
 
 
 def out_weight_copies(info, count, mine, other, target, sem):
@@ -575,74 +554,95 @@
     )(info, *heads, x_own, vec, mine, other)
 
 
-def feed_kernel(count, micro, info, *refs):
-    n2 = refs[:SEQ]
-    cot, vec = refs[SEQ : SEQ + 2]
-    up_ref, down_ref = refs[SEQ + 2 : SEQ + 4]
-    act_out, gh_out, down_chip, down_sib, up_chip, up_sib, sums = refs[SEQ + 4 : SEQ + 11]
-    w_up, w_down, n2_in, c_in, up_sem, down_sem, n2_sem, c_sem = refs[SEQ + 11 :]
-    rows = n2[0].shape[0]
+def feed_kernel(micros, *refs):
+    n2, cot = refs[:SEQ], refs[SEQ : 2 * SEQ]
+    vec, down_ref, up_ref = refs[2 * SEQ : 2 * SEQ + 3]
+    down_chip, down_sib, up_chip, up_sib, grads, sums = refs[2 * SEQ + 3 : 2 * SEQ + 9]
+    w_up, w_down, n2_in, c_in, act, gh, weight_sem, n2_sem, c_sem = refs[2 * SEQ + 9 :]
+    rows = n2[0].shape[0] // micros
     hidden = w_up.shape[1]
-    ups = [pltpu.make_async_copy(up_ref, w_up, up_sem)]
-    downs = [pltpu.make_async_copy(down_ref, w_down, down_sem)]
-    n2_copies = row_copies(n2, n2_in, n2_sem)
-    c_copies = row_copies([cot.at[info[count + 2 + k], micro] for k in range(SEQ)], c_in, c_sem)
-    for copy in n2_copies + ups + c_copies + downs:
+    up_copy = pltpu.make_async_copy(up_ref, w_up, weight_sem.at[0])
+    down_copies = [pltpu.make_async_copy(down_ref, w_down, weight_sem.at[1])]
+    by_micro = lambda pieces: [p.at[pl.ds(m * rows, rows), :] for m in range(micros) for p in pieces]
+    n2_copies = row_copies(by_micro(n2), n2_in, n2_sem)
+    c_copies = row_copies(by_micro(cot), c_in, c_sem)
+    for copy in n2_copies + [up_copy] + c_copies + down_copies:
         copy.start()
-    for copy in n2_copies + ups:
+    for copy in n2_copies + [up_copy]:
         copy.wait()
     total = jnp.zeros((1, hidden), F32)
-    for half in range(2):
-        span = slice(half * 2 * rows, (half + 1) * 2 * rows)
+    for part in range(2 * micros):
+        micro, half = part // 2, part % 2
+        span = slice(part * 2 * rows, (part + 1) * 2 * rows)
         values = plain_dot(n2_in[span], w_up[...]) + vec[8:9, :]
         normal = 0.5 * (1.0 + lax.erf(values * (2.0**-0.5)))
         slope = normal + values * (jnp.exp(values * values * -0.5) * 0.3989422804014327)
         active = (values * normal).astype(BF)
-        act_out[span] = active
-        if half == 0:
-            for copy in c_copies + downs:
+        act[span] = active
+        if part == 0:
+            for copy in c_copies + down_copies:
                 copy.wait()
         grad_hidden = (slope * cols_dot(c_in[span], w_down[...])).astype(BF)
-        gh_out[span] = grad_hidden
+        gh[span] = grad_hidden
         total = total + column_sums(grad_hidden.astype(F32))
-        shape = up_chip.shape
-        (down_chip, down_sib)[half][...] = plain_dot(active, w_down[...]).astype(BF).reshape(shape)
-        (up_chip, up_sib)[half][...] = cols_dot(grad_hidden, w_up[...]).astype(BF).reshape(shape)
+        place = slice(micro * rows, (micro + 1) * rows)
+        down_part = plain_dot(active, w_down[...]).astype(BF)
+        up_part = cols_dot(grad_hidden, w_up[...]).astype(BF)
+        for k in range(2):
+            (down_chip, down_sib)[half][k, place] = down_part[k * rows : (k + 1) * rows]
+            (up_chip, up_sib)[half][k, place] = up_part[k * rows : (k + 1) * rows]
     sums[...] = jnp.zeros(sums.shape, F32)
     sums[8:9, :] = total
-
-
-def feed(info, count, micro, n2_pieces, c_all, vec, w_up, w_down):
-    rows, model = n2_pieces[0].shape
+    block = grads.shape[2]
+    step = max(256 // block, 1)
+    for which, (left, right) in enumerate(((act, c_in), (n2_in, gh))):
+        for at in range(0, grads.shape[0], step):
+            part = rows_dot(left[:, at * block : (at + step) * block], right[...]).astype(BF)
+            grads[at : at + step, which] = part.reshape(step, block, part.shape[1])
+
+
+def feed(fsdp, micros, n2_pieces, c_pieces, vec, w_down, w_up):
+    rows, model = c_pieces[0].shape
     hidden = w_down.shape[0]
-    hiddens = jax.ShapeDtypeStruct((SEQ * rows, hidden), BF)
     pair = jax.ShapeDtypeStruct((2, rows, model), BF)
-    return pl.pallas_call(
-        functools.partial(feed_kernel, count, micro),
-        in_specs=[SMEM] + [ANY] * (SEQ + 1) + [VMEM] + [ANY] * 2,
-        out_specs=[VMEM] * 7,
-        out_shape=[hiddens, hiddens] + [pair] * 4 + [jax.ShapeDtypeStruct((16, model), F32)],
+    group = SEQ * rows
+    return pl.pallas_call(
+        functools.partial(feed_kernel, micros),
+        in_specs=[ANY] * (2 * SEQ) + [VMEM] + [ANY] * 2,
+        out_specs=[VMEM] * 6,
+        out_shape=[pair] * 4
+        + [
+            jax.ShapeDtypeStruct((fsdp, 2, model // fsdp, model), BF),
+            jax.ShapeDtypeStruct((16, model), F32),
+        ],
         scratch_shapes=[
             pltpu.VMEM((model, hidden), BF),
             pltpu.VMEM((hidden, model), BF),
-            pltpu.VMEM((SEQ * rows, model), BF),
-            pltpu.VMEM((SEQ * rows, model), BF),
-            pltpu.SemaphoreType.DMA,
-            pltpu.SemaphoreType.DMA,
-            pltpu.SemaphoreType.DMA((SEQ,)),
-            pltpu.SemaphoreType.DMA((SEQ,)),
-        ],
-        compiler_params=params(),
-        cost_estimate=estimate(8 * SEQ * rows * model * hidden, 16 * 2**20),
+            pltpu.VMEM((group, model), BF),
+            pltpu.VMEM((group, model), BF),
+            pltpu.VMEM((group, hidden), BF),
+            pltpu.VMEM((group, hidden), BF),
+            pltpu.SemaphoreType.DMA((2,)),
+            pltpu.SemaphoreType.DMA((SEQ * micros,)),
+            pltpu.SemaphoreType.DMA((SEQ * micros,)),
+        ],
+        compiler_params=params(),
+        cost_estimate=estimate(12 * group * model * hidden, 24 * 2**20),
         name="feed",
-    )(info, *n2_pieces, c_all, vec, w_up, w_down)
-
-
-def middle_back_kernel(count, info, p0, p1, p2, mid_ref, c_ref, vec, mine, other, gm_ref, gb_ref, g0, g1, g2, g3, sums, weight, scratch, sem):
+    )(*n2_pieces, *c_pieces, vec, w_down, w_up)
+
+
+def middle_back_kernel(count, micros, info, *refs):
+    chips, cames, fars = refs[:micros], refs[micros : 2 * micros], refs[2 * micros : 3 * micros]
+    mid_ref, c_ref, vec, mine, other = refs[3 * micros : 3 * micros + 5]
+    gm_ref, gb_ref, g0, g1, g2, g3, sums, weight, scratch, sem = refs[3 * micros + 5 :]
     copies = out_weight_copies(info, count, mine, other, weight, sem)
     for copy in copies:
         copy.start()
-    grad_two = p0[0].astype(F32) + p1[0].astype(F32) + p2[...].astype(F32)
+    grad_two = jnp.concatenate(
+        [a[0].astype(F32) + b[0].astype(F32) + c[...].astype(F32) for a, b, c in zip(chips, cames, fars)],
+        axis=0,
+    )
     hat, scale = norm_parts(mid_ref[...])
     cot = c_ref[...].astype(F32)
     grad_middle = cot + norm_back(grad_two, hat, scale, vec[5:6, :])
@@ -665,10 +665,11 @@
 
 def middle_back(info, count, parts, middle, c_own, vec, mine, other):
     rows, model = middle.shape
+    micros = len(parts)
     piece = jax.ShapeDtypeStruct((rows, model // SEQ), BF)
     return pl.pallas_call(
-        functools.partial(middle_back_kernel, count),
-        in_specs=[SMEM] + [VMEM] * 6 + [ANY] * 2,
+        functools.partial(middle_back_kernel, count, micros),
+        in_specs=[SMEM] + [VMEM] * (3 * micros + 3) + [ANY] * 2,
         out_specs=[VMEM] * 7,
         out_shape=[
             jax.ShapeDtypeStruct((rows, model), F32),
@@ -684,25 +685,27 @@
         compiler_params=params(),
         cost_estimate=estimate(2 * rows * model * model, 4 * 2**20),
         name="middle_back",
-    )(info, *parts, middle, c_own, vec, mine, other)
-
-
-def attention_back_kernel(count, info, joined_ref, probs_ref, g0, g1, g2, g3, hat_ref, source, *refs):
-    out_ref, chip_ref, sib_ref, sums, weight, sem = refs
+    )(info, *[p for at in range(3) for p in [part[at] for part in parts]], middle, c_own, vec, mine, other)
+
+
+def attention_back_kernel(count, info, joined_ref, probs_ref, g0, g1, g2, g3, hat_ref, *refs):
+    pieces = refs[:count]
+    out_ref, chip_ref, sib_ref, sums, weight, sem = refs[count:]
     tokens = joined_ref.shape[2]
     rows = SEQ * tokens
     triple = joined_ref.shape[3]
     width = triple // 3
     model = weight.shape[0]
-    fetch = pltpu.make_async_copy(source, weight, sem)
+    copies = piece_copies(info, pieces, 0, weight, sem)
 
     @pl.when(pl.program_id(0) == 0)
     def _():
-        fetch.start()
+        for copy in copies:
+            copy.start()
         sums[...] = jnp.zeros(sums.shape, F32)
 
     joined = joined_ref[...].reshape(rows, triple)
-    grad = jnp.concatenate([g0[0], g1[0], g2[0], g3[0]], axis=0)
+    grad = jnp.concatenate([g0[...], g1[...], g2[...], g3[...]], axis=0)
     queries, keys, values = [], [], []
     for head in range(width // HEAD_DIM):
         low = head * HEAD_DIM
@@ -729,7 +732,8 @@
 
     @pl.when(pl.program_id(0) == 0)
     def _():
-        fetch.wait()
+        for copy in copies:
+            copy.wait()
 
     partial = cols_dot(grad_joined, weight[...])
     hat = hat_ref[...].reshape(rows, model).astype(F32)
@@ -741,7 +745,8 @@
     sib_ref[...] = low[half:].reshape(sib_ref.shape)
 
 
-def attention_back(info, count, joined, probs, grads, hat, weight):
+def attention_back(info, joined, probs, grads, hat, pieces):
+    count = len(pieces)
     _, images, tokens, triple = joined.shape
     model = hat.shape[3]
     width = triple // 3
@@ -757,8 +762,9 @@
             group_block(SEQ, triple),
             pl.BlockSpec((1, heads, rows, rows), lambda i: (i, 0, 0, 0)),
         ]
-        + [pl.BlockSpec((1, tokens, width), lambda i: (i, 0, 0))] * SEQ
-        + [group_block(SEQ, model), ANY],
+        + [pl.BlockSpec((tokens, width), lambda i: (i, 0))] * SEQ
+        + [group_block(SEQ, model)]
+        + [ANY] * count,
         out_specs=[
             group_block(SEQ, triple),
             group_block(2, model),
@@ -771,13 +777,13 @@
             pair,
             jax.ShapeDtypeStruct((16, model), F32),
         ],
-        scratch_shapes=[pltpu.VMEM((model, triple), BF), pltpu.SemaphoreType.DMA],
+        scratch_shapes=[pltpu.VMEM((model, triple), BF), pltpu.SemaphoreType.DMA((count,))],
         compiler_params=params(),
         cost_estimate=estimate(
             2 * images * rows * (model * triple + 8 * width * rows), 8 * 2**20
         ),
         name="attention_back",
-    )(info, joined, probs, *grads, hat, weight)
+    )(info, joined, probs, *grads, hat, *pieces)
 
 
 def on_device(
@@ -836,176 +842,98 @@
     early = triple + LANES
     bias_column = jnp.pad(up_bias[:, None], ((0, 0), (VECTORS, LANES - VECTORS - 1)))
     first_group = jnp.concatenate(
-        [arrived[:, :triple], arrived[:, triple:early] + bias_column], axis=1
-    )
-    second_group = arrived[:, early:]
-    x_all = lax.all_gather(inputs, "seq")
-    c_all = lax.all_gather(cotangent.reshape(micros, rows, model), "seq")
-    ordered = len(digits_of(fsdp)) == 2 and digits_of(fsdp)[1][1] == 4
-    if ordered:
-        down = Gather(down_weight, fsdp)
-        down.send(0), down.send(1), down.forward(None)
-        first = Gather(first_group, fsdp)
-        first.send(0, down.came[0])
-        first.send(1, down.came[1])
-        first.send(2, down.passed[None])
-        first.forward(None, down.passed[None])
-        for at in range(3):
-            first.forward(at)
-        second = Gather(second_group, fsdp)
-        second.send(0, first.came[0], first.came[1])
-        second.send(1, first.came[2])
-        second.forward(None, first.passed[0])
-        down.forward(0, first.passed[1])
-        down.forward(1, first.passed[1])
-        first_pieces = first.pieces()
-    else:
-        first_pieces = fsdp_gather(first_group, fsdp)
-        second_pieces = fsdp_gather(second_group, fsdp)
-        down_pieces = fsdp_gather(down_weight, fsdp)
-    x_own = [inputs[m].reshape(rows, model) for m in micro_range]
-    c_own = [cotangent[m].reshape(rows, model) for m in micro_range]
-
-    w_qkv, _, vec = placed(info, first_pieces, (0, triple), (triple, LANES), vectors=True)
-    n1s, hats, joineds, probs, heads_in = [], [], [], [], []
-    for m in micro_range:
-        keep = keep_mask[m].reshape(images, SEQ, tokens)
-        keep = jnp.stack(
-            [lax.dynamic_index_in_dim(keep, at_s ^ mask, 1, keepdims=False) for mask in ORDER], axis=1
-        )
-        keep = after(keep, *joineds[-1:])
-        n1, hat, joined, *heads_out, prob = attention(
-            info,
-            fsdp,
-            m,
-            x_all,
-            keep.reshape(images, SEQ * tokens, 1),
-            vec,
-            w_qkv,
-        )
-        n1s.append(n1)
-        hats.append(hat)
-        joineds.append(joined)
-        probs.append(prob)
-        heads_in.append(seq_exchange([h.reshape(rows, width) for h in heads_out]))
-        if ordered and m == 0:
-            second.send(2, joined)
-            second.forward(0, joined)
-            second.forward(1, joined)
-            down.send(2, joined, second.came[0])
-        if ordered and m == micros - 1:
-            second.forward(2, joined)
-            down.forward(2, joined)
-            second_pieces, down_pieces = second.pieces(), down.pieces()
-
-    out_mine, w_up = placed(info, second_pieces, (0, half), (half, units))
-    (w_down,) = placed(info, down_pieces, (0, model))
+        [
+            arrived[:, :triple],
+            arrived[:, triple:early] + bias_column,
+            arrived[:, early : early + half],
+        ],
+        axis=1,
+    )
+    x_pieces = seq_gather(inputs.reshape(micros * rows, model))
+    first_pieces = fsdp_gather(first_group, fsdp)
+    w_down = lax.all_gather(down_weight, "fsdp", tiled=True)
+    w_up = lax.all_gather(arrived[:, early + half :], "fsdp", tiled=True)
+
+    x_own = inputs.reshape(micros * rows, model)
+    c_own = cotangent.reshape(micros * rows, model)
+    keep = keep_mask.reshape(micros * images, SEQ, tokens)
+    keep = jnp.stack(
+        [lax.dynamic_index_in_dim(keep, at_s ^ mask, 1, keepdims=False) for mask in ORDER], axis=1
+    )
+    n1, hat_one, joined, *heads_out, probs, vec = attention(
+        info,
+        [x.reshape(micros * images, tokens, model) for x in x_pieces],
+        keep.reshape(micros * images, SEQ * tokens, 1),
+        first_pieces,
+        triple,
+    )
+    c_pieces = seq_gather(after(c_own, x_pieces[1]))
+    heads_out[1:] = [after(h, c_pieces[1]) for h in heads_out[1:]]
+    heads_in = seq_exchange(heads_out)
+    out_mine = placed(info, first_pieces, early, half)
     out_other = hop(out_mine, 1)
-
-    attendeds, middles, n2_pieces = [], [], []
-    heads_in[0][0] = after(heads_in[0][0], joineds[-1])
-    for m in micro_range:
-        attended, middle, normed = middle_part(
-            info, fsdp, heads_in[m], x_own[m], vec, out_mine, out_other
-        )
-        attendeds.append(attended)
-        middles.append(middle)
-        if m + 1 < micros:
-            heads_in[m + 1][0] = after(heads_in[m + 1][0], middle)
-        n2_pieces.append(seq_gather(normed))
-
-    actives, grad_hiddens, two_parts, down_parts, sums = [], [], [], [], []
-    n2_pieces[0][0] = after(n2_pieces[0][0], middles[-1])
-    for m in micro_range:
-        active, grad_hidden, down_chip, down_sib, up_chip, up_sib, part = feed(
-            info, fsdp, m, n2_pieces[m], c_all, vec, w_up, w_down
-        )
-        actives.append(active)
-        grad_hiddens.append(grad_hidden)
-        sums.append(part)
-        down_parts.append((down_chip, down_sib))
-        came, far = seq_scatter(up_chip, up_sib)
-        two_parts.append((up_chip, came, hop(far, 2)))
-        if m + 1 < micros:
-            n2_pieces[m + 1][0] = after(n2_pieces[m + 1][0], far)
-        else:
-            actives[0] = after(actives[0], far)
+    attended, middle, normed = middle_part(
+        info, fsdp, heads_in, x_own, vec, out_mine, out_other
+    )
+    n2_pieces = seq_gather(normed)
 
     group_rows = micros * SEQ * rows
-
-    feed_grad = feed_grads(info, fsdp, n2_pieces[0] + n2_pieces[1], actives, grad_hiddens, c_all)
+    down_chip, down_sib, up_chip, up_sib, feed_grad, part = feed(
+        fsdp, micros, n2_pieces, c_pieces, vec, w_down, w_up
+    )
+    sums = [part]
     down_grad, up_grad = lax.psum_scatter(feed_grad, "fsdp", scatter_dimension=0, tiled=False)
     down_grad = down_grad.astype(F32)
-
-    grad_middles, branches, grads_in = [], [], []
-    for m in micro_range:
-        grad_middle, branch, *grads_out, part = middle_back(
-            info, fsdp, two_parts[m], after(middles[m], feed_grad), c_own[m], vec, out_mine, out_other
-        )
-        grad_middles.append(grad_middle)
-        branches.append(branch)
-        sums.append(part)
-        if m + 1 < micros:
-            middles[m + 1] = after(middles[m + 1], branch)
-        grads_in.append(seq_exchange(grads_out))
-
-    out_here, out_there = core_grad(info, fsdp, attendeds, branches)
+    came, far = seq_scatter(up_chip, up_sib)
+    two_parts = [(up_chip, came, hop(far, 2))]
+    down_parts = [(down_chip, down_sib)]
+
+    grad_middle, branch, *grads_out, part = middle_back(
+        info, fsdp, two_parts, middle, c_own, vec, out_mine, out_other
+    )
+    sums.append(part)
+    grads_in = seq_exchange(grads_out)
+    out_here, out_there = core_grad(info, fsdp, [attended], [branch])
+    down_sums = []
+    for chip, sib in down_parts:
+        came, far = seq_scatter(chip, after(sib, branch))
+        down_sums.append((chip[0], came[0], far))
     out_blocks = core_split(info, fsdp, out_here, hop(out_there, 1))
-    out_grad = scatter_far(scatter_near(*out_blocks, fsdp, at_f), fsdp, at_f)
-
-    grads_in[0][0] = after(grads_in[0][0], branches[-1])
-    joined_grads, inputs_back = [], []
-    one_parts = []
-    for m in micro_range:
-        grad_joined, chip, sib, part = attention_back(
-            info,
-            fsdp,
-            joineds[m],
-            probs[m],
-            [g.reshape(images, tokens, width) for g in grads_in[m]],
-            hats[m],
-            w_qkv,
-        )
-        joined_grads.append(grad_joined.reshape(SEQ * rows, triple))
-        sums.append(part)
-        if m + 1 < micros:
-            joineds[m + 1] = after(joineds[m + 1], grad_joined)
-        chip = chip.reshape(2, rows, model)
-        came, far = seq_scatter(chip, sib.reshape(2, rows, model))
-        one_parts.append((chip[0], came[0], hop(far, 2)))
-    outputs = []
-    for m in micro_range:
-        chip, sib = down_parts[m]
-        came, far = seq_scatter(chip, after(sib, branches[-1]))
-        total = chip[0].astype(F32) + came[0].astype(F32) + hop(far, 2).astype(F32)
-        result = middles[m] + total + vec[7:8]
-        outputs.append(result.astype(BF).reshape(images, tokens, model))
-    for m in micro_range:
-        a, b, c = one_parts[m]
-        grad_one = a.astype(F32) + b.astype(F32) + c.astype(F32)
-        hat, scale = norm_parts(x_own[m].astype(F32))
-        back = grad_middles[m] + norm_back(grad_one, hat, scale, vec[0:1])
-        inputs_back.append(back.astype(BF).reshape(images, tokens, model))
-
-    qkv_grad = weight_grad(
+    grads_in[0] = after(grads_in[0], *[far for _, _, far in down_sums], out_blocks[1])
+
+    grad_joined, chip, sib, part = attention_back(info, joined, probs, grads_in, hat_one, first_pieces)
+    sums.append(part)
+    qkv_blocks = weight_grad(
         info,
         fsdp,
-        [n.reshape(SEQ * rows, model) for n in n1s],
-        joined_grads,
+        [n1.reshape(group_rows, model)],
+        [grad_joined.reshape(group_rows, triple)],
         sums=sums,
         shape=(group_rows, model, triple),
     )
-    qkv_grad = scatter_far(scatter_near(*qkv_grad, fsdp, at_f), fsdp, at_f)
-    up_bias_grad = qkv_grad[:, triple + VECTORS]
-
-    last = jnp.concatenate([qkv_grad.astype(BF), out_grad.astype(BF), up_grad], axis=1)
+    chip = chip.reshape(2, micros * rows, model)
+    came, far = seq_scatter(chip, sib.reshape(2, micros * rows, model))
+    grad_one = chip[0].astype(F32) + came[0].astype(F32) + hop(far, 2).astype(F32)
+
+    [(a, b, c)] = down_sums
+    total = a.astype(F32) + b.astype(F32) + hop(c, 2).astype(F32)
+    layer_out = (middle + total + vec[7:8]).astype(BF).reshape(micros, images, tokens, model)
+    hat, scale = norm_parts(x_own.astype(F32))
+    input_grad = grad_middle + norm_back(grad_one, hat, scale, vec[0:1])
+    input_grad = input_grad.astype(BF).reshape(micros, images, tokens, model)
+
+    out_parts = scatter_far(scatter_near(*out_blocks, fsdp, at_f), fsdp, at_f)
+    qkv_parts = scatter_far(scatter_near(*qkv_blocks, fsdp, at_f), fsdp, at_f)
+
+    last, own_vectors = collect(qkv_parts, out_parts, [up_grad])
+    up_bias_grad = own_vectors[:, VECTORS]
     last = lax.all_to_all(last.reshape(SEQ, depth, -1), "seq", 0, 0, tiled=True)
     qkv_weight_grad, out_weight_grad, up_weight_grad, vector_grads = unpack(last, model, units)
     vector_grads = vector_grads[:, :VECTORS].T
 
     return (
-        jnp.stack(outputs),
-        jnp.stack(inputs_back),
+        layer_out,
+        input_grad,
         vector_grads[0],
         vector_grads[1],
         qkv_weight_grad,

time: 372 us -> 322 us (0.87); the launches traced: 365 us -> 321 us
  starting transfers between devices: 68.9 us -> 36.1 us
  Pallas kernels: 120 us -> 91.9 us
  blocking collectives: 0 us -> 14.1 us
  waiting for transfers between devices: 122 us -> 136 us
  local copies, waits for them, and re-layouts: 21.9 us -> 15.3 us
    ppermute x29 -> x15, starting transfers between devices: 41.7 us -> 20.3 us  [shift(): return lax.ppermute(array, 'fsdp', pairs)]
    pallas_call x8 -> x4, Pallas kernels: 53.5 us -> 35.3 us  [the longest x1 23.7 us: feed(): pl.pallas_call(functools.partial(feed_kernel, micros), in_specs=[ANY] * (...]
    ppermute x32 -> x23, waiting for transfers between devices: 32 us -> 46.5 us  [hop(): return lax.ppermute(array, 'seq', [(i, i ^ mask) for i in range(SEQ)])]
    all_to_all x0 -> x1, blocking collectives: none -> 14.1 us  [on_device(): lax.all_to_all(to_send, 'seq', 0, 0, tiled=True).reshape(block, -1)]
    ppermute x29 -> x15, waiting for transfers between devices: 72.3 us -> 81.9 us  [shift(): return lax.ppermute(array, 'fsdp', pairs)]
    all_to_all x1 -> x0, waiting for transfers between devices: 7.79 us -> none  [on_device(): lax.all_to_all(to_send, 'seq', 0, 0, tiled=True).reshape(block, -1)]
    ppermute x32 -> x23, starting transfers between devices: 19.3 us -> 12.2 us  [hop(): return lax.ppermute(array, 'seq', [(i, i ^ mask) for i in range(SEQ)])]
    unnamed x166 -> x74, local copies, waits for them, and re-layouts: 12.1 us -> 7.66 us
  transfers between devices with their start and end apart: 66 -> 42, of which waited for: 24 -> 18; matrix products, arithmetic and copies ran while one was open for 6% -> 6% of each run, Pallas kernels for 23% -> 20%
where the time goes in v3:
time: 322 us; the launch traced here: 321 us
  waiting for transfers between devices  136 us (42%)
  Pallas kernels  91.9 us (29%)
  starting transfers between devices  36.1 us (11%)
  local copies, waits for them, and re-layouts  15.3 us (5%)
  between operations  14.2 us (4%)
  blocking collectives  14.1 us (4%)
  other arithmetic  13.8 us (4%)
    ppermute x15, waiting for transfers between devices, shift(): return lax.ppermute(array, 'fsdp', pairs)  81.9 us
    ppermute x23, waiting for transfers between devices, hop(): return lax.ppermute(array, 'seq', [(i, i ^ mask) for i in range(SEQ)])  46.5 us
    pallas_call x1, Pallas kernels, feed(): pl.pallas_call(functools.partial(feed_kernel, micros), in_specs=[ANY] * (...  23.7 us
    ppermute x15, starting transfers between devices, shift(): return lax.ppermute(array, 'fsdp', pairs)  20.3 us
    pallas_call x1, Pallas kernels, attention(): pl.pallas_call(functools.partial(attention_kernel, count), grid=(images,)...  15.4 us
    all_to_all x1, blocking collectives, on_device(): lax.all_to_all(to_send, 'seq', 0, 0, tiled=True).reshape(block, -1)  14.1 us
    pallas_call x1, Pallas kernels, attention_back(): pl.pallas_call(functools.partial(attention_back_kernel, count), grid=(ima...  13.7 us
    ppermute x23, starting transfers between devices, hop(): return lax.ppermute(array, 'seq', [(i, i ^ mask) for i in range(SEQ)])  12.2 us
  transfers between devices with their start and end apart: 42, of which 18 were waited for; matrix products, arithmetic and copies ran while one was open for 6% of the time, Pallas kernels for 20%

profile of v3, /device:TPU:0, one launch (start us, length us, event | category | flops | bytes accessed | tf_op | source)
XLA Modules:
  0.0 320.9 jit_solution(18012006863924679694)
XLA Ops:
  9.5 2.0 pack.1
  11.5 14.1 %all_to_all.10 = bf16[4,32,2432]{2,1,0:T(8,128)(2,1)S(1)} all-to-all(bf16[4,32,2432]{2,1,0:T(8,128)(2,1)} %pack.1), channel_id=1, replica_groups=mesh['fsdp'=8,'seq'=4] {'seq'}, dimensions={0} | all-to-all | bytes 1245184 | tf_op jit(solution)/shard_map/all_to_all | solution.py:841
  26.7 2.3 collective-permute-start.3
  29.0 2.1 collective-permute-start.4
  32.4 1.5 collective-permute-start.6
  33.9 8.7 %collective-permute-done.3.refs_1_ = bf16[128,1408]{1,0:T(8,128)(2,1)S(1)} collective-permute-done((bf16[128,1408]{1,0:T(8,128)(2,1)S(1)}, bf16[128,1408]{1,0:T(8,128)(2,1)S(1)}, u32[]{:S(2)}, u32[]{:S(2)}) %collective-permute-start.3) | collective-permute-done | bytes 360480 | tf_op jit(solution)/shard_map/ppermute | solution.py:66
  43.5 5.8 %collective-permute-done.4.refs_2_ = bf16[128,1408]{1,0:T(8,128)(2,1)S(1)} collective-permute-done((bf16[128,1408]{1,0:T(8,128)(2,1)S(1)}, bf16[128,1408]{1,0:T(8,128)(2,1)S(1)}, u32[]{:S(2)}, u32[]{:S(2)}) %collective-permute-start.4) | collective-permute-done | bytes 360480 | tf_op jit(solution)/shard_map/ppermute | solution.py:66
  49.3 1.3 collective-permute-start.8
  50.6 30.5 %collective-permute-done.5.refs_3_ = bf16[128,1408]{1,0:T(8,128)(2,1)S(1)} collective-permute-done((bf16[128,1408]{1,0:T(8,128)(2,1)S(1)}, bf16[128,1408]{1,0:T(8,128)(2,1)S(1)}, u32[]{:S(2)}, u32[]{:S(2)}) %collective-permute-start.5) | collective-permute-done | bytes 360480 | tf_op jit(solution)/shard_map/ppermute | solution.py:66
  84.1 7.3 %collective-permute-done.9.refs_7_ = bf16[128,1408]{1,0:T(8,128)(2,1)} collective-permute-done((bf16[128,1408]{1,0:T(8,128)(2,1)S(1)}, bf16[128,1408]{1,0:T(8,128)(2,1)}, u32[]{:S(2)}, u32[]{:S(2)}) %collective-permute-start.9) | collective-permute-done | bytes 360480 | tf_op jit(solution)/shard_map/ppermute | solution.py:66
  91.5 3.1 placed.1.mine.refs_6_
  94.7 1.1 collective-permute-start.10
  97.1 15.4 %attention.1 = (bf16[4,4,80,1024]{3,2,1,0:T(8,128)(2,1)}, bf16[4,4,80,1024]{3,2,1,0:T(8,128)(2,1)}, bf16[4,4,80,768]{3,2,1,0:T(8,128)(2,1)}, bf16[320,256]{1,0:T...) custom-call(s32[14]{0:T(128)} %stack.90.info, ...), custom_call_target="tpu_custom_call" | custom-call | flops 2852126720 | bytes 16777216 | tf_op jit(solution)/shard_map/attention/pallas_call | solution.py:478
  115.5 4.2 %collective-permute-done.13.e3 = bf16[320,256]{1,0:T(8,128)(2,1)S(1)} collective-permute-done((bf16[320,256]{1,0:T(8,128)(2,1)}, bf16[320,256]{1,0:T(8,128)(2,1)S(1)}, u32[]{:S(2)}, u32[]{:S(2)}) %collective-permute-start.13) | collective-permute-done | bytes 163872 | tf_op jit(solution)/shard_map/ppermute | solution.py:30
  119.8 3.8 %collective-permute-done.11.e1 = bf16[320,256]{1,0:T(8,128)(2,1)S(1)} collective-permute-done((bf16[320,256]{1,0:T(8,128)(2,1)}, bf16[320,256]{1,0:T(8,128)(2,1)S(1)}, u32[]{:S(2)}, u32[]{:S(2)}) %collective-permute-start.11) | collective-permute-done | bytes 163872 | tf_op jit(solution)/shard_map/ppermute | solution.py:30
  124.6 5.2 %middle.1 = (bf16[320,1024]{1,0:T(8,128)(2,1)}, f32[320,1024]{1,0:T(8,128)}, bf16[320,1024]{1,0:T(8,128)(2,1)}) custom-call(s32[14]{0:T(128)} %stack.90.info, bf16[320,256]{1,0:T(8,128)(2,1)} %get-tuple-element.70.e0, bf16[320,256]{1,0:T(8,128)(2,1)} %copy-done.24, bf16[320,256]{1,0:T(8,128)(2,1)} %copy-done.23, bf16[320,256]{1,0:T(8,128)(2,1)} %copy-done.22, ...), custom_call_target="tpu_custom_call" | custom-call | flops 671088640 | bytes 4194304 | tf_op jit(solution)/shard_map/middle/pallas_call | solution.py:538
  131.3 15.3 %collective-permute-done.15.refs_1_ = bf16[320,1024]{1,0:T(8,128)(2,1)S(1)} collective-permute-done((bf16[320,1024]{1,0:T(8,128)(2,1)}, bf16[320,1024]{1,0:T(8,128)(2,1)S(1)}, u32[]{:S(2)}, u32[]{:S(2)}) %collective-permute-start.15) | collective-permute-done | bytes 655392 | tf_op jit(solution)/shard_map/ppermute | solution.py:30
  146.7 2.2 collective-permute-done.17.refs_3_
  148.9 23.7 %feed.1 = (bf16[2,320,1024]{2,1,0:T(8,128)(2,1)}, bf16[2,320,1024]{2,1,0:T(8,128)(2,1)}, bf16[2,320,1024]{2,1,0:T(8,128)(2,1)}, bf16[2,320,1024]{2,1,0:T(8,128)(...) custom-call(bf16[320,1024]{1,0:T(8,128)(2,1)} %get-tuple-element.80.refs_0_, bf16[320,1024]{1,0:T(8,128)(2,1)} %copy-done.31, ...), custom_call_target="tpu_custom_call" | custom-call | flops 16106127360 | bytes 25165824 | tf_op jit(solution)/shard_map/feed/pallas_call | solution.py:609
  172.9 3.1 collective-permute-done.20.refs_1_
  177.2 15.9 %collective-permute-done.21.refs_2_ = bf16[320,1024]{1,0:T(8,128)(2,1)S(1)} collective-permute-done((bf16[320,1024]{1,0:T(8,128)(2,1)S(1)}, bf16[320,1024]{1,0:T(8,128)(2,1)S(1)}, u32[]{:S(2)}, u32[]{:S(2)}) %collective-permute-start.21) | collective-permute-done | bytes 655392 | tf_op jit(solution)/shard_map/ppermute | solution.py:30
  193.9 6.0 %middle_back.1 = (f32[320,1024]{1,0:T(8,128)}, bf16[320,1024]{1,0:T(8,128)(2,1)}, bf16[320,256]{1,0:T(8,128)(2,1)}, bf16[320,256]{1,0:T(8,128)(2,1)}, bf16[320,2...) custom-call(s32[14]{0:T(128)} %stack.90.info, bf16[2,320,1024]{2,1,0:T(8,128)(2,1)} %get-tuple-element.83.refs_0_, ...), custom_call_target="tpu_custom_call" | custom-call | flops 671088640 | bytes 4194304 | tf_op jit(solution)/shard_map/middle_back/pallas_call | solution.py:670
  200.0 3.7 %core_grad.1 = (bf16[1024,512]{1,0:T(8,128)(2,1)}, bf16[1024,512]{1,0:T(8,128)(2,1)}) custom-call(s32[14]{0:T(128)} %stack.90.info, bf16[320,1024]{1,0:T(8,128)(2,1)} %get-tuple-element.91.refs_0_, bf16[320,1024]{1,0:T(8,128)(2,1)} %get-tuple-element.85.refs_1_), custom_call_target="tpu_custom_call" | custom-call | flops 671088640 | bytes 4194304 | tf_op jit(solution)/shard_map/core_grad/pallas_call | solution.py:387
  205.0 1.3 collective-permute-start.27
  207.7 2.8 core_split.1
  210.5 1.3 fusion.9
  211.7 1.5 collective-permute-done.27.g3
  213.3 13.7 %attention_back.1 = (bf16[4,4,80,768]{3,2,1,0:T(8,128)(2,1)}, bf16[2,4,80,1024]{3,2,1,0:T(8,128)(2,1)}, bf16[2,4,80,1024]{3,2,1,0:T(8,128)(2,1)}, f32[16,1024]{1,0:T(8,128)}) custom-call(s32[14]{0:T(128)} %stack.90.info, bf16[4,4,80,768]{3,2,1,0:T(8,128)(2,1)} %get-tuple-element.88.joined_ref, bf16[4,4,320,320]{3,2,1,0:T(8,128)(2,1)} %get-tuple-element.89.probs_ref, ...), custom_call_target="tpu_custom_call" | custom-call | flops 3690987520 | bytes 8388608 | tf_op jit(solution)/shard_map/attention_back/pallas_call | solution.py:757
  228.5 1.5 collective-permute-start.34
  230.5 7.2 %weight_grad.1 = (bf16[4,128,896]{2,1,0:T(8,128)(2,1)}, bf16[4,128,896]{2,1,0:T(8,128)(2,1)}) custom-call(s32[14]{0:T(128)} %stack.90.info, bf16[1280,1024]{1,0:T(8,128)(2,1)} %bitcast.111, bf16[1280,768]{1,0:T(8,128)(2,1)} %bitcast.112, f32[16,1024]{1,0:T(8,128)} %get-tuple-element.104.refs_2_, f32[16,1024]{1,0:T(8,128)} %get-tuple-element.105.refs_3_, ...), custom_call_target="tpu_custom_call" | custom-call | flops 2013265920 | bytes 6160384 | tf_op jit(solution)/shard_map/weight_grad/pallas_call | solution.py:352
  237.8 1.1 collective-permute-start.30
  239.1 2.3 fusion.2
  244.1 2.0 split.3
  246.1 3.8 %collective-permute-start.36 = (bf16[1,128,512]{2,1,0:T(8,128)(2,1)}, bf16[1,128,512]{2,1,0:T(8,128)(2,1)}, u32[]{:S(2)}, u32[]{:S(2)}) collective-permute-start(bf16[1,128,512]{2,1,0:T(8,128)(2,1)} %get-tuple-element.116), channel_id=1, source_target_pairs={{0,24},{4,28},{8,0},{12,4},{16,8},{20,12},{24,16},{28,20},{1,25},{... | collective-permute-start | bytes 393224 | tf_op jit(solution)/shard_map/ppermute | solution.py:66
  250.0 2.8 fusion.7
  252.7 15.2 %collective-permute-done.30 = bf16[4,128,896]{2,1,0:T(8,128)(2,1)S(1)} collective-permute-done((bf16[4,128,896]{2,1,0:T(8,128)(2,1)}, bf16[4,128,896]{2,1,0:T(8,128)(2,1)S(1)}, u32[]{:S(2)}, u32[]{:S(2)}) %collective-permute-start.30) | collective-permute-done | bytes 917536 | tf_op jit(solution)/shard_map/ppermute | solution.py:66
  268.9 2.4 split.2
  271.3 3.8 %collective-permute-start.32 = (bf16[1,128,896]{2,1,0:T(8,128)(2,1)}, bf16[1,128,896]{2,1,0:T(8,128)(2,1)S(1)}, u32[]{:S(2)}, u32[]{:S(2)}) collective-permute-start(bf16[1,128,896]{2,1,0:T(8,128)(2,1)} %get-tuple-element.111), channel_id=1, source_target_pairs={{0,24},{4,28},{8,0},{12,4},{16,8},{20,12},{24,16},{28,20},{1,25},{... | collective-permute-start | bytes 688136 | tf_op jit(solution)/shard_map/ppermute | solution.py:66
  275.1 1.6 fusion.4
  277.8 2.0 fusion.10
  279.8 2.0 collective-permute-done.31.refs_1_
  281.8 2.4 collective-permute-done.32.refs_2_
  284.2 9.2 %collective-permute-done.33.refs_3_ = bf16[1,128,896]{2,1,0:T(8,128)(2,1)S(1)} collective-permute-done((bf16[1,128,896]{2,1,0:T(8,128)(2,1)S(1)}, bf16[1,128,896]{2,1,0:T(8,128)(2,1)S(1)}, u32[]{:S(2)}, u32[]{:S(2)}) %collective-permute-start.33) | collective-permute-done | bytes 229408 | tf_op jit(solution)/shard_map/ppermute | solution.py:66
  294.1 2.5 collect.1
  296.6 3.5 %all-to-all-start.1 = ((bf16[4,32,2432]{2,1,0:T(8,128)(2,1)}), bf16[4,32,2432]{2,1,0:T(8,128)(2,1)S(1)}, u32[]{:S(2)}, u32[]{:S(2)}) async-start(bf16[4,32,2432]{2,1,0:T(8,128)(2,1)} %bitcast.97), calls=%async_computation.2 | async-start | bytes 1245184 | tf_op jit(solution)/shard_map/all_to_all | solution.py:930
  300.1 2.6 add_convert_fusion
  303.4 6.5 %all-to-all-done.1.ref = bf16[4,32,2432]{2,1,0:T(8,128)(2,1)S(1)} async-done(((bf16[4,32,2432]{2,1,0:T(8,128)(2,1)}), bf16[4,32,2432]{2,1,0:T(8,128)(2,1)S(1)}, u32[]{:S(2)}, u32[]{:S(2)}) %all-to-all-start.1) | async-done | bytes 622624 | tf_op jit(solution)/shard_map/all_to_all | solution.py:930
  310.8 2.1 unpack.1
  (162 shorter events, 31.1 us)
Async XLA Ops:
  7.2 141.7 %all-gather.3.cloned.1.call-start = ((), (), s32[]{:S(2)}) async-start(), calls=%async_computation.3 | async-start | bytes 2359296 | tf_op jit(solution)/shard_map/all_gather | solution.py:854
  7.9 141.0 %all-gather.5.cloned.1.call-start = ((), (), s32[]{:S(2)}) async-start(), calls=%async_computation.4 | async-start | bytes 2359296 | tf_op jit(solution)/shard_map/all_gather | solution.py:855
  9.5 16.9 %copy-start.28 = (bf16[128]{0:T(256)(128)(2,1)S(1)}, bf16[128]{0:T(256)(128)(2,1)}, u32[]{:S(2)}) copy-start(bf16[128]{0:T(256)(128)(2,1)} %param.29) | copy-start | bytes 772
  26.3 251.5 %reduce-scatter.2.cloned.1.call-start = ((), (), s32[]{:S(2)}) async-start(), calls=%async_computation.5 | async-start | bytes 4718592 | tf_op jit(solution)/shard_map/reduce_scatter | solution.py:885
  26.7 64.8 %copy-start.7 = (bf16[128,1408]{1,0:T(8,128)(2,1)}, bf16[128,1408]{1,0:T(8,128)(2,1)S(1)}, u32[]{:S(2)}) copy-start(bf16[128,1408]{1,0:T(8,128)(2,1)S(1)} %pad_maximum_fusion.refs_0_) | copy-start | bytes 1081348
  26.7 16.0 %collective-permute-start.3 = (bf16[128,1408]{1,0:T(8,128)(2,1)S(1)}, bf16[128,1408]{1,0:T(8,128)(2,1)S(1)}, u32[]{:S(2)}, u32[]{:S(2)}) collective-permute-start(bf16[128,1408]{1,0:T(8,128)(2,1)S(1)} %pad_maximum_fusion.refs_0_), channel_id=1, source_target_pairs={{0,8},{4,12},{8,16},{12,20},{16,24},{20,28},{24,0},{28,4},{1,9},{5... | collective-permute-start | bytes 1081352 | tf_op jit(solution)/shard_map/ppermute | solution.py:66
  29.0 20.3 %collective-permute-start.4 = (bf16[128,1408]{1,0:T(8,128)(2,1)S(1)}, bf16[128,1408]{1,0:T(8,128)(2,1)S(1)}, u32[]{:S(2)}, u32[]{:S(2)}) collective-permute-start(bf16[128,1408]{1,0:T(8,128)(2,1)S(1)} %pad_maximum_fusion.refs_0_), channel_id=1, source_target_pairs={{0,24},{4,28},{8,0},{12,4},{16,8},{20,12},{24,16},{28,20},{1,25},{... | collective-permute-start | bytes 1081352 | tf_op jit(solution)/shard_map/ppermute | solution.py:66
  31.1 50.0 %collective-permute-start.5 = (bf16[128,1408]{1,0:T(8,128)(2,1)S(1)}, bf16[128,1408]{1,0:T(8,128)(2,1)S(1)}, u32[]{:S(2)}, u32[]{:S(2)}) collective-permute-start(bf16[128,1408]{1,0:T(8,128)(2,1)S(1)} %pad_maximum_fusion.refs_0_), channel_id=1, source_target_pairs={{0,16},{4,20},{8,24},{12,28},{16,0},{20,4},{24,8},{28,12},{1,17},{... | collective-permute-start | bytes 1081352 | tf_op jit(solution)/shard_map/ppermute | solution.py:66
  32.1 50.2 %collective-permute-start = (bf16[320,1024]{1,0:T(8,128)(2,1)S(1)}, bf16[320,1024]{1,0:T(8,128)(2,1)}, u32[]{:S(2)}, u32[]{:S(2)}) collective-permute-start(bf16[320,1024]{1,0:T(8,128)(2,1)S(1)} %bitcast.82), channel_id=1, source_target_pairs={{0,2},{1,3},{2,0},{3,1},{4,6},{5,7},{6,4},{7,5},{8,10},{9,11},{10,... | collective-permute-start | bytes 1966088 | tf_op jit(solution)/shard_map/ppermute | solution.py:30
  32.4 49.8 %collective-permute-start.6 = (bf16[128,1408]{1,0:T(8,128)(2,1)S(1)}, bf16[128,1408]{1,0:T(8,128)(2,1)S(1)}, u32[]{:S(2)}, u32[]{:S(2)}) collective-permute-start(bf16[128,1408]{1,0:T(8,128)(2,1)S(1)} %pad_maximum_fusion.refs_0_), channel_id=1, source_target_pairs={{0,4},{4,0},{8,12},{12,8},{16,20},{20,16},{24,28},{28,24},{1,5},{5... | collective-permute-start | bytes 1081352 | tf_op jit(solution)/shard_map/ppermute | solution.py:66
  42.7 48.8 %copy-start.15 = (bf16[128,1408]{1,0:T(8,128)(2,1)}, bf16[128,1408]{1,0:T(8,128)(2,1)S(1)}, u32[]{:S(2)}) copy-start(bf16[128,1408]{1,0:T(8,128)(2,1)S(1)} %collective-permute-done.3.refs_1_) | copy-start | bytes 1081348
  42.7 41.5 %collective-permute-start.7 = (bf16[128,1408]{1,0:T(8,128)(2,1)S(1)}, bf16[128,1408]{1,0:T(8,128)(2,1)}, u32[]{:S(2)}, u32[]{:S(2)}) collective-permute-start(bf16[128,1408]{1,0:T(8,128)(2,1)S(1)} %collective-permute-done.3.refs_1_), channel_id=1, source_target_pairs={{0,4},{4,0},{8,12},{12,8},{16,20},{20,16},{24,28},{28,24},{1,5},{5... | collective-permute-start | bytes 1081352 | tf_op jit(solution)/shard_map/ppermute | solution.py:66
  49.3 42.2 %copy-start.16 = (bf16[128,1408]{1,0:T(8,128)(2,1)}, bf16[128,1408]{1,0:T(8,128)(2,1)S(1)}, u32[]{:S(2)}) copy-start(bf16[128,1408]{1,0:T(8,128)(2,1)S(1)} %collective-permute-done.4.refs_2_) | copy-start | bytes 1081348
  49.3 34.8 %collective-permute-start.8 = (bf16[128,1408]{1,0:T(8,128)(2,1)S(1)}, bf16[128,1408]{1,0:T(8,128)(2,1)}, u32[]{:S(2)}, u32[]{:S(2)}) collective-permute-start(bf16[128,1408]{1,0:T(8,128)(2,1)S(1)} %collective-permute-done.4.refs_2_), channel_id=1, source_target_pairs={{0,4},{4,0},{8,12},{12,8},{16,20},{20,16},{24,28},{28,24},{1,5},{5... | collective-permute-start | bytes 1081352 | tf_op jit(solution)/shard_map/ppermute | solution.py:66
  81.1 10.3 %collective-permute-start.9 = (bf16[128,1408]{1,0:T(8,128)(2,1)S(1)}, bf16[128,1408]{1,0:T(8,128)(2,1)}, u32[]{:S(2)}, u32[]{:S(2)}) collective-permute-start(bf16[128,1408]{1,0:T(8,128)(2,1)S(1)} %collective-permute-done.5.refs_3_), channel_id=1, source_target_pairs={{0,4},{4,0},{8,12},{12,8},{16,20},{20,16},{24,28},{28,24},{1,5},{5... | collective-permute-start | bytes 1081352 | tf_op jit(solution)/shard_map/ppermute | solution.py:66
  82.2 14.9 %collective-permute-start.1 = (bf16[320,1024]{1,0:T(8,128)(2,1)S(1)}, bf16[320,1024]{1,0:T(8,128)(2,1)}, u32[]{:S(2)}, u32[]{:S(2)}) collective-permute-start(bf16[320,1024]{1,0:T(8,128)(2,1)S(1)} %bitcast.83), channel_id=1, source_target_pairs={{0,1},{1,0},{2,3},{3,2},{4,5},{5,4},{6,7},{7,6},{8,9},{9,8},{10,11... | collective-permute-start | bytes 1966088 | tf_op jit(solution)/shard_map/ppermute | solution.py:30
  83.0 14.2 %collective-permute-start.2 = (bf16[320,1024]{1,0:T(8,128)(2,1)}, bf16[320,1024]{1,0:T(8,128)(2,1)}, u32[]{:S(2)}, u32[]{:S(2)}) collective-permute-start(bf16[320,1024]{1,0:T(8,128)(2,1)} %collective-permute-done), channel_id=1, source_target_pairs={{0,1},{1,0},{2,3},{3,2},{4,5},{5,4},{6,7},{7,6},{8,9},{9,8},{10,11... | collective-permute-start | bytes 1966088 | tf_op jit(solution)/shard_map/ppermute | solution.py:30
  94.6 29.0 %collective-permute-start.14 = (bf16[1024,512]{1,0:T(8,128)(2,1)}, bf16[1024,512]{1,0:T(8,128)(2,1)S(1)}, u32[]{:S(2)}, u32[]{:S(2)}) collective-permute-start(bf16[1024,512]{1,0:T(8,128)(2,1)} %placed.1.mine.refs_6_), channel_id=1, source_target_pairs={{0,1},{1,0},{2,3},{3,2},{4,5},{5,4},{6,7},{7,6},{8,9},{9,8},{10,11... | collective-permute-start | bytes 3145736 | tf_op jit(solution)/shard_map/ppermute | solution.py:30
  94.7 17.8 %collective-permute-start.10 = (bf16[320,1024]{1,0:T(8,128)(2,1)S(1)}, bf16[320,1024]{1,0:T(8,128)(2,1)S(1)}, u32[]{:S(2)}, u32[]{:S(2)}) collective-permute-start(bf16[320,1024]{1,0:T(8,128)(2,1)S(1)} %bitcast.94), channel_id=1, source_target_pairs={{0,2},{1,3},{2,0},{3,1},{4,6},{5,7},{6,4},{7,5},{8,10},{9,11},{10,... | collective-permute-start | bytes 1966088 | tf_op jit(solution)/shard_map/ppermute | solution.py:30
  113.4 6.4 %collective-permute-start.13 = (bf16[320,256]{1,0:T(8,128)(2,1)}, bf16[320,256]{1,0:T(8,128)(2,1)S(1)}, u32[]{:S(2)}, u32[]{:S(2)}) collective-permute-start(bf16[320,256]{1,0:T(8,128)(2,1)} %get-tuple-element.77), channel_id=1, source_target_pairs={{0,3},{1,2},{2,1},{3,0},{4,7},{5,6},{6,5},{7,4},{8,11},{9,10},{10,... | collective-permute-start | bytes 491528 | tf_op jit(solution)/shard_map/ppermute | solution.py:30
  114.1 5.7 %collective-permute-start.12 = (bf16[320,256]{1,0:T(8,128)(2,1)}, bf16[320,256]{1,0:T(8,128)(2,1)S(1)}, u32[]{:S(2)}, u32[]{:S(2)}) collective-permute-start(bf16[320,256]{1,0:T(8,128)(2,1)} %get-tuple-element.75), channel_id=1, source_target_pairs={{0,1},{1,0},{2,3},{3,2},{4,5},{5,4},{6,7},{7,6},{8,9},{9,8},{10,11... | collective-permute-start | bytes 491528 | tf_op jit(solution)/shard_map/ppermute | solution.py:30
  114.4 9.2 %collective-permute-start.11 = (bf16[320,256]{1,0:T(8,128)(2,1)}, bf16[320,256]{1,0:T(8,128)(2,1)S(1)}, u32[]{:S(2)}, u32[]{:S(2)}) collective-permute-start(bf16[320,256]{1,0:T(8,128)(2,1)} %get-tuple-element.73), channel_id=1, source_target_pairs={{0,2},{1,3},{2,0},{3,1},{4,6},{5,7},{6,4},{7,5},{8,10},{9,11},{10,... | collective-permute-start | bytes 491528 | tf_op jit(solution)/shard_map/ppermute | solution.py:30
  129.9 16.8 %collective-permute-start.15 = (bf16[320,1024]{1,0:T(8,128)(2,1)}, bf16[320,1024]{1,0:T(8,128)(2,1)S(1)}, u32[]{:S(2)}, u32[]{:S(2)}) collective-permute-start(bf16[320,1024]{1,0:T(8,128)(2,1)} %get-tuple-element.80.refs_0_), channel_id=1, source_target_pairs={{0,2},{1,3},{2,0},{3,1},{4,6},{5,7},{6,4},{7,5},{8,10},{9,11},{10,... | collective-permute-start | bytes 1966088 | tf_op jit(solution)/shard_map/ppermute | solution.py:30
  130.8 15.9 %collective-permute-start.18 = (bf16[320,1024]{1,0:T(8,128)(2,1)S(1)}, bf16[320,1024]{1,0:T(8,128)(2,1)S(1)}, u32[]{:S(2)}, u32[]{:S(2)}) collective-permute-start(bf16[320,1024]{1,0:T(8,128)(2,1)S(1)} %bitcast.95), channel_id=1, source_target_pairs={{0,1},{1,0},{2,3},{3,2},{4,5},{5,4},{6,7},{7,6},{8,9},{9,8},{10,11... | collective-permute-start | bytes 1966088 | tf_op jit(solution)/shard_map/ppermute | solution.py:30
  130.8 15.9 %collective-permute-start.19 = (bf16[320,1024]{1,0:T(8,128)(2,1)S(1)}, bf16[320,1024]{1,0:T(8,128)(2,1)S(1)}, u32[]{:S(2)}, u32[]{:S(2)}) collective-permute-start(bf16[320,1024]{1,0:T(8,128)(2,1)S(1)} %copy-done.30), channel_id=1, source_target_pairs={{0,1},{1,0},{2,3},{3,2},{4,5},{5,4},{6,7},{7,6},{8,9},{9,8},{10,11... | collective-permute-start | bytes 1966088 | tf_op jit(solution)/shard_map/ppermute | solution.py:30
  131.3 15.4 %collective-permute-start.16 = (bf16[320,1024]{1,0:T(8,128)(2,1)}, bf16[320,1024]{1,0:T(8,128)(2,1)}, u32[]{:S(2)}, u32[]{:S(2)}) collective-permute-start(bf16[320,1024]{1,0:T(8,128)(2,1)} %get-tuple-element.80.refs_0_), channel_id=1, source_target_pairs={{0,1},{1,0},{2,3},{3,2},{4,5},{5,4},{6,7},{7,6},{8,9},{9,8},{10,11... | collective-permute-start | bytes 1966088 | tf_op jit(solution)/shard_map/ppermute | solution.py:30
  146.7 2.2 collective-permute-start.17
  172.7 3.3 %collective-permute-start.20 = (bf16[2,320,1024]{2,1,0:T(8,128)(2,1)}, bf16[2,320,1024]{2,1,0:T(8,128)(2,1)S(1)}, u32[]{:S(2)}, u32[]{:S(2)}) collective-permute-start(bf16[2,320,1024]{2,1,0:T(8,128)(2,1)} %get-tuple-element.84), channel_id=1, source_target_pairs={{0,1},{1,0},{2,3},{3,2},{4,5},{5,4},{6,7},{7,6},{8,9},{9,8},{10,11... | collective-permute-start | bytes 3932168 | tf_op jit(solution)/shard_map/ppermute | solution.py:30
  176.0 17.1 %copy-start.5 = (bf16[2,320,1024]{2,1,0:T(8,128)(2,1)}, bf16[2,320,1024]{2,1,0:T(8,128)(2,1)S(1)}, u32[]{:S(2)}) copy-start(bf16[2,320,1024]{2,1,0:T(8,128)(2,1)S(1)} %collective-permute-done.20.refs_1_) | copy-start | bytes 3932164
  176.2 16.8 %collective-permute-start.21 = (bf16[320,1024]{1,0:T(8,128)(2,1)S(1)}, bf16[320,1024]{1,0:T(8,128)(2,1)S(1)}, u32[]{:S(2)}, u32[]{:S(2)}) collective-permute-start(bf16[320,1024]{1,0:T(8,128)(2,1)S(1)} %fusion.8), channel_id=1, source_target_pairs={{0,2},{1,3},{2,0},{3,1},{4,6},{5,7},{6,4},{7,5},{8,10},{9,11},{10,... | collective-permute-start | bytes 1966088 | tf_op jit(solution)/shard_map/ppermute | solution.py:30
  199.9 10.5 %collective-permute-start.22 = (bf16[2,320,1024]{2,1,0:T(8,128)(2,1)}, bf16[2,320,1024]{2,1,0:T(8,128)(2,1)S(1)}, u32[]{:S(2)}, u32[]{:S(2)}) collective-permute-start(bf16[2,320,1024]{2,1,0:T(8,128)(2,1)} %get-tuple-element.86), channel_id=1, source_target_pairs={{0,1},{1,0},{2,3},{3,2},{4,5},{5,4},{6,7},{7,6},{8,9},{9,8},{10,11... | collective-permute-start | bytes 3932168 | tf_op jit(solution)/shard_map/ppermute | solution.py:30
  203.7 2.9 collective-permute-start.24
  204.1 7.6 %collective-permute-start.25 = (bf16[320,256]{1,0:T(8,128)(2,1)}, bf16[320,256]{1,0:T(8,128)(2,1)}, u32[]{:S(2)}, u32[]{:S(2)}) collective-permute-start(bf16[320,256]{1,0:T(8,128)(2,1)} %get-tuple-element.96), channel_id=1, source_target_pairs={{0,2},{1,3},{2,0},{3,1},{4,6},{5,7},{6,4},{7,5},{8,10},{9,11},{10,... | collective-permute-start | bytes 491528 | tf_op jit(solution)/shard_map/ppermute | solution.py:30
  205.0 6.7 %collective-permute-start.26 = (bf16[320,256]{1,0:T(8,128)(2,1)S(1)}, bf16[320,256]{1,0:T(8,128)(2,1)}, u32[]{:S(2)}, u32[]{:S(2)}) collective-permute-start(bf16[320,256]{1,0:T(8,128)(2,1)S(1)} %copy-done.36), channel_id=1, source_target_pairs={{0,1},{1,0},{2,3},{3,2},{4,5},{5,4},{6,7},{7,6},{8,9},{9,8},{10,11... | collective-permute-start | bytes 491528 | tf_op jit(solution)/shard_map/ppermute | solution.py:30
  205.0 8.2 %collective-permute-start.27 = (bf16[320,256]{1,0:T(8,128)(2,1)S(1)}, bf16[320,256]{1,0:T(8,128)(2,1)}, u32[]{:S(2)}, u32[]{:S(2)}) collective-permute-start(bf16[320,256]{1,0:T(8,128)(2,1)S(1)} %copy-done.35), channel_id=1, source_target_pairs={{0,3},{1,2},{2,1},{3,0},{4,7},{5,6},{6,5},{7,4},{8,11},{9,10},{10,... | collective-permute-start | bytes 491528 | tf_op jit(solution)/shard_map/ppermute | solution.py:30
  210.5 16.5 %copy-start.10 = (bf16[2,320,1024]{2,1,0:T(8,128)(2,1)}, bf16[2,320,1024]{2,1,0:T(8,128)(2,1)S(1)}, u32[]{:S(2)}) copy-start(bf16[2,320,1024]{2,1,0:T(8,128)(2,1)S(1)} %collective-permute-done.22) | copy-start | bytes 3932164
  227.0 12.1 %collective-permute-start.28 = (bf16[2,320,1024]{2,1,0:T(8,128)(2,1)}, bf16[2,320,1024]{2,1,0:T(8,128)(2,1)}, u32[]{:S(2)}, u32[]{:S(2)}) collective-permute-start(bf16[2,320,1024]{2,1,0:T(8,128)(2,1)} %bitcast.110), channel_id=1, source_target_pairs={{0,1},{1,0},{2,3},{3,2},{4,5},{5,4},{6,7},{7,6},{8,9},{9,8},{10,11... | collective-permute-start | bytes 3932168 | tf_op jit(solution)/shard_map/ppermute | solution.py:30
  228.5 15.6 %collective-permute-start.34 = (bf16[4,128,512]{2,1,0:T(8,128)(2,1)}, bf16[4,128,512]{2,1,0:T(8,128)(2,1)}, u32[]{:S(2)}, u32[]{:S(2)}) collective-permute-start(bf16[4,128,512]{2,1,0:T(8,128)(2,1)} %get-tuple-element.94), channel_id=1, source_target_pairs={{0,4},{4,0},{8,12},{12,8},{16,20},{20,16},{24,28},{28,24},{1,5},{5... | collective-permute-start | bytes 1572872 | tf_op jit(solution)/shard_map/ppermute | solution.py:66
  230.0 20.0 %collective-permute-start.23 = (bf16[320,1024]{1,0:T(8,128)(2,1)}, bf16[320,1024]{1,0:T(8,128)(2,1)}, u32[]{:S(2)}, u32[]{:S(2)}) collective-permute-start(bf16[320,1024]{1,0:T(8,128)(2,1)} %fusion.9), channel_id=1, source_target_pairs={{0,2},{1,3},{2,0},{3,1},{4,6},{5,7},{6,4},{7,5},{8,10},{9,11},{10,... | collective-permute-start | bytes 1966088 | tf_op jit(solution)/shard_map/ppermute | solution.py:30
  237.8 30.2 %collective-permute-start.30 = (bf16[4,128,896]{2,1,0:T(8,128)(2,1)}, bf16[4,128,896]{2,1,0:T(8,128)(2,1)S(1)}, u32[]{:S(2)}, u32[]{:S(2)}) collective-permute-start(bf16[4,128,896]{2,1,0:T(8,128)(2,1)} %get-tuple-element.108), channel_id=1, source_target_pairs={{0,4},{4,0},{8,12},{12,8},{16,20},{20,16},{24,28},{28,24},{1,5},{5... | collective-permute-start | bytes 2752520 | tf_op jit(solution)/shard_map/ppermute | solution.py:66
  241.3 30.0 %collective-permute-start.29 = (bf16[320,1024]{1,0:T(8,128)(2,1)}, bf16[320,1024]{1,0:T(8,128)(2,1)}, u32[]{:S(2)}, u32[]{:S(2)}) collective-permute-start(bf16[320,1024]{1,0:T(8,128)(2,1)} %fusion.2), channel_id=1, source_target_pairs={{0,2},{1,3},{2,0},{3,1},{4,6},{5,7},{6,4},{7,5},{8,10},{9,11},{10,... | collective-permute-start | bytes 1966088 | tf_op jit(solution)/shard_map/ppermute | solution.py:30
  246.1 31.0 %collective-permute-start.35 = (bf16[1,128,512]{2,1,0:T(8,128)(2,1)}, bf16[1,128,512]{2,1,0:T(8,128)(2,1)S(1)}, u32[]{:S(2)}, u32[]{:S(2)}) collective-permute-start(bf16[1,128,512]{2,1,0:T(8,128)(2,1)} %get-tuple-element.115), channel_id=1, source_target_pairs={{0,8},{4,12},{8,16},{12,20},{16,24},{20,28},{24,0},{28,4},{1,9},{5... | collective-permute-start | bytes 393224 | tf_op jit(solution)/shard_map/ppermute | solution.py:66
  246.1 33.7 %collective-permute-start.36 = (bf16[1,128,512]{2,1,0:T(8,128)(2,1)}, bf16[1,128,512]{2,1,0:T(8,128)(2,1)}, u32[]{:S(2)}, u32[]{:S(2)}) collective-permute-start(bf16[1,128,512]{2,1,0:T(8,128)(2,1)} %get-tuple-element.116), channel_id=1, source_target_pairs={{0,24},{4,28},{8,0},{12,4},{16,8},{20,12},{24,16},{28,20},{1,25},{... | collective-permute-start | bytes 393224 | tf_op jit(solution)/shard_map/ppermute | solution.py:66
  250.0 29.8 %collective-permute-start.37 = (bf16[1,128,512]{2,1,0:T(8,128)(2,1)}, bf16[1,128,512]{2,1,0:T(8,128)(2,1)}, u32[]{:S(2)}, u32[]{:S(2)}) collective-permute-start(bf16[1,128,512]{2,1,0:T(8,128)(2,1)} %get-tuple-element.117), channel_id=1, source_target_pairs={{0,16},{4,20},{8,24},{12,28},{16,0},{20,4},{24,8},{28,12},{1,17},{... | collective-permute-start | bytes 393224 | tf_op jit(solution)/shard_map/ppermute | solution.py:66
  271.3 10.6 %collective-permute-start.31 = (bf16[1,128,896]{2,1,0:T(8,128)(2,1)}, bf16[1,128,896]{2,1,0:T(8,128)(2,1)S(1)}, u32[]{:S(2)}, u32[]{:S(2)}) collective-permute-start(bf16[1,128,896]{2,1,0:T(8,128)(2,1)} %get-tuple-element.110), channel_id=1, source_target_pairs={{0,8},{4,12},{8,16},{12,20},{16,24},{20,28},{24,0},{28,4},{1,9},{5... | collective-permute-start | bytes 688136 | tf_op jit(solution)/shard_map/ppermute | solution.py:66
  271.3 12.9 %collective-permute-start.32 = (bf16[1,128,896]{2,1,0:T(8,128)(2,1)}, bf16[1,128,896]{2,1,0:T(8,128)(2,1)S(1)}, u32[]{:S(2)}, u32[]{:S(2)}) collective-permute-start(bf16[1,128,896]{2,1,0:T(8,128)(2,1)} %get-tuple-element.111), channel_id=1, source_target_pairs={{0,24},{4,28},{8,0},{12,4},{16,8},{20,12},{24,16},{28,20},{1,25},{... | collective-permute-start | bytes 688136 | tf_op jit(solution)/shard_map/ppermute | solution.py:66
  277.8 15.5 %collective-permute-start.33 = (bf16[1,128,896]{2,1,0:T(8,128)(2,1)S(1)}, bf16[1,128,896]{2,1,0:T(8,128)(2,1)S(1)}, u32[]{:S(2)}, u32[]{:S(2)}) collective-permute-start(bf16[1,128,896]{2,1,0:T(8,128)(2,1)S(1)} %copy-done.34), channel_id=1, source_target_pairs={{0,16},{4,20},{8,24},{12,28},{16,0},{20,4},{24,8},{28,12},{1,17},{... | collective-permute-start | bytes 688136 | tf_op jit(solution)/shard_map/ppermute | solution.py:66
  296.6 13.4 %all-to-all-start.1 = ((bf16[4,32,2432]{2,1,0:T(8,128)(2,1)}), bf16[4,32,2432]{2,1,0:T(8,128)(2,1)S(1)}, u32[]{:S(2)}, u32[]{:S(2)}) async-start(bf16[4,32,2432]{2,1,0:T(8,128)(2,1)} %bitcast.97), calls=%async_computation.2 | async-start | bytes 1245184 | tf_op jit(solution)/shard_map/all_to_all | solution.py:930
  (31 other events, 146.9 us)
Sparse Core Ops, SparseCore 0:
  10.1 72.4 all-gather.2
  85.3 48.3 all-gather.4
  172.8 100.2 reduce-scatter.1

commit v4 on v3

--- a/solution.py
+++ b/solution.py
@@ -110,12 +110,11 @@
     )(digit, *[part.reshape(outer, radix, rows, cols) for part in parts])
 
 
-def scatter_near(keep, send, size, place):
+def scatter_near(parts, size, place):
     digits = digits_of(size)
-    parts = [keep, shift(send, size, *digits[0], 1)]
     stride, radix = digits[1]
     digit = place // stride % radix
-    outer = keep.shape[0] // radix
+    outer = parts[0].shape[0] // radix
     return split_sum(parts, outer, radix, jnp.asarray(digit, jnp.int32).reshape(1))
 
 
@@ -240,34 +239,46 @@
     )(*parts)
 
 
-def unpack_kernel(ref, qkv, out, up, vectors):
+def unpack_up_kernel(ref, up):
+    block = ref.shape[1] * SEQ
+    for s in range(SEQ):
+        for part in range(ref.shape[2] // block):
+            at = (part * SEQ + s) * block
+            up[:, at : at + block] = ref[s, :, part * block : (part + 1) * block].astype(F32)
+
+
+def unpack_up(came):
+    return pl.pallas_call(
+        unpack_up_kernel,
+        in_specs=[VMEM],
+        out_specs=VMEM,
+        out_shape=jax.ShapeDtypeStruct((came.shape[1], SEQ * came.shape[2]), F32),
+        compiler_params=params(),
+        name="unpack_up",
+    )(came)
+
+
+def unpack_kernel(ref, qkv, out, vectors):
     width = qkv.shape[1] // 3 // SEQ
     half = out.shape[1] // 2
-    units = up.shape[1] // SEQ
     low = 3 * width + LANES
-    block = ref.shape[1] * SEQ
     for s in range(SEQ):
         for part in range(3):
             at = (part * SEQ + s) * width
             qkv[:, at : at + width] = ref[s, :, part * width : (part + 1) * width].astype(F32)
-        for part in range(units // block):
-            at = (part * SEQ + s) * block
-            start = low + half + part * block
-            up[:, at : at + block] = ref[s, :, start : start + block].astype(F32)
     wide = lambda s, start, cols: ref[s, :, start : start + cols].astype(F32)
     vectors[...] = functools.reduce(jnp.add, [wide(s, 3 * width, LANES) for s in range(SEQ)])
     for core in range(2):
         out[:, core * half : (core + 1) * half] = wide(core, low, half) + wide(core + 2, low, half)
 
 
-def unpack(came, model, units):
+def unpack(came, model):
     depth = came.shape[1]
-    cols = (3 * model, model, SEQ * units, LANES)
     return pl.pallas_call(
         unpack_kernel,
         in_specs=[VMEM],
-        out_specs=[VMEM] * 4,
-        out_shape=[jax.ShapeDtypeStruct((depth, n), F32) for n in cols],
+        out_specs=[VMEM] * 3,
+        out_shape=[jax.ShapeDtypeStruct((depth, n), F32) for n in (3 * model, model, LANES)],
         compiler_params=params(),
         name="unpack",
     )(came)
@@ -306,26 +317,7 @@
     return copies
 
 
-def weight_grad_kernel(lefts, rights, left_at, right_at, info, *refs):
-    more = len(refs) - lefts - rights - 8
-    left_refs, right_refs = refs[:lefts], refs[lefts : lefts + rights]
-    extra = refs[lefts + rights : lefts + rights + more]
-    keep, send, left, right, out, left_sem, right_sem, out_sem = refs[lefts + rights + more :]
-    copies = row_copies(left_at(info, left_refs), left, left_sem) + row_copies(
-        right_at(info, right_refs), right, right_sem
-    )
-    for copy in copies:
-        copy.start()
-    total, cols = left.shape[1], right.shape[1]
-    if more:
-        sums = functools.reduce(jnp.add, [ref[...] for ref in extra])
-        sums = jnp.concatenate([sums, jnp.zeros((LANES - sums.shape[0], total), F32)], axis=0)
-        out[:, cols:] = sums.T.astype(BF)
-    for copy in copies:
-        copy.wait()
-    tile = min(256, total)
-    for low in range(0, total, tile):
-        out[low : low + tile, :cols] = rows_dot(left[:, low : low + tile], right[...]).astype(BF)
+def digit_moves(info, out, keep, send, sem):
     groups, block = keep.shape[:2]
     low_digit = info[0] % 2
     moves = []
@@ -333,88 +325,36 @@
         for which, (ref, side) in enumerate(((keep, low_digit), (send, 1 - low_digit))):
             start = pl.multiple_of((2 * at + side) * block, block)
             moves.append(
-                pltpu.make_async_copy(out.at[pl.ds(start, block), :], ref.at[at], out_sem.at[2 * at + which])
+                pltpu.make_async_copy(out.at[pl.ds(start, block), :], ref.at[at], sem.at[2 * at + which])
             )
-    for move in moves:
-        move.start()
-    for move in moves:
-        move.wait()
-
-
-def plain_rows(info, refs):
-    return refs
-
-
-def weight_grad(info, fsdp, lefts, rights, left_at=plain_rows, right_at=plain_rows, sums=(), shape=None):
-    rows, total, cols = shape
-    wide = cols + (LANES if sums else 0)
-    out = jax.ShapeDtypeStruct((fsdp // 2, total // fsdp, wide), BF)
-    return pl.pallas_call(
-        functools.partial(weight_grad_kernel, len(lefts), len(rights), left_at, right_at),
-        in_specs=[SMEM] + [ANY] * (len(lefts) + len(rights)) + [VMEM] * len(sums),
-        out_specs=[ANY] * 2,
-        out_shape=[out] * 2,
-        scratch_shapes=[
-            pltpu.VMEM((rows, total), BF),
-            pltpu.VMEM((rows, cols), BF),
-            pltpu.VMEM((total, wide), BF),
-            pltpu.SemaphoreType.DMA((16,)),
-            pltpu.SemaphoreType.DMA((16,)),
-            pltpu.SemaphoreType.DMA((fsdp,)),
-        ],
-        compiler_params=params(),
-        cost_estimate=estimate(2 * rows * total * cols, 2 * rows * (total + cols) + 2 * total * cols),
-        name="weight_grad",
-    )(info, *lefts, *rights, *sums)
-
-
-def core_grad_kernel(count, core_at, info, *refs):
-    lefts, rights = refs[:count], refs[count : 2 * count]
-    here, there = refs[2 * count :]
-    total, half = here.shape
-    core = info[core_at]
+    return moves
+
+
+def core_grad_kernel(core_at, info, left, right, here, there, product):
+    groups, block, half = here.shape[1:]
+    core, low_digit = info[core_at], info[0] % 2
     for ref, side in ((here, core), (there, 1 - core)):
         cols = pl.ds(pl.multiple_of(side * half, half), half)
-        ref[...] = functools.reduce(
-            jnp.add, [rows_dot(left[...], right[:, cols]) for left, right in zip(lefts, rights)]
-        ).astype(BF)
-
-
-def core_grad(info, fsdp, lefts, rights):
-    model = lefts[0].shape[1]
-    half = jax.ShapeDtypeStruct((model, model // 2), BF)
-    rows = lefts[0].shape[0] * len(lefts)
-    return pl.pallas_call(
-        functools.partial(core_grad_kernel, len(lefts), fsdp + 1),
-        in_specs=[SMEM] + [VMEM] * (2 * len(lefts)),
+        product[...] = rows_dot(left[...], right[:, cols]).astype(BF)
+        for at in range(groups):
+            for which, digit in enumerate((low_digit, 1 - low_digit)):
+                start = pl.multiple_of((2 * at + digit) * block, block)
+                ref[which, at] = product[pl.ds(start, block), :]
+
+
+def core_grad(info, fsdp, left, right):
+    rows, model = left.shape
+    half = jax.ShapeDtypeStruct((2, fsdp // 2, model // fsdp, model // 2), BF)
+    return pl.pallas_call(
+        functools.partial(core_grad_kernel, fsdp + 1),
+        in_specs=[SMEM] + [VMEM] * 2,
         out_specs=[VMEM] * 2,
         out_shape=[half] * 2,
+        scratch_shapes=[pltpu.VMEM((model, model // 2), BF)],
         compiler_params=params(),
         cost_estimate=estimate(2 * rows * model * model, 4 * 2**20),
         name="core_grad",
-    )(info, *lefts, *rights)
-
-
-def core_split_kernel(info, here, came, keep, send):
-    groups, block = keep.shape[:2]
-    low_digit = info[0] % 2
-    for at in range(groups):
-        for ref, side in ((keep, low_digit), (send, 1 - low_digit)):
-            place = pl.ds(pl.multiple_of((2 * at + side) * block, block), block)
-            ref[at] = (here[place].astype(F32) + came[place].astype(F32)).astype(BF)
-
-
-def core_split(info, fsdp, here, came):
-    total, half = here.shape
-    out = jax.ShapeDtypeStruct((fsdp // 2, total // fsdp, half), BF)
-    return pl.pallas_call(
-        core_split_kernel,
-        in_specs=[SMEM] + [VMEM] * 2,
-        out_specs=[VMEM] * 2,
-        out_shape=[out] * 2,
-        compiler_params=params(),
-        name="core_split",
-    )(info, here, came)
+    )(info, left, right)
 
 
 def attention_kernel(count, info, x0, x1, x2, x3, keep_ref, *refs):
@@ -430,13 +370,17 @@
     def _():
         for copy in copies:
             copy.start()
+
+    values = jnp.concatenate([x[0].astype(F32) for x in (x0, x1, x2, x3)], axis=0)
+    hat, _ = norm_parts(values)
+    hat_ref[...] = hat.astype(BF).reshape(hat_ref.shape)
+
+    @pl.when(pl.program_id(0) == 0)
+    def _():
         for copy in copies:
             copy.wait()
         vec[...] = weight[:, triple:].astype(F32).T[: vec.shape[0]]
 
-    values = jnp.concatenate([x[0].astype(F32) for x in (x0, x1, x2, x3)], axis=0)
-    hat, _ = norm_parts(values)
-    hat_ref[...] = hat.astype(BF).reshape(hat_ref.shape)
     normed = (hat * vec[0:1, :] + vec[1:2, :]).astype(BF)
     n1_ref[...] = normed.reshape(n1_ref.shape)
     place = pl.multiple_of(info[count] * width, width)
@@ -689,20 +633,26 @@
 
 
 def attention_back_kernel(count, info, joined_ref, probs_ref, g0, g1, g2, g3, hat_ref, *refs):
-    pieces = refs[:count]
-    out_ref, chip_ref, sib_ref, sums, weight, sem = refs[count:]
+    pieces, n1_ref = refs[:count], refs[count]
+    more = len(refs) - count - 13
+    extra = refs[count + 1 : count + 1 + more]
+    keep, send, chip_ref, sib_ref = refs[count + 1 + more : count + 5 + more]
+    sums, weight, sem, n1_in, n1_sem, grads, out, out_sem = refs[count + 5 + more :]
+    image = pl.program_id(0)
     tokens = joined_ref.shape[2]
     rows = SEQ * tokens
     triple = joined_ref.shape[3]
     width = triple // 3
     model = weight.shape[0]
     copies = piece_copies(info, pieces, 0, weight, sem)
+    n1_copy = pltpu.make_async_copy(n1_ref, n1_in, n1_sem)
 
     @pl.when(pl.program_id(0) == 0)
     def _():
         for copy in copies:
             copy.start()
-        sums[...] = jnp.zeros(sums.shape, F32)
+        n1_copy.start()
+        sums[...] = functools.reduce(jnp.add, [ref[...] for ref in extra])
 
     joined = joined_ref[...].reshape(rows, triple)
     grad = jnp.concatenate([g0[...], g1[...], g2[...], g3[...]], axis=0)
@@ -724,7 +674,7 @@
     grad_joined = jnp.concatenate(
         [jnp.concatenate(queries, axis=0).T.astype(BF)] + keys + values, axis=1
     )
-    out_ref[...] = grad_joined.reshape(out_ref.shape)
+    grads[:, image] = grad_joined.reshape(SEQ, tokens, triple)
     wide = grad_joined.astype(F32)
     place = pl.multiple_of(info[count] * width, width)
     sums[2:3, pl.ds(place, width)] += column_sums(wide[:, :width])
@@ -744,8 +694,23 @@
     chip_ref[...] = low[:half].reshape(chip_ref.shape)
     sib_ref[...] = low[half:].reshape(sib_ref.shape)
 
-
-def attention_back(info, joined, probs, grads, hat, pieces):
+    @pl.when(image == pl.num_programs(0) - 1)
+    def _():
+        n1_copy.wait()
+        right = grads[...].reshape(n1_in.shape[0], triple)
+        total = jnp.concatenate([sums[...], jnp.zeros((LANES - sums.shape[0], model), F32)], axis=0)
+        out[:, triple:] = total.T.astype(BF)
+        tile = min(256, model)
+        for at in range(0, model, tile):
+            out[at : at + tile, :triple] = rows_dot(n1_in[:, at : at + tile], right).astype(BF)
+        moves = digit_moves(info, out, keep, send, out_sem)
+        for move in moves:
+            move.start()
+        for move in moves:
+            move.wait()
+
+
+def attention_back(info, joined, probs, grads, hat, pieces, n1, extra):
     count = len(pieces)
     _, images, tokens, triple = joined.shape
     model = hat.shape[3]
@@ -754,6 +719,7 @@
     heads = width // HEAD_DIM
     pair = jax.ShapeDtypeStruct((2, images, tokens, model), BF)
     group_block = lambda n, cols: pl.BlockSpec((n, 1, tokens, cols), lambda i: (0, i, 0, 0))
+    part = jax.ShapeDtypeStruct((count // 2, model // count, triple + LANES), BF)
     return pl.pallas_call(
         functools.partial(attention_back_kernel, count),
         grid=(images,),
@@ -764,26 +730,26 @@
         ]
         + [pl.BlockSpec((tokens, width), lambda i: (i, 0))] * SEQ
         + [group_block(SEQ, model)]
-        + [ANY] * count,
-        out_specs=[
-            group_block(SEQ, triple),
-            group_block(2, model),
-            group_block(2, model),
-            pl.BlockSpec((16, model), lambda i: (0, 0)),
-        ],
-        out_shape=[
-            jax.ShapeDtypeStruct(joined.shape, BF),
-            pair,
-            pair,
-            jax.ShapeDtypeStruct((16, model), F32),
-        ],
-        scratch_shapes=[pltpu.VMEM((model, triple), BF), pltpu.SemaphoreType.DMA((count,))],
+        + [ANY] * (count + 1)
+        + [pl.BlockSpec((16, model), lambda i: (0, 0))] * len(extra),
+        out_specs=[ANY, ANY, group_block(2, model), group_block(2, model)],
+        out_shape=[part, part, pair, pair],
+        scratch_shapes=[
+            pltpu.VMEM((16, model), F32),
+            pltpu.VMEM((model, triple), BF),
+            pltpu.SemaphoreType.DMA((count,)),
+            pltpu.VMEM((images * rows, model), BF),
+            pltpu.SemaphoreType.DMA,
+            pltpu.VMEM((SEQ, images, tokens, triple), BF),
+            pltpu.VMEM((model, triple + LANES), BF),
+            pltpu.SemaphoreType.DMA((count,)),
+        ],
         compiler_params=params(),
         cost_estimate=estimate(
-            2 * images * rows * (model * triple + 8 * width * rows), 8 * 2**20
+            2 * images * rows * (2 * model * triple + 8 * width * rows), 12 * 2**20
         ),
         name="attention_back",
-    )(info, joined, probs, *grads, hat, *pieces)
+    )(info, joined, probs, *grads, hat, *pieces, n1, *extra)
 
 
 def on_device(
@@ -893,27 +859,31 @@
     )
     sums.append(part)
     grads_in = seq_exchange(grads_out)
-    out_here, out_there = core_grad(info, fsdp, [attended], [branch])
+    out_here, out_there = core_grad(info, fsdp, attended, branch)
     down_sums = []
     for chip, sib in down_parts:
         came, far = seq_scatter(chip, after(sib, branch))
         down_sums.append((chip[0], came[0], far))
-    out_blocks = core_split(info, fsdp, out_here, hop(out_there, 1))
-    grads_in[0] = after(grads_in[0], *[far for _, _, far in down_sums], out_blocks[1])
-
-    grad_joined, chip, sib, part = attention_back(info, joined, probs, grads_in, hat_one, first_pieces)
-    sums.append(part)
-    qkv_blocks = weight_grad(
+    out_sib = hop(out_there, 1)
+    out_send = (out_here[1].astype(F32) + out_sib[1].astype(F32)).astype(BF)
+    grads_in[0] = after(grads_in[0], *[far for _, _, far in down_sums], out_send)
+
+    *qkv_blocks, chip, sib = attention_back(
         info,
-        fsdp,
-        [n1.reshape(group_rows, model)],
-        [grad_joined.reshape(group_rows, triple)],
-        sums=sums,
-        shape=(group_rows, model, triple),
-    )
+        joined,
+        probs,
+        grads_in,
+        hat_one,
+        first_pieces,
+        n1.reshape(group_rows, model),
+        sums,
+    )
+    out_came = shift(out_send, fsdp, *digits_of(fsdp)[0], 1)
+    sib, qkv_blocks[1] = after(sib, out_came), after(qkv_blocks[1], out_came)
+    out_parts = scatter_far(scatter_near([out_here[0], out_sib[0], out_came], fsdp, at_f), fsdp, at_f)
     chip = chip.reshape(2, micros * rows, model)
     came, far = seq_scatter(chip, sib.reshape(2, micros * rows, model))
-    grad_one = chip[0].astype(F32) + came[0].astype(F32) + hop(far, 2).astype(F32)
+    grad_one = chip[0].astype(F32) + came[0].astype(F32) + hop(after(far, *out_parts[1:]), 2).astype(F32)
 
     [(a, b, c)] = down_sums
     total = a.astype(F32) + b.astype(F32) + hop(c, 2).astype(F32)
@@ -922,13 +892,15 @@
     input_grad = grad_middle + norm_back(grad_one, hat, scale, vec[0:1])
     input_grad = input_grad.astype(BF).reshape(micros, images, tokens, model)
 
-    out_parts = scatter_far(scatter_near(*out_blocks, fsdp, at_f), fsdp, at_f)
-    qkv_parts = scatter_far(scatter_near(*qkv_blocks, fsdp, at_f), fsdp, at_f)
-
-    last, own_vectors = collect(qkv_parts, out_parts, [up_grad])
+    qkv_came = shift(qkv_blocks[1], fsdp, *digits_of(fsdp)[0], 1)
+    qkv_parts = scatter_far(scatter_near([qkv_blocks[0], qkv_came], fsdp, at_f), fsdp, at_f)
+
+    over_seq = lambda part: lax.all_to_all(part.reshape(SEQ, depth, -1), "seq", 0, 0, tiled=True)
+    up_weight_grad = unpack_up(over_seq(up_grad))
+    qkv_parts[0] = after(qkv_parts[0], up_weight_grad)
+    last, own_vectors = collect(qkv_parts, out_parts)
     up_bias_grad = own_vectors[:, VECTORS]
-    last = lax.all_to_all(last.reshape(SEQ, depth, -1), "seq", 0, 0, tiled=True)
-    qkv_weight_grad, out_weight_grad, up_weight_grad, vector_grads = unpack(last, model, units)
+    qkv_weight_grad, out_weight_grad, vector_grads = unpack(over_seq(last), model)
     vector_grads = vector_grads[:, :VECTORS].T
 
     return (

time: 322 us -> 321 us (level); the launches traced: 321 us -> 316 us
  waiting for transfers between devices: 136 us -> 128 us
  starting transfers between devices: 36.1 us -> 40.8 us
  Pallas kernels: 91.9 us -> 88 us
    ppermute x15, waiting for transfers between devices: 81.9 us -> 68.8 us  [shift(): return lax.ppermute(array, 'fsdp', pairs)]
    pallas_call x4 -> x3, Pallas kernels: 15.8 us -> 7.79 us  [the longest x1 4.2 us: core_grad(): pl.pallas_call(functools.partial(core_grad_kernel, fsdp + 1), in_specs=[S...]
    pallas_call x1, Pallas kernels: 13.7 us -> 17.4 us  [attention_back(): pl.pallas_call(functools.partial(attention_back_kernel, count), grid=(ima...]
    all_to_all x1 -> x2, starting transfers between devices: 3.48 us -> 6.86 us  [on_device(): lax.all_to_all(part.reshape(SEQ, depth, -1), 'seq', 0, 0, tiled=True)]
    all_to_all x1 -> x2, waiting for transfers between devices: 6.51 us -> 9.7 us  [on_device(): lax.all_to_all(part.reshape(SEQ, depth, -1), 'seq', 0, 0, tiled=True)]
    unnamed x74 -> x88, local copies, waits for them, and re-layouts: 7.66 us -> 6.37 us
  transfers between devices with their start and end apart: 42 -> 43, of which waited for: 18 -> 18; matrix products, arithmetic and copies ran while one was open for 6% -> 7% of each run, Pallas kernels for 20% -> 19%
where the time goes in v4:
time: 321 us; the launch traced here: 316 us
  waiting for transfers between devices  128 us (40%)
  Pallas kernels  88 us (27%)
  starting transfers between devices  40.8 us (13%)
  local copies, waits for them, and re-layouts  15.6 us (5%)
  other arithmetic  15.1 us (5%)
  between operations  14.5 us (5%)
  blocking collectives  14.1 us (4%)
    ppermute x15, waiting for transfers between devices, shift(): return lax.ppermute(array, 'fsdp', pairs)  68.8 us
    ppermute x23, waiting for transfers between devices, hop(): return lax.ppermute(array, 'seq', [(i, i ^ mask) for i in range(SEQ)])  48.8 us
    pallas_call x1, Pallas kernels, feed(): pl.pallas_call(functools.partial(feed_kernel, micros), in_specs=[ANY] * (...  23.6 us
    ppermute x15, starting transfers between devices, shift(): return lax.ppermute(array, 'fsdp', pairs)  19.9 us
    pallas_call x1, Pallas kernels, attention_back(): pl.pallas_call(functools.partial(attention_back_kernel, count), grid=(ima...  17.4 us
    pallas_call x1, Pallas kernels, attention(): pl.pallas_call(functools.partial(attention_kernel, count), grid=(images,)...  15.8 us
    all_to_all x1, blocking collectives, on_device(): lax.all_to_all(to_send, 'seq', 0, 0, tiled=True).reshape(block, -1)  14.1 us
    ppermute x23, starting transfers between devices, hop(): return lax.ppermute(array, 'seq', [(i, i ^ mask) for i in range(SEQ)])  13.9 us
  transfers between devices with their start and end apart: 43, of which 18 were waited for; matrix products, arithmetic and copies ran while one was open for 7% of the time, Pallas kernels for 19%

profile of v4, /device:TPU:0, one launch (start us, length us, event | category | flops | bytes accessed | tf_op | source)
XLA Modules:
  0.0 316.1 jit_solution(12116495604799930681)
XLA Ops:
  9.5 2.0 pack.1
  11.5 14.1 %all_to_all.15 = bf16[4,32,2432]{2,1,0:T(8,128)(2,1)S(1)} all-to-all(bf16[4,32,2432]{2,1,0:T(8,128)(2,1)} %pack.1), channel_id=1, replica_groups=mesh['fsdp'=8,'seq'=4] {'seq'}, dimensions={0} | all-to-all | bytes 1245184 | tf_op jit(solution)/shard_map/all_to_all | solution.py:807
  26.7 2.3 collective-permute-start.3
  29.0 2.1 collective-permute-start.4
  32.4 1.5 collective-permute-start.6
  33.9 8.7 %collective-permute-done.3.refs_1_ = bf16[128,1408]{1,0:T(8,128)(2,1)S(1)} collective-permute-done((bf16[128,1408]{1,0:T(8,128)(2,1)S(1)}, bf16[128,1408]{1,0:T(8,128)(2,1)S(1)}, u32[]{:S(2)}, u32[]{:S(2)}) %collective-permute-start.3) | collective-permute-done | bytes 360480 | tf_op jit(solution)/shard_map/ppermute | solution.py:66
  43.5 5.8 %collective-permute-done.4.refs_2_ = bf16[128,1408]{1,0:T(8,128)(2,1)S(1)} collective-permute-done((bf16[128,1408]{1,0:T(8,128)(2,1)S(1)}, bf16[128,1408]{1,0:T(8,128)(2,1)S(1)}, u32[]{:S(2)}, u32[]{:S(2)}) %collective-permute-start.4) | collective-permute-done | bytes 360480 | tf_op jit(solution)/shard_map/ppermute | solution.py:66
  49.3 1.3 collective-permute-start.8
  50.6 30.6 %collective-permute-done.5.refs_3_ = bf16[128,1408]{1,0:T(8,128)(2,1)S(1)} collective-permute-done((bf16[128,1408]{1,0:T(8,128)(2,1)S(1)}, bf16[128,1408]{1,0:T(8,128)(2,1)S(1)}, u32[]{:S(2)}, u32[]{:S(2)}) %collective-permute-start.5) | collective-permute-done | bytes 360480 | tf_op jit(solution)/shard_map/ppermute | solution.py:66
  84.2 7.4 %collective-permute-done.9.refs_7_ = bf16[128,1408]{1,0:T(8,128)(2,1)} collective-permute-done((bf16[128,1408]{1,0:T(8,128)(2,1)S(1)}, bf16[128,1408]{1,0:T(8,128)(2,1)}, u32[]{:S(2)}, u32[]{:S(2)}) %collective-permute-start.9) | collective-permute-done | bytes 360480 | tf_op jit(solution)/shard_map/ppermute | solution.py:66
  91.6 3.1 placed.1.mine.refs_6_
  97.1 15.8 %attention.1 = (bf16[4,4,80,1024]{3,2,1,0:T(8,128)(2,1)}, bf16[4,4,80,1024]{3,2,1,0:T(8,128)(2,1)}, bf16[4,4,80,768]{3,2,1,0:T(8,128)(2,1)}, bf16[320,256]{1,0:T...) custom-call(s32[14]{0:T(128)} %stack.90.info, ...), custom_call_target="tpu_custom_call" | custom-call | flops 2852126720 | bytes 16777216 | tf_op jit(solution)/shard_map/attention/pallas_call | solution.py:422
  116.0 4.2 %collective-permute-done.13.e3 = bf16[320,256]{1,0:T(8,128)(2,1)S(1)} collective-permute-done((bf16[320,256]{1,0:T(8,128)(2,1)}, bf16[320,256]{1,0:T(8,128)(2,1)S(1)}, u32[]{:S(2)}, u32[]{:S(2)}) %collective-permute-start.13) | collective-permute-done | bytes 163872 | tf_op jit(solution)/shard_map/ppermute | solution.py:30
  120.2 3.8 %collective-permute-done.11.e1 = bf16[320,256]{1,0:T(8,128)(2,1)S(1)} collective-permute-done((bf16[320,256]{1,0:T(8,128)(2,1)}, bf16[320,256]{1,0:T(8,128)(2,1)S(1)}, u32[]{:S(2)}, u32[]{:S(2)}) %collective-permute-start.11) | collective-permute-done | bytes 163872 | tf_op jit(solution)/shard_map/ppermute | solution.py:30
  125.1 5.2 %middle.1 = (bf16[320,1024]{1,0:T(8,128)(2,1)}, f32[320,1024]{1,0:T(8,128)}, bf16[320,1024]{1,0:T(8,128)(2,1)}) custom-call(s32[14]{0:T(128)} %stack.90.info, bf16[320,256]{1,0:T(8,128)(2,1)} %get-tuple-element.69.e0, bf16[320,256]{1,0:T(8,128)(2,1)} %copy-done.25, bf16[320,256]{1,0:T(8,128)(2,1)} %copy-done.24, bf16[320,256]{1,0:T(8,128)(2,1)} %copy-done.23, ...), custom_call_target="tpu_custom_call" | custom-call | flops 671088640 | bytes 4194304 | tf_op jit(solution)/shard_map/middle/pallas_call | solution.py:482
  131.9 15.2 %collective-permute-done.15.refs_1_ = bf16[320,1024]{1,0:T(8,128)(2,1)S(1)} collective-permute-done((bf16[320,1024]{1,0:T(8,128)(2,1)}, bf16[320,1024]{1,0:T(8,128)(2,1)S(1)}, u32[]{:S(2)}, u32[]{:S(2)}) %collective-permute-start.15) | collective-permute-done | bytes 655392 | tf_op jit(solution)/shard_map/ppermute | solution.py:30
  147.1 2.2 collective-permute-done.17.refs_3_
  149.3 23.6 %feed.1 = (bf16[2,320,1024]{2,1,0:T(8,128)(2,1)}, bf16[2,320,1024]{2,1,0:T(8,128)(2,1)}, bf16[2,320,1024]{2,1,0:T(8,128)(2,1)}, bf16[2,320,1024]{2,1,0:T(8,128)(...) custom-call(bf16[320,1024]{1,0:T(8,128)(2,1)} %get-tuple-element.79.refs_0_, bf16[320,1024]{1,0:T(8,128)(2,1)} %copy-done.35, ...), custom_call_target="tpu_custom_call" | custom-call | flops 16106127360 | bytes 25165824 | tf_op jit(solution)/shard_map/feed/pallas_call | solution.py:553
  173.2 3.1 collective-permute-done.20.refs_1_
  177.6 15.8 %collective-permute-done.21.refs_2_ = bf16[320,1024]{1,0:T(8,128)(2,1)S(1)} collective-permute-done((bf16[320,1024]{1,0:T(8,128)(2,1)S(1)}, bf16[320,1024]{1,0:T(8,128)(2,1)S(1)}, u32[]{:S(2)}, u32[]{:S(2)}) %collective-permute-start.21) | collective-permute-done | bytes 655392 | tf_op jit(solution)/shard_map/ppermute | solution.py:30
  194.3 6.0 %middle_back.1 = (f32[320,1024]{1,0:T(8,128)}, bf16[320,1024]{1,0:T(8,128)(2,1)}, bf16[320,256]{1,0:T(8,128)(2,1)}, bf16[320,256]{1,0:T(8,128)(2,1)}, bf16[320,2...) custom-call(s32[14]{0:T(128)} %stack.90.info, bf16[2,320,1024]{2,1,0:T(8,128)(2,1)} %get-tuple-element.82.refs_0_, ...), custom_call_target="tpu_custom_call" | custom-call | flops 671088640 | bytes 4194304 | tf_op jit(solution)/shard_map/middle_back/pallas_call | solution.py:614
  200.3 4.2 %core_grad.1 = (bf16[2,4,128,512]{3,2,1,0:T(8,128)(2,1)}, bf16[2,4,128,512]{3,2,1,0:T(8,128)(2,1)}) custom-call(s32[14]{0:T(128)} %stack.90.info, bf16[320,1024]{1,0:T(8,128)(2,1)} %get-tuple-element.90.left, bf16[320,1024]{1,0:T(8,128)(2,1)} %get-tuple-element.84.right), custom_call_target="tpu_custom_call" | custom-call | flops 671088640 | bytes 4194304 | tf_op jit(solution)/shard_map/core_grad/pallas_call | solution.py:348
  208.2 1.5 fusion.10
  209.7 1.5 collective-permute-start.28
  211.2 1.3 fusion.9
  212.5 1.4 collective-permute-done.27.g3
  214.5 17.4 %attention_back.1 = (bf16[4,128,896]{2,1,0:T(8,128)(2,1)}, bf16[4,128,896]{2,1,0:T(8,128)(2,1)}, bf16[2,4,80,1024]{3,2,1,0:T(8,128)(2,1)}, bf16[2,4,80,1024]{3,2,1,0:T(8,128)(2,1)}) custom-call(s32[14]{0:T(128)} %stack.90.info, bf16[4,4,80,768]{3,2,1,0:T(8,128)(2,1)} %get-tuple-element.87.joined_ref, bf16[4,4,320,320]{3,2,1,0:T(8,128)(2,1)} %get-tuple-element.88.probs_ref, ...), custom_call_target="tpu_custom_call" | custom-call | flops 5704253440 | bytes 12582912 | tf_op jit(solution)/shard_map/attention_back/pallas_call | solution.py:723
  237.2 2.3 split.2
  239.4 3.8 %collective-permute-start.31 = (bf16[1,128,512]{2,1,0:T(8,128)(2,1)}, bf16[1,128,512]{2,1,0:T(8,128)(2,1)S(1)}, u32[]{:S(2)}, u32[]{:S(2)}) collective-permute-start(bf16[1,128,512]{2,1,0:T(8,128)(2,1)} %get-tuple-element.105), channel_id=1, source_target_pairs={{0,24},{4,28},{8,0},{12,4},{16,8},{20,12},{24,16},{28,20},{1,25},{... | collective-permute-start | bytes 393224 | tf_op jit(solution)/shard_map/ppermute | solution.py:66
  243.3 2.2 fusion.2
  245.5 2.4 collective-permute-done.30.refs_5_
  247.8 1.4 collective-permute-done.31.refs_6_
  249.2 12.6 %collective-permute-done.32.refs_7_ = bf16[1,128,512]{2,1,0:T(8,128)(2,1)S(1)} collective-permute-done((bf16[1,128,512]{2,1,0:T(8,128)(2,1)}, bf16[1,128,512]{2,1,0:T(8,128)(2,1)S(1)}, u32[]{:S(2)}, u32[]{:S(2)}) %collective-permute-start.32) | collective-permute-done | bytes 131104 | tf_op jit(solution)/shard_map/ppermute | solution.py:66
  261.8 2.0 collective-permute-start.33
  264.8 2.8 fusion.7
  267.6 2.5 split.3
  270.1 3.8 %collective-permute-start.36 = (bf16[1,128,896]{2,1,0:T(8,128)(2,1)}, bf16[1,128,896]{2,1,0:T(8,128)(2,1)}, u32[]{:S(2)}, u32[]{:S(2)}) collective-permute-start(bf16[1,128,896]{2,1,0:T(8,128)(2,1)} %get-tuple-element.115), channel_id=1, source_target_pairs={{0,24},{4,28},{8,0},{12,4},{16,8},{20,12},{24,16},{28,20},{1,25},{... | collective-permute-start | bytes 688136 | tf_op jit(solution)/shard_map/ppermute | solution.py:66
  273.9 2.1 collective-permute-done.33
  276.0 1.4 fusion.4
  277.9 2.0 fusion.11
  279.8 3.4 %all-to-all-start.1 = ((bf16[4,32,1024]{2,1,0:T(8,128)(2,1)}), bf16[4,32,1024]{2,1,0:T(8,128)(2,1)S(1)}, u32[]{:S(2)}, u32[]{:S(2)}) async-start(bf16[4,32,1024]{2,1,0:T(8,128)(2,1)} %bitcast.47), calls=%async_computation.2 | async-start | bytes 524288 | tf_op jit(solution)/shard_map/all_to_all | solution.py:898
  283.3 6.0 %all-to-all-done.1.ref = bf16[4,32,1024]{2,1,0:T(8,128)(2,1)S(1)} async-done(((bf16[4,32,1024]{2,1,0:T(8,128)(2,1)}), bf16[4,32,1024]{2,1,0:T(8,128)(2,1)S(1)}, u32[]{:S(2)}, u32[]{:S(2)}) %all-to-all-start.1) | async-done | bytes 262176 | tf_op jit(solution)/shard_map/all_to_all | solution.py:898
  289.9 1.8 unpack_up.1
  292.4 2.3 collect.1
  294.8 3.5 %all-to-all-start.2 = ((bf16[4,32,1408]{2,1,0:T(8,128)(2,1)}), bf16[4,32,1408]{2,1,0:T(8,128)(2,1)S(1)}, u32[]{:S(2)}, u32[]{:S(2)}) async-start(bf16[4,32,1408]{2,1,0:T(8,128)(2,1)} %bitcast.96), calls=%async_computation.3 | async-start | bytes 720896 | tf_op jit(solution)/shard_map/all_to_all | solution.py:898
  298.2 2.6 add_convert_fusion
  301.6 3.7 %all-to-all-done.2.ref = bf16[4,32,1408]{2,1,0:T(8,128)(2,1)S(1)} async-done(((bf16[4,32,1408]{2,1,0:T(8,128)(2,1)}), bf16[4,32,1408]{2,1,0:T(8,128)(2,1)S(1)}, u32[]{:S(2)}, u32[]{:S(2)}) %all-to-all-start.2) | async-done | bytes 360480 | tf_op jit(solution)/shard_map/all_to_all | solution.py:898
  306.1 1.8 unpack.1
  (180 shorter events, 34.3 us)
Async XLA Ops:
  7.2 142.1 %all-gather.3.cloned.1.call-start = ((), (), s32[]{:S(2)}) async-start(), calls=%async_computation.4 | async-start | bytes 2359296 | tf_op jit(solution)/shard_map/all_gather | solution.py:820
  7.9 141.4 %all-gather.5.cloned.1.call-start = ((), (), s32[]{:S(2)}) async-start(), calls=%async_computation.5 | async-start | bytes 2359296 | tf_op jit(solution)/shard_map/all_gather | solution.py:821
  26.3 251.5 %reduce-scatter.2.cloned.1.call-start = ((), (), s32[]{:S(2)}) async-start(), calls=%async_computation.6 | async-start | bytes 4718592 | tf_op jit(solution)/shard_map/reduce_scatter | solution.py:851
  26.7 64.8 %copy-start.7 = (bf16[128,1408]{1,0:T(8,128)(2,1)}, bf16[128,1408]{1,0:T(8,128)(2,1)S(1)}, u32[]{:S(2)}) copy-start(bf16[128,1408]{1,0:T(8,128)(2,1)S(1)} %pad_maximum_fusion.refs_0_) | copy-start | bytes 1081348
  26.7 16.0 %collective-permute-start.3 = (bf16[128,1408]{1,0:T(8,128)(2,1)S(1)}, bf16[128,1408]{1,0:T(8,128)(2,1)S(1)}, u32[]{:S(2)}, u32[]{:S(2)}) collective-permute-start(bf16[128,1408]{1,0:T(8,128)(2,1)S(1)} %pad_maximum_fusion.refs_0_), channel_id=1, source_target_pairs={{0,8},{4,12},{8,16},{12,20},{16,24},{20,28},{24,0},{28,4},{1,9},{5... | collective-permute-start | bytes 1081352 | tf_op jit(solution)/shard_map/ppermute | solution.py:66
  29.0 20.3 %collective-permute-start.4 = (bf16[128,1408]{1,0:T(8,128)(2,1)S(1)}, bf16[128,1408]{1,0:T(8,128)(2,1)S(1)}, u32[]{:S(2)}, u32[]{:S(2)}) collective-permute-start(bf16[128,1408]{1,0:T(8,128)(2,1)S(1)} %pad_maximum_fusion.refs_0_), channel_id=1, source_target_pairs={{0,24},{4,28},{8,0},{12,4},{16,8},{20,12},{24,16},{28,20},{1,25},{... | collective-permute-start | bytes 1081352 | tf_op jit(solution)/shard_map/ppermute | solution.py:66
  31.1 50.0 %collective-permute-start.5 = (bf16[128,1408]{1,0:T(8,128)(2,1)S(1)}, bf16[128,1408]{1,0:T(8,128)(2,1)S(1)}, u32[]{:S(2)}, u32[]{:S(2)}) collective-permute-start(bf16[128,1408]{1,0:T(8,128)(2,1)S(1)} %pad_maximum_fusion.refs_0_), channel_id=1, source_target_pairs={{0,16},{4,20},{8,24},{12,28},{16,0},{20,4},{24,8},{28,12},{1,17},{... | collective-permute-start | bytes 1081352 | tf_op jit(solution)/shard_map/ppermute | solution.py:66
  32.1 50.1 %collective-permute-start = (bf16[320,1024]{1,0:T(8,128)(2,1)S(1)}, bf16[320,1024]{1,0:T(8,128)(2,1)}, u32[]{:S(2)}, u32[]{:S(2)}) collective-permute-start(bf16[320,1024]{1,0:T(8,128)(2,1)S(1)} %bitcast.81), channel_id=1, source_target_pairs={{0,2},{1,3},{2,0},{3,1},{4,6},{5,7},{6,4},{7,5},{8,10},{9,11},{10,... | collective-permute-start | bytes 1966088 | tf_op jit(solution)/shard_map/ppermute | solution.py:30
  32.4 49.8 %collective-permute-start.6 = (bf16[128,1408]{1,0:T(8,128)(2,1)S(1)}, bf16[128,1408]{1,0:T(8,128)(2,1)S(1)}, u32[]{:S(2)}, u32[]{:S(2)}) collective-permute-start(bf16[128,1408]{1,0:T(8,128)(2,1)S(1)} %pad_maximum_fusion.refs_0_), channel_id=1, source_target_pairs={{0,4},{4,0},{8,12},{12,8},{16,20},{20,16},{24,28},{28,24},{1,5},{5... | collective-permute-start | bytes 1081352 | tf_op jit(solution)/shard_map/ppermute | solution.py:66
  42.7 48.9 %copy-start.18 = (bf16[128,1408]{1,0:T(8,128)(2,1)}, bf16[128,1408]{1,0:T(8,128)(2,1)S(1)}, u32[]{:S(2)}) copy-start(bf16[128,1408]{1,0:T(8,128)(2,1)S(1)} %collective-permute-done.3.refs_1_) | copy-start | bytes 1081348
  42.7 41.5 %collective-permute-start.7 = (bf16[128,1408]{1,0:T(8,128)(2,1)S(1)}, bf16[128,1408]{1,0:T(8,128)(2,1)}, u32[]{:S(2)}, u32[]{:S(2)}) collective-permute-start(bf16[128,1408]{1,0:T(8,128)(2,1)S(1)} %collective-permute-done.3.refs_1_), channel_id=1, source_target_pairs={{0,4},{4,0},{8,12},{12,8},{16,20},{20,16},{24,28},{28,24},{1,5},{5... | collective-permute-start | bytes 1081352 | tf_op jit(solution)/shard_map/ppermute | solution.py:66
  49.3 42.2 %copy-start.19 = (bf16[128,1408]{1,0:T(8,128)(2,1)}, bf16[128,1408]{1,0:T(8,128)(2,1)S(1)}, u32[]{:S(2)}) copy-start(bf16[128,1408]{1,0:T(8,128)(2,1)S(1)} %collective-permute-done.4.refs_2_) | copy-start | bytes 1081348
  49.3 34.8 %collective-permute-start.8 = (bf16[128,1408]{1,0:T(8,128)(2,1)S(1)}, bf16[128,1408]{1,0:T(8,128)(2,1)}, u32[]{:S(2)}, u32[]{:S(2)}) collective-permute-start(bf16[128,1408]{1,0:T(8,128)(2,1)S(1)} %collective-permute-done.4.refs_2_), channel_id=1, source_target_pairs={{0,4},{4,0},{8,12},{12,8},{16,20},{20,16},{24,28},{28,24},{1,5},{5... | collective-permute-start | bytes 1081352 | tf_op jit(solution)/shard_map/ppermute | solution.py:66
  81.2 10.4 %collective-permute-start.9 = (bf16[128,1408]{1,0:T(8,128)(2,1)S(1)}, bf16[128,1408]{1,0:T(8,128)(2,1)}, u32[]{:S(2)}, u32[]{:S(2)}) collective-permute-start(bf16[128,1408]{1,0:T(8,128)(2,1)S(1)} %collective-permute-done.5.refs_3_), channel_id=1, source_target_pairs={{0,4},{4,0},{8,12},{12,8},{16,20},{20,16},{24,28},{28,24},{1,5},{5... | collective-permute-start | bytes 1081352 | tf_op jit(solution)/shard_map/ppermute | solution.py:66
  82.2 14.9 %collective-permute-start.1 = (bf16[320,1024]{1,0:T(8,128)(2,1)S(1)}, bf16[320,1024]{1,0:T(8,128)(2,1)}, u32[]{:S(2)}, u32[]{:S(2)}) collective-permute-start(bf16[320,1024]{1,0:T(8,128)(2,1)S(1)} %bitcast.82), channel_id=1, source_target_pairs={{0,1},{1,0},{2,3},{3,2},{4,5},{5,4},{6,7},{7,6},{8,9},{9,8},{10,11... | collective-permute-start | bytes 1966088 | tf_op jit(solution)/shard_map/ppermute | solution.py:30
  83.0 14.2 %collective-permute-start.2 = (bf16[320,1024]{1,0:T(8,128)(2,1)}, bf16[320,1024]{1,0:T(8,128)(2,1)}, u32[]{:S(2)}, u32[]{:S(2)}) collective-permute-start(bf16[320,1024]{1,0:T(8,128)(2,1)} %collective-permute-done), channel_id=1, source_target_pairs={{0,1},{1,0},{2,3},{3,2},{4,5},{5,4},{6,7},{7,6},{8,9},{9,8},{10,11... | collective-permute-start | bytes 1966088 | tf_op jit(solution)/shard_map/ppermute | solution.py:30
  94.6 29.4 %collective-permute-start.14 = (bf16[1024,512]{1,0:T(8,128)(2,1)}, bf16[1024,512]{1,0:T(8,128)(2,1)S(1)}, u32[]{:S(2)}, u32[]{:S(2)}) collective-permute-start(bf16[1024,512]{1,0:T(8,128)(2,1)} %placed.1.mine.refs_6_), channel_id=1, source_target_pairs={{0,1},{1,0},{2,3},{3,2},{4,5},{5,4},{6,7},{7,6},{8,9},{9,8},{10,11... | collective-permute-start | bytes 3145736 | tf_op jit(solution)/shard_map/ppermute | solution.py:30
  94.7 18.2 %collective-permute-start.10 = (bf16[320,1024]{1,0:T(8,128)(2,1)S(1)}, bf16[320,1024]{1,0:T(8,128)(2,1)S(1)}, u32[]{:S(2)}, u32[]{:S(2)}) collective-permute-start(bf16[320,1024]{1,0:T(8,128)(2,1)S(1)} %bitcast.92), channel_id=1, source_target_pairs={{0,2},{1,3},{2,0},{3,1},{4,6},{5,7},{6,4},{7,5},{8,10},{9,11},{10,... | collective-permute-start | bytes 1966088 | tf_op jit(solution)/shard_map/ppermute | solution.py:30
  113.8 6.4 %collective-permute-start.13 = (bf16[320,256]{1,0:T(8,128)(2,1)}, bf16[320,256]{1,0:T(8,128)(2,1)S(1)}, u32[]{:S(2)}, u32[]{:S(2)}) collective-permute-start(bf16[320,256]{1,0:T(8,128)(2,1)} %get-tuple-element.76), channel_id=1, source_target_pairs={{0,3},{1,2},{2,1},{3,0},{4,7},{5,6},{6,5},{7,4},{8,11},{9,10},{10,... | collective-permute-start | bytes 491528 | tf_op jit(solution)/shard_map/ppermute | solution.py:30
  114.6 5.6 %collective-permute-start.12 = (bf16[320,256]{1,0:T(8,128)(2,1)}, bf16[320,256]{1,0:T(8,128)(2,1)S(1)}, u32[]{:S(2)}, u32[]{:S(2)}) collective-permute-start(bf16[320,256]{1,0:T(8,128)(2,1)} %get-tuple-element.74), channel_id=1, source_target_pairs={{0,1},{1,0},{2,3},{3,2},{4,5},{5,4},{6,7},{7,6},{8,9},{9,8},{10,11... | collective-permute-start | bytes 491528 | tf_op jit(solution)/shard_map/ppermute | solution.py:30
  115.0 9.1 %collective-permute-start.11 = (bf16[320,256]{1,0:T(8,128)(2,1)}, bf16[320,256]{1,0:T(8,128)(2,1)S(1)}, u32[]{:S(2)}, u32[]{:S(2)}) collective-permute-start(bf16[320,256]{1,0:T(8,128)(2,1)} %get-tuple-element.72), channel_id=1, source_target_pairs={{0,2},{1,3},{2,0},{3,1},{4,6},{5,7},{6,4},{7,5},{8,10},{9,11},{10,... | collective-permute-start | bytes 491528 | tf_op jit(solution)/shard_map/ppermute | solution.py:30
  130.3 16.8 %collective-permute-start.15 = (bf16[320,1024]{1,0:T(8,128)(2,1)}, bf16[320,1024]{1,0:T(8,128)(2,1)S(1)}, u32[]{:S(2)}, u32[]{:S(2)}) collective-permute-start(bf16[320,1024]{1,0:T(8,128)(2,1)} %get-tuple-element.79.refs_0_), channel_id=1, source_target_pairs={{0,2},{1,3},{2,0},{3,1},{4,6},{5,7},{6,4},{7,5},{8,10},{9,11},{10,... | collective-permute-start | bytes 1966088 | tf_op jit(solution)/shard_map/ppermute | solution.py:30
  131.3 15.7 %collective-permute-start.18 = (bf16[320,1024]{1,0:T(8,128)(2,1)S(1)}, bf16[320,1024]{1,0:T(8,128)(2,1)S(1)}, u32[]{:S(2)}, u32[]{:S(2)}) collective-permute-start(bf16[320,1024]{1,0:T(8,128)(2,1)S(1)} %bitcast.93), channel_id=1, source_target_pairs={{0,1},{1,0},{2,3},{3,2},{4,5},{5,4},{6,7},{7,6},{8,9},{9,8},{10,11... | collective-permute-start | bytes 1966088 | tf_op jit(solution)/shard_map/ppermute | solution.py:30
  131.4 15.7 %collective-permute-start.19 = (bf16[320,1024]{1,0:T(8,128)(2,1)S(1)}, bf16[320,1024]{1,0:T(8,128)(2,1)S(1)}, u32[]{:S(2)}, u32[]{:S(2)}) collective-permute-start(bf16[320,1024]{1,0:T(8,128)(2,1)S(1)} %copy-done.34), channel_id=1, source_target_pairs={{0,1},{1,0},{2,3},{3,2},{4,5},{5,4},{6,7},{7,6},{8,9},{9,8},{10,11... | collective-permute-start | bytes 1966088 | tf_op jit(solution)/shard_map/ppermute | solution.py:30
  131.9 15.3 %collective-permute-start.16 = (bf16[320,1024]{1,0:T(8,128)(2,1)}, bf16[320,1024]{1,0:T(8,128)(2,1)}, u32[]{:S(2)}, u32[]{:S(2)}) collective-permute-start(bf16[320,1024]{1,0:T(8,128)(2,1)} %get-tuple-element.79.refs_0_), channel_id=1, source_target_pairs={{0,1},{1,0},{2,3},{3,2},{4,5},{5,4},{6,7},{7,6},{8,9},{9,8},{10,11... | collective-permute-start | bytes 1966088 | tf_op jit(solution)/shard_map/ppermute | solution.py:30
  147.1 2.2 collective-permute-start.17
  173.0 3.3 %collective-permute-start.20 = (bf16[2,320,1024]{2,1,0:T(8,128)(2,1)}, bf16[2,320,1024]{2,1,0:T(8,128)(2,1)S(1)}, u32[]{:S(2)}, u32[]{:S(2)}) collective-permute-start(bf16[2,320,1024]{2,1,0:T(8,128)(2,1)} %get-tuple-element.83), channel_id=1, source_target_pairs={{0,1},{1,0},{2,3},{3,2},{4,5},{5,4},{6,7},{7,6},{8,9},{9,8},{10,11... | collective-permute-start | bytes 3932168 | tf_op jit(solution)/shard_map/ppermute | solution.py:30
  176.6 16.8 %collective-permute-start.21 = (bf16[320,1024]{1,0:T(8,128)(2,1)S(1)}, bf16[320,1024]{1,0:T(8,128)(2,1)S(1)}, u32[]{:S(2)}, u32[]{:S(2)}) collective-permute-start(bf16[320,1024]{1,0:T(8,128)(2,1)S(1)} %fusion.8), channel_id=1, source_target_pairs={{0,2},{1,3},{2,0},{3,1},{4,6},{5,7},{6,4},{7,5},{8,10},{9,11},{10,... | collective-permute-start | bytes 1966088 | tf_op jit(solution)/shard_map/ppermute | solution.py:30
  204.5 3.6 %collective-permute-start.24 = (bf16[2,4,128,512]{3,2,1,0:T(8,128)(2,1)}, bf16[2,4,128,512]{3,2,1,0:T(8,128)(2,1)S(1)}, u32[]{:S(2)}, u32[]{:S(2)}) collective-permute-start(bf16[2,4,128,512]{3,2,1,0:T(8,128)(2,1)} %get-tuple-element.92), channel_id=1, source_target_pairs={{0,1},{1,0},{2,3},{3,2},{4,5},{5,4},{6,7},{7,6},{8,9},{9,8},{10,11... | collective-permute-start | bytes 3145736 | tf_op jit(solution)/shard_map/ppermute | solution.py:30
  204.5 6.6 %collective-permute-start.22 = (bf16[2,320,1024]{2,1,0:T(8,128)(2,1)S(1)}, bf16[2,320,1024]{2,1,0:T(8,128)(2,1)S(1)}, u32[]{:S(2)}, u32[]{:S(2)}) collective-permute-start(bf16[2,320,1024]{2,1,0:T(8,128)(2,1)S(1)} %copy-done.32), channel_id=1, source_target_pairs={{0,1},{1,0},{2,3},{3,2},{4,5},{5,4},{6,7},{7,6},{8,9},{9,8},{10,11... | collective-permute-start | bytes 3932168 | tf_op jit(solution)/shard_map/ppermute | solution.py:30
  205.0 7.4 %collective-permute-start.25 = (bf16[320,256]{1,0:T(8,128)(2,1)S(1)}, bf16[320,256]{1,0:T(8,128)(2,1)S(1)}, u32[]{:S(2)}, u32[]{:S(2)}) collective-permute-start(bf16[320,256]{1,0:T(8,128)(2,1)S(1)} %copy-done.42), channel_id=1, source_target_pairs={{0,2},{1,3},{2,0},{3,1},{4,6},{5,7},{6,4},{7,5},{8,10},{9,11},{10,... | collective-permute-start | bytes 491528 | tf_op jit(solution)/shard_map/ppermute | solution.py:30
  206.1 6.3 %collective-permute-start.26 = (bf16[320,256]{1,0:T(8,128)(2,1)S(1)}, bf16[320,256]{1,0:T(8,128)(2,1)S(1)}, u32[]{:S(2)}, u32[]{:S(2)}) collective-permute-start(bf16[320,256]{1,0:T(8,128)(2,1)S(1)} %copy-done.40), channel_id=1, source_target_pairs={{0,1},{1,0},{2,3},{3,2},{4,5},{5,4},{6,7},{7,6},{8,9},{9,8},{10,11... | collective-permute-start | bytes 491528 | tf_op jit(solution)/shard_map/ppermute | solution.py:30
  206.1 7.7 %collective-permute-start.27 = (bf16[320,256]{1,0:T(8,128)(2,1)S(1)}, bf16[320,256]{1,0:T(8,128)(2,1)S(1)}, u32[]{:S(2)}, u32[]{:S(2)}) collective-permute-start(bf16[320,256]{1,0:T(8,128)(2,1)S(1)} %copy-done.38), channel_id=1, source_target_pairs={{0,3},{1,2},{2,1},{3,0},{4,7},{5,6},{6,5},{7,4},{8,11},{9,10},{10,... | collective-permute-start | bytes 491528 | tf_op jit(solution)/shard_map/ppermute | solution.py:30
  209.7 22.2 %collective-permute-start.28 = (bf16[4,128,512]{2,1,0:T(8,128)(2,1)S(1)}, bf16[4,128,512]{2,1,0:T(8,128)(2,1)S(1)}, u32[]{:S(2)}, u32[]{:S(2)}) collective-permute-start(bf16[4,128,512]{2,1,0:T(8,128)(2,1)S(1)} %fusion.10), channel_id=1, source_target_pairs={{0,4},{4,0},{8,12},{12,8},{16,20},{20,16},{24,28},{28,24},{1,5},{5... | collective-permute-start | bytes 1572872 | tf_op jit(solution)/shard_map/ppermute | solution.py:66
  214.5 18.5 %copy-start.1 = (bf16[2,2,80,1024]{3,2,1,0:T(8,128)(2,1)S(1)}, bf16[2,2,80,1024]{3,2,1,0:T(8,128)(2,1)}, u32[]{:S(2)}) copy-start(bf16[2,2,80,1024]{3,2,1,0:T(8,128)(2,1)} %param.16) | copy-start | bytes 1966084
  231.9 11.3 %collective-permute-start.29 = (bf16[2,320,1024]{2,1,0:T(8,128)(2,1)}, bf16[2,320,1024]{2,1,0:T(8,128)(2,1)}, u32[]{:S(2)}, u32[]{:S(2)}) collective-permute-start(bf16[2,320,1024]{2,1,0:T(8,128)(2,1)} %bitcast.108), channel_id=1, source_target_pairs={{0,1},{1,0},{2,3},{3,2},{4,5},{5,4},{6,7},{7,6},{8,9},{9,8},{10,11... | collective-permute-start | bytes 3932168 | tf_op jit(solution)/shard_map/ppermute | solution.py:30
  235.2 29.6 %collective-permute-start.23 = (bf16[320,1024]{1,0:T(8,128)(2,1)}, bf16[320,1024]{1,0:T(8,128)(2,1)}, u32[]{:S(2)}, u32[]{:S(2)}) collective-permute-start(bf16[320,1024]{1,0:T(8,128)(2,1)} %fusion.9), channel_id=1, source_target_pairs={{0,2},{1,3},{2,0},{3,1},{4,6},{5,7},{6,4},{7,5},{8,10},{9,11},{10,... | collective-permute-start | bytes 1966088 | tf_op jit(solution)/shard_map/ppermute | solution.py:30
  236.4 31.2 %collective-permute-start.34 = (bf16[4,128,896]{2,1,0:T(8,128)(2,1)}, bf16[4,128,896]{2,1,0:T(8,128)(2,1)}, u32[]{:S(2)}, u32[]{:S(2)}) collective-permute-start(bf16[4,128,896]{2,1,0:T(8,128)(2,1)} %get-tuple-element.110), channel_id=1, source_target_pairs={{0,4},{4,0},{8,12},{12,8},{16,20},{20,16},{24,28},{28,24},{1,5},{5... | collective-permute-start | bytes 2752520 | tf_op jit(solution)/shard_map/ppermute | solution.py:66
  239.4 25.4 %copy-start.2 = (f32[320,1024]{1,0:T(8,128)S(1)}, f32[320,1024]{1,0:T(8,128)}, u32[]{:S(2)}) copy-start(f32[320,1024]{1,0:T(8,128)} %get-tuple-element.78.refs_3_) | copy-start | bytes 3932164
  239.4 8.4 %collective-permute-start.30 = (bf16[1,128,512]{2,1,0:T(8,128)(2,1)}, bf16[1,128,512]{2,1,0:T(8,128)(2,1)S(1)}, u32[]{:S(2)}, u32[]{:S(2)}) collective-permute-start(bf16[1,128,512]{2,1,0:T(8,128)(2,1)} %get-tuple-element.104), channel_id=1, source_target_pairs={{0,8},{4,12},{8,16},{12,20},{16,24},{20,28},{24,0},{28,4},{1,9},{5... | collective-permute-start | bytes 393224 | tf_op jit(solution)/shard_map/ppermute | solution.py:66
  239.4 9.7 %collective-permute-start.31 = (bf16[1,128,512]{2,1,0:T(8,128)(2,1)}, bf16[1,128,512]{2,1,0:T(8,128)(2,1)S(1)}, u32[]{:S(2)}, u32[]{:S(2)}) collective-permute-start(bf16[1,128,512]{2,1,0:T(8,128)(2,1)} %get-tuple-element.105), channel_id=1, source_target_pairs={{0,24},{4,28},{8,0},{12,4},{16,8},{20,12},{24,16},{28,20},{1,25},{... | collective-permute-start | bytes 393224 | tf_op jit(solution)/shard_map/ppermute | solution.py:66
  243.3 18.5 %collective-permute-start.32 = (bf16[1,128,512]{2,1,0:T(8,128)(2,1)}, bf16[1,128,512]{2,1,0:T(8,128)(2,1)S(1)}, u32[]{:S(2)}, u32[]{:S(2)}) collective-permute-start(bf16[1,128,512]{2,1,0:T(8,128)(2,1)} %get-tuple-element.106), channel_id=1, source_target_pairs={{0,16},{4,20},{8,24},{12,28},{16,0},{20,4},{24,8},{28,12},{1,17},{... | collective-permute-start | bytes 393224 | tf_op jit(solution)/shard_map/ppermute | solution.py:66
  261.8 14.2 %collective-permute-start.33 = (bf16[320,1024]{1,0:T(8,128)(2,1)}, bf16[320,1024]{1,0:T(8,128)(2,1)S(1)}, u32[]{:S(2)}, u32[]{:S(2)}) collective-permute-start(bf16[320,1024]{1,0:T(8,128)(2,1)} %fusion.2), channel_id=1, source_target_pairs={{0,2},{1,3},{2,0},{3,1},{4,6},{5,7},{6,4},{7,5},{8,10},{9,11},{10,... | collective-permute-start | bytes 1966088 | tf_op jit(solution)/shard_map/ppermute | solution.py:30
  270.1 21.7 %collective-permute-start.35 = (bf16[1,128,896]{2,1,0:T(8,128)(2,1)}, bf16[1,128,896]{2,1,0:T(8,128)(2,1)S(1)}, u32[]{:S(2)}, u32[]{:S(2)}) collective-permute-start(bf16[1,128,896]{2,1,0:T(8,128)(2,1)} %get-tuple-element.114), channel_id=1, source_target_pairs={{0,8},{4,12},{8,16},{12,20},{16,24},{20,28},{24,0},{28,4},{1,9},{5... | collective-permute-start | bytes 688136 | tf_op jit(solution)/shard_map/ppermute | solution.py:66
  270.1 21.7 %collective-permute-start.36 = (bf16[1,128,896]{2,1,0:T(8,128)(2,1)}, bf16[1,128,896]{2,1,0:T(8,128)(2,1)}, u32[]{:S(2)}, u32[]{:S(2)}) collective-permute-start(bf16[1,128,896]{2,1,0:T(8,128)(2,1)} %get-tuple-element.115), channel_id=1, source_target_pairs={{0,24},{4,28},{8,0},{12,4},{16,8},{20,12},{24,16},{28,20},{1,25},{... | collective-permute-start | bytes 688136 | tf_op jit(solution)/shard_map/ppermute | solution.py:66
  273.9 17.9 %collective-permute-start.37 = (bf16[1,128,896]{2,1,0:T(8,128)(2,1)}, bf16[1,128,896]{2,1,0:T(8,128)(2,1)}, u32[]{:S(2)}, u32[]{:S(2)}) collective-permute-start(bf16[1,128,896]{2,1,0:T(8,128)(2,1)} %get-tuple-element.116), channel_id=1, source_target_pairs={{0,16},{4,20},{8,24},{12,28},{16,0},{20,4},{24,8},{28,12},{1,17},{... | collective-permute-start | bytes 688136 | tf_op jit(solution)/shard_map/ppermute | solution.py:66
  279.8 9.4 %all-to-all-start.1 = ((bf16[4,32,1024]{2,1,0:T(8,128)(2,1)}), bf16[4,32,1024]{2,1,0:T(8,128)(2,1)S(1)}, u32[]{:S(2)}, u32[]{:S(2)}) async-start(bf16[4,32,1024]{2,1,0:T(8,128)(2,1)} %bitcast.47), calls=%async_computation.2 | async-start | bytes 524288 | tf_op jit(solution)/shard_map/all_to_all | solution.py:898
  294.8 10.5 %all-to-all-start.2 = ((bf16[4,32,1408]{2,1,0:T(8,128)(2,1)}), bf16[4,32,1408]{2,1,0:T(8,128)(2,1)S(1)}, u32[]{:S(2)}, u32[]{:S(2)}) async-start(bf16[4,32,1408]{2,1,0:T(8,128)(2,1)} %bitcast.96), calls=%async_computation.3 | async-start | bytes 720896 | tf_op jit(solution)/shard_map/all_to_all | solution.py:898
  (39 other events, 169.1 us)
Sparse Core Ops, SparseCore 0:
  10.1 72.4 all-gather.2
  84.7 48.3 all-gather.4
  173.1 99.3 reduce-scatter.1

commit v5 on v4

--- a/solution.py
+++ b/solution.py
@@ -501,8 +501,8 @@
 def feed_kernel(micros, *refs):
     n2, cot = refs[:SEQ], refs[SEQ : 2 * SEQ]
     vec, down_ref, up_ref = refs[2 * SEQ : 2 * SEQ + 3]
-    down_chip, down_sib, up_chip, up_sib, grads, sums = refs[2 * SEQ + 3 : 2 * SEQ + 9]
-    w_up, w_down, n2_in, c_in, act, gh, weight_sem, n2_sem, c_sem = refs[2 * SEQ + 9 :]
+    down_chip, down_sib, *ups, grads, sums = refs[2 * SEQ + 3 : 3 * SEQ + 7]
+    w_up, w_down, n2_in, c_in, act, gh, weight_sem, n2_sem, c_sem = refs[3 * SEQ + 7 :]
     rows = n2[0].shape[0] // micros
     hidden = w_up.shape[1]
     up_copy = pltpu.make_async_copy(up_ref, w_up, weight_sem.at[0])
@@ -515,15 +515,14 @@
     for copy in n2_copies + [up_copy]:
         copy.wait()
     total = jnp.zeros((1, hidden), F32)
-    for part in range(2 * micros):
-        micro, half = part // 2, part % 2
-        span = slice(part * 2 * rows, (part + 1) * 2 * rows)
+    for micro in range(micros):
+        span = slice(micro * SEQ * rows, (micro + 1) * SEQ * rows)
         values = plain_dot(n2_in[span], w_up[...]) + vec[8:9, :]
         normal = 0.5 * (1.0 + lax.erf(values * (2.0**-0.5)))
         slope = normal + values * (jnp.exp(values * values * -0.5) * 0.3989422804014327)
         active = (values * normal).astype(BF)
         act[span] = active
-        if part == 0:
+        if micro == 0:
             for copy in c_copies + down_copies:
                 copy.wait()
         grad_hidden = (slope * cols_dot(c_in[span], w_down[...])).astype(BF)
@@ -532,13 +531,13 @@
         place = slice(micro * rows, (micro + 1) * rows)
         down_part = plain_dot(active, w_down[...]).astype(BF)
         up_part = cols_dot(grad_hidden, w_up[...]).astype(BF)
-        for k in range(2):
-            (down_chip, down_sib)[half][k, place] = down_part[k * rows : (k + 1) * rows]
-            (up_chip, up_sib)[half][k, place] = up_part[k * rows : (k + 1) * rows]
+        for k in range(SEQ):
+            (down_chip, down_sib)[k // 2][k % 2, place] = down_part[k * rows : (k + 1) * rows]
+            ups[k][place] = up_part[k * rows : (k + 1) * rows]
     sums[...] = jnp.zeros(sums.shape, F32)
     sums[8:9, :] = total
     block = grads.shape[2]
-    step = max(256 // block, 1)
+    step = max(512 // block, 1)
     for which, (left, right) in enumerate(((act, c_in), (n2_in, gh))):
         for at in range(0, grads.shape[0], step):
             part = rows_dot(left[:, at * block : (at + step) * block], right[...]).astype(BF)
@@ -553,8 +552,9 @@
     return pl.pallas_call(
         functools.partial(feed_kernel, micros),
         in_specs=[ANY] * (2 * SEQ) + [VMEM] + [ANY] * 2,
-        out_specs=[VMEM] * 6,
-        out_shape=[pair] * 4
+        out_specs=[VMEM] * (SEQ + 4),
+        out_shape=[pair] * 2
+        + [jax.ShapeDtypeStruct((rows, model), BF)] * SEQ
         + [
             jax.ShapeDtypeStruct((fsdp, 2, model // fsdp, model), BF),
             jax.ShapeDtypeStruct((16, model), F32),
@@ -584,7 +584,7 @@
     for copy in copies:
         copy.start()
     grad_two = jnp.concatenate(
-        [a[0].astype(F32) + b[0].astype(F32) + c[...].astype(F32) for a, b, c in zip(chips, cames, fars)],
+        [a[...].astype(F32) + b[...].astype(F32) + c[...].astype(F32) for a, b, c in zip(chips, cames, fars)],
         axis=0,
     )
     hat, scale = norm_parts(mid_ref[...])
@@ -700,7 +700,7 @@
         right = grads[...].reshape(n1_in.shape[0], triple)
         total = jnp.concatenate([sums[...], jnp.zeros((LANES - sums.shape[0], model), F32)], axis=0)
         out[:, triple:] = total.T.astype(BF)
-        tile = min(256, model)
+        tile = min(512, model)
         for at in range(0, model, tile):
             out[at : at + tile, :triple] = rows_dot(n1_in[:, at : at + tile], right).astype(BF)
         moves = digit_moves(info, out, keep, send, out_sem)
@@ -844,14 +844,14 @@
     n2_pieces = seq_gather(normed)
 
     group_rows = micros * SEQ * rows
-    down_chip, down_sib, up_chip, up_sib, feed_grad, part = feed(
+    down_chip, down_sib, *ups, feed_grad, part = feed(
         fsdp, micros, n2_pieces, c_pieces, vec, w_down, w_up
     )
     sums = [part]
     down_grad, up_grad = lax.psum_scatter(feed_grad, "fsdp", scatter_dimension=0, tiled=False)
     down_grad = down_grad.astype(F32)
-    came, far = seq_scatter(up_chip, up_sib)
-    two_parts = [(up_chip, came, hop(far, 2))]
+    up_far = (ups[1].astype(F32) + hop(ups[3], 1).astype(F32)).astype(BF)
+    two_parts = [(ups[0], hop(ups[2], 1), hop(up_far, 2))]
     down_parts = [(down_chip, down_sib)]
 
     grad_middle, branch, *grads_out, part = middle_back(

time: 321 us -> 315 us (0.981); the launches traced: 316 us -> 314 us
    ppermute x23 -> x24, waiting for transfers between devices: 48.8 us -> 45.6 us  [hop(): return lax.ppermute(array, 'seq', [(i, i ^ mask) for i in range(SEQ)])]
    unnamed x88 -> x92, local copies, waits for them, and re-layouts: 6.37 us -> 7.65 us
    ppermute x23 -> x24, starting transfers between devices: 13.9 us -> 14.1 us  [hop(): return lax.ppermute(array, 'seq', [(i, i ^ mask) for i in range(SEQ)])]
  transfers between devices with their start and end apart: 43 -> 44, of which waited for: 18 -> 19; matrix products, arithmetic and copies ran while one was open for 7% -> 7% of each run, Pallas kernels for 19% -> 19%
where the time goes in v5:
time: 315 us; the launch traced here: 314 us
  waiting for transfers between devices  125 us (40%)
  Pallas kernels  87.7 us (28%)
  starting transfers between devices  41.2 us (13%)
  local copies, waits for them, and re-layouts  16.9 us (5%)
  other arithmetic  15.1 us (5%)
  between operations  14.3 us (5%)
  blocking collectives  14.1 us (4%)
    ppermute x15, waiting for transfers between devices, shift(): return lax.ppermute(array, 'fsdp', pairs)  68.7 us
    ppermute x24, waiting for transfers between devices, hop(): return lax.ppermute(array, 'seq', [(i, i ^ mask) for i in range(SEQ)])  45.6 us
    pallas_call x1, Pallas kernels, feed(): pl.pallas_call(functools.partial(feed_kernel, micros), in_specs=[ANY] * (...  24.3 us
    ppermute x15, starting transfers between devices, shift(): return lax.ppermute(array, 'fsdp', pairs)  20.1 us
    pallas_call x1, Pallas kernels, attention_back(): pl.pallas_call(functools.partial(attention_back_kernel, count), grid=(ima...  17.1 us
    pallas_call x1, Pallas kernels, attention(): pl.pallas_call(functools.partial(attention_kernel, count), grid=(images,)...  15.5 us
    all_to_all x1, blocking collectives, on_device(): lax.all_to_all(to_send, 'seq', 0, 0, tiled=True).reshape(block, -1)  14.1 us
    ppermute x24, starting transfers between devices, hop(): return lax.ppermute(array, 'seq', [(i, i ^ mask) for i in range(SEQ)])  14.1 us
  transfers between devices with their start and end apart: 44, of which 19 were waited for; matrix products, arithmetic and copies ran while one was open for 7% of the time, Pallas kernels for 19%

profile of v5, /device:TPU:0, one launch (start us, length us, event | category | flops | bytes accessed | tf_op | source)
XLA Modules:
  0.0 313.9 jit_solution(3657912520469382327)
XLA Ops:
  9.5 2.0 pack.1
  11.5 14.1 %all_to_all.15 = bf16[4,32,2432]{2,1,0:T(8,128)(2,1)S(1)} all-to-all(bf16[4,32,2432]{2,1,0:T(8,128)(2,1)} %pack.1), channel_id=1, replica_groups=mesh['fsdp'=8,'seq'=4] {'seq'}, dimensions={0} | all-to-all | bytes 1245184 | tf_op jit(solution)/shard_map/all_to_all | solution.py:807
  26.7 2.3 collective-permute-start.3
  29.0 2.1 collective-permute-start.4
  32.4 1.5 collective-permute-start.6
  33.9 8.7 %collective-permute-done.3.refs_1_ = bf16[128,1408]{1,0:T(8,128)(2,1)S(1)} collective-permute-done((bf16[128,1408]{1,0:T(8,128)(2,1)S(1)}, bf16[128,1408]{1,0:T(8,128)(2,1)S(1)}, u32[]{:S(2)}, u32[]{:S(2)}) %collective-permute-start.3) | collective-permute-done | bytes 360480 | tf_op jit(solution)/shard_map/ppermute | solution.py:66
  43.5 5.8 %collective-permute-done.4.refs_2_ = bf16[128,1408]{1,0:T(8,128)(2,1)S(1)} collective-permute-done((bf16[128,1408]{1,0:T(8,128)(2,1)S(1)}, bf16[128,1408]{1,0:T(8,128)(2,1)S(1)}, u32[]{:S(2)}, u32[]{:S(2)}) %collective-permute-start.4) | collective-permute-done | bytes 360480 | tf_op jit(solution)/shard_map/ppermute | solution.py:66
  49.3 1.3 collective-permute-start.8
  50.6 30.5 %collective-permute-done.5.refs_3_ = bf16[128,1408]{1,0:T(8,128)(2,1)S(1)} collective-permute-done((bf16[128,1408]{1,0:T(8,128)(2,1)S(1)}, bf16[128,1408]{1,0:T(8,128)(2,1)S(1)}, u32[]{:S(2)}, u32[]{:S(2)}) %collective-permute-start.5) | collective-permute-done | bytes 360480 | tf_op jit(solution)/shard_map/ppermute | solution.py:66
  83.4 8.1 %collective-permute-done.9.refs_7_ = bf16[128,1408]{1,0:T(8,128)(2,1)} collective-permute-done((bf16[128,1408]{1,0:T(8,128)(2,1)S(1)}, bf16[128,1408]{1,0:T(8,128)(2,1)}, u32[]{:S(2)}, u32[]{:S(2)}) %collective-permute-start.9) | collective-permute-done | bytes 360480 | tf_op jit(solution)/shard_map/ppermute | solution.py:66
  91.5 3.2 %placed.1.mine.refs_6_ = bf16[1024,512]{1,0:T(8,128)(2,1)} custom-call(s32[14]{0:T(128)} %stack.90.info, bf16[128,1408]{1,0:T(8,128)(2,1)} %copy-done.5, bf16[128,1408]{1,0:T(8,128)(2,1)} %copy-done.18, bf16[128,1408]{1,0:T(8,128)(2,1)} %copy-done.19, bf16[128,1408]{1,0:T(8,128)(2,1)} %copy-done.20, bf16[128,1408]{1,0:T(8,128)(2,1)} %copy-done.21, ...), custom_call_target="tpu_custom_call" | custom-call | tf_op jit(solution)/shard_map/placed/pallas_call | solution.py:300
  97.2 15.5 %attention.1 = (bf16[4,4,80,1024]{3,2,1,0:T(8,128)(2,1)}, bf16[4,4,80,1024]{3,2,1,0:T(8,128)(2,1)}, bf16[4,4,80,768]{3,2,1,0:T(8,128)(2,1)}, bf16[320,256]{1,0:T...) custom-call(s32[14]{0:T(128)} %stack.90.info, ...), custom_call_target="tpu_custom_call" | custom-call | flops 2852126720 | bytes 16777216 | tf_op jit(solution)/shard_map/attention/pallas_call | solution.py:422
  115.0 4.3 %collective-permute-done.13.e3 = bf16[320,256]{1,0:T(8,128)(2,1)S(1)} collective-permute-done((bf16[320,256]{1,0:T(8,128)(2,1)}, bf16[320,256]{1,0:T(8,128)(2,1)S(1)}, u32[]{:S(2)}, u32[]{:S(2)}) %collective-permute-start.13) | collective-permute-done | bytes 163872 | tf_op jit(solution)/shard_map/ppermute | solution.py:30
  119.3 3.8 %collective-permute-done.11.e1 = bf16[320,256]{1,0:T(8,128)(2,1)S(1)} collective-permute-done((bf16[320,256]{1,0:T(8,128)(2,1)}, bf16[320,256]{1,0:T(8,128)(2,1)S(1)}, u32[]{:S(2)}, u32[]{:S(2)}) %collective-permute-start.11) | collective-permute-done | bytes 163872 | tf_op jit(solution)/shard_map/ppermute | solution.py:30
  124.2 5.2 %middle.1 = (bf16[320,1024]{1,0:T(8,128)(2,1)}, f32[320,1024]{1,0:T(8,128)}, bf16[320,1024]{1,0:T(8,128)(2,1)}) custom-call(s32[14]{0:T(128)} %stack.90.info, bf16[320,256]{1,0:T(8,128)(2,1)} %get-tuple-element.71.e0, bf16[320,256]{1,0:T(8,128)(2,1)} %copy-done.25, bf16[320,256]{1,0:T(8,128)(2,1)} %copy-done.24, bf16[320,256]{1,0:T(8,128)(2,1)} %copy-done.23, ...), custom_call_target="tpu_custom_call" | custom-call | flops 671088640 | bytes 4194304 | tf_op jit(solution)/shard_map/middle/pallas_call | solution.py:482
  130.8 15.4 %collective-permute-done.15.refs_1_ = bf16[320,1024]{1,0:T(8,128)(2,1)S(1)} collective-permute-done((bf16[320,1024]{1,0:T(8,128)(2,1)}, bf16[320,1024]{1,0:T(8,128)(2,1)S(1)}, u32[]{:S(2)}, u32[]{:S(2)}) %collective-permute-start.15) | collective-permute-done | bytes 655392 | tf_op jit(solution)/shard_map/ppermute | solution.py:30
  148.4 24.3 %feed.1 = (bf16[2,320,1024]{2,1,0:T(8,128)(2,1)}, bf16[2,320,1024]{2,1,0:T(8,128)(2,1)}, bf16[320,1024]{1,0:T(8,128)(2,1)}, bf16[320,1024]{1,0:T(8,128)(2,1)}, b...) custom-call(bf16[320,1024]{1,0:T(8,128)(2,1)} %get-tuple-element.81., ...), custom_call_target="tpu_custom_call" | custom-call | flops 16106127360 | bytes 25165824 | tf_op jit(solution)/shard_map/feed/pallas_call | solution.py:552
  174.3 1.6 collective-permute-done.21
  177.1 15.9 %collective-permute-done.22.refs_2_ = bf16[320,1024]{1,0:T(8,128)(2,1)S(1)} collective-permute-done((bf16[320,1024]{1,0:T(8,128)(2,1)S(1)}, bf16[320,1024]{1,0:T(8,128)(2,1)S(1)}, u32[]{:S(2)}, u32[]{:S(2)}) %collective-permute-start.22) | collective-permute-done | bytes 655392 | tf_op jit(solution)/shard_map/ppermute | solution.py:30
  193.9 5.6 %middle_back.1 = (f32[320,1024]{1,0:T(8,128)}, bf16[320,1024]{1,0:T(8,128)(2,1)}, bf16[320,256]{1,0:T(8,128)(2,1)}, bf16[320,256]{1,0:T(8,128)(2,1)}, bf16[320,2...) custom-call(s32[14]{0:T(128)} %stack.90.info, bf16[320,1024]{1,0:T(8,128)(2,1)} %get-tuple-element.84.refs_0_, ...), custom_call_target="tpu_custom_call" | custom-call | flops 671088640 | bytes 4194304 | tf_op jit(solution)/shard_map/middle_back/pallas_call | solution.py:614
  199.5 4.3 %core_grad.1 = (bf16[2,4,128,512]{3,2,1,0:T(8,128)(2,1)}, bf16[2,4,128,512]{3,2,1,0:T(8,128)(2,1)}) custom-call(s32[14]{0:T(128)} %stack.90.info, bf16[320,1024]{1,0:T(8,128)(2,1)} %get-tuple-element.94.left, bf16[320,1024]{1,0:T(8,128)(2,1)} %get-tuple-element.88.right), custom_call_target="tpu_custom_call" | custom-call | flops 671088640 | bytes 4194304 | tf_op jit(solution)/shard_map/core_grad/pallas_call | solution.py:348
  205.1 1.3 collective-permute-start.28
  207.4 1.6 fusion.9
  208.9 1.3 collective-permute-start.29
  210.3 1.3 fusion.8
  211.5 1.5 collective-permute-done.28.g3
  213.7 17.1 %attention_back.1 = (bf16[4,128,896]{2,1,0:T(8,128)(2,1)}, bf16[4,128,896]{2,1,0:T(8,128)(2,1)}, bf16[2,4,80,1024]{3,2,1,0:T(8,128)(2,1)}, bf16[2,4,80,1024]{3,2,1,0:T(8,128)(2,1)}) custom-call(s32[14]{0:T(128)} %stack.90.info, bf16[4,4,80,768]{3,2,1,0:T(8,128)(2,1)} %get-tuple-element.91.joined_ref, bf16[4,4,320,320]{3,2,1,0:T(8,128)(2,1)} %get-tuple-element.92.probs_ref, ...), custom_call_target="tpu_custom_call" | custom-call | flops 5704253440 | bytes 12582912 | tf_op jit(solution)/shard_map/attention_back/pallas_call | solution.py:723
  230.9 1.2 collective-permute-start.30
  236.2 2.3 split.2
  238.5 3.8 %collective-permute-start.32 = (bf16[1,128,512]{2,1,0:T(8,128)(2,1)}, bf16[1,128,512]{2,1,0:T(8,128)(2,1)S(1)}, u32[]{:S(2)}, u32[]{:S(2)}) collective-permute-start(bf16[1,128,512]{2,1,0:T(8,128)(2,1)} %get-tuple-element.109), channel_id=1, source_target_pairs={{0,24},{4,28},{8,0},{12,4},{16,8},{20,12},{24,16},{28,20},{1,25},{... | collective-permute-start | bytes 393224 | tf_op jit(solution)/shard_map/ppermute | solution.py:66
  242.3 2.2 fusion.2
  244.5 2.4 collective-permute-done.31.refs_5_
  247.5 12.4 %collective-permute-done.33.refs_7_ = bf16[1,128,512]{2,1,0:T(8,128)(2,1)S(1)} collective-permute-done((bf16[1,128,512]{2,1,0:T(8,128)(2,1)}, bf16[1,128,512]{2,1,0:T(8,128)(2,1)S(1)}, u32[]{:S(2)}, u32[]{:S(2)}) %collective-permute-start.33) | collective-permute-done | bytes 131104 | tf_op jit(solution)/shard_map/ppermute | solution.py:66
  259.9 2.3 collective-permute-start.34
  263.3 2.8 fusion.7
  266.1 2.4 split.3
  268.5 3.8 %collective-permute-start.37 = (bf16[1,128,896]{2,1,0:T(8,128)(2,1)}, bf16[1,128,896]{2,1,0:T(8,128)(2,1)}, u32[]{:S(2)}, u32[]{:S(2)}) collective-permute-start(bf16[1,128,896]{2,1,0:T(8,128)(2,1)} %get-tuple-element.119), channel_id=1, source_target_pairs={{0,24},{4,28},{8,0},{12,4},{16,8},{20,12},{24,16},{28,20},{1,25},{... | collective-permute-start | bytes 688136 | tf_op jit(solution)/shard_map/ppermute | solution.py:66
  272.4 1.7 collective-permute-done.34
  274.0 1.4 fusion.4
  275.9 2.0 fusion.10
  277.8 3.4 %all-to-all-start.1 = ((bf16[4,32,1024]{2,1,0:T(8,128)(2,1)}), bf16[4,32,1024]{2,1,0:T(8,128)(2,1)S(1)}, u32[]{:S(2)}, u32[]{:S(2)}) async-start(bf16[4,32,1024]{2,1,0:T(8,128)(2,1)} %bitcast.46), calls=%async_computation.2 | async-start | bytes 524288 | tf_op jit(solution)/shard_map/all_to_all | solution.py:898
  281.3 6.0 %all-to-all-done.1.ref = bf16[4,32,1024]{2,1,0:T(8,128)(2,1)S(1)} async-done(((bf16[4,32,1024]{2,1,0:T(8,128)(2,1)}), bf16[4,32,1024]{2,1,0:T(8,128)(2,1)S(1)}, u32[]{:S(2)}, u32[]{:S(2)}) %all-to-all-start.1) | async-done | bytes 262176 | tf_op jit(solution)/shard_map/all_to_all | solution.py:898
  288.0 1.8 unpack_up.1
  290.5 2.3 collect.1
  292.8 3.5 %all-to-all-start.2 = ((bf16[4,32,1408]{2,1,0:T(8,128)(2,1)}), bf16[4,32,1408]{2,1,0:T(8,128)(2,1)S(1)}, u32[]{:S(2)}, u32[]{:S(2)}) async-start(bf16[4,32,1408]{2,1,0:T(8,128)(2,1)} %bitcast.94), calls=%async_computation.3 | async-start | bytes 720896 | tf_op jit(solution)/shard_map/all_to_all | solution.py:898
  296.3 2.6 add_convert_fusion
  299.6 3.7 %all-to-all-done.2.ref = bf16[4,32,1408]{2,1,0:T(8,128)(2,1)S(1)} async-done(((bf16[4,32,1408]{2,1,0:T(8,128)(2,1)}), bf16[4,32,1408]{2,1,0:T(8,128)(2,1)S(1)}, u32[]{:S(2)}, u32[]{:S(2)}) %all-to-all-start.2) | async-done | bytes 360480 | tf_op jit(solution)/shard_map/all_to_all | solution.py:898
  304.1 1.8 unpack.1
  (186 shorter events, 34.3 us)
Async XLA Ops:
  7.2 141.2 %all-gather.3.cloned.1.call-start = ((), (), s32[]{:S(2)}) async-start(), calls=%async_computation.4 | async-start | bytes 2359296 | tf_op jit(solution)/shard_map/all_gather | solution.py:820
  7.9 140.5 %all-gather.5.cloned.1.call-start = ((), (), s32[]{:S(2)}) async-start(), calls=%async_computation.5 | async-start | bytes 2359296 | tf_op jit(solution)/shard_map/all_gather | solution.py:821
  26.3 249.5 %reduce-scatter.2.cloned.1.call-start = ((), (), s32[]{:S(2)}) async-start(), calls=%async_computation.6 | async-start | bytes 4718592 | tf_op jit(solution)/shard_map/reduce_scatter | solution.py:851
  26.7 64.8 %copy-start.5 = (bf16[128,1408]{1,0:T(8,128)(2,1)}, bf16[128,1408]{1,0:T(8,128)(2,1)S(1)}, u32[]{:S(2)}) copy-start(bf16[128,1408]{1,0:T(8,128)(2,1)S(1)} %pad_maximum_fusion.refs_0_) | copy-start | bytes 1081348
  26.7 16.0 %collective-permute-start.3 = (bf16[128,1408]{1,0:T(8,128)(2,1)S(1)}, bf16[128,1408]{1,0:T(8,128)(2,1)S(1)}, u32[]{:S(2)}, u32[]{:S(2)}) collective-permute-start(bf16[128,1408]{1,0:T(8,128)(2,1)S(1)} %pad_maximum_fusion.refs_0_), channel_id=1, source_target_pairs={{0,8},{4,12},{8,16},{12,20},{16,24},{20,28},{24,0},{28,4},{1,9},{5... | collective-permute-start | bytes 1081352 | tf_op jit(solution)/shard_map/ppermute | solution.py:66
  29.0 20.3 %collective-permute-start.4 = (bf16[128,1408]{1,0:T(8,128)(2,1)S(1)}, bf16[128,1408]{1,0:T(8,128)(2,1)S(1)}, u32[]{:S(2)}, u32[]{:S(2)}) collective-permute-start(bf16[128,1408]{1,0:T(8,128)(2,1)S(1)} %pad_maximum_fusion.refs_0_), channel_id=1, source_target_pairs={{0,24},{4,28},{8,0},{12,4},{16,8},{20,12},{24,16},{28,20},{1,25},{... | collective-permute-start | bytes 1081352 | tf_op jit(solution)/shard_map/ppermute | solution.py:66
  31.1 50.0 %collective-permute-start.5 = (bf16[128,1408]{1,0:T(8,128)(2,1)S(1)}, bf16[128,1408]{1,0:T(8,128)(2,1)S(1)}, u32[]{:S(2)}, u32[]{:S(2)}) collective-permute-start(bf16[128,1408]{1,0:T(8,128)(2,1)S(1)} %pad_maximum_fusion.refs_0_), channel_id=1, source_target_pairs={{0,16},{4,20},{8,24},{12,28},{16,0},{20,4},{24,8},{28,12},{1,17},{... | collective-permute-start | bytes 1081352 | tf_op jit(solution)/shard_map/ppermute | solution.py:66
  32.1 50.2 %collective-permute-start = (bf16[320,1024]{1,0:T(8,128)(2,1)S(1)}, bf16[320,1024]{1,0:T(8,128)(2,1)}, u32[]{:S(2)}, u32[]{:S(2)}) collective-permute-start(bf16[320,1024]{1,0:T(8,128)(2,1)S(1)} %bitcast.79), channel_id=1, source_target_pairs={{0,2},{1,3},{2,0},{3,1},{4,6},{5,7},{6,4},{7,5},{8,10},{9,11},{10,... | collective-permute-start | bytes 1966088 | tf_op jit(solution)/shard_map/ppermute | solution.py:30
  32.4 49.8 %collective-permute-start.6 = (bf16[128,1408]{1,0:T(8,128)(2,1)S(1)}, bf16[128,1408]{1,0:T(8,128)(2,1)S(1)}, u32[]{:S(2)}, u32[]{:S(2)}) collective-permute-start(bf16[128,1408]{1,0:T(8,128)(2,1)S(1)} %pad_maximum_fusion.refs_0_), channel_id=1, source_target_pairs={{0,4},{4,0},{8,12},{12,8},{16,20},{20,16},{24,28},{28,24},{1,5},{5... | collective-permute-start | bytes 1081352 | tf_op jit(solution)/shard_map/ppermute | solution.py:66
  42.7 48.8 %copy-start.18 = (bf16[128,1408]{1,0:T(8,128)(2,1)}, bf16[128,1408]{1,0:T(8,128)(2,1)S(1)}, u32[]{:S(2)}) copy-start(bf16[128,1408]{1,0:T(8,128)(2,1)S(1)} %collective-permute-done.3.refs_1_) | copy-start | bytes 1081348
  42.7 40.7 %collective-permute-start.7 = (bf16[128,1408]{1,0:T(8,128)(2,1)S(1)}, bf16[128,1408]{1,0:T(8,128)(2,1)}, u32[]{:S(2)}, u32[]{:S(2)}) collective-permute-start(bf16[128,1408]{1,0:T(8,128)(2,1)S(1)} %collective-permute-done.3.refs_1_), channel_id=1, source_target_pairs={{0,4},{4,0},{8,12},{12,8},{16,20},{20,16},{24,28},{28,24},{1,5},{5... | collective-permute-start | bytes 1081352 | tf_op jit(solution)/shard_map/ppermute | solution.py:66
  49.3 42.2 %copy-start.19 = (bf16[128,1408]{1,0:T(8,128)(2,1)}, bf16[128,1408]{1,0:T(8,128)(2,1)S(1)}, u32[]{:S(2)}) copy-start(bf16[128,1408]{1,0:T(8,128)(2,1)S(1)} %collective-permute-done.4.refs_2_) | copy-start | bytes 1081348
  49.3 34.0 %collective-permute-start.8 = (bf16[128,1408]{1,0:T(8,128)(2,1)S(1)}, bf16[128,1408]{1,0:T(8,128)(2,1)}, u32[]{:S(2)}, u32[]{:S(2)}) collective-permute-start(bf16[128,1408]{1,0:T(8,128)(2,1)S(1)} %collective-permute-done.4.refs_2_), channel_id=1, source_target_pairs={{0,4},{4,0},{8,12},{12,8},{16,20},{20,16},{24,28},{28,24},{1,5},{5... | collective-permute-start | bytes 1081352 | tf_op jit(solution)/shard_map/ppermute | solution.py:66
  81.1 10.4 %collective-permute-start.9 = (bf16[128,1408]{1,0:T(8,128)(2,1)S(1)}, bf16[128,1408]{1,0:T(8,128)(2,1)}, u32[]{:S(2)}, u32[]{:S(2)}) collective-permute-start(bf16[128,1408]{1,0:T(8,128)(2,1)S(1)} %collective-permute-done.5.refs_3_), channel_id=1, source_target_pairs={{0,4},{4,0},{8,12},{12,8},{16,20},{20,16},{24,28},{28,24},{1,5},{5... | collective-permute-start | bytes 1081352 | tf_op jit(solution)/shard_map/ppermute | solution.py:66
  82.2 15.0 %collective-permute-start.1 = (bf16[320,1024]{1,0:T(8,128)(2,1)S(1)}, bf16[320,1024]{1,0:T(8,128)(2,1)}, u32[]{:S(2)}, u32[]{:S(2)}) collective-permute-start(bf16[320,1024]{1,0:T(8,128)(2,1)S(1)} %bitcast.80), channel_id=1, source_target_pairs={{0,1},{1,0},{2,3},{3,2},{4,5},{5,4},{6,7},{7,6},{8,9},{9,8},{10,11... | collective-permute-start | bytes 1966088 | tf_op jit(solution)/shard_map/ppermute | solution.py:30
  82.2 15.0 %collective-permute-start.2 = (bf16[320,1024]{1,0:T(8,128)(2,1)}, bf16[320,1024]{1,0:T(8,128)(2,1)}, u32[]{:S(2)}, u32[]{:S(2)}) collective-permute-start(bf16[320,1024]{1,0:T(8,128)(2,1)} %collective-permute-done), channel_id=1, source_target_pairs={{0,1},{1,0},{2,3},{3,2},{4,5},{5,4},{6,7},{7,6},{8,9},{9,8},{10,11... | collective-permute-start | bytes 1966088 | tf_op jit(solution)/shard_map/ppermute | solution.py:30
  94.7 28.4 %collective-permute-start.14 = (bf16[1024,512]{1,0:T(8,128)(2,1)}, bf16[1024,512]{1,0:T(8,128)(2,1)S(1)}, u32[]{:S(2)}, u32[]{:S(2)}) collective-permute-start(bf16[1024,512]{1,0:T(8,128)(2,1)} %placed.1.mine.refs_6_), channel_id=1, source_target_pairs={{0,1},{1,0},{2,3},{3,2},{4,5},{5,4},{6,7},{7,6},{8,9},{9,8},{10,11... | collective-permute-start | bytes 3145736 | tf_op jit(solution)/shard_map/ppermute | solution.py:30
  94.8 18.0 %collective-permute-start.10 = (bf16[320,1024]{1,0:T(8,128)(2,1)S(1)}, bf16[320,1024]{1,0:T(8,128)(2,1)S(1)}, u32[]{:S(2)}, u32[]{:S(2)}) collective-permute-start(bf16[320,1024]{1,0:T(8,128)(2,1)S(1)} %bitcast.89), channel_id=1, source_target_pairs={{0,2},{1,3},{2,0},{3,1},{4,6},{5,7},{6,4},{7,5},{8,10},{9,11},{10,... | collective-permute-start | bytes 1966088 | tf_op jit(solution)/shard_map/ppermute | solution.py:30
  112.8 35.7 %copy-start.33 = (bf16[320,1024]{1,0:T(8,128)(2,1)}, bf16[320,1024]{1,0:T(8,128)(2,1)S(1)}, u32[]{:S(2)}) copy-start(bf16[320,1024]{1,0:T(8,128)(2,1)S(1)} %collective-permute-done.10.refs_5_) | copy-start | bytes 1966084
  112.8 6.5 %collective-permute-start.13 = (bf16[320,256]{1,0:T(8,128)(2,1)}, bf16[320,256]{1,0:T(8,128)(2,1)S(1)}, u32[]{:S(2)}, u32[]{:S(2)}) collective-permute-start(bf16[320,256]{1,0:T(8,128)(2,1)} %get-tuple-element.78), channel_id=1, source_target_pairs={{0,3},{1,2},{2,1},{3,0},{4,7},{5,6},{6,5},{7,4},{8,11},{9,10},{10,... | collective-permute-start | bytes 491528 | tf_op jit(solution)/shard_map/ppermute | solution.py:30
  113.5 5.7 %collective-permute-start.12 = (bf16[320,256]{1,0:T(8,128)(2,1)}, bf16[320,256]{1,0:T(8,128)(2,1)S(1)}, u32[]{:S(2)}, u32[]{:S(2)}) collective-permute-start(bf16[320,256]{1,0:T(8,128)(2,1)} %get-tuple-element.76), channel_id=1, source_target_pairs={{0,1},{1,0},{2,3},{3,2},{4,5},{5,4},{6,7},{7,6},{8,9},{9,8},{10,11... | collective-permute-start | bytes 491528 | tf_op jit(solution)/shard_map/ppermute | solution.py:30
  113.9 9.2 %collective-permute-start.11 = (bf16[320,256]{1,0:T(8,128)(2,1)}, bf16[320,256]{1,0:T(8,128)(2,1)S(1)}, u32[]{:S(2)}, u32[]{:S(2)}) collective-permute-start(bf16[320,256]{1,0:T(8,128)(2,1)} %get-tuple-element.74), channel_id=1, source_target_pairs={{0,2},{1,3},{2,0},{3,1},{4,6},{5,7},{6,4},{7,5},{8,10},{9,11},{10,... | collective-permute-start | bytes 491528 | tf_op jit(solution)/shard_map/ppermute | solution.py:30
  129.4 16.8 %collective-permute-start.15 = (bf16[320,1024]{1,0:T(8,128)(2,1)}, bf16[320,1024]{1,0:T(8,128)(2,1)S(1)}, u32[]{:S(2)}, u32[]{:S(2)}) collective-permute-start(bf16[320,1024]{1,0:T(8,128)(2,1)} %get-tuple-element.81.refs_0_), channel_id=1, source_target_pairs={{0,2},{1,3},{2,0},{3,1},{4,6},{5,7},{6,4},{7,5},{8,10},{9,11},{10,... | collective-permute-start | bytes 1966088 | tf_op jit(solution)/shard_map/ppermute | solution.py:30
  130.3 15.9 %collective-permute-start.18 = (bf16[320,1024]{1,0:T(8,128)(2,1)S(1)}, bf16[320,1024]{1,0:T(8,128)(2,1)S(1)}, u32[]{:S(2)}, u32[]{:S(2)}) collective-permute-start(bf16[320,1024]{1,0:T(8,128)(2,1)S(1)} %bitcast.90), channel_id=1, source_target_pairs={{0,1},{1,0},{2,3},{3,2},{4,5},{5,4},{6,7},{7,6},{8,9},{9,8},{10,11... | collective-permute-start | bytes 1966088 | tf_op jit(solution)/shard_map/ppermute | solution.py:30
  130.3 15.9 %collective-permute-start.19 = (bf16[320,1024]{1,0:T(8,128)(2,1)S(1)}, bf16[320,1024]{1,0:T(8,128)(2,1)S(1)}, u32[]{:S(2)}, u32[]{:S(2)}) collective-permute-start(bf16[320,1024]{1,0:T(8,128)(2,1)S(1)} %collective-permute-done.10.refs_5_), channel_id=1, source_target_pairs={{0,1},{1,0},{2,3},{3,2},{4,5},{5,4},{6,7},{7,6},{8,9},{9,8},{10,11... | collective-permute-start | bytes 1966088 | tf_op jit(solution)/shard_map/ppermute | solution.py:30
  130.8 16.3 %collective-permute-start.16 = (bf16[320,1024]{1,0:T(8,128)(2,1)}, bf16[320,1024]{1,0:T(8,128)(2,1)S(1)}, u32[]{:S(2)}, u32[]{:S(2)}) collective-permute-start(bf16[320,1024]{1,0:T(8,128)(2,1)} %get-tuple-element.81.refs_0_), channel_id=1, source_target_pairs={{0,1},{1,0},{2,3},{3,2},{4,5},{5,4},{6,7},{7,6},{8,9},{9,8},{10,11... | collective-permute-start | bytes 1966088 | tf_op jit(solution)/shard_map/ppermute | solution.py:30
  146.2 2.2 collective-permute-start.17
  173.8 2.1 collective-permute-start.21
  174.0 3.1 collective-permute-start.20
  176.2 16.8 %collective-permute-start.22 = (bf16[320,1024]{1,0:T(8,128)(2,1)S(1)}, bf16[320,1024]{1,0:T(8,128)(2,1)S(1)}, u32[]{:S(2)}, u32[]{:S(2)}) collective-permute-start(bf16[320,1024]{1,0:T(8,128)(2,1)S(1)} %add_convert_fusion.2), channel_id=1, source_target_pairs={{0,2},{1,3},{2,0},{3,1},{4,6},{5,7},{6,4},{7,5},{8,10},{9,11},{10,... | collective-permute-start | bytes 1966088 | tf_op jit(solution)/shard_map/ppermute | solution.py:30
  203.7 3.6 %collective-permute-start.25 = (bf16[2,4,128,512]{3,2,1,0:T(8,128)(2,1)}, bf16[2,4,128,512]{3,2,1,0:T(8,128)(2,1)S(1)}, u32[]{:S(2)}, u32[]{:S(2)}) collective-permute-start(bf16[2,4,128,512]{3,2,1,0:T(8,128)(2,1)} %get-tuple-element.96), channel_id=1, source_target_pairs={{0,1},{1,0},{2,3},{3,2},{4,5},{5,4},{6,7},{7,6},{8,9},{9,8},{10,11... | collective-permute-start | bytes 3145736 | tf_op jit(solution)/shard_map/ppermute | solution.py:30
  203.7 6.5 %collective-permute-start.23 = (bf16[2,320,1024]{2,1,0:T(8,128)(2,1)S(1)}, bf16[2,320,1024]{2,1,0:T(8,128)(2,1)S(1)}, u32[]{:S(2)}, u32[]{:S(2)}) collective-permute-start(bf16[2,320,1024]{2,1,0:T(8,128)(2,1)S(1)} %copy-done.32), channel_id=1, source_target_pairs={{0,1},{1,0},{2,3},{3,2},{4,5},{5,4},{6,7},{7,6},{8,9},{9,8},{10,11... | collective-permute-start | bytes 3932168 | tf_op jit(solution)/shard_map/ppermute | solution.py:30
  204.2 7.3 %collective-permute-start.26 = (bf16[320,256]{1,0:T(8,128)(2,1)S(1)}, bf16[320,256]{1,0:T(8,128)(2,1)S(1)}, u32[]{:S(2)}, u32[]{:S(2)}) collective-permute-start(bf16[320,256]{1,0:T(8,128)(2,1)S(1)} %copy-done.44), channel_id=1, source_target_pairs={{0,2},{1,3},{2,0},{3,1},{4,6},{5,7},{6,4},{7,5},{8,10},{9,11},{10,... | collective-permute-start | bytes 491528 | tf_op jit(solution)/shard_map/ppermute | solution.py:30
  205.0 6.5 %collective-permute-start.27 = (bf16[320,256]{1,0:T(8,128)(2,1)S(1)}, bf16[320,256]{1,0:T(8,128)(2,1)S(1)}, u32[]{:S(2)}, u32[]{:S(2)}) collective-permute-start(bf16[320,256]{1,0:T(8,128)(2,1)S(1)} %copy-done.42), channel_id=1, source_target_pairs={{0,1},{1,0},{2,3},{3,2},{4,5},{5,4},{6,7},{7,6},{8,9},{9,8},{10,11... | collective-permute-start | bytes 491528 | tf_op jit(solution)/shard_map/ppermute | solution.py:30
  205.1 8.0 %collective-permute-start.28 = (bf16[320,256]{1,0:T(8,128)(2,1)S(1)}, bf16[320,256]{1,0:T(8,128)(2,1)S(1)}, u32[]{:S(2)}, u32[]{:S(2)}) collective-permute-start(bf16[320,256]{1,0:T(8,128)(2,1)S(1)} %copy-done.40), channel_id=1, source_target_pairs={{0,3},{1,2},{2,1},{3,0},{4,7},{5,6},{6,5},{7,4},{8,11},{9,10},{10,... | collective-permute-start | bytes 491528 | tf_op jit(solution)/shard_map/ppermute | solution.py:30
  208.9 21.9 %collective-permute-start.29 = (bf16[4,128,512]{2,1,0:T(8,128)(2,1)S(1)}, bf16[4,128,512]{2,1,0:T(8,128)(2,1)S(1)}, u32[]{:S(2)}, u32[]{:S(2)}) collective-permute-start(bf16[4,128,512]{2,1,0:T(8,128)(2,1)S(1)} %fusion.9), channel_id=1, source_target_pairs={{0,4},{4,0},{8,12},{12,8},{16,20},{20,16},{24,28},{28,24},{1,5},{5... | collective-permute-start | bytes 1572872 | tf_op jit(solution)/shard_map/ppermute | solution.py:66
  230.9 11.4 %collective-permute-start.30 = (bf16[2,320,1024]{2,1,0:T(8,128)(2,1)}, bf16[2,320,1024]{2,1,0:T(8,128)(2,1)}, u32[]{:S(2)}, u32[]{:S(2)}) collective-permute-start(bf16[2,320,1024]{2,1,0:T(8,128)(2,1)} %bitcast.106), channel_id=1, source_target_pairs={{0,1},{1,0},{2,3},{3,2},{4,5},{5,4},{6,7},{7,6},{8,9},{9,8},{10,11... | collective-permute-start | bytes 3932168 | tf_op jit(solution)/shard_map/ppermute | solution.py:30
  234.3 29.0 %collective-permute-start.24 = (bf16[320,1024]{1,0:T(8,128)(2,1)}, bf16[320,1024]{1,0:T(8,128)(2,1)}, u32[]{:S(2)}, u32[]{:S(2)}) collective-permute-start(bf16[320,1024]{1,0:T(8,128)(2,1)} %fusion.8), channel_id=1, source_target_pairs={{0,2},{1,3},{2,0},{3,1},{4,6},{5,7},{6,4},{7,5},{8,10},{9,11},{10,... | collective-permute-start | bytes 1966088 | tf_op jit(solution)/shard_map/ppermute | solution.py:30
  235.1 31.0 %collective-permute-start.35 = (bf16[4,128,896]{2,1,0:T(8,128)(2,1)}, bf16[4,128,896]{2,1,0:T(8,128)(2,1)}, u32[]{:S(2)}, u32[]{:S(2)}) collective-permute-start(bf16[4,128,896]{2,1,0:T(8,128)(2,1)} %get-tuple-element.114), channel_id=1, source_target_pairs={{0,4},{4,0},{8,12},{12,8},{16,20},{20,16},{24,28},{28,24},{1,5},{5... | collective-permute-start | bytes 2752520 | tf_op jit(solution)/shard_map/ppermute | solution.py:66
  238.5 8.4 %collective-permute-start.31 = (bf16[1,128,512]{2,1,0:T(8,128)(2,1)}, bf16[1,128,512]{2,1,0:T(8,128)(2,1)S(1)}, u32[]{:S(2)}, u32[]{:S(2)}) collective-permute-start(bf16[1,128,512]{2,1,0:T(8,128)(2,1)} %get-tuple-element.108), channel_id=1, source_target_pairs={{0,8},{4,12},{8,16},{12,20},{16,24},{20,28},{24,0},{28,4},{1,9},{5... | collective-permute-start | bytes 393224 | tf_op jit(solution)/shard_map/ppermute | solution.py:66
  238.5 8.9 %collective-permute-start.32 = (bf16[1,128,512]{2,1,0:T(8,128)(2,1)}, bf16[1,128,512]{2,1,0:T(8,128)(2,1)S(1)}, u32[]{:S(2)}, u32[]{:S(2)}) collective-permute-start(bf16[1,128,512]{2,1,0:T(8,128)(2,1)} %get-tuple-element.109), channel_id=1, source_target_pairs={{0,24},{4,28},{8,0},{12,4},{16,8},{20,12},{24,16},{28,20},{1,25},{... | collective-permute-start | bytes 393224 | tf_op jit(solution)/shard_map/ppermute | solution.py:66
  242.3 17.6 %collective-permute-start.33 = (bf16[1,128,512]{2,1,0:T(8,128)(2,1)}, bf16[1,128,512]{2,1,0:T(8,128)(2,1)S(1)}, u32[]{:S(2)}, u32[]{:S(2)}) collective-permute-start(bf16[1,128,512]{2,1,0:T(8,128)(2,1)} %get-tuple-element.110), channel_id=1, source_target_pairs={{0,16},{4,20},{8,24},{12,28},{16,0},{20,4},{24,8},{28,12},{1,17},{... | collective-permute-start | bytes 393224 | tf_op jit(solution)/shard_map/ppermute | solution.py:66
  259.9 14.1 %collective-permute-start.34 = (bf16[320,1024]{1,0:T(8,128)(2,1)}, bf16[320,1024]{1,0:T(8,128)(2,1)S(1)}, u32[]{:S(2)}, u32[]{:S(2)}) collective-permute-start(bf16[320,1024]{1,0:T(8,128)(2,1)} %fusion.2), channel_id=1, source_target_pairs={{0,2},{1,3},{2,0},{3,1},{4,6},{5,7},{6,4},{7,5},{8,10},{9,11},{10,... | collective-permute-start | bytes 1966088 | tf_op jit(solution)/shard_map/ppermute | solution.py:30
  268.5 21.2 %collective-permute-start.36 = (bf16[1,128,896]{2,1,0:T(8,128)(2,1)}, bf16[1,128,896]{2,1,0:T(8,128)(2,1)S(1)}, u32[]{:S(2)}, u32[]{:S(2)}) collective-permute-start(bf16[1,128,896]{2,1,0:T(8,128)(2,1)} %get-tuple-element.118), channel_id=1, source_target_pairs={{0,8},{4,12},{8,16},{12,20},{16,24},{20,28},{24,0},{28,4},{1,9},{5... | collective-permute-start | bytes 688136 | tf_op jit(solution)/shard_map/ppermute | solution.py:66
  268.5 21.2 %collective-permute-start.37 = (bf16[1,128,896]{2,1,0:T(8,128)(2,1)}, bf16[1,128,896]{2,1,0:T(8,128)(2,1)}, u32[]{:S(2)}, u32[]{:S(2)}) collective-permute-start(bf16[1,128,896]{2,1,0:T(8,128)(2,1)} %get-tuple-element.119), channel_id=1, source_target_pairs={{0,24},{4,28},{8,0},{12,4},{16,8},{20,12},{24,16},{28,20},{1,25},{... | collective-permute-start | bytes 688136 | tf_op jit(solution)/shard_map/ppermute | solution.py:66
  272.3 17.6 %collective-permute-start.38 = (bf16[1,128,896]{2,1,0:T(8,128)(2,1)}, bf16[1,128,896]{2,1,0:T(8,128)(2,1)}, u32[]{:S(2)}, u32[]{:S(2)}) collective-permute-start(bf16[1,128,896]{2,1,0:T(8,128)(2,1)} %get-tuple-element.120), channel_id=1, source_target_pairs={{0,16},{4,20},{8,24},{12,28},{16,0},{20,4},{24,8},{28,12},{1,17},{... | collective-permute-start | bytes 688136 | tf_op jit(solution)/shard_map/ppermute | solution.py:66
  277.8 9.4 %all-to-all-start.1 = ((bf16[4,32,1024]{2,1,0:T(8,128)(2,1)}), bf16[4,32,1024]{2,1,0:T(8,128)(2,1)S(1)}, u32[]{:S(2)}, u32[]{:S(2)}) async-start(bf16[4,32,1024]{2,1,0:T(8,128)(2,1)} %bitcast.46), calls=%async_computation.2 | async-start | bytes 524288 | tf_op jit(solution)/shard_map/all_to_all | solution.py:898
  292.8 10.5 %all-to-all-start.2 = ((bf16[4,32,1408]{2,1,0:T(8,128)(2,1)}), bf16[4,32,1408]{2,1,0:T(8,128)(2,1)S(1)}, u32[]{:S(2)}, u32[]{:S(2)}) async-start(bf16[4,32,1408]{2,1,0:T(8,128)(2,1)} %bitcast.94), calls=%async_computation.3 | async-start | bytes 720896 | tf_op jit(solution)/shard_map/all_to_all | solution.py:898
  (42 other events, 215.2 us)
Sparse Core Ops, SparseCore 0:
  10.1 72.4 all-gather.2
  84.8 48.0 all-gather.4
  172.9 98.5 reduce-scatter.1

commit v6 on v5

--- a/solution.py
+++ b/solution.py
@@ -394,7 +394,7 @@
     )
     joined = (plain_dot(normed, weight[:, :triple]) + bias).astype(BF)
     joined_ref[...] = joined.reshape(joined_ref.shape)
-    keep = keep_ref[0] > 0
+    keep = jnp.broadcast_to(keep_ref[0], (8, rows)).T[:, :1] > 0
     outs = []
     for head in range(width // HEAD_DIM):
         low = head * HEAD_DIM
@@ -424,7 +424,7 @@
         grid=(images,),
         in_specs=[SMEM]
         + [pl.BlockSpec((1, tokens, model), lambda i: (i, 0, 0))] * SEQ
-        + [pl.BlockSpec((1, rows, 1), lambda i: (i, 0, 0))]
+        + [pl.BlockSpec((1, 1, rows), lambda i: (i, 0, 0))]
         + [ANY] * count,
         out_specs=[group_block(model), group_block(model), group_block(triple)]
         + [pl.BlockSpec((tokens, width), lambda i: (i, 0))] * SEQ
@@ -829,7 +829,7 @@
     n1, hat_one, joined, *heads_out, probs, vec = attention(
         info,
         [x.reshape(micros * images, tokens, model) for x in x_pieces],
-        keep.reshape(micros * images, SEQ * tokens, 1),
+        keep.reshape(micros * images, 1, SEQ * tokens).astype(F32),
         first_pieces,
         triple,
     )

time: 315 us -> 315 us (level)
  no operation moved by 1% of the time
where the time goes in v6:
time: 315 us; the launch traced here: 314 us
  waiting for transfers between devices  126 us (40%)
  Pallas kernels  87.9 us (28%)
  starting transfers between devices  40.5 us (13%)
  local copies, waits for them, and re-layouts  16.2 us (5%)
  other arithmetic  15.1 us (5%)
  between operations  14.3 us (5%)
  blocking collectives  14.1 us (4%)
    ppermute x15, waiting for transfers between devices, shift(): return lax.ppermute(array, 'fsdp', pairs)  69.5 us
    ppermute x24, waiting for transfers between devices, hop(): return lax.ppermute(array, 'seq', [(i, i ^ mask) for i in range(SEQ)])  45.9 us
    pallas_call x1, Pallas kernels, feed(): pl.pallas_call(functools.partial(feed_kernel, micros), in_specs=[ANY] * (...  24.3 us
    ppermute x15, starting transfers between devices, shift(): return lax.ppermute(array, 'fsdp', pairs)  20.5 us
    pallas_call x1, Pallas kernels, attention_back(): pl.pallas_call(functools.partial(attention_back_kernel, count), grid=(ima...  17.1 us
    pallas_call x1, Pallas kernels, attention(): pl.pallas_call(functools.partial(attention_kernel, count), grid=(images,)...  15.6 us
    all_to_all x1, blocking collectives, on_device(): lax.all_to_all(to_send, 'seq', 0, 0, tiled=True).reshape(block, -1)  14.1 us
    ppermute x24, starting transfers between devices, hop(): return lax.ppermute(array, 'seq', [(i, i ^ mask) for i in range(SEQ)])  13 us
  transfers between devices with their start and end apart: 44, of which 19 were waited for; matrix products, arithmetic and copies ran while one was open for 7% of the time, Pallas kernels for 19%

profile of v6, /device:TPU:0, one launch (start us, length us, event | category | flops | bytes accessed | tf_op | source)
XLA Modules:
  0.0 313.8 jit_solution(15390637247067329334)
XLA Ops:
  9.5 2.0 pack.1
  11.5 14.1 %all_to_all.15 = bf16[4,32,2432]{2,1,0:T(8,128)(2,1)S(1)} all-to-all(bf16[4,32,2432]{2,1,0:T(8,128)(2,1)} %pack.1), channel_id=1, replica_groups=mesh['fsdp'=8,'seq'=4] {'seq'}, dimensions={0} | all-to-all | bytes 1245184 | tf_op jit(solution)/shard_map/all_to_all | solution.py:807
  26.7 2.3 collective-permute-start.3
  29.0 2.1 collective-permute-start.4
  32.4 1.5 collective-permute-start.6
  33.9 8.7 %collective-permute-done.3.refs_1_ = bf16[128,1408]{1,0:T(8,128)(2,1)S(1)} collective-permute-done((bf16[128,1408]{1,0:T(8,128)(2,1)S(1)}, bf16[128,1408]{1,0:T(8,128)(2,1)S(1)}, u32[]{:S(2)}, u32[]{:S(2)}) %collective-permute-start.3) | collective-permute-done | bytes 360480 | tf_op jit(solution)/shard_map/ppermute | solution.py:66
  43.5 5.8 %collective-permute-done.4.refs_2_ = bf16[128,1408]{1,0:T(8,128)(2,1)S(1)} collective-permute-done((bf16[128,1408]{1,0:T(8,128)(2,1)S(1)}, bf16[128,1408]{1,0:T(8,128)(2,1)S(1)}, u32[]{:S(2)}, u32[]{:S(2)}) %collective-permute-start.4) | collective-permute-done | bytes 360480 | tf_op jit(solution)/shard_map/ppermute | solution.py:66
  49.3 1.3 collective-permute-start.8
  50.6 30.5 %collective-permute-done.5.refs_3_ = bf16[128,1408]{1,0:T(8,128)(2,1)S(1)} collective-permute-done((bf16[128,1408]{1,0:T(8,128)(2,1)S(1)}, bf16[128,1408]{1,0:T(8,128)(2,1)S(1)}, u32[]{:S(2)}, u32[]{:S(2)}) %collective-permute-start.5) | collective-permute-done | bytes 360480 | tf_op jit(solution)/shard_map/ppermute | solution.py:66
  83.4 8.1 %collective-permute-done.9.refs_7_ = bf16[128,1408]{1,0:T(8,128)(2,1)} collective-permute-done((bf16[128,1408]{1,0:T(8,128)(2,1)S(1)}, bf16[128,1408]{1,0:T(8,128)(2,1)}, u32[]{:S(2)}, u32[]{:S(2)}) %collective-permute-start.9) | collective-permute-done | bytes 360480 | tf_op jit(solution)/shard_map/ppermute | solution.py:66
  91.5 3.2 %placed.1.mine.refs_6_ = bf16[1024,512]{1,0:T(8,128)(2,1)} custom-call(s32[14]{0:T(128)} %stack.90.info, bf16[128,1408]{1,0:T(8,128)(2,1)} %copy-done.5, bf16[128,1408]{1,0:T(8,128)(2,1)} %copy-done.18, bf16[128,1408]{1,0:T(8,128)(2,1)} %copy-done.19, bf16[128,1408]{1,0:T(8,128)(2,1)} %copy-done.20, bf16[128,1408]{1,0:T(8,128)(2,1)} %copy-done.21, ...), custom_call_target="tpu_custom_call" | custom-call | tf_op jit(solution)/shard_map/placed/pallas_call | solution.py:300
  94.8 1.2 collective-permute-start.10
  96.8 15.6 %attention.1 = (bf16[4,4,80,1024]{3,2,1,0:T(8,128)(2,1)}, bf16[4,4,80,1024]{3,2,1,0:T(8,128)(2,1)}, bf16[4,4,80,768]{3,2,1,0:T(8,128)(2,1)}, bf16[320,256]{1,0:T...) custom-call(s32[14]{0:T(128)} %stack.90.info, ...), custom_call_target="tpu_custom_call" | custom-call | flops 2852126720 | bytes 16777216 | tf_op jit(solution)/shard_map/attention/pallas_call | solution.py:422
  114.7 4.2 %collective-permute-done.13.e3 = bf16[320,256]{1,0:T(8,128)(2,1)S(1)} collective-permute-done((bf16[320,256]{1,0:T(8,128)(2,1)}, bf16[320,256]{1,0:T(8,128)(2,1)S(1)}, u32[]{:S(2)}, u32[]{:S(2)}) %collective-permute-start.13) | collective-permute-done | bytes 163872 | tf_op jit(solution)/shard_map/ppermute | solution.py:30
  118.9 3.8 %collective-permute-done.11.e1 = bf16[320,256]{1,0:T(8,128)(2,1)S(1)} collective-permute-done((bf16[320,256]{1,0:T(8,128)(2,1)}, bf16[320,256]{1,0:T(8,128)(2,1)S(1)}, u32[]{:S(2)}, u32[]{:S(2)}) %collective-permute-start.11) | collective-permute-done | bytes 163872 | tf_op jit(solution)/shard_map/ppermute | solution.py:30
  123.9 5.2 %middle.1 = (bf16[320,1024]{1,0:T(8,128)(2,1)}, f32[320,1024]{1,0:T(8,128)}, bf16[320,1024]{1,0:T(8,128)(2,1)}) custom-call(s32[14]{0:T(128)} %stack.90.info, bf16[320,256]{1,0:T(8,128)(2,1)} %get-tuple-element.71.e0, bf16[320,256]{1,0:T(8,128)(2,1)} %copy-done.25, bf16[320,256]{1,0:T(8,128)(2,1)} %copy-done.24, bf16[320,256]{1,0:T(8,128)(2,1)} %copy-done.23, ...), custom_call_target="tpu_custom_call" | custom-call | flops 671088640 | bytes 4194304 | tf_op jit(solution)/shard_map/middle/pallas_call | solution.py:482
  130.5 15.4 %collective-permute-done.15.refs_1_ = bf16[320,1024]{1,0:T(8,128)(2,1)S(1)} collective-permute-done((bf16[320,1024]{1,0:T(8,128)(2,1)}, bf16[320,1024]{1,0:T(8,128)(2,1)S(1)}, u32[]{:S(2)}, u32[]{:S(2)}) %collective-permute-start.15) | collective-permute-done | bytes 655392 | tf_op jit(solution)/shard_map/ppermute | solution.py:30
  148.1 24.3 %feed.1 = (bf16[2,320,1024]{2,1,0:T(8,128)(2,1)}, bf16[2,320,1024]{2,1,0:T(8,128)(2,1)}, bf16[320,1024]{1,0:T(8,128)(2,1)}, bf16[320,1024]{1,0:T(8,128)(2,1)}, b...) custom-call(bf16[320,1024]{1,0:T(8,128)(2,1)} %get-tuple-element.81., ...), custom_call_target="tpu_custom_call" | custom-call | flops 16106127360 | bytes 25165824 | tf_op jit(solution)/shard_map/feed/pallas_call | solution.py:552
  174.0 1.6 collective-permute-done.21
  176.8 15.9 %collective-permute-done.22.refs_2_ = bf16[320,1024]{1,0:T(8,128)(2,1)S(1)} collective-permute-done((bf16[320,1024]{1,0:T(8,128)(2,1)S(1)}, bf16[320,1024]{1,0:T(8,128)(2,1)S(1)}, u32[]{:S(2)}, u32[]{:S(2)}) %collective-permute-start.22) | collective-permute-done | bytes 655392 | tf_op jit(solution)/shard_map/ppermute | solution.py:30
  193.5 5.5 %middle_back.1 = (f32[320,1024]{1,0:T(8,128)}, bf16[320,1024]{1,0:T(8,128)(2,1)}, bf16[320,256]{1,0:T(8,128)(2,1)}, bf16[320,256]{1,0:T(8,128)(2,1)}, bf16[320,2...) custom-call(s32[14]{0:T(128)} %stack.90.info, bf16[320,1024]{1,0:T(8,128)(2,1)} %get-tuple-element.84.refs_0_, ...), custom_call_target="tpu_custom_call" | custom-call | flops 671088640 | bytes 4194304 | tf_op jit(solution)/shard_map/middle_back/pallas_call | solution.py:614
  199.1 4.3 %core_grad.1 = (bf16[2,4,128,512]{3,2,1,0:T(8,128)(2,1)}, bf16[2,4,128,512]{3,2,1,0:T(8,128)(2,1)}) custom-call(s32[14]{0:T(128)} %stack.90.info, bf16[320,1024]{1,0:T(8,128)(2,1)} %get-tuple-element.94.left, bf16[320,1024]{1,0:T(8,128)(2,1)} %get-tuple-element.88.right), custom_call_target="tpu_custom_call" | custom-call | flops 671088640 | bytes 4194304 | tf_op jit(solution)/shard_map/core_grad/pallas_call | solution.py:348
  204.8 1.3 collective-permute-start.28
  207.0 1.6 fusion.9
  208.6 1.4 collective-permute-start.29
  210.0 1.3 fusion.8
  211.3 1.4 collective-permute-done.28.g3
  213.4 17.1 %attention_back.1 = (bf16[4,128,896]{2,1,0:T(8,128)(2,1)}, bf16[4,128,896]{2,1,0:T(8,128)(2,1)}, bf16[2,4,80,1024]{3,2,1,0:T(8,128)(2,1)}, bf16[2,4,80,1024]{3,2,1,0:T(8,128)(2,1)}) custom-call(s32[14]{0:T(128)} %stack.90.info, bf16[4,4,80,768]{3,2,1,0:T(8,128)(2,1)} %get-tuple-element.91.joined_ref, bf16[4,4,320,320]{3,2,1,0:T(8,128)(2,1)} %get-tuple-element.92.probs_ref, ...), custom_call_target="tpu_custom_call" | custom-call | flops 5704253440 | bytes 12582912 | tf_op jit(solution)/shard_map/attention_back/pallas_call | solution.py:723
  234.8 1.4 collective-permute-start.35
  236.2 2.3 split.2
  238.5 3.8 %collective-permute-start.32 = (bf16[1,128,512]{2,1,0:T(8,128)(2,1)}, bf16[1,128,512]{2,1,0:T(8,128)(2,1)S(1)}, u32[]{:S(2)}, u32[]{:S(2)}) collective-permute-start(bf16[1,128,512]{2,1,0:T(8,128)(2,1)} %get-tuple-element.109), channel_id=1, source_target_pairs={{0,24},{4,28},{8,0},{12,4},{16,8},{20,12},{24,16},{28,20},{1,25},{... | collective-permute-start | bytes 393224 | tf_op jit(solution)/shard_map/ppermute | solution.py:66
  242.3 2.2 fusion.2
  244.5 2.4 collective-permute-done.31.refs_5_
  247.6 12.8 %collective-permute-done.33.refs_7_ = bf16[1,128,512]{2,1,0:T(8,128)(2,1)S(1)} collective-permute-done((bf16[1,128,512]{2,1,0:T(8,128)(2,1)}, bf16[1,128,512]{2,1,0:T(8,128)(2,1)S(1)}, u32[]{:S(2)}, u32[]{:S(2)}) %collective-permute-start.33) | collective-permute-done | bytes 131104 | tf_op jit(solution)/shard_map/ppermute | solution.py:66
  262.6 2.8 fusion.7
  265.4 2.5 split.3
  267.9 3.8 %collective-permute-start.37 = (bf16[1,128,896]{2,1,0:T(8,128)(2,1)}, bf16[1,128,896]{2,1,0:T(8,128)(2,1)}, u32[]{:S(2)}, u32[]{:S(2)}) collective-permute-start(bf16[1,128,896]{2,1,0:T(8,128)(2,1)} %get-tuple-element.119), channel_id=1, source_target_pairs={{0,24},{4,28},{8,0},{12,4},{16,8},{20,12},{24,16},{28,20},{1,25},{... | collective-permute-start | bytes 688136 | tf_op jit(solution)/shard_map/ppermute | solution.py:66
  271.7 2.2 collective-permute-done.34
  273.9 1.4 fusion.4
  275.7 2.0 fusion.10
  277.7 3.4 %all-to-all-start.1 = ((bf16[4,32,1024]{2,1,0:T(8,128)(2,1)}), bf16[4,32,1024]{2,1,0:T(8,128)(2,1)S(1)}, u32[]{:S(2)}, u32[]{:S(2)}) async-start(bf16[4,32,1024]{2,1,0:T(8,128)(2,1)} %bitcast.46), calls=%async_computation.2 | async-start | bytes 524288 | tf_op jit(solution)/shard_map/all_to_all | solution.py:898
  281.1 6.0 %all-to-all-done.1.ref = bf16[4,32,1024]{2,1,0:T(8,128)(2,1)S(1)} async-done(((bf16[4,32,1024]{2,1,0:T(8,128)(2,1)}), bf16[4,32,1024]{2,1,0:T(8,128)(2,1)S(1)}, u32[]{:S(2)}, u32[]{:S(2)}) %all-to-all-start.1) | async-done | bytes 262176 | tf_op jit(solution)/shard_map/all_to_all | solution.py:898
  287.8 1.8 unpack_up.1
  290.3 2.3 collect.1
  292.7 3.5 %all-to-all-start.2 = ((bf16[4,32,1408]{2,1,0:T(8,128)(2,1)}), bf16[4,32,1408]{2,1,0:T(8,128)(2,1)S(1)}, u32[]{:S(2)}, u32[]{:S(2)}) async-start(bf16[4,32,1408]{2,1,0:T(8,128)(2,1)} %bitcast.94), calls=%async_computation.3 | async-start | bytes 720896 | tf_op jit(solution)/shard_map/all_to_all | solution.py:898
  296.1 2.6 add_convert_fusion
  299.5 3.7 %all-to-all-done.2.ref = bf16[4,32,1408]{2,1,0:T(8,128)(2,1)S(1)} async-done(((bf16[4,32,1408]{2,1,0:T(8,128)(2,1)}), bf16[4,32,1408]{2,1,0:T(8,128)(2,1)S(1)}, u32[]{:S(2)}, u32[]{:S(2)}) %all-to-all-start.2) | async-done | bytes 360480 | tf_op jit(solution)/shard_map/all_to_all | solution.py:898
  304.0 1.8 unpack.1
  (186 shorter events, 34.2 us)
Async XLA Ops:
  7.2 140.9 %all-gather.3.cloned.1.call-start = ((), (), s32[]{:S(2)}) async-start(), calls=%async_computation.4 | async-start | bytes 2359296 | tf_op jit(solution)/shard_map/all_gather | solution.py:820
  7.9 140.2 %all-gather.5.cloned.1.call-start = ((), (), s32[]{:S(2)}) async-start(), calls=%async_computation.5 | async-start | bytes 2359296 | tf_op jit(solution)/shard_map/all_gather | solution.py:821
  26.3 249.4 %reduce-scatter.2.cloned.1.call-start = ((), (), s32[]{:S(2)}) async-start(), calls=%async_computation.6 | async-start | bytes 4718592 | tf_op jit(solution)/shard_map/reduce_scatter | solution.py:851
  26.7 64.8 %copy-start.5 = (bf16[128,1408]{1,0:T(8,128)(2,1)}, bf16[128,1408]{1,0:T(8,128)(2,1)S(1)}, u32[]{:S(2)}) copy-start(bf16[128,1408]{1,0:T(8,128)(2,1)S(1)} %pad_maximum_fusion.refs_0_) | copy-start | bytes 1081348
  26.7 16.0 %collective-permute-start.3 = (bf16[128,1408]{1,0:T(8,128)(2,1)S(1)}, bf16[128,1408]{1,0:T(8,128)(2,1)S(1)}, u32[]{:S(2)}, u32[]{:S(2)}) collective-permute-start(bf16[128,1408]{1,0:T(8,128)(2,1)S(1)} %pad_maximum_fusion.refs_0_), channel_id=1, source_target_pairs={{0,8},{4,12},{8,16},{12,20},{16,24},{20,28},{24,0},{28,4},{1,9},{5... | collective-permute-start | bytes 1081352 | tf_op jit(solution)/shard_map/ppermute | solution.py:66
  29.0 20.3 %collective-permute-start.4 = (bf16[128,1408]{1,0:T(8,128)(2,1)S(1)}, bf16[128,1408]{1,0:T(8,128)(2,1)S(1)}, u32[]{:S(2)}, u32[]{:S(2)}) collective-permute-start(bf16[128,1408]{1,0:T(8,128)(2,1)S(1)} %pad_maximum_fusion.refs_0_), channel_id=1, source_target_pairs={{0,24},{4,28},{8,0},{12,4},{16,8},{20,12},{24,16},{28,20},{1,25},{... | collective-permute-start | bytes 1081352 | tf_op jit(solution)/shard_map/ppermute | solution.py:66
  31.1 50.0 %collective-permute-start.5 = (bf16[128,1408]{1,0:T(8,128)(2,1)S(1)}, bf16[128,1408]{1,0:T(8,128)(2,1)S(1)}, u32[]{:S(2)}, u32[]{:S(2)}) collective-permute-start(bf16[128,1408]{1,0:T(8,128)(2,1)S(1)} %pad_maximum_fusion.refs_0_), channel_id=1, source_target_pairs={{0,16},{4,20},{8,24},{12,28},{16,0},{20,4},{24,8},{28,12},{1,17},{... | collective-permute-start | bytes 1081352 | tf_op jit(solution)/shard_map/ppermute | solution.py:66
  32.1 50.2 %collective-permute-start = (bf16[320,1024]{1,0:T(8,128)(2,1)S(1)}, bf16[320,1024]{1,0:T(8,128)(2,1)}, u32[]{:S(2)}, u32[]{:S(2)}) collective-permute-start(bf16[320,1024]{1,0:T(8,128)(2,1)S(1)} %bitcast.79), channel_id=1, source_target_pairs={{0,2},{1,3},{2,0},{3,1},{4,6},{5,7},{6,4},{7,5},{8,10},{9,11},{10,... | collective-permute-start | bytes 1966088 | tf_op jit(solution)/shard_map/ppermute | solution.py:30
  32.4 49.8 %collective-permute-start.6 = (bf16[128,1408]{1,0:T(8,128)(2,1)S(1)}, bf16[128,1408]{1,0:T(8,128)(2,1)S(1)}, u32[]{:S(2)}, u32[]{:S(2)}) collective-permute-start(bf16[128,1408]{1,0:T(8,128)(2,1)S(1)} %pad_maximum_fusion.refs_0_), channel_id=1, source_target_pairs={{0,4},{4,0},{8,12},{12,8},{16,20},{20,16},{24,28},{28,24},{1,5},{5... | collective-permute-start | bytes 1081352 | tf_op jit(solution)/shard_map/ppermute | solution.py:66
  42.7 48.8 %copy-start.18 = (bf16[128,1408]{1,0:T(8,128)(2,1)}, bf16[128,1408]{1,0:T(8,128)(2,1)S(1)}, u32[]{:S(2)}) copy-start(bf16[128,1408]{1,0:T(8,128)(2,1)S(1)} %collective-permute-done.3.refs_1_) | copy-start | bytes 1081348
  42.7 40.7 %collective-permute-start.7 = (bf16[128,1408]{1,0:T(8,128)(2,1)S(1)}, bf16[128,1408]{1,0:T(8,128)(2,1)}, u32[]{:S(2)}, u32[]{:S(2)}) collective-permute-start(bf16[128,1408]{1,0:T(8,128)(2,1)S(1)} %collective-permute-done.3.refs_1_), channel_id=1, source_target_pairs={{0,4},{4,0},{8,12},{12,8},{16,20},{20,16},{24,28},{28,24},{1,5},{5... | collective-permute-start | bytes 1081352 | tf_op jit(solution)/shard_map/ppermute | solution.py:66
  49.3 42.2 %copy-start.19 = (bf16[128,1408]{1,0:T(8,128)(2,1)}, bf16[128,1408]{1,0:T(8,128)(2,1)S(1)}, u32[]{:S(2)}) copy-start(bf16[128,1408]{1,0:T(8,128)(2,1)S(1)} %collective-permute-done.4.refs_2_) | copy-start | bytes 1081348
  49.3 34.0 %collective-permute-start.8 = (bf16[128,1408]{1,0:T(8,128)(2,1)S(1)}, bf16[128,1408]{1,0:T(8,128)(2,1)}, u32[]{:S(2)}, u32[]{:S(2)}) collective-permute-start(bf16[128,1408]{1,0:T(8,128)(2,1)S(1)} %collective-permute-done.4.refs_2_), channel_id=1, source_target_pairs={{0,4},{4,0},{8,12},{12,8},{16,20},{20,16},{24,28},{28,24},{1,5},{5... | collective-permute-start | bytes 1081352 | tf_op jit(solution)/shard_map/ppermute | solution.py:66
  81.1 10.4 %collective-permute-start.9 = (bf16[128,1408]{1,0:T(8,128)(2,1)S(1)}, bf16[128,1408]{1,0:T(8,128)(2,1)}, u32[]{:S(2)}, u32[]{:S(2)}) collective-permute-start(bf16[128,1408]{1,0:T(8,128)(2,1)S(1)} %collective-permute-done.5.refs_3_), channel_id=1, source_target_pairs={{0,4},{4,0},{8,12},{12,8},{16,20},{20,16},{24,28},{28,24},{1,5},{5... | collective-permute-start | bytes 1081352 | tf_op jit(solution)/shard_map/ppermute | solution.py:66
  82.2 14.6 %collective-permute-start.1 = (bf16[320,1024]{1,0:T(8,128)(2,1)S(1)}, bf16[320,1024]{1,0:T(8,128)(2,1)}, u32[]{:S(2)}, u32[]{:S(2)}) collective-permute-start(bf16[320,1024]{1,0:T(8,128)(2,1)S(1)} %bitcast.80), channel_id=1, source_target_pairs={{0,1},{1,0},{2,3},{3,2},{4,5},{5,4},{6,7},{7,6},{8,9},{9,8},{10,11... | collective-permute-start | bytes 1966088 | tf_op jit(solution)/shard_map/ppermute | solution.py:30
  82.2 14.6 %collective-permute-start.2 = (bf16[320,1024]{1,0:T(8,128)(2,1)}, bf16[320,1024]{1,0:T(8,128)(2,1)}, u32[]{:S(2)}, u32[]{:S(2)}) collective-permute-start(bf16[320,1024]{1,0:T(8,128)(2,1)} %collective-permute-done), channel_id=1, source_target_pairs={{0,1},{1,0},{2,3},{3,2},{4,5},{5,4},{6,7},{7,6},{8,9},{9,8},{10,11... | collective-permute-start | bytes 1966088 | tf_op jit(solution)/shard_map/ppermute | solution.py:30
  94.7 28.1 %collective-permute-start.14 = (bf16[1024,512]{1,0:T(8,128)(2,1)}, bf16[1024,512]{1,0:T(8,128)(2,1)S(1)}, u32[]{:S(2)}, u32[]{:S(2)}) collective-permute-start(bf16[1024,512]{1,0:T(8,128)(2,1)} %placed.1.mine.refs_6_), channel_id=1, source_target_pairs={{0,1},{1,0},{2,3},{3,2},{4,5},{5,4},{6,7},{7,6},{8,9},{9,8},{10,11... | collective-permute-start | bytes 3145736 | tf_op jit(solution)/shard_map/ppermute | solution.py:30
  94.8 17.7 %collective-permute-start.10 = (bf16[320,1024]{1,0:T(8,128)(2,1)S(1)}, bf16[320,1024]{1,0:T(8,128)(2,1)S(1)}, u32[]{:S(2)}, u32[]{:S(2)}) collective-permute-start(bf16[320,1024]{1,0:T(8,128)(2,1)S(1)} %bitcast.89), channel_id=1, source_target_pairs={{0,2},{1,3},{2,0},{3,1},{4,6},{5,7},{6,4},{7,5},{8,10},{9,11},{10,... | collective-permute-start | bytes 1966088 | tf_op jit(solution)/shard_map/ppermute | solution.py:30
  112.5 35.6 %copy-start.33 = (bf16[320,1024]{1,0:T(8,128)(2,1)}, bf16[320,1024]{1,0:T(8,128)(2,1)S(1)}, u32[]{:S(2)}) copy-start(bf16[320,1024]{1,0:T(8,128)(2,1)S(1)} %collective-permute-done.10.refs_5_) | copy-start | bytes 1966084
  112.5 6.4 %collective-permute-start.13 = (bf16[320,256]{1,0:T(8,128)(2,1)}, bf16[320,256]{1,0:T(8,128)(2,1)S(1)}, u32[]{:S(2)}, u32[]{:S(2)}) collective-permute-start(bf16[320,256]{1,0:T(8,128)(2,1)} %get-tuple-element.78), channel_id=1, source_target_pairs={{0,3},{1,2},{2,1},{3,0},{4,7},{5,6},{6,5},{7,4},{8,11},{9,10},{10,... | collective-permute-start | bytes 491528 | tf_op jit(solution)/shard_map/ppermute | solution.py:30
  113.2 5.7 %collective-permute-start.12 = (bf16[320,256]{1,0:T(8,128)(2,1)}, bf16[320,256]{1,0:T(8,128)(2,1)S(1)}, u32[]{:S(2)}, u32[]{:S(2)}) collective-permute-start(bf16[320,256]{1,0:T(8,128)(2,1)} %get-tuple-element.76), channel_id=1, source_target_pairs={{0,1},{1,0},{2,3},{3,2},{4,5},{5,4},{6,7},{7,6},{8,9},{9,8},{10,11... | collective-permute-start | bytes 491528 | tf_op jit(solution)/shard_map/ppermute | solution.py:30
  113.6 9.2 %collective-permute-start.11 = (bf16[320,256]{1,0:T(8,128)(2,1)}, bf16[320,256]{1,0:T(8,128)(2,1)S(1)}, u32[]{:S(2)}, u32[]{:S(2)}) collective-permute-start(bf16[320,256]{1,0:T(8,128)(2,1)} %get-tuple-element.74), channel_id=1, source_target_pairs={{0,2},{1,3},{2,0},{3,1},{4,6},{5,7},{6,4},{7,5},{8,10},{9,11},{10,... | collective-permute-start | bytes 491528 | tf_op jit(solution)/shard_map/ppermute | solution.py:30
  129.1 16.8 %collective-permute-start.15 = (bf16[320,1024]{1,0:T(8,128)(2,1)}, bf16[320,1024]{1,0:T(8,128)(2,1)S(1)}, u32[]{:S(2)}, u32[]{:S(2)}) collective-permute-start(bf16[320,1024]{1,0:T(8,128)(2,1)} %get-tuple-element.81.refs_0_), channel_id=1, source_target_pairs={{0,2},{1,3},{2,0},{3,1},{4,6},{5,7},{6,4},{7,5},{8,10},{9,11},{10,... | collective-permute-start | bytes 1966088 | tf_op jit(solution)/shard_map/ppermute | solution.py:30
  130.0 15.9 %collective-permute-start.18 = (bf16[320,1024]{1,0:T(8,128)(2,1)S(1)}, bf16[320,1024]{1,0:T(8,128)(2,1)S(1)}, u32[]{:S(2)}, u32[]{:S(2)}) collective-permute-start(bf16[320,1024]{1,0:T(8,128)(2,1)S(1)} %bitcast.90), channel_id=1, source_target_pairs={{0,1},{1,0},{2,3},{3,2},{4,5},{5,4},{6,7},{7,6},{8,9},{9,8},{10,11... | collective-permute-start | bytes 1966088 | tf_op jit(solution)/shard_map/ppermute | solution.py:30
  130.0 15.9 %collective-permute-start.19 = (bf16[320,1024]{1,0:T(8,128)(2,1)S(1)}, bf16[320,1024]{1,0:T(8,128)(2,1)S(1)}, u32[]{:S(2)}, u32[]{:S(2)}) collective-permute-start(bf16[320,1024]{1,0:T(8,128)(2,1)S(1)} %collective-permute-done.10.refs_5_), channel_id=1, source_target_pairs={{0,1},{1,0},{2,3},{3,2},{4,5},{5,4},{6,7},{7,6},{8,9},{9,8},{10,11... | collective-permute-start | bytes 1966088 | tf_op jit(solution)/shard_map/ppermute | solution.py:30
  130.5 16.3 %collective-permute-start.16 = (bf16[320,1024]{1,0:T(8,128)(2,1)}, bf16[320,1024]{1,0:T(8,128)(2,1)S(1)}, u32[]{:S(2)}, u32[]{:S(2)}) collective-permute-start(bf16[320,1024]{1,0:T(8,128)(2,1)} %get-tuple-element.81.refs_0_), channel_id=1, source_target_pairs={{0,1},{1,0},{2,3},{3,2},{4,5},{5,4},{6,7},{7,6},{8,9},{9,8},{10,11... | collective-permute-start | bytes 1966088 | tf_op jit(solution)/shard_map/ppermute | solution.py:30
  145.9 2.2 collective-permute-start.17
  173.5 2.1 collective-permute-start.21
  173.7 3.1 collective-permute-start.20
  175.8 16.8 %collective-permute-start.22 = (bf16[320,1024]{1,0:T(8,128)(2,1)S(1)}, bf16[320,1024]{1,0:T(8,128)(2,1)S(1)}, u32[]{:S(2)}, u32[]{:S(2)}) collective-permute-start(bf16[320,1024]{1,0:T(8,128)(2,1)S(1)} %add_convert_fusion.2), channel_id=1, source_target_pairs={{0,2},{1,3},{2,0},{3,1},{4,6},{5,7},{6,4},{7,5},{8,10},{9,11},{10,... | collective-permute-start | bytes 1966088 | tf_op jit(solution)/shard_map/ppermute | solution.py:30
  203.4 3.6 %collective-permute-start.25 = (bf16[2,4,128,512]{3,2,1,0:T(8,128)(2,1)}, bf16[2,4,128,512]{3,2,1,0:T(8,128)(2,1)S(1)}, u32[]{:S(2)}, u32[]{:S(2)}) collective-permute-start(bf16[2,4,128,512]{3,2,1,0:T(8,128)(2,1)} %get-tuple-element.96), channel_id=1, source_target_pairs={{0,1},{1,0},{2,3},{3,2},{4,5},{5,4},{6,7},{7,6},{8,9},{9,8},{10,11... | collective-permute-start | bytes 3145736 | tf_op jit(solution)/shard_map/ppermute | solution.py:30
  203.4 6.6 %collective-permute-start.23 = (bf16[2,320,1024]{2,1,0:T(8,128)(2,1)S(1)}, bf16[2,320,1024]{2,1,0:T(8,128)(2,1)S(1)}, u32[]{:S(2)}, u32[]{:S(2)}) collective-permute-start(bf16[2,320,1024]{2,1,0:T(8,128)(2,1)S(1)} %copy-done.32), channel_id=1, source_target_pairs={{0,1},{1,0},{2,3},{3,2},{4,5},{5,4},{6,7},{7,6},{8,9},{9,8},{10,11... | collective-permute-start | bytes 3932168 | tf_op jit(solution)/shard_map/ppermute | solution.py:30
  203.9 7.4 %collective-permute-start.26 = (bf16[320,256]{1,0:T(8,128)(2,1)S(1)}, bf16[320,256]{1,0:T(8,128)(2,1)S(1)}, u32[]{:S(2)}, u32[]{:S(2)}) collective-permute-start(bf16[320,256]{1,0:T(8,128)(2,1)S(1)} %copy-done.44), channel_id=1, source_target_pairs={{0,2},{1,3},{2,0},{3,1},{4,6},{5,7},{6,4},{7,5},{8,10},{9,11},{10,... | collective-permute-start | bytes 491528 | tf_op jit(solution)/shard_map/ppermute | solution.py:30
  204.8 6.5 %collective-permute-start.27 = (bf16[320,256]{1,0:T(8,128)(2,1)S(1)}, bf16[320,256]{1,0:T(8,128)(2,1)S(1)}, u32[]{:S(2)}, u32[]{:S(2)}) collective-permute-start(bf16[320,256]{1,0:T(8,128)(2,1)S(1)} %copy-done.42), channel_id=1, source_target_pairs={{0,1},{1,0},{2,3},{3,2},{4,5},{5,4},{6,7},{7,6},{8,9},{9,8},{10,11... | collective-permute-start | bytes 491528 | tf_op jit(solution)/shard_map/ppermute | solution.py:30
  204.8 7.9 %collective-permute-start.28 = (bf16[320,256]{1,0:T(8,128)(2,1)S(1)}, bf16[320,256]{1,0:T(8,128)(2,1)S(1)}, u32[]{:S(2)}, u32[]{:S(2)}) collective-permute-start(bf16[320,256]{1,0:T(8,128)(2,1)S(1)} %copy-done.40), channel_id=1, source_target_pairs={{0,3},{1,2},{2,1},{3,0},{4,7},{5,6},{6,5},{7,4},{8,11},{9,10},{10,... | collective-permute-start | bytes 491528 | tf_op jit(solution)/shard_map/ppermute | solution.py:30
  208.6 21.9 %collective-permute-start.29 = (bf16[4,128,512]{2,1,0:T(8,128)(2,1)S(1)}, bf16[4,128,512]{2,1,0:T(8,128)(2,1)S(1)}, u32[]{:S(2)}, u32[]{:S(2)}) collective-permute-start(bf16[4,128,512]{2,1,0:T(8,128)(2,1)S(1)} %fusion.9), channel_id=1, source_target_pairs={{0,4},{4,0},{8,12},{12,8},{16,20},{20,16},{24,28},{28,24},{1,5},{5... | collective-permute-start | bytes 1572872 | tf_op jit(solution)/shard_map/ppermute | solution.py:66
  230.5 11.8 %collective-permute-start.30 = (bf16[2,320,1024]{2,1,0:T(8,128)(2,1)}, bf16[2,320,1024]{2,1,0:T(8,128)(2,1)}, u32[]{:S(2)}, u32[]{:S(2)}) collective-permute-start(bf16[2,320,1024]{2,1,0:T(8,128)(2,1)} %bitcast.106), channel_id=1, source_target_pairs={{0,1},{1,0},{2,3},{3,2},{4,5},{5,4},{6,7},{7,6},{8,9},{9,8},{10,11... | collective-permute-start | bytes 3932168 | tf_op jit(solution)/shard_map/ppermute | solution.py:30
  233.9 28.7 %collective-permute-start.24 = (bf16[320,1024]{1,0:T(8,128)(2,1)}, bf16[320,1024]{1,0:T(8,128)(2,1)}, u32[]{:S(2)}, u32[]{:S(2)}) collective-permute-start(bf16[320,1024]{1,0:T(8,128)(2,1)} %fusion.8), channel_id=1, source_target_pairs={{0,2},{1,3},{2,0},{3,1},{4,6},{5,7},{6,4},{7,5},{8,10},{9,11},{10,... | collective-permute-start | bytes 1966088 | tf_op jit(solution)/shard_map/ppermute | solution.py:30
  234.8 30.6 %collective-permute-start.35 = (bf16[4,128,896]{2,1,0:T(8,128)(2,1)}, bf16[4,128,896]{2,1,0:T(8,128)(2,1)}, u32[]{:S(2)}, u32[]{:S(2)}) collective-permute-start(bf16[4,128,896]{2,1,0:T(8,128)(2,1)} %get-tuple-element.114), channel_id=1, source_target_pairs={{0,4},{4,0},{8,12},{12,8},{16,20},{20,16},{24,28},{28,24},{1,5},{5... | collective-permute-start | bytes 2752520 | tf_op jit(solution)/shard_map/ppermute | solution.py:66
  238.5 8.4 %collective-permute-start.31 = (bf16[1,128,512]{2,1,0:T(8,128)(2,1)}, bf16[1,128,512]{2,1,0:T(8,128)(2,1)S(1)}, u32[]{:S(2)}, u32[]{:S(2)}) collective-permute-start(bf16[1,128,512]{2,1,0:T(8,128)(2,1)} %get-tuple-element.108), channel_id=1, source_target_pairs={{0,8},{4,12},{8,16},{12,20},{16,24},{20,28},{24,0},{28,4},{1,9},{5... | collective-permute-start | bytes 393224 | tf_op jit(solution)/shard_map/ppermute | solution.py:66
  238.5 9.1 %collective-permute-start.32 = (bf16[1,128,512]{2,1,0:T(8,128)(2,1)}, bf16[1,128,512]{2,1,0:T(8,128)(2,1)S(1)}, u32[]{:S(2)}, u32[]{:S(2)}) collective-permute-start(bf16[1,128,512]{2,1,0:T(8,128)(2,1)} %get-tuple-element.109), channel_id=1, source_target_pairs={{0,24},{4,28},{8,0},{12,4},{16,8},{20,12},{24,16},{28,20},{1,25},{... | collective-permute-start | bytes 393224 | tf_op jit(solution)/shard_map/ppermute | solution.py:66
  242.3 18.1 %collective-permute-start.33 = (bf16[1,128,512]{2,1,0:T(8,128)(2,1)}, bf16[1,128,512]{2,1,0:T(8,128)(2,1)S(1)}, u32[]{:S(2)}, u32[]{:S(2)}) collective-permute-start(bf16[1,128,512]{2,1,0:T(8,128)(2,1)} %get-tuple-element.110), channel_id=1, source_target_pairs={{0,16},{4,20},{8,24},{12,28},{16,0},{20,4},{24,8},{28,12},{1,17},{... | collective-permute-start | bytes 393224 | tf_op jit(solution)/shard_map/ppermute | solution.py:66
  260.4 13.5 %collective-permute-start.34 = (bf16[320,1024]{1,0:T(8,128)(2,1)}, bf16[320,1024]{1,0:T(8,128)(2,1)S(1)}, u32[]{:S(2)}, u32[]{:S(2)}) collective-permute-start(bf16[320,1024]{1,0:T(8,128)(2,1)} %fusion.2), channel_id=1, source_target_pairs={{0,2},{1,3},{2,0},{3,1},{4,6},{5,7},{6,4},{7,5},{8,10},{9,11},{10,... | collective-permute-start | bytes 1966088 | tf_op jit(solution)/shard_map/ppermute | solution.py:30
  267.9 21.8 %collective-permute-start.36 = (bf16[1,128,896]{2,1,0:T(8,128)(2,1)}, bf16[1,128,896]{2,1,0:T(8,128)(2,1)S(1)}, u32[]{:S(2)}, u32[]{:S(2)}) collective-permute-start(bf16[1,128,896]{2,1,0:T(8,128)(2,1)} %get-tuple-element.118), channel_id=1, source_target_pairs={{0,8},{4,12},{8,16},{12,20},{16,24},{20,28},{24,0},{28,4},{1,9},{5... | collective-permute-start | bytes 688136 | tf_op jit(solution)/shard_map/ppermute | solution.py:66
  267.9 21.8 %collective-permute-start.37 = (bf16[1,128,896]{2,1,0:T(8,128)(2,1)}, bf16[1,128,896]{2,1,0:T(8,128)(2,1)}, u32[]{:S(2)}, u32[]{:S(2)}) collective-permute-start(bf16[1,128,896]{2,1,0:T(8,128)(2,1)} %get-tuple-element.119), channel_id=1, source_target_pairs={{0,24},{4,28},{8,0},{12,4},{16,8},{20,12},{24,16},{28,20},{1,25},{... | collective-permute-start | bytes 688136 | tf_op jit(solution)/shard_map/ppermute | solution.py:66
  271.7 18.2 %collective-permute-start.38 = (bf16[1,128,896]{2,1,0:T(8,128)(2,1)}, bf16[1,128,896]{2,1,0:T(8,128)(2,1)}, u32[]{:S(2)}, u32[]{:S(2)}) collective-permute-start(bf16[1,128,896]{2,1,0:T(8,128)(2,1)} %get-tuple-element.120), channel_id=1, source_target_pairs={{0,16},{4,20},{8,24},{12,28},{16,0},{20,4},{24,8},{28,12},{1,17},{... | collective-permute-start | bytes 688136 | tf_op jit(solution)/shard_map/ppermute | solution.py:66
  277.7 9.4 %all-to-all-start.1 = ((bf16[4,32,1024]{2,1,0:T(8,128)(2,1)}), bf16[4,32,1024]{2,1,0:T(8,128)(2,1)S(1)}, u32[]{:S(2)}, u32[]{:S(2)}) async-start(bf16[4,32,1024]{2,1,0:T(8,128)(2,1)} %bitcast.46), calls=%async_computation.2 | async-start | bytes 524288 | tf_op jit(solution)/shard_map/all_to_all | solution.py:898
  292.7 10.5 %all-to-all-start.2 = ((bf16[4,32,1408]{2,1,0:T(8,128)(2,1)}), bf16[4,32,1408]{2,1,0:T(8,128)(2,1)S(1)}, u32[]{:S(2)}, u32[]{:S(2)}) async-start(bf16[4,32,1408]{2,1,0:T(8,128)(2,1)} %bitcast.94), calls=%async_computation.3 | async-start | bytes 720896 | tf_op jit(solution)/shard_map/all_to_all | solution.py:898
  (42 other events, 214.2 us)
Sparse Core Ops, SparseCore 0:
  10.1 72.4 all-gather.2
  84.8 48.1 all-gather.4
  172.6 101.4 reduce-scatter.1
